TPU v7x, 32 devices: a whole 2x2x4 slice. The times are simulated.
32 devices in a mesh: expert: 8 (over z, y), tensor: 4 (over x, core).
Axes of the slice: x: 2, y: 2, z: 4, core: 2. Of those that a mesh axis runs over, the one named last changes fastest.
Arguments:
- tokens: bfloat16 [8192, 1024], P('expert'), may hold values from -6 to 6
- cotangent: bfloat16 [8192, 1024], P('expert'), may hold values from -6 to 6
- routes: int32 [8192, 8], P('expert'), may hold values from 0 to 31, all different within a row; in each aligned block of 1024 rows (0 to 1023, 1024 to 2047, ...) at most 320 rows name the same one
- norm_gains: float32 [2, 1024], P(None, 'expert'), may hold values from 0.5 to 1.5
- gains_moment: float32 [2, 1024], P(None, 'expert'), may hold values from -64 to 64
- gains_second: float32 [2, 1024], P(None, 'expert'), may hold values from 4.096 to 65.536
- query_weight: float32 [1024, 1024], P('expert', 'tensor'), may hold values from -0.1875 to 0.1875
- query_moment: float32 [1024, 1024], P('expert', 'tensor'), may hold values from -16 to 16
- query_second: float32 [1024, 1024], P('expert', 'tensor'), may hold values from 0.36864 to 5.89824
- keyval_weight: float32 [2, 1024, 512], P(None, 'expert', 'tensor'), may hold values from -0.1875 to 0.1875
- keyval_moment: float32 [2, 1024, 512], P(None, 'expert', 'tensor'), may hold values from -32 to 32
- keyval_second: float32 [2, 1024, 512], P(None, 'expert', 'tensor'), may hold values from 1.024 to 16.384
- output_weight: float32 [1024, 1024], P('tensor', 'expert'), may hold values from -0.5 to 0.5
- output_moment: float32 [1024, 1024], P('tensor', 'expert'), may hold values from -16 to 16
- output_second: float32 [1024, 1024], P('tensor', 'expert'), may hold values from 0.36864 to 5.89824
- router_weight: float32 [1024, 32], P('expert'), may hold values from -0.09375 to 0.09375
- router_moment: float32 [1024, 32], P('expert'), may hold values from -320 to 320
- router_second: float32 [1024, 32], P('expert'), may hold values from 102.4 to 1638.4
- gateup_weight: float32 [32, 2, 1024, 512], P('expert', None, None, 'tensor'), may hold values from -0.1875 to 0.1875
- gateup_moment: float32 [32, 2, 1024, 512], P('expert', None, None, 'tensor'), may hold values from -16 to 16
- gateup_second: float32 [32, 2, 1024, 512], P('expert', None, None, 'tensor'), may hold values from 0.256 to 4.096
- down_weight: float32 [32, 512, 1024], P('expert', 'tensor'), may hold values from -1 to 1
- down_moment: float32 [32, 512, 1024], P('expert', 'tensor'), may hold values from -3 to 3
- down_second: float32 [32, 512, 1024], P('expert', 'tensor'), may hold values from 0.01024 to 0.16384
Outputs:
- block_out: bfloat16 [8192, 1024], P('expert')
- input_grad: bfloat16 [8192, 1024], P('expert')
- new_gains: float32 [2, 1024], P(None, 'expert')
- new_gains_moment: float32 [2, 1024], P(None, 'expert')
- new_gains_second: float32 [2, 1024], P(None, 'expert')
- new_query: float32 [1024, 1024], P('expert', 'tensor')
- new_query_moment: float32 [1024, 1024], P('expert', 'tensor')
- new_query_second: float32 [1024, 1024], P('expert', 'tensor')
- new_keyval: float32 [2, 1024, 512], P(None, 'expert', 'tensor')
- new_keyval_moment: float32 [2, 1024, 512], P(None, 'expert', 'tensor')
- new_keyval_second: float32 [2, 1024, 512], P(None, 'expert', 'tensor')
- new_output: float32 [1024, 1024], P('tensor', 'expert')
- new_output_moment: float32 [1024, 1024], P('tensor', 'expert')
- new_output_second: float32 [1024, 1024], P('tensor', 'expert')
- new_router: float32 [1024, 32], P('expert')
- new_router_moment: float32 [1024, 32], P('expert')
- new_router_second: float32 [1024, 32], P('expert')
- new_gateup: float32 [32, 2, 1024, 512], P('expert', None, None, 'tensor')
- new_gateup_moment: float32 [32, 2, 1024, 512], P('expert', None, None, 'tensor')
- new_gateup_second: float32 [32, 2, 1024, 512], P('expert', None, None, 'tensor')
- new_down: float32 [32, 512, 1024], P('expert', 'tensor')
- new_down_moment: float32 [32, 512, 1024], P('expert', 'tensor')
- new_down_second: float32 [32, 512, 1024], P('expert', 'tensor')
Inputs may be any that keep to these rules, and one draw needn't show every extreme that they name: `routes`: each row names 8 different experts. In each aligned block of 1024 rows (the rows of one device) no expert is named by more than 320 rows, a bound that some block reaches.
All inputs are finite; a program needn't handle non-finite values.
Results may differ from a plain program's by a relative error of at most 0.025.
Values may be sent and summed in bfloat16 or wider, within the bound.
No kernel may reach another device: no remote copies, remote signals or barrier semaphores. Data moves between devices by JAX's collectives and lax.ppermute only.
A program may use at most 384 MiB of HBM per device.

v0:
```python
import jax
import jax.numpy as jnp
from jax import lax
from jax.sharding import PartitionSpec as P

HEADS = 16
KV_HEADS = 8
HD = 64
EXPERTS = 32
TOPK = 8
STEP = 10
CAP = 320


NORM_EPS = 1e-06
BETA_ONE = 0.9
BETA_TWO = 0.999
ADAM_EPS = 1e-08
MATRIX_RATE = 0.08
GAIN_RATE = 0.6
MATRIX_DECAY = 0.1
NEG_LARGE = -1e30


def normalize(values):
    inverse = lax.rsqrt(jnp.mean(values * values, axis=-1, keepdims=True) + NORM_EPS)
    return (values * inverse, inverse)


def norm_backward(grad_unit, unit, inverse):
    return inverse * (grad_unit - unit * jnp.mean(grad_unit * unit, axis=-1, keepdims=True))


def rope_tables(length, head_size):
    half_size = head_size // 2
    frequency = 10000.0 ** (-(jnp.arange(half_size, dtype=jnp.float32) * 2.0) / head_size)
    angles = jnp.arange(length, dtype=jnp.float32)[:, None] * frequency[None, :]
    return (jnp.cos(angles), jnp.sin(angles))


def rotate(values, cosine_table, sine_table):
    half_size = values.shape[-1] // 2
    first_half = values[..., :half_size]
    second_half = values[..., half_size:]
    c = cosine_table[:, None, :]
    s = sine_table[:, None, :]
    return jnp.concatenate(
        [first_half * c - second_half * s, second_half * c + first_half * s], axis=-1
    )


def unrotate(values, cosine_table, sine_table):
    half_size = values.shape[-1] // 2
    first_half = values[..., :half_size]
    second_half = values[..., half_size:]
    c = cosine_table[:, None, :]
    s = sine_table[:, None, :]
    return jnp.concatenate(
        [first_half * c + second_half * s, second_half * c - first_half * s], axis=-1
    )


def slot_targets(routes):
    flat_ids = routes.reshape(-1)
    onehot = (flat_ids[:, None] == jnp.arange(EXPERTS, dtype=jnp.int32)[None, :]).astype(jnp.int32)
    slot_index = jnp.sum(jnp.cumsum(onehot, axis=0) * onehot, axis=1) - 1
    return flat_ids * CAP + slot_index


def expert_forward(row_data, gateup_low, down_low):
    gate_pre = jnp.einsum(
        "erd,edf->erf", row_data, gateup_low[:, 0], preferred_element_type=jnp.float32
    )
    up_pre = jnp.einsum(
        "erd,edf->erf", row_data, gateup_low[:, 1], preferred_element_type=jnp.float32
    )
    activation = (jax.nn.silu(gate_pre) * up_pre).astype(jnp.bfloat16)
    partial_out = jnp.einsum(
        "erf,efd->erd", activation, down_low, preferred_element_type=jnp.float32
    )
    return (gate_pre, up_pre, activation, partial_out)


def expert_backward(row_data, grad_rows, gate_pre, up_pre, activation, gateup_low, down_low):
    grad_act = jnp.einsum("erd,efd->erf", grad_rows, down_low, preferred_element_type=jnp.float32)
    sigmoid_gate = jax.nn.sigmoid(gate_pre)
    grad_gate = (grad_act * up_pre * sigmoid_gate * (1.0 + gate_pre * (1.0 - sigmoid_gate))).astype(
        jnp.bfloat16
    )
    grad_up = (grad_act * gate_pre * sigmoid_gate).astype(jnp.bfloat16)
    grad_down = jnp.einsum(
        "erf,erd->efd", activation, grad_rows, preferred_element_type=jnp.float32
    )
    grad_gate_w = jnp.einsum(
        "erd,erf->edf", row_data, grad_gate, preferred_element_type=jnp.float32
    )
    grad_up_w = jnp.einsum("erd,erf->edf", row_data, grad_up, preferred_element_type=jnp.float32)
    grad_in = jnp.einsum(
        "erf,edf->erd", grad_gate, gateup_low[:, 0], preferred_element_type=jnp.float32
    )
    grad_in = grad_in + jnp.einsum(
        "erf,edf->erd", grad_up, gateup_low[:, 1], preferred_element_type=jnp.float32
    )
    return (jnp.stack([grad_gate_w, grad_up_w], axis=1), grad_down, grad_in)


def adamw_update(weight, moment, second, gradient, rate, decay):
    moment_new = BETA_ONE * moment + (1.0 - BETA_ONE) * gradient
    second_new = BETA_TWO * second + (1.0 - BETA_TWO) * gradient * gradient
    fix_one = 1.0 - BETA_ONE**STEP
    fix_two = 1.0 - BETA_TWO**STEP
    update = moment_new / fix_one / (jnp.sqrt(second_new / fix_two) + ADAM_EPS)
    return (weight - rate * (update + decay * weight), moment_new, second_new)


def body(
    tokens,
    cotangent,
    routes,
    norm_gains,
    gains_moment,
    gains_second,
    query_weight,
    query_moment,
    query_second,
    keyval_weight,
    keyval_moment,
    keyval_second,
    output_weight,
    output_moment,
    output_second,
    router_weight,
    router_moment,
    router_second,
    gateup_weight,
    gateup_moment,
    gateup_second,
    down_weight,
    down_moment,
    down_second,
):
    length = tokens.shape[0]
    width = tokens.shape[1]
    gains_all, query_all, keyval_all, output_all, router_all = (
        lax.all_gather(norm_gains, "expert", axis=1, tiled=True),
        lax.all_gather(query_weight, "expert", axis=0, tiled=True),
        lax.all_gather(keyval_weight, "expert", axis=1, tiled=True),
        lax.all_gather(output_weight, "expert", axis=1, tiled=True),
        lax.all_gather(router_weight, "expert", axis=0, tiled=True),
    )
    query_low = query_all.astype(jnp.bfloat16)
    key_low = keyval_all[0].astype(jnp.bfloat16)
    value_low = keyval_all[1].astype(jnp.bfloat16)
    output_low = output_all.astype(jnp.bfloat16)
    router_low = router_all.astype(jnp.bfloat16)
    local_heads = query_low.shape[1] // HD
    local_groups = key_low.shape[1] // HD
    group_size = HEADS // KV_HEADS
    score_scale = HD ** (-0.5)
    x = tokens.astype(jnp.float32)
    unit_one, inverse_one = normalize(x)
    a = (unit_one * gains_all[0]).astype(jnp.bfloat16)
    query_pre = jnp.dot(a, query_low, preferred_element_type=jnp.float32)
    key_pre = jnp.dot(a, key_low, preferred_element_type=jnp.float32)
    value_pre = jnp.dot(a, value_low, preferred_element_type=jnp.float32)
    cosine_table, sine_table = rope_tables(length, HD)
    query_rot = rotate(query_pre.reshape(length, local_heads, HD), cosine_table, sine_table).astype(
        jnp.bfloat16
    )
    query_rot = query_rot.reshape(length, local_groups, group_size, HD)
    key_rot = rotate(key_pre.reshape(length, local_groups, HD), cosine_table, sine_table).astype(
        jnp.bfloat16
    )
    value_rot = value_pre.astype(jnp.bfloat16).reshape(length, local_groups, HD)
    block_rows = min(512, length)
    mixture_parts = []
    lse_parts = []
    for block_begin in range(0, length, block_rows):
        block_end = block_begin + block_rows
        query_block = query_rot[block_begin:block_end]
        scores = (
            jnp.einsum(
                "qhgd,khd->hgqk",
                query_block,
                key_rot[:block_end],
                preferred_element_type=jnp.float32,
            )
            * score_scale
        )
        causal = (block_begin + jnp.arange(block_rows))[:, None] >= jnp.arange(block_end)[None, :]
        scores = jnp.where(causal, scores, NEG_LARGE)
        row_peak = jnp.max(scores, axis=-1, keepdims=True)
        exponent = jnp.exp(scores - row_peak)
        row_total = jnp.sum(exponent, axis=-1, keepdims=True)
        lse_parts.append(row_peak + jnp.log(row_total))
        weights_block = (exponent / row_total).astype(jnp.bfloat16)
        mixture_parts.append(
            jnp.einsum(
                "hgqk,khd->qhgd",
                weights_block,
                value_rot[:block_end],
                preferred_element_type=jnp.float32,
            )
        )
    mixture = (
        jnp.concatenate(mixture_parts, axis=0)
        .reshape(length, local_heads * HD)
        .astype(jnp.bfloat16)
    )
    attention = lax.psum(jnp.dot(mixture, output_low, preferred_element_type=jnp.float32), "tensor")
    x_mid = x + attention
    unit_two, inverse_two = normalize(x_mid)
    b = (unit_two * gains_all[1]).astype(jnp.bfloat16)
    logits = jnp.dot(b, router_low, preferred_element_type=jnp.float32)
    chosen = jnp.take_along_axis(logits, routes, axis=1)
    gating = jax.nn.softmax(chosen, axis=-1)
    targets = slot_targets(routes)
    repeated = jnp.repeat(b, TOPK, axis=0)
    dispatched = (
        jnp.zeros((EXPERTS * CAP, width), jnp.bfloat16)
        .at[targets]
        .set(repeated)
        .reshape(EXPERTS, CAP, width)
    )
    gateup_low = gateup_weight.astype(jnp.bfloat16)
    down_low = down_weight.astype(jnp.bfloat16)
    all_gateup, all_down = (gateup_low, down_low)
    slot_rows = CAP
    row_data = lax.all_to_all(dispatched, "expert", split_axis=0, concat_axis=1, tiled=True)
    gate_pre, up_pre, activation, partial_out = expert_forward(row_data, all_gateup, all_down)
    local_experts = row_data.shape[0]
    sources = row_data.shape[1] // slot_rows
    share = lax.psum_scatter(
        partial_out.reshape(local_experts, sources, CAP, width),
        "tensor",
        scatter_dimension=2,
        tiled=True,
    ).astype(jnp.bfloat16)
    arrived = lax.all_to_all(share, "expert", split_axis=1, concat_axis=0, tiled=True)
    expert_out = lax.all_gather(arrived, "tensor", axis=2, tiled=True).reshape(EXPERTS * CAP, width)
    picked = expert_out[targets].reshape(length, TOPK, width)
    moe_sum = jnp.sum(gating[:, :, None] * picked.astype(jnp.float32), axis=1)
    block_out = (x_mid + moe_sum).astype(jnp.bfloat16)
    grad_out = cotangent.astype(jnp.float32)
    grad_gating = jnp.einsum("lkd,ld->lk", picked, cotangent, preferred_element_type=jnp.float32)
    grad_picked = (
        (gating[:, :, None] * grad_out[:, None, :])
        .astype(jnp.bfloat16)
        .reshape(length * TOPK, width)
    )
    grad_chosen = gating * (grad_gating - jnp.sum(gating * grad_gating, axis=1, keepdims=True))
    expert_ids = jnp.arange(EXPERTS, dtype=jnp.int32)
    grad_logits = jnp.sum(
        grad_chosen[:, :, None]
        * (routes[:, :, None] == expert_ids[None, None, :]).astype(jnp.float32),
        axis=1,
    ).astype(jnp.bfloat16)
    grad_router = jnp.einsum("ld,le->de", b, grad_logits, preferred_element_type=jnp.float32)
    grad_b = jnp.einsum("le,de->ld", grad_logits, router_low, preferred_element_type=jnp.float32)
    grad_buffer = (
        jnp.zeros((EXPERTS * CAP, width), jnp.bfloat16)
        .at[targets]
        .set(grad_picked)
        .reshape(EXPERTS, CAP, width)
    )
    grad_rows = lax.all_to_all(grad_buffer, "expert", split_axis=0, concat_axis=1, tiled=True)
    grad_gateup, grad_down, grad_in = expert_backward(
        row_data, grad_rows, gate_pre, up_pre, activation, all_gateup, all_down
    )
    grad_share = lax.psum_scatter(
        grad_in.reshape(local_experts, sources, CAP, width),
        "tensor",
        scatter_dimension=2,
        tiled=True,
    ).astype(jnp.bfloat16)
    grad_arrived = lax.all_to_all(grad_share, "expert", split_axis=1, concat_axis=0, tiled=True)
    grad_dispatched = lax.all_gather(grad_arrived, "tensor", axis=2, tiled=True).reshape(
        EXPERTS * CAP, width
    )
    grad_b = grad_b + jnp.sum(
        grad_dispatched[targets].reshape(length, TOPK, width).astype(jnp.float32), axis=1
    )
    grad_gain_two = jnp.sum(grad_b * unit_two, axis=0)
    grad_mid = grad_out + norm_backward(grad_b * gains_all[1], unit_two, inverse_two)
    grad_attention = grad_mid.astype(jnp.bfloat16)
    grad_output_w = jnp.einsum(
        "lf,ld->fd", mixture, grad_attention, preferred_element_type=jnp.float32
    )
    grad_mixture = jnp.einsum(
        "ld,fd->lf", grad_attention, output_low, preferred_element_type=jnp.float32
    ).astype(jnp.bfloat16)
    grad_mixture = grad_mixture.reshape(length, local_groups, group_size, HD)
    grad_key = jnp.zeros((length, local_groups, HD), jnp.float32)
    grad_value = jnp.zeros((length, local_groups, HD), jnp.float32)
    grad_query_parts = []
    for block_index, block_begin in enumerate(range(0, length, block_rows)):
        block_end = block_begin + block_rows
        query_block = query_rot[block_begin:block_end]
        key_block = key_rot[:block_end]
        grad_block = grad_mixture[block_begin:block_end]
        scores = (
            jnp.einsum("qhgd,khd->hgqk", query_block, key_block, preferred_element_type=jnp.float32)
            * score_scale
        )
        causal = (block_begin + jnp.arange(block_rows))[:, None] >= jnp.arange(block_end)[None, :]
        weights_block = jnp.where(causal, jnp.exp(scores - lse_parts[block_index]), 0.0)
        grad_weights = jnp.einsum(
            "qhgd,khd->hgqk", grad_block, value_rot[:block_end], preferred_element_type=jnp.float32
        )
        row_delta = jnp.sum(weights_block * grad_weights, axis=-1, keepdims=True)
        grad_scores = (weights_block * (grad_weights - row_delta)).astype(jnp.bfloat16)
        grad_query_parts.append(
            jnp.einsum("hgqk,khd->qhgd", grad_scores, key_block, preferred_element_type=jnp.float32)
            * score_scale
        )
        grad_key = grad_key.at[:block_end].add(
            jnp.einsum(
                "hgqk,qhgd->khd", grad_scores, query_block, preferred_element_type=jnp.float32
            )
            * score_scale
        )
        grad_value = grad_value.at[:block_end].add(
            jnp.einsum(
                "hgqk,qhgd->khd",
                weights_block.astype(jnp.bfloat16),
                grad_block,
                preferred_element_type=jnp.float32,
            )
        )
    grad_query = jnp.concatenate(grad_query_parts, axis=0).reshape(length, local_heads, HD)
    grad_query_low = (
        unrotate(grad_query, cosine_table, sine_table)
        .astype(jnp.bfloat16)
        .reshape(length, local_heads * HD)
    )
    grad_key_low = (
        unrotate(grad_key, cosine_table, sine_table)
        .astype(jnp.bfloat16)
        .reshape(length, local_groups * HD)
    )
    grad_value_low = grad_value.astype(jnp.bfloat16).reshape(length, local_groups * HD)
    grad_query_w = jnp.einsum("ld,lf->df", a, grad_query_low, preferred_element_type=jnp.float32)
    grad_keyval_w = jnp.stack(
        [
            jnp.einsum("ld,lf->df", a, grad_key_low, preferred_element_type=jnp.float32),
            jnp.einsum("ld,lf->df", a, grad_value_low, preferred_element_type=jnp.float32),
        ]
    )
    grad_a_local = jnp.einsum(
        "lf,df->ld", grad_query_low, query_low, preferred_element_type=jnp.float32
    )
    grad_a_local = grad_a_local + jnp.einsum(
        "lf,df->ld", grad_key_low, key_low, preferred_element_type=jnp.float32
    )
    grad_a_local = grad_a_local + jnp.einsum(
        "lf,df->ld", grad_value_low, value_low, preferred_element_type=jnp.float32
    )
    grad_a = lax.psum(grad_a_local.astype(jnp.bfloat16), "tensor").astype(jnp.float32)
    grad_gain_one = jnp.sum(grad_a * unit_one, axis=0)
    input_grad = (grad_mid + norm_backward(grad_a * gains_all[0], unit_one, inverse_one)).astype(
        jnp.bfloat16
    )
    grad_gains = jnp.stack([grad_gain_one, grad_gain_two])
    gains_sum, query_sum, keyval_sum, output_sum, router_sum = (
        lax.psum_scatter(
            grad_gains.astype(jnp.bfloat16), "expert", scatter_dimension=1, tiled=True
        ).astype(jnp.float32),
        lax.psum_scatter(
            grad_query_w.astype(jnp.bfloat16), "expert", scatter_dimension=0, tiled=True
        ).astype(jnp.float32),
        lax.psum_scatter(
            grad_keyval_w.astype(jnp.bfloat16), "expert", scatter_dimension=1, tiled=True
        ).astype(jnp.float32),
        lax.psum_scatter(
            grad_output_w.astype(jnp.bfloat16), "expert", scatter_dimension=1, tiled=True
        ).astype(jnp.float32),
        lax.psum_scatter(
            grad_router.astype(jnp.bfloat16), "expert", scatter_dimension=0, tiled=True
        ).astype(jnp.float32),
    )
    new_gains = adamw_update(norm_gains, gains_moment, gains_second, gains_sum, GAIN_RATE, 0.0)
    new_query = adamw_update(
        query_weight, query_moment, query_second, query_sum, MATRIX_RATE, MATRIX_DECAY
    )
    new_keyval = adamw_update(
        keyval_weight, keyval_moment, keyval_second, keyval_sum, MATRIX_RATE, MATRIX_DECAY
    )
    new_output = adamw_update(
        output_weight, output_moment, output_second, output_sum, MATRIX_RATE, MATRIX_DECAY
    )
    new_router = adamw_update(
        router_weight, router_moment, router_second, router_sum, MATRIX_RATE, MATRIX_DECAY
    )
    new_gateup = adamw_update(
        gateup_weight, gateup_moment, gateup_second, grad_gateup, MATRIX_RATE, MATRIX_DECAY
    )
    new_down = adamw_update(
        down_weight, down_moment, down_second, grad_down, MATRIX_RATE, MATRIX_DECAY
    )
    return (
        block_out,
        input_grad,
        new_gains[0],
        new_gains[1],
        new_gains[2],
        new_query[0],
        new_query[1],
        new_query[2],
        new_keyval[0],
        new_keyval[1],
        new_keyval[2],
        new_output[0],
        new_output[1],
        new_output[2],
        new_router[0],
        new_router[1],
        new_router[2],
        new_gateup[0],
        new_gateup[1],
        new_gateup[2],
        new_down[0],
        new_down[1],
        new_down[2],
    )


def solution(mesh):
    placed = (
        P("expert", None),
        P("expert", None),
        P("expert", None),
        P(None, "expert"),
        P(None, "expert"),
        P(None, "expert"),
        P("expert", "tensor"),
        P("expert", "tensor"),
        P("expert", "tensor"),
        P(None, "expert", "tensor"),
        P(None, "expert", "tensor"),
        P(None, "expert", "tensor"),
        P("tensor", "expert"),
        P("tensor", "expert"),
        P("tensor", "expert"),
        P("expert", None),
        P("expert", None),
        P("expert", None),
        P("expert", None, None, "tensor"),
        P("expert", None, None, "tensor"),
        P("expert", None, None, "tensor"),
        P("expert", "tensor", None),
        P("expert", "tensor", None),
        P("expert", "tensor", None),
    )
    return jax.shard_map(
        body,
        mesh=mesh,
        in_specs=placed,
        out_specs=(
            P("expert", None),
            P("expert", None),
            P(None, "expert"),
            P(None, "expert"),
            P(None, "expert"),
            P("expert", "tensor"),
            P("expert", "tensor"),
            P("expert", "tensor"),
            P(None, "expert", "tensor"),
            P(None, "expert", "tensor"),
            P(None, "expert", "tensor"),
            P("tensor", "expert"),
            P("tensor", "expert"),
            P("tensor", "expert"),
            P("expert", None),
            P("expert", None),
            P("expert", None),
            P("expert", None, None, "tensor"),
            P("expert", None, None, "tensor"),
            P("expert", None, None, "tensor"),
            P("expert", "tensor", None),
            P("expert", "tensor", None),
            P("expert", "tensor", None),
        ),
        check_vma=False,
    )
```

profile of v0, /device:TPU:0, one launch (start us, length us, event | category | flops | bytes accessed | tf_op | source)
XLA Modules:
  0.0 2995.7 jit_solution(3496697511436505631)
XLA Ops:
  7.4 2.3 fusion.31
  9.7 22.5 all_gather.21
  35.5 31.5 %all_gather.22 = bf16[2,1024,128]{2,1,0:T(8,128)(2,1)S(1)} all-gather(bf16[2,128,128]{2,1,0:T(8,128)(2,1)S(1)} %convert.77), channel_id=1, replica_groups=mesh['expert'=8,'tensor'=4] {'expert'}, dimensions={1}, use_global_device_ids=true | all-gather | bytes 589824 | tf_op jit(solution)/shard_map/all_gather | solution.py:147
  67.9 28.0 all_gather.24
  95.9 31.3 %all_gather.23 = bf16[1024,256]{1,0:T(8,128)(2,1)S(1)} all-gather(bf16[128,256]{1,0:T(8,128)(2,1)S(1)} %convert.78), channel_id=1, replica_groups=mesh['expert'=8,'tensor'=4] {'expert'}, dimensions={0}, use_global_device_ids=true | all-gather | bytes 589824 | tf_op jit(solution)/shard_map/all_gather | solution.py:146
  136.1 2.3 fusion.18
  139.4 2.5 fusion.78
  142.8 2.8 fusion.164
  148.1 17.1 reduce-window.6
  168.1 60.4 %all-reduce.5.cloned.1.call-done = f32[1024,1024]{1,0:T(8,128)} async-done(((f32[1024,1024]{1,0:T(8,128)}), f32[1024,1024]{1,0:T(8,128)}) %all-reduce.5.cloned.1.call-update) | async-done | bytes 4194320 | tf_op jit(solution)/shard_map/psum | solution.py:210
  228.5 2.8 multiply_reduce_fusion.3
  231.3 2.0 copy-done.4
  233.7 48.1 %scatter_custom_fusion = bf16[10240,1024]{1,0:T(8,128)(2,1)} fusion(s32[8192]{0:T(1024)S(1)} %bitcast.363, bf16[]{:T(256)} %constant.243.clone.1, bf16[1024,1024]{1,0:T(8,128)(2,1)S(1)} %multiply_convert_fusion.3), kind=kCustom, calls=%fused_computation.13 | custom fusion | bytes 23068674 | tf_op jit(solution)/shard_map/scatter | solution.py:222
  281.8 6.1 all-to-all-start
  287.9 3.8 copy.239
  291.8 448.9 %all-to-all-done = bf16[32,320,1024]{2,1,0:T(8,128)(2,1)} async-done(((bf16[32,320,1024]{2,1,0:T(8,128)(2,1)}), bf16[32,320,1024]{2,1,0:T(8,128)(2,1)}, u32[]{:S(2)}, u32[]{:S(2)}) %all-to-all-start) | async-done | bytes 20971552 | tf_op jit(solution)/shard_map/all_to_all | solution.py:229
  740.7 10.8 copy.178
  751.6 7.0 copy-done
  758.6 8.4 fusion.85
  766.9 13.5 multiply_convert_fusion.2
  780.5 16.3 fusion.89
  796.7 29.2 copy.180
  826.0 287.2 %reduce-scatter.14.cloned.1.call-done = f32[4,8,80,1024]{3,2,0,1:T(8,128)} async-done(((f32[4,8,320,1024]{3,2,0,1:T(8,128)}), f32[4,8,80,1024]{3,2,0,1:T(8,128)}) %reduce-scatter.14.cloned.1.call-update) | async-done | bytes 10485776 | tf_op jit(solution)/shard_map/reduce_scatter | solution.py:233
  1113.3 4.8 convert_element_type.189
  1118.1 121.1 %all_to_all.72 = bf16[4,8,80,1024]{3,2,0,1:T(8,128)(2,1)} all-to-all(bf16[4,8,80,1024]{3,2,0,1:T(8,128)(2,1)S(1)} %convert_element_type.189), channel_id=1, replica_groups=mesh['expert'=8,'tensor'=4] {'expert'}, dimensions={1} | all-to-all | bytes 10485760 | tf_op jit(solution)/shard_map/all_to_all | solution.py:239
  1240.3 4.3 convert_element_type.192
  1244.6 26.0 all_gather.25
  1272.0 65.9 %gather_fusion.2 = f32[8192]{0:T(1024)S(1)} fusion(f32[1024,32]{0,1:T(8,128)S(1)} %fusion.167, s32[8192]{0:T(1024)S(1)} %reshape.448), kind=kCustom, calls=%fused_computation.2 | custom fusion | bytes 131072 | tf_op jit(solution)/shard_map/jit(take_along_axis)/gather | solution.py:215
  1338.5 30.4 %all-gather.3.cloned.1.call-done = bf16[32,1,320,1024]{3,2,0,1:T(8,128)(2,1)} async-done(((bf16[32,1,80,1024]{3,2,0,1:T(8,128)(2,1)}), bf16[32,1,320,1024]{3,2,0,1:T(8,128)(2,1)}) %all-gather.3.cloned.1.call-update) | async-done | bytes 20971536 | tf_op jit(solution)/shard_map/all_gather | solution.py:240
  1368.9 50.4 %gather_fusion = bf16[8192,1024]{1,0:T(8,128)(2,1)} fusion(bf16[10240,1024]{1,0:T(8,128)(2,1)} %bitcast.321, s32[8192]{0:T(1024)S(1)} %copy-done.57), kind=kCustom, calls=%fused_computation | custom fusion | bytes 33587200 | tf_op jit(solution)/shard_map/gather | solution.py:241
  1419.3 8.7 fusion.3
  1428.8 50.9 %scatter_custom_fusion.1 = bf16[10240,1024]{1,0:T(8,128)(2,1)} fusion(s32[8192]{0:T(1024)} %bitcast.365, f32[1024,1024]{1,0:T(8,128)} %convert_element_type.192, f32[8192]{0:T(1024)S(1)} %mul.794, bf16[]{:T(256)} %constant.243.clone.1), kind=kCustom, calls=%fused_computation.10 | custom fusion | flops 16777216 | bytes 25199104 | tf_op jit(solution)/shard_map/scatter | solution.py:263
  1479.7 458.8 %all_to_all.73 = bf16[32,320,1024]{2,1,0:T(8,128)(2,1)S(1)} all-to-all(bf16[32,320,1024]{2,1,0:T(8,128)(2,1)} %bitcast.331), channel_id=1, replica_groups=mesh['expert'=8,'tensor'=4] {'expert'}, dimensions={0} | all-to-all | bytes 41943040 | tf_op jit(solution)/shard_map/all_to_all | solution.py:266
  1938.5 7.2 copy.182
  1945.7 15.0 multiply_convert_fusion
  1960.7 16.3 fusion.84
  1977.0 27.5 convolution_add_fusion
  2004.5 29.2 copy.183
  2033.7 287.0 %reduce-scatter.16.cloned.1.call-done = f32[4,8,80,1024]{3,2,0,1:T(8,128)} async-done(((f32[4,8,320,1024]{3,2,0,1:T(8,128)}), f32[4,8,80,1024]{3,2,0,1:T(8,128)}) %reduce-scatter.16.cloned.1.call-update) | async-done | bytes 10485776 | tf_op jit(solution)/shard_map/reduce_scatter | solution.py:270
  2320.7 7.2 convert_element_type.197
  2327.9 5.7 all-to-all-start.3
  2335.2 116.3 %all-to-all-done.3 = bf16[4,8,80,1024]{3,2,0,1:T(8,128)(2,1)} async-done(((bf16[4,8,80,1024]{3,2,0,1:T(8,128)(2,1)}), bf16[4,8,80,1024]{3,2,0,1:T(8,128)(2,1)}, u32[]{:S(2)}, u32[]{:S(2)}) %all-to-all-start.3) | async-done | bytes 5242912 | tf_op jit(solution)/shard_map/all_to_all | solution.py:276
  2451.7 15.8 multiply_reduce_fusion
  2469.0 19.6 multiply_subtract_fusion.1
  2488.7 109.4 %all-gather.5.cloned.1.call-done = bf16[32,1,320,1024]{3,2,0,1:T(8,128)(2,1)} async-done(((bf16[32,1,80,1024]{3,2,0,1:T(8,128)(2,1)}), bf16[32,1,320,1024]{3,2,0,1:T(8,128)(2,1)}) %all-gather.5.cloned.1.call-update) | async-done | bytes 20971536 | tf_op jit(solution)/shard_map/all_gather | solution.py:277
  2598.1 50.3 %gather_fusion.1 = bf16[8192,1024]{1,0:T(8,128)(2,1)} fusion(bf16[10240,1024]{1,0:T(8,128)(2,1)} %bitcast.320, s32[8192]{0:T(1024)S(1)} %copy-done.58), kind=kCustom, calls=%fused_computation.1 | custom fusion | bytes 33587200 | tf_op jit(solution)/shard_map/gather | solution.py:281
  2648.4 13.4 convert_reduce_fusion
  2664.7 2.5 multiply_add_fusion
  2678.0 5.6 fusion.11
  2683.9 2.6 fusion.13
  2691.5 1.9 fusion.65
  2693.4 2.2 add_convert_fusion
  2695.7 13.4 convolution_bitcast_fusion
  2710.7 12.9 convolution_bitcast_fusion.1
  2726.1 7.8 multiply_subtract_fusion
  2734.0 2.3 copy.197
  2736.2 2.3 copy.198
  2738.5 2.3 copy.199
  2741.9 51.5 %all-reduce.7.cloned.1.call-done = bf16[1024,1024]{1,0:T(8,128)(2,1)} async-done(((bf16[1024,1024]{1,0:T(8,128)(2,1)}), bf16[1024,1024]{1,0:T(8,128)(2,1)}) %all-reduce.7.cloned.1.call-update) | async-done | bytes 2097168 | tf_op jit(solution)/shard_map/psum | solution.py:358
  2793.3 3.0 fusion.30
  2798.2 4.6 fusion.27
  2802.8 56.3 %reduce-scatter.18.cloned.1.call-done = bf16[128,256]{1,0:T(8,128)(2,1)} async-done(((bf16[1024,256]{1,0:T(8,128)(2,1)}), bf16[128,256]{1,0:T(8,128)(2,1)}) %reduce-scatter.18.cloned.1.call-update) | async-done | bytes 65552 | tf_op jit(solution)/shard_map/reduce_scatter | solution.py:368
  2860.7 62.6 %reduce-scatter.20.cloned.1.call-done = bf16[2,128,128]{2,1,0:T(8,128)(2,1)} async-done(((bf16[2,1024,128]{2,1,0:T(8,128)(2,1)}), bf16[2,128,128]{2,1,0:T(8,128)(2,1)}) %reduce-scatter.20.cloned.1.call-update) | async-done | bytes 65552 | tf_op jit(solution)/shard_map/reduce_scatter | solution.py:371
  2924.9 62.3 %reduce-scatter.22.cloned.1.call-done = bf16[128,2]{1,0:T(8,128)(2,1)} async-done(((bf16[1024,2]{1,0:T(8,128)(2,1)}), bf16[128,2]{1,0:T(8,128)(2,1)}) %reduce-scatter.22.cloned.1.call-update) | async-done | bytes 528
  (306 shorter events, 57.7 us)
Async XLA Ops:
  7.2 120.5 %copy-start.7 = (bf16[1024,1024]{1,0:T(8,128)(2,1)S(1)}, bf16[1024,1024]{1,0:T(8,128)(2,1)}, u32[]{:S(2)}) copy-start(bf16[1024,1024]{1,0:T(8,128)(2,1)} %param.36) | copy-start | bytes 6291460
  7.2 221.2 %all-reduce.5.cloned.1.call-start = ((), (), s32[]{:S(2)}) async-start(), calls=%async_computation.11 | async-start | bytes 8388608 | tf_op jit(solution)/shard_map/psum | solution.py:210
  7.4 125.6 %copy-start.20 = (pred[512,512]{0,1:T(8,128)(4,1)}, pred[512,512]{0,1:T(8,128)(4,1)S(1)}, u32[]{:S(2)}) copy-start(pred[512,512]{0,1:T(8,128)(4,1)S(1)} %iota_compare_fusion.4) | copy-start | bytes 786436
  9.6 118.6 %copy-start.71 = (f32[1024]{0:T(1024)}, f32[1024]{0:T(1024)S(1)}, u32[]{:S(2)}) copy-start(f32[1024]{0:T(1024)S(1)} %add_rsqrt_fusion.1) | copy-start | bytes 12292
  32.2 96.0 %copy-start.73 = (f32[1,1024]{1,0:T(1,128)}, f32[1,1024]{1,0:T(1,128)S(1)}, u32[]{:S(2)}) copy-start(f32[1,1024]{1,0:T(1,128)S(1)} %get-tuple-element.248) | copy-start | bytes 12292
  32.2 199.1 %copy-start.77 = (f32[1,1024]{1,0:T(1,128)}, f32[1,1024]{1,0:T(1,128)S(1)}, u32[]{:S(2)}) copy-start(f32[1,1024]{1,0:T(1,128)S(1)} %get-tuple-element.247) | copy-start | bytes 12292
  35.5 95.4 %copy-start.34 = (f32[1024,32]{0,1:T(8,128)}, f32[1024,32]{0,1:T(8,128)S(1)}, u32[]{:S(2)}) copy-start(f32[1024,32]{0,1:T(8,128)S(1)} %get-tuple-element.249) | copy-start | bytes 393220
  35.5 95.4 %copy-start.36 = (f32[1024,32]{0,1:T(8,128)}, f32[1024,32]{0,1:T(8,128)S(1)}, u32[]{:S(2)}) copy-start(f32[1024,32]{0,1:T(8,128)S(1)} %get-tuple-element.250) | copy-start | bytes 393220
  67.0 62.1 %copy-start.32 = (bf16[2,1024,128]{2,1,0:T(8,128)(2,1)}, bf16[2,1024,128]{2,1,0:T(8,128)(2,1)S(1)}, u32[]{:S(2)}) copy-start(bf16[2,1024,128]{2,1,0:T(8,128)(2,1)S(1)} %all_gather.22) | copy-start | bytes 1572868
  95.9 46.0 %copy-start.30 = (bf16[256,1024]{1,0:T(8,128)(2,1)}, bf16[256,1024]{1,0:T(8,128)(2,1)S(1)}, u32[]{:S(2)}) copy-start(bf16[256,1024]{1,0:T(8,128)(2,1)S(1)} %all_gather.24) | copy-start | bytes 1572868
  95.9 33.2 %copy-start.59 = (bf16[128,1024]{1,0:T(8,128)(2,1)S(1)}, bf16[128,1024]{1,0:T(8,128)(2,1)}, u32[]{:S(2)}) copy-start(bf16[128,1024]{1,0:T(8,128)(2,1)} %copy.169) | copy-start | bytes 786436
  127.6 10.8 copy-start.15
  129.1 9.3 copy-start.44
  168.1 1102.5 %copy-start.60 = (s32[8192,1]{0,1:T(1,128)}, s32[8192,1]{0,1:T(1,128)S(1)}, u32[]{:S(2)}) copy-start(s32[8192,1]{0,1:T(1,128)S(1)} %compare_select_fusion) | copy-start | bytes 98308
  231.3 50.6 %copy-start.75 = (f32[1024]{0:T(1024)}, f32[1024]{0:T(1024)S(1)}, u32[]{:S(2)}) copy-start(f32[1024]{0:T(1024)S(1)} %add_rsqrt_fusion) | copy-start | bytes 12292
  233.7 1037.5 %copy-start.9 = (bf16[1024,1024]{1,0:T(8,128)(2,1)}, bf16[1024,1024]{1,0:T(8,128)(2,1)S(1)}, u32[]{:S(2)}) copy-start(bf16[1024,1024]{1,0:T(8,128)(2,1)S(1)} %multiply_convert_fusion.3) | copy-start | bytes 6291460
  281.8 458.9 %all-to-all-start = ((bf16[32,320,1024]{2,1,0:T(8,128)(2,1)}), bf16[32,320,1024]{2,1,0:T(8,128)(2,1)}, u32[]{:S(2)}, u32[]{:S(2)}) async-start(bf16[32,320,1024]{2,1,0:T(8,128)(2,1)} %bitcast.330), calls=%async_computation | async-start | bytes 41943040 | tf_op jit(solution)/shard_map/all_to_all | solution.py:229
  287.9 825.4 %reduce-scatter.14.cloned.1.call-start = ((), (), s32[]{:S(2)}) async-start(), calls=%async_computation.12 | async-start | bytes 52428800 | tf_op jit(solution)/shard_map/reduce_scatter | solution.py:233
  766.9 13.5 copy-start.22
  780.4 16.3 copy-start.17
  826.0 542.9 %all-gather.3.cloned.1.call-start = ((), (), s32[]{:S(2)}) async-start(), calls=%async_computation.13 | async-start | bytes 26214400 | tf_op jit(solution)/shard_map/all_gather | solution.py:240
  1239.2 1081.6 %reduce-scatter.16.cloned.1.call-start = ((), (), s32[]{:S(2)}) async-start(), calls=%async_computation.14 | async-start | bytes 52428800 | tf_op jit(solution)/shard_map/reduce_scatter | solution.py:270
  1271.9 66.4 %copy-start.47 = (s32[1024,8]{0,1:T(8,128)S(1)}, s32[1024,8]{0,1:T(8,128)}, u32[]{:S(2)}) copy-start(s32[1024,8]{0,1:T(8,128)} %param.38) | copy-start | bytes 98308
  1272.0 96.9 %copy-start.57 = (s32[8192]{0:T(1024)S(1)}, s32[8192]{0:T(1024)}, u32[]{:S(2)}) copy-start(s32[8192]{0:T(1024)} %broadcast_clamp_fusion) | copy-start | bytes 98308
  1368.9 50.4 %copy-start.24 = (bf16[1024,1024]{1,0:T(8,128)(2,1)S(1)}, bf16[1024,1024]{1,0:T(8,128)(2,1)}, u32[]{:S(2)}) copy-start(bf16[1024,1024]{1,0:T(8,128)(2,1)} %param.37) | copy-start | bytes 6291460
  1945.7 15.0 copy-start.14
  1960.7 16.3 copy-start.19
  2327.9 123.6 %all-to-all-start.3 = ((bf16[4,8,80,1024]{3,2,0,1:T(8,128)(2,1)}), bf16[4,8,80,1024]{3,2,0,1:T(8,128)(2,1)}, u32[]{:S(2)}, u32[]{:S(2)}) async-start(bf16[4,8,80,1024]{3,2,0,1:T(8,128)(2,1)} %convert_element_type.197), calls=%async_computation.5 | async-start | bytes 10485760 | tf_op jit(solution)/shard_map/all_to_all | solution.py:276
  2333.6 118.0 %copy-start.68 = (f32[2,2,512]{2,1,0:T(2,128)S(1)}, f32[2,2,512]{2,1,0:T(2,128)}, u32[]{:S(2)}) copy-start(f32[2,2,512]{2,1,0:T(2,128)} %copy-done.67) | copy-start | bytes 24580
  2333.6 118.0 %copy-start.80 = (f32[2,2,512]{2,1,0:T(2,128)S(1)}, f32[2,2,512]{2,1,0:T(2,128)}, u32[]{:S(2)}) copy-start(f32[2,2,512]{2,1,0:T(2,128)} %copy-done.79) | copy-start | bytes 24580
  2333.6 118.0 %copy-start.82 = (f32[2,2,512]{2,1,0:T(2,128)S(1)}, f32[2,2,512]{2,1,0:T(2,128)}, u32[]{:S(2)}) copy-start(f32[2,2,512]{2,1,0:T(2,128)} %copy-done.81) | copy-start | bytes 24580
  2333.6 118.0 %copy-start.84 = (f32[2,2,512]{2,1,0:T(2,128)S(1)}, f32[2,2,512]{2,1,0:T(2,128)}, u32[]{:S(2)}) copy-start(f32[2,2,512]{2,1,0:T(2,128)} %copy-done.83) | copy-start | bytes 24580
  2333.6 133.9 %reduce-scatter.26.cloned.1.call-start = ((), (), s32[]{:S(2)}) async-start(), calls=%async_computation.21 | async-start | bytes 294912
  2335.2 262.9 %all-gather.5.cloned.1.call-start = ((), (), s32[]{:S(2)}) async-start(), calls=%async_computation.15 | async-start | bytes 26214400 | tf_op jit(solution)/shard_map/all_gather | solution.py:277
  2451.5 289.3 %reduce-scatter.24.cloned.1.call-start = ((), (), s32[]{:S(2)}) async-start(), calls=%async_computation.20 | async-start | bytes 589824
  2451.7 16.7 copy-start.70
  2451.7 16.7 copy-start.85
  2451.7 16.7 copy-start.86
  2451.7 17.3 copy-start.18
  2469.0 129.1 %copy-start.58 = (s32[8192]{0:T(1024)S(1)}, s32[8192]{0:T(1024)}, u32[]{:S(2)}) copy-start(s32[8192]{0:T(1024)} %broadcast_clamp_fusion) | copy-start | bytes 98308
  2648.4 13.4 copy-start.5
  2648.4 13.4 copy-start.51
  2648.4 13.4 copy-start.76
  2648.4 13.4 copy-start.78
  2677.9 115.4 %all-reduce.7.cloned.1.call-start = ((), (), s32[]{:S(2)}) async-start(), calls=%async_computation.16 | async-start | bytes 4194304 | tf_op jit(solution)/shard_map/psum | solution.py:358
  2695.6 13.5 copy-start.12
  2695.6 163.4 %reduce-scatter.18.cloned.1.call-start = ((), (), s32[]{:S(2)}) async-start(), calls=%async_computation.17 | async-start | bytes 589824 | tf_op jit(solution)/shard_map/reduce_scatter | solution.py:368
  2710.7 212.6 %reduce-scatter.20.cloned.1.call-start = ((), (), s32[]{:S(2)}) async-start(), calls=%async_computation.18 | async-start | bytes 589824 | tf_op jit(solution)/shard_map/reduce_scatter | solution.py:371
  2726.1 261.1 %reduce-scatter.22.cloned.1.call-start = ((), (), s32[]{:S(2)}) async-start(), calls=%async_computation.19 | async-start | bytes 294912
  2738.5 54.8 %copy-start.8 = (bf16[1024,1024]{1,0:T(8,128)(2,1)S(1)}, bf16[1024,1024]{1,0:T(8,128)(2,1)}, u32[]{:S(2)}) copy-start(bf16[1024,1024]{1,0:T(8,128)(2,1)} %param.36) | copy-start | bytes 6291460
  2738.5 54.8 %copy-start.72 = (f32[1024]{0:T(1024)S(1)}, f32[1024]{0:T(1024)}, u32[]{:S(2)}) copy-start(f32[1024]{0:T(1024)} %copy-done.71) | copy-start | bytes 12292
  2738.5 54.8 %copy-start.74 = (f32[1,1024]{1,0:T(1,128)S(1)}, f32[1,1024]{1,0:T(1,128)}, u32[]{:S(2)}) copy-start(f32[1,1024]{1,0:T(1,128)} %copy-done.73) | copy-start | bytes 12292
  2740.8 56.5 %copy-start.54 = (f32[256,128]{1,0:T(8,128)S(1)}, f32[256,128]{1,0:T(8,128)}, u32[]{:S(2)}) copy-start(f32[256,128]{1,0:T(8,128)} %param.48) | copy-start | bytes 393220
  2740.8 56.5 %copy-start.61 = (f32[256,128]{1,0:T(8,128)S(1)}, f32[256,128]{1,0:T(8,128)}, u32[]{:S(2)}) copy-start(f32[256,128]{1,0:T(8,128)} %param.49) | copy-start | bytes 393220
  2740.8 56.5 %copy-start.62 = (f32[256,128]{1,0:T(8,128)S(1)}, f32[256,128]{1,0:T(8,128)}, u32[]{:S(2)}) copy-start(f32[256,128]{1,0:T(8,128)} %param.50) | copy-start | bytes 393220
  2798.1 60.9 %copy-start.55 = (f32[128,256]{1,0:T(8,128)S(1)}, f32[128,256]{1,0:T(8,128)}, u32[]{:S(2)}) copy-start(f32[128,256]{1,0:T(8,128)} %param.42) | copy-start | bytes 393220
  2798.1 60.9 %copy-start.63 = (f32[128,256]{1,0:T(8,128)S(1)}, f32[128,256]{1,0:T(8,128)}, u32[]{:S(2)}) copy-start(f32[128,256]{1,0:T(8,128)} %param.43) | copy-start | bytes 393220
  2798.1 60.9 %copy-start.64 = (f32[128,256]{1,0:T(8,128)S(1)}, f32[128,256]{1,0:T(8,128)}, u32[]{:S(2)}) copy-start(f32[128,256]{1,0:T(8,128)} %param.44) | copy-start | bytes 393220
  2798.1 125.1 %copy-start.56 = (f32[2,128,128]{2,1,0:T(8,128)S(1)}, f32[2,128,128]{2,1,0:T(8,128)}, u32[]{:S(2)}) copy-start(f32[2,128,128]{2,1,0:T(8,128)} %param.45) | copy-start | bytes 393220
  2798.1 125.1 %copy-start.65 = (f32[2,128,128]{2,1,0:T(8,128)S(1)}, f32[2,128,128]{2,1,0:T(8,128)}, u32[]{:S(2)}) copy-start(f32[2,128,128]{2,1,0:T(8,128)} %param.46) | copy-start | bytes 393220
  2798.2 125.1 %copy-start.66 = (f32[2,128,128]{2,1,0:T(8,128)S(1)}, f32[2,128,128]{2,1,0:T(8,128)}, u32[]{:S(2)}) copy-start(f32[2,128,128]{2,1,0:T(8,128)} %param.47) | copy-start | bytes 393220
  2798.2 189.9 %copy-start.87 = (f32[2,128]{1,0:T(2,128)S(1)}, f32[2,128]{1,0:T(2,128)}, u32[]{:S(2)}) copy-start(f32[2,128]{1,0:T(2,128)} %param.39) | copy-start | bytes 3076
  2798.2 189.9 %copy-start.88 = (f32[2,128]{1,0:T(2,128)S(1)}, f32[2,128]{1,0:T(2,128)}, u32[]{:S(2)}) copy-start(f32[2,128]{1,0:T(2,128)} %param.40) | copy-start | bytes 3076
  2798.2 189.9 %copy-start.89 = (f32[2,128]{1,0:T(2,128)S(1)}, f32[2,128]{1,0:T(2,128)}, u32[]{:S(2)}) copy-start(f32[2,128]{1,0:T(2,128)} %param.41) | copy-start | bytes 3076
  (42 other events, 113.7 us)
Sparse Core Ops, SparseCore 0:
  145.7 82.7 all-reduce.4
  826.1 287.1 reduce-scatter.13
  1239.3 129.5 all-gather.2
  2033.8 286.8 reduce-scatter.15
  2338.4 127.5 reduce-scatter.25
  2467.5 130.4 all-gather.4
  2678.0 61.9 reduce-scatter.23
  2742.9 50.3 all-reduce.6
  2797.0 61.9 reduce-scatter.17
  2862.2 60.9 reduce-scatter.19
  2927.0 60.2 reduce-scatter.21
where the time goes:
time: 3010 us; the launch traced here: 3000 us
  waiting for transfers between devices  1570 us (52%)
  blocking collectives  719 us (24%)
  local copies, waits for them, and re-layouts  329 us (11%)
  matrix products  188 us (6%)
  other arithmetic  159 us (5%)
    all_to_all x1, blocking collectives, body(): lax.all_to_all(grad_buffer, 'expert', split_axis=0, concat_axis=1, tiled=...  459 us
    all_to_all x1, waiting for transfers between devices, body(): lax.all_to_all(dispatched, 'expert', split_axis=0, concat_axis=1, tiled=T...  449 us
    reduce_scatter x1, waiting for transfers between devices, body(): lax.psum_scatter(partial_out.reshape(local_experts, sources, CAP, width),...  287 us
    reduce_scatter x1, waiting for transfers between devices, body(): lax.psum_scatter(grad_in.reshape(local_experts, sources, CAP, width), 'te...  287 us
    all_to_all x1, blocking collectives, body(): lax.all_to_all(share, 'expert', split_axis=1, concat_axis=0, tiled=True)  121 us
    all_to_all x1, waiting for transfers between devices, body(): lax.all_to_all(grad_share, 'expert', split_axis=1, concat_axis=0, tiled=T...  116 us
    all_gather x1, waiting for transfers between devices, body(): lax.all_gather(grad_arrived, 'tensor', axis=2, tiled=True)  109 us
    gather x5, local copies, waits for them, and re-layouts, body(): chosen = jnp.take_along_axis(logits, routes, axis=1)  66.9 us
  transfers between devices with their start and end apart: 13, of which 11 were waited for; matrix products, arithmetic and copies ran while one was open for 7% of the time, Pallas kernels for 0%

commit v1 on v0

v1 whole, which is shorter than its diff:
```python
import functools

import jax
import jax.numpy as jnp
from jax import lax
from jax.experimental import pallas as pl
from jax.experimental.pallas import tpu as pltpu
from jax.sharding import PartitionSpec as P

HEADS = 16
KV_HEADS = 8
HD = 64
EXPERTS = 32
STEP = 10
PAD = 128

NORM_EPS = 1e-06
BETA_ONE = 0.9
BETA_TWO = 0.999
ADAM_EPS = 1e-08
MATRIX_RATE = 0.08
GAIN_RATE = 0.6
MATRIX_DECAY = 0.1
NEG_LARGE = -1e30
BF = jnp.bfloat16
F32 = jnp.float32


def dot(left, right, dims):
    return lax.dot_general(left, right, (dims, ((), ())), preferred_element_type=F32)


def normalize(values):
    inverse = lax.rsqrt(jnp.mean(values * values, axis=-1, keepdims=True) + NORM_EPS)
    return (values * inverse, inverse)


def norm_backward(grad_unit, unit, inverse):
    return inverse * (grad_unit - unit * jnp.mean(grad_unit * unit, axis=-1, keepdims=True))


def rope_tables(length, head_size):
    half_size = head_size // 2
    frequency = 10000.0 ** (-(jnp.arange(half_size, dtype=F32) * 2.0) / head_size)
    angles = jnp.arange(length, dtype=F32)[:, None] * frequency[None, :]
    return (jnp.cos(angles), jnp.sin(angles))


def rotate(values, cosine_table, sine_table):
    half_size = values.shape[-1] // 2
    first_half = values[..., :half_size]
    second_half = values[..., half_size:]
    c = cosine_table[:, None, :]
    s = sine_table[:, None, :]
    return jnp.concatenate(
        [first_half * c - second_half * s, second_half * c + first_half * s], axis=-1
    )


def unrotate(values, cosine_table, sine_table):
    return rotate(values, cosine_table, -sine_table)


def adamw_update(weight, moment, second, gradient, rate, decay):
    moment_new = BETA_ONE * moment + (1.0 - BETA_ONE) * gradient
    second_new = BETA_TWO * second + (1.0 - BETA_TWO) * gradient * gradient
    fix_one = 1.0 - BETA_ONE**STEP
    fix_two = 1.0 - BETA_TWO**STEP
    update = moment_new / fix_one / (jnp.sqrt(second_new / fix_two) + ADAM_EPS)
    return (weight - rate * (update + decay * weight), moment_new, second_new)


def split_pieces(values, count):
    pieces = []
    for _ in range(count):
        high = lax.reduce_precision(values, 8, 7)
        pieces.append(high.astype(BF))
        values = values - high
    return pieces


def ring_order(size):
    return list(range(0, size, 2)) + list(range(1, size, 2))[::-1]


def ring_perm(size, step):
    order = ring_order(size)
    return [(order[i], order[(i + step) % size]) for i in range(size)]


def ring_index(size, offset):
    me = lax.axis_index("expert")
    place = jnp.where(me % 2 == 0, me // 2, size - 1 - me // 2)
    place = (place + offset) % size
    return jnp.where(place < (size + 1) // 2, 2 * place, 2 * (size - 1 - place) + 1)


def ring_gather(block, size):
    blocks = {0: block}
    ahead = behind = block
    for hop in range(1, size // 2 + 1):
        ahead = lax.ppermute(ahead, "expert", ring_perm(size, 1))
        blocks[-hop] = ahead
        if hop <= (size - 1) // 2:
            behind = lax.ppermute(behind, "expert", ring_perm(size, -1))
            blocks[hop] = behind
    return blocks


def ring_reduce(part, size):
    down = up = None
    for hop in range(size // 2, 0, -1):
        mine = part(-hop).astype(F32)
        total = mine if down is None else down.astype(F32) + mine
        down = lax.ppermute(total.astype(BF), "expert", ring_perm(size, -1))
        side = hop - 1 if size % 2 == 0 else hop
        if side > 0:
            mine = part(side).astype(F32)
            total = mine if up is None else up.astype(F32) + mine
            up = lax.ppermute(total.astype(BF), "expert", ring_perm(size, 1))
    total = part(0).astype(F32) + down.astype(F32)
    return total if up is None else total + up.astype(F32)


def tensor_perm(size, along, core):
    chips = size // 2
    return [(t, ((t // 2 + along) % chips) * 2 + ((t % 2) ^ core)) for t in range(size)]


def tensor_gather(shard, size):
    own = [shard] + [
        lax.ppermute(shard, "tensor", tensor_perm(size, -step, 0)) for step in range(1, size // 2)
    ]
    other = [lax.ppermute(piece, "tensor", tensor_perm(size, 0, 1)) for piece in own]
    return own + other


def tensor_reduce(parts, size):
    chips = size // 2
    sums = []
    for step in range(chips):
        came = lax.ppermute(parts[chips + step], "tensor", tensor_perm(size, 0, 1))
        sums.append(parts[step].astype(F32) + came.astype(F32))
    total = sums[0]
    for step in range(1, chips):
        came = lax.ppermute(sums[step].astype(BF), "tensor", tensor_perm(size, step, 0))
        total = total + came.astype(F32)
    return total


def tensor_sum(values, size):
    values = values + lax.ppermute(values, "tensor", tensor_perm(size, 0, 1))
    moved = [
        lax.ppermute(values, "tensor", tensor_perm(size, step, 0)) for step in range(1, size // 2)
    ]
    return sum(moved, values)


def expert_kernel(
    first_ref,
    one_ref,
    two_ref,
    dy_one_ref,
    dy_two_ref,
    gateup_ref,
    down_ref,
    grads_ref,
    scaled_ref,
    y_one_ref,
    y_two_ref,
    back_one_ref,
    back_two_ref,
    rows_ref,
    dy_ref,
    y_acc,
    back_acc,
    tail_acc,
):
    expert = pl.program_id(0)
    count = pl.num_programs(0)
    rows, width = dy_one_ref.shape

    @pl.when(expert == 0)
    def _():
        rows_ref[:rows] = one_ref[...]
        rows_ref[rows:] = two_ref[...]
        dy_ref[:rows] = dy_one_ref[...]
        dy_ref[rows:] = dy_two_ref[...]
        y_acc[...] = jnp.zeros_like(y_acc)
        back_acc[...] = jnp.zeros_like(back_acc)
        tail_acc[...] = jnp.zeros_like(tail_acc)

    b = rows_ref[:, :width]
    dy = dy_ref[...]
    gate_w = gateup_ref[0, 0]
    up_w = gateup_ref[0, 1]
    down_w = down_ref[0]
    gate_pre = dot(b, gate_w, ((1,), (0,)))
    up_pre = dot(b, up_w, ((1,), (0,)))
    sig = jax.nn.sigmoid(gate_pre)
    silu = gate_pre * sig
    act = (silu * up_pre).astype(BF).astype(F32)
    grad_act = dot(dy, down_w, ((1,), (1,)))
    grad_gating = jnp.sum(act * grad_act, axis=1, keepdims=True)
    column = first_ref[0] + expert
    lane = lax.broadcasted_iota(jnp.int32, (2 * rows, PAD), 1)
    chosen = (lane == column) | (lane == column + EXPERTS)
    tail = rows_ref[:, width:].astype(F32)
    gating = jnp.sum(jnp.where(chosen, tail, 0.0), axis=1, keepdims=True)
    tail_acc[...] += jnp.where(chosen, grad_gating, 0.0)
    grad_act = grad_act * gating
    grad_gate = (grad_act * up_pre * (sig * (1.0 + gate_pre * (1.0 - sig)))).astype(BF)
    grad_up = (grad_act * silu).astype(BF)
    scaled = (act * gating).astype(BF)
    grads_ref[0, 0] = grad_gate
    grads_ref[1, 0] = grad_up
    scaled_ref[0] = scaled
    back_acc[...] += dot(grad_gate, gate_w, ((1,), (1,))) + dot(grad_up, up_w, ((1,), (1,)))
    y_acc[...] += dot(scaled, down_w, ((1,), (0,)))

    @pl.when(expert == count - 1)
    def _():
        y = y_acc[...].astype(BF)
        y_one_ref[...] = y[:rows]
        y_two_ref[...] = y[rows:]
        back = back_acc[...].astype(BF)
        total = tail_acc[...]
        high = total.astype(BF)
        low = (total - high.astype(F32)).astype(BF)
        ends = jnp.where(lane < EXPERTS, high.astype(F32), low.astype(F32)).astype(BF)
        back_one_ref[:, :width] = back[:rows]
        back_one_ref[:, width:] = ends[:rows]
        back_two_ref[:, :width] = back[rows:]
        back_two_ref[:, width:] = ends[rows:]


def expert_blocks(first, one, two, dy_one, dy_two, gateup, down):
    experts, _, width, hidden = gateup.shape
    rows = one.shape[0]
    message = one.shape[1]
    whole = lambda e, s: (0, 0)
    block = pl.BlockSpec((rows, message), whole)
    plain = pl.BlockSpec((rows, width), whole)
    return pl.pallas_call(
        expert_kernel,
        grid_spec=pltpu.PrefetchScalarGridSpec(
            num_scalar_prefetch=1,
            grid=(experts,),
            in_specs=[
                block,
                block,
                plain,
                plain,
                pl.BlockSpec((1, 2, width, hidden), lambda e, s: (e, 0, 0, 0)),
                pl.BlockSpec((1, hidden, width), lambda e, s: (e, 0, 0)),
            ],
            out_specs=[
                pl.BlockSpec((2, 1, 2 * rows, hidden), lambda e, s: (0, e, 0, 0)),
                pl.BlockSpec((1, 2 * rows, hidden), lambda e, s: (e, 0, 0)),
                plain,
                plain,
                block,
                block,
            ],
            scratch_shapes=[
                pltpu.VMEM((2 * rows, message), BF),
                pltpu.VMEM((2 * rows, width), BF),
                pltpu.VMEM((2 * rows, width), F32),
                pltpu.VMEM((2 * rows, width), F32),
                pltpu.VMEM((2 * rows, PAD), F32),
            ],
        ),
        out_shape=[
            jax.ShapeDtypeStruct((2, experts, 2 * rows, hidden), BF),
            jax.ShapeDtypeStruct((experts, 2 * rows, hidden), BF),
            jax.ShapeDtypeStruct((rows, width), BF),
            jax.ShapeDtypeStruct((rows, width), BF),
            jax.ShapeDtypeStruct((rows, message), BF),
            jax.ShapeDtypeStruct((rows, message), BF),
        ],
        compiler_params=pltpu.CompilerParams(vmem_limit_bytes=48 * 1024 * 1024),
        name="expert_blocks",
    )(first, one, two, dy_one, dy_two, gateup, down)


def gateup_grad_kernel(pairs, *refs):
    out_ref = refs[-1]
    total = None
    for pair in range(pairs):
        grads = refs[2 * pairs + pair][0, 0]
        rows = grads.shape[0] // 2
        for half in range(2):
            term = dot(refs[2 * pair + half][...], grads[half * rows : (half + 1) * rows], ((0,), (0,)))
            total = term if total is None else total + term
    out_ref[0, 0] = total.astype(BF)


def gateup_grad(inputs, grads):
    pairs = len(grads)
    _, experts, both, hidden = grads[0].shape
    rows = both // 2
    width = inputs[0].shape[1] - PAD
    return pl.pallas_call(
        functools.partial(gateup_grad_kernel, pairs),
        grid=(experts, 2),
        in_specs=[pl.BlockSpec((rows, width), lambda e, k: (0, 0))] * (2 * pairs)
        + [pl.BlockSpec((1, 1, both, hidden), lambda e, k: (k, e, 0, 0))] * pairs,
        out_specs=pl.BlockSpec((1, 1, width, hidden), lambda e, k: (e, k, 0, 0)),
        out_shape=jax.ShapeDtypeStruct((experts, 2, width, hidden), BF),
        compiler_params=pltpu.CompilerParams(vmem_limit_bytes=56 * 1024 * 1024),
        name="gateup_grad",
    )(*inputs, *grads)


def down_grad_kernel(pairs, *refs):
    out_ref = refs[-1]
    total = None
    for pair in range(pairs):
        scaled = refs[2 * pairs + pair][0]
        rows = scaled.shape[0] // 2
        for half in range(2):
            term = dot(scaled[half * rows : (half + 1) * rows], refs[2 * pair + half][...], ((0,), (0,)))
            total = term if total is None else total + term
    out_ref[0] = total.astype(BF)


def down_grad(outputs, scaled):
    pairs = len(scaled)
    experts, both, hidden = scaled[0].shape
    rows, width = outputs[0].shape
    return pl.pallas_call(
        functools.partial(down_grad_kernel, pairs),
        grid=(experts,),
        in_specs=[pl.BlockSpec((rows, width), lambda e: (0, 0))] * (2 * pairs)
        + [pl.BlockSpec((1, both, hidden), lambda e: (e, 0, 0))] * pairs,
        out_specs=pl.BlockSpec((1, hidden, width), lambda e: (e, 0, 0)),
        out_shape=jax.ShapeDtypeStruct((experts, hidden, width), BF),
        compiler_params=pltpu.CompilerParams(vmem_limit_bytes=56 * 1024 * 1024),
        name="down_grad",
    )(*outputs, *scaled)


def attention_forward(query_rot, key_rot, value_rot):
    length, local_groups, group_size, _ = query_rot.shape
    block_rows = min(512, length)
    mixture_parts = []
    lse_parts = []
    for begin in range(0, length, block_rows):
        end = begin + block_rows
        scores = jnp.einsum(
            "qhgd,khd->hgqk", query_rot[begin:end], key_rot[:end], preferred_element_type=F32
        ) * HD ** (-0.5)
        causal = (begin + jnp.arange(block_rows))[:, None] >= jnp.arange(end)[None, :]
        scores = jnp.where(causal, scores, NEG_LARGE)
        row_peak = jnp.max(scores, axis=-1, keepdims=True)
        exponent = jnp.exp(scores - row_peak)
        row_total = jnp.sum(exponent, axis=-1, keepdims=True)
        lse_parts.append(row_peak + jnp.log(row_total))
        weights_block = (exponent / row_total).astype(BF)
        mixture_parts.append(
            jnp.einsum("hgqk,khd->qhgd", weights_block, value_rot[:end], preferred_element_type=F32)
        )
    mixture = jnp.concatenate(mixture_parts, axis=0).reshape(length, -1).astype(BF)
    return mixture, lse_parts


def attention_backward(query_rot, key_rot, value_rot, lse_parts, grad_mixture):
    length, local_groups, group_size, _ = query_rot.shape
    block_rows = min(512, length)
    score_scale = HD ** (-0.5)
    grad_key = jnp.zeros((length, local_groups, HD), F32)
    grad_value = jnp.zeros((length, local_groups, HD), F32)
    grad_query_parts = []
    for index, begin in enumerate(range(0, length, block_rows)):
        end = begin + block_rows
        query_block = query_rot[begin:end]
        key_block = key_rot[:end]
        grad_block = grad_mixture[begin:end]
        scores = (
            jnp.einsum("qhgd,khd->hgqk", query_block, key_block, preferred_element_type=F32)
            * score_scale
        )
        causal = (begin + jnp.arange(block_rows))[:, None] >= jnp.arange(end)[None, :]
        weights_block = jnp.where(causal, jnp.exp(scores - lse_parts[index]), 0.0)
        grad_weights = jnp.einsum(
            "qhgd,khd->hgqk", grad_block, value_rot[:end], preferred_element_type=F32
        )
        row_delta = jnp.sum(weights_block * grad_weights, axis=-1, keepdims=True)
        grad_scores = (weights_block * (grad_weights - row_delta)).astype(BF)
        grad_query_parts.append(
            jnp.einsum("hgqk,khd->qhgd", grad_scores, key_block, preferred_element_type=F32)
            * score_scale
        )
        grad_key = grad_key.at[:end].add(
            jnp.einsum("hgqk,qhgd->khd", grad_scores, query_block, preferred_element_type=F32)
            * score_scale
        )
        grad_value = grad_value.at[:end].add(
            jnp.einsum(
                "hgqk,qhgd->khd", weights_block.astype(BF), grad_block, preferred_element_type=F32
            )
        )
    return jnp.concatenate(grad_query_parts, axis=0), grad_key, grad_value


def body(
    ring,
    tensors,
    tokens,
    cotangent,
    routes,
    norm_gains,
    gains_moment,
    gains_second,
    query_weight,
    query_moment,
    query_second,
    keyval_weight,
    keyval_moment,
    keyval_second,
    output_weight,
    output_moment,
    output_second,
    router_weight,
    router_moment,
    router_second,
    gateup_weight,
    gateup_moment,
    gateup_second,
    down_weight,
    down_moment,
    down_second,
):
    length, width = tokens.shape
    rows = length // tensors
    experts = gateup_weight.shape[0]
    shard = gateup_weight.shape[3]
    lane_t = lax.axis_index("tensor")
    own_rows = lambda array: lax.dynamic_slice_in_dim(array, lane_t * rows, rows, axis=0)

    q_cols = query_weight.shape[1]
    k_cols = keyval_weight.shape[2]
    o_cols = output_weight.shape[0]
    heads_cols = q_cols + 2 * k_cols
    gain_pieces = split_pieces(norm_gains.T, 3)
    packed = jnp.concatenate(
        [
            query_weight.astype(BF),
            keyval_weight[0].astype(BF),
            keyval_weight[1].astype(BF),
            output_weight.T.astype(BF),
            router_weight.astype(BF),
        ]
        + gain_pieces,
        axis=1,
    )
    packed = lax.all_gather(packed, "expert", axis=0, tiled=True)
    attn_low = packed[:, : heads_cols + o_cols]
    qkv_low = packed[:, :heads_cols]
    router_low = packed[:, heads_cols + o_cols : heads_cols + o_cols + EXPERTS]
    gains_at = heads_cols + o_cols + EXPERTS
    gains_all = (
        packed[:, gains_at : gains_at + 2].astype(F32)
        + packed[:, gains_at + 2 : gains_at + 4].astype(F32)
        + packed[:, gains_at + 4 : gains_at + 6].astype(F32)
    ).T

    gateup_low = jnp.concatenate(tensor_gather(gateup_weight.astype(BF), tensors), axis=3)
    down_low = jnp.concatenate(tensor_gather(down_weight.astype(BF), tensors), axis=1)
    dy_own = own_rows(cotangent)
    dy_blocks = ring_gather(dy_own, ring)
    attn_all = lax.all_gather(attn_low, "tensor")

    x = tokens.astype(F32)
    unit_one, inverse_one = normalize(x)
    a = (unit_one * gains_all[0]).astype(BF)
    pre = jnp.dot(a, qkv_low, preferred_element_type=F32)
    local_heads = q_cols // HD
    local_groups = k_cols // HD
    group_size = local_heads // local_groups
    cosine_table, sine_table = rope_tables(length, HD)
    query_rot = rotate(
        pre[:, :q_cols].reshape(length, local_heads, HD), cosine_table, sine_table
    ).astype(BF)
    query_rot = query_rot.reshape(length, local_groups, group_size, HD)
    key_rot = rotate(
        pre[:, q_cols : q_cols + k_cols].reshape(length, local_groups, HD), cosine_table, sine_table
    ).astype(BF)
    value_rot = pre[:, q_cols + k_cols :].astype(BF).reshape(length, local_groups, HD)
    mixture, lse_parts = attention_forward(query_rot, key_rot, value_rot)

    mixture_rows = lax.all_to_all(
        mixture.reshape(tensors, rows, o_cols), "tensor", split_axis=0, concat_axis=0, tiled=True
    )
    attention = sum(
        dot(mixture_rows[t], attn_all[t, :, heads_cols:], ((1,), (1,))) for t in range(tensors)
    )
    x_mid = own_rows(x) + attention
    unit_two, inverse_two = normalize(x_mid)
    b = (unit_two * gains_all[1]).astype(BF)
    logits = jnp.dot(b, router_low, preferred_element_type=F32)
    own_routes = own_rows(routes)
    routed = jnp.any(
        own_routes[:, :, None] == jnp.arange(EXPERTS, dtype=jnp.int32)[None, None, :], axis=1
    )
    masked = jnp.where(routed, logits, NEG_LARGE)
    exponent = jnp.where(routed, jnp.exp(masked - jnp.max(masked, axis=1, keepdims=True)), 0.0)
    gating = exponent / jnp.sum(exponent, axis=1, keepdims=True)
    message = jnp.concatenate(
        [b] + split_pieces(gating, 2) + [jnp.zeros((rows, PAD - 2 * EXPERTS), BF)], axis=1
    )
    blocks = ring_gather(message, ring)

    first = (lax.axis_index("expert") * experts).astype(jnp.int32).reshape(1)
    back = {}
    forth = {}
    grads = []
    scaled = []
    order = []
    for k in range(ring // 2):
        one = -(ring // 2 - k)
        two = ring // 2 - 1 - k
        order += [one, two]
        result = expert_blocks(
            first, blocks[one], blocks[two], dy_blocks[one], dy_blocks[two], gateup_low, down_low
        )
        grads.append(result[0])
        scaled.append(result[1])
        forth[one], forth[two] = result[2], result[3]
        back[one], back[two] = result[4], result[5]
    returned = ring_reduce(lambda offset: back[offset], ring)
    moe_sum = ring_reduce(lambda offset: forth[offset], ring)
    block_out = lax.all_gather(
        (x_mid + moe_sum).astype(BF), "tensor", axis=0, tiled=True
    )
    gateup_grads = gateup_grad([blocks[o] for o in order], grads)
    down_grads = down_grad([dy_blocks[o] for o in order], scaled)
    gateup_sum = tensor_reduce(
        [gateup_grads[..., j * shard : (j + 1) * shard] for j in range(tensors)], tensors
    )
    down_sum = tensor_reduce(
        [down_grads[:, j * shard : (j + 1) * shard] for j in range(tensors)], tensors
    )
    new_gateup = adamw_update(
        gateup_weight, gateup_moment, gateup_second, gateup_sum, MATRIX_RATE, MATRIX_DECAY
    )
    new_down = adamw_update(
        down_weight, down_moment, down_second, down_sum, MATRIX_RATE, MATRIX_DECAY
    )

    grad_gating = (
        returned[:, width : width + EXPERTS] + returned[:, width + EXPERTS : width + 2 * EXPERTS]
    )
    grad_logits = (
        gating * (grad_gating - jnp.sum(gating * grad_gating, axis=1, keepdims=True))
    ).astype(BF)
    grad_b = dot(grad_logits, router_low, ((1,), (1,))) + returned[:, :width]
    grad_mid = dy_own.astype(F32) + norm_backward(grad_b * gains_all[1], unit_two, inverse_two)
    grad_attention = grad_mid.astype(BF)
    grad_mixture = jnp.stack(
        [dot(grad_attention, attn_all[t, :, heads_cols:], ((1,), (0,))).astype(BF) for t in range(tensors)]
    )
    grad_mixture = lax.all_to_all(
        grad_mixture, "tensor", split_axis=0, concat_axis=0, tiled=True
    ).reshape(length, local_groups, group_size, HD)

    small = jnp.concatenate(
        [
            dot(b, grad_logits, ((0,), (0,))),
            jnp.sum(grad_b * unit_two, axis=0)[:, None],
        ],
        axis=1,
    )
    small = tensor_sum(small, tensors)
    grad_attention_all = lax.all_gather(grad_attention, "tensor", axis=0, tiled=True)
    early = jnp.concatenate(
        [dot(grad_attention_all, mixture, ((0,), (0,))), small], axis=1
    ).astype(BF)
    piece = width // ring
    cut = lambda array: lambda offset: lax.dynamic_slice_in_dim(
        array, ring_index(ring, offset) * piece, piece, axis=0
    )
    early_sum = ring_reduce(cut(early), ring)
    output_sum = early_sum[:, :o_cols].T
    router_sum = early_sum[:, o_cols : o_cols + EXPERTS]
    gain_two_sum = early_sum[:, o_cols + EXPERTS]

    grad_query, grad_key, grad_value = attention_backward(
        query_rot, key_rot, value_rot, lse_parts, grad_mixture
    )
    grad_query_low = (
        unrotate(grad_query.reshape(length, local_heads, HD), cosine_table, sine_table)
        .astype(BF)
        .reshape(length, q_cols)
    )
    grad_key_low = unrotate(grad_key, cosine_table, sine_table).astype(BF).reshape(length, k_cols)
    grad_value_low = grad_value.astype(BF).reshape(length, k_cols)
    grad_pre = jnp.concatenate([grad_query_low, grad_key_low, grad_value_low], axis=1)
    grad_pre_rows = lax.all_to_all(
        grad_pre.reshape(tensors, rows, heads_cols), "tensor", split_axis=0, concat_axis=0, tiled=True
    )
    late = dot(a, grad_pre, ((0,), (0,)))
    gain_one = jnp.sum(late * qkv_low.astype(F32), axis=1) / gains_all[0]
    gain_one = tensor_sum(gain_one[:, None], tensors)
    late = jnp.concatenate([late, gain_one], axis=1).astype(BF)
    late_sum = ring_reduce(cut(late), ring)
    grad_a = sum(
        dot(grad_pre_rows[t], attn_all[t, :, :heads_cols], ((1,), (1,))) for t in range(tensors)
    )
    input_grad = (
        grad_mid
        + norm_backward(grad_a * gains_all[0], own_rows(unit_one), own_rows(inverse_one))
    ).astype(BF)
    input_grad = lax.all_gather(input_grad, "tensor", axis=0, tiled=True)

    query_sum = late_sum[:, :q_cols]
    keyval_sum = jnp.stack(
        [late_sum[:, q_cols : q_cols + k_cols], late_sum[:, q_cols + k_cols : heads_cols]]
    )
    gains_sum = jnp.stack([late_sum[:, heads_cols], gain_two_sum])
    new_gains = adamw_update(norm_gains, gains_moment, gains_second, gains_sum, GAIN_RATE, 0.0)
    new_query = adamw_update(
        query_weight, query_moment, query_second, query_sum, MATRIX_RATE, MATRIX_DECAY
    )
    new_keyval = adamw_update(
        keyval_weight, keyval_moment, keyval_second, keyval_sum, MATRIX_RATE, MATRIX_DECAY
    )
    new_output = adamw_update(
        output_weight, output_moment, output_second, output_sum, MATRIX_RATE, MATRIX_DECAY
    )
    new_router = adamw_update(
        router_weight, router_moment, router_second, router_sum, MATRIX_RATE, MATRIX_DECAY
    )
    return (
        (block_out, input_grad)
        + tuple(new_gains)
        + tuple(new_query)
        + tuple(new_keyval)
        + tuple(new_output)
        + tuple(new_router)
        + tuple(new_gateup)
        + tuple(new_down)
    )


def solution(mesh):
    rows = P("expert", None)
    gains = P(None, "expert")
    query = P("expert", "tensor")
    keyval = P(None, "expert", "tensor")
    output = P("tensor", "expert")
    gateup = P("expert", None, None, "tensor")
    down = P("expert", "tensor", None)
    weights = tuple(
        spec for spec in (gains, query, keyval, output, rows, gateup, down) for _ in range(3)
    )
    return jax.shard_map(
        functools.partial(body, mesh.shape["expert"], mesh.shape["tensor"]),
        mesh=mesh,
        in_specs=(rows, rows, rows) + weights,
        out_specs=(rows, rows) + weights,
        check_vma=False,
    )
```

time: 3010 us -> 666 us (0.22)
  waiting for transfers between devices: 1570 us -> 250 us
  blocking collectives: 719 us -> 0 us
  local copies, waits for them, and re-layouts: 329 us -> 61.6 us
  matrix products: 188 us -> 55.2 us
  Pallas kernels: 0 us -> 113 us
  other arithmetic: 159 us -> 90 us
  starting transfers between devices: 12.2 us -> 69.7 us
    reduce_scatter x4 -> x0, waiting for transfers between devices: 693 us -> none  [the longest x1 287 us: body(): lax.psum_scatter(partial_out.reshape(local_experts, sources, CAP, width),...]
    all_to_all x2 -> x0, blocking collectives: 580 us -> none  [the longest x1 459 us: body(): lax.all_to_all(grad_buffer, 'expert', split_axis=0, concat_axis=1, tiled=...]
    all_to_all x2 -> x3, waiting for transfers between devices: 565 us -> 4.17 us  [the longest x1 2.78 us: body(): lax.all_to_all(grad_mixture, 'tensor', split_axis=0, concat_axis=0, tiled...]
    ppermute x0 -> x58, waiting for transfers between devices: none -> 176 us  [the longest x16 51.5 us: ring_reduce(): down = lax.ppermute(total.astype(BF), 'expert', ring_perm(size, -1))]
    gather x7 -> x0, local copies, waits for them, and re-layouts: 168 us -> none  [the longest x5 66.9 us: body(): chosen = jnp.take_along_axis(logits, routes, axis=1)]
    all_gather x5 -> x0, blocking collectives: 139 us -> none  [the longest x1 31.5 us: body(): lax.all_gather(keyval_weight, 'expert', axis=1, tiled=True)]
    dot_general x37 -> x30, matrix products: 188 us -> 55.2 us  [the longest x16 25.8 us: dot(): lax.dot_general(left, right, (dims, ((), ())), preferred_element_type=F32)]
    pallas_call x0 -> x6, Pallas kernels: none -> 113 us  [the longest x4 75.8 us: expert_blocks(): pl.pallas_call(expert_kernel, grid_spec=pltpu.PrefetchScalarGridSpec(num_...]
  transfers between devices with their start and end apart: 13 -> 66, of which waited for: 11 -> 26; matrix products, arithmetic and copies ran while one was open for 7% -> 28% of each run, Pallas kernels for 0% -> 14%
where the time goes in v1:
time: 666 us; the launch traced here: 655 us
  waiting for transfers between devices  250 us (38%)
  Pallas kernels  113 us (17%)
  other arithmetic  90 us (14%)
  starting transfers between devices  69.7 us (10%)
  local copies, waits for them, and re-layouts  61.6 us (9%)
  matrix products  55.2 us (8%)
  between operations  16 us (2%)
    pallas_call x4, Pallas kernels, expert_blocks(): pl.pallas_call(expert_kernel, grid_spec=pltpu.PrefetchScalarGridSpec(num_...  75.8 us
    ppermute x16, waiting for transfers between devices, ring_reduce(): down = lax.ppermute(total.astype(BF), 'expert', ring_perm(size, -1))  51.5 us
    all_gather x1, waiting for transfers between devices, body(): packed = lax.all_gather(packed, 'expert', axis=0, tiled=True)  48.9 us
    ppermute x2, waiting for transfers between devices, tensor_gather(): lax.ppermute(shard, 'tensor', tensor_perm(size, -step, 0))  39.7 us
    ppermute x2, waiting for transfers between devices, tensor_sum(): lax.ppermute(values, 'tensor', tensor_perm(size, step, 0))  32.6 us
    ppermute x6, waiting for transfers between devices, ring_gather(): behind = lax.ppermute(behind, 'expert', ring_perm(size, -1))  29 us
    dot_general x16, matrix products, dot(): lax.dot_general(left, right, (dims, ((), ())), preferred_element_type=F32)  25.8 us
    unnamed x206, local copies, waits for them, and re-layouts  25.4 us
  transfers between devices with their start and end apart: 66, of which 26 were waited for; matrix products, arithmetic and copies ran while one was open for 28% of the time, Pallas kernels for 14%

profile of v1, /device:TPU:0, one launch (start us, length us, event | category | flops | bytes accessed | tf_op | source)
XLA Modules:
  0.0 655.2 jit_solution(14883547492744137941)
XLA Ops:
  11.7 3.7 concatenate.59
  15.5 48.9 %all-gather.7.cloned.1.call-done = bf16[1024,806]{0,1:T(8,128)(2,1)} async-done(((bf16[128,806]{0,1:T(8,128)(2,1)}), bf16[1024,806]{0,1:T(8,128)(2,1)}) %all-gather.7.cloned.1.call-update) | async-done | bytes 1650704 | tf_op jit(solution)/shard_map/all_gather | solution.py:457
  64.4 2.7 slice.379
  68.6 2.2 multiply_reduce_fusion
  72.4 3.4 fusion.136
  83.3 2.5 fusion.28
  88.7 3.5 all-to-all-start
  92.2 2.9 convert_element_type.437
  95.1 2.0 collective-permute-start.5
  97.1 2.2 collective-permute-start.17
  99.2 3.9 convert_element_type.436
  103.4 2.5 convert_element_type.415
  106.2 20.5 %all-gather.15.cloned.1.call-done = bf16[4096,768]{0,1:T(8,128)(2,1)} async-done(((bf16[1024,768]{0,1:T(8,128)(2,1)}), bf16[4096,768]{0,1:T(8,128)(2,1)}) %all-gather.15.cloned.1.call-update) | async-done | bytes 6291472 | tf_op jit(solution)/shard_map/all_gather | solution.py:472
  126.7 8.7 %copy.260 = bf16[4096,768]{1,0:T(8,128)(2,1)} copy(bf16[4096,768]{0,1:T(8,128)(2,1)} %all-gather.15.cloned.1.call-done) | data formatting | bytes 12582912 | tf_op jit(solution)/shard_map/all_gather | solution.py:472
  143.6 39.7 %collective-permute-done.2 = bf16[4,2,1024,128]{3,2,1,0:T(8,128)(2,1)} collective-permute-done((bf16[4,2,1024,128]{3,2,1,0:T(8,128)(2,1)}, bf16[4,2,1024,128]{3,2,1,0:T(8,128)(2,1)}, u32[]{:S(2)}, u32[]{:S(2)}) %collective-permute-start.2) | collective-permute-done | bytes 2097184 | tf_op jit(solution)/shard_map/ppermute | solution.py:132
  185.8 13.5 %collective-permute-done.18.dy_two_ref.refs_3_ = bf16[256,1024]{1,0:T(8,128)(2,1)S(1)} collective-permute-done((bf16[256,1024]{1,0:T(8,128)(2,1)S(1)}, bf16[256,1024]{1,0:T(8,128)(2,1)S(1)}, u32[]{:S(2)}, u32[]{:S(2)}) %collective-permute-start.18) | collective-permute-done | bytes 524320 | tf_op jit(solution)/shard_map/ppermute | solution.py:105
  202.9 11.1 %collective-permute-done.11.two_ref.refs_5_ = bf16[256,1152]{1,0:T(8,128)(2,1)S(1)} collective-permute-done((bf16[256,1152]{1,0:T(8,128)(2,1)S(1)}, bf16[256,1152]{1,0:T(8,128)(2,1)S(1)}, u32[]{:S(2)}, u32[]{:S(2)}) %collective-permute-start.11) | collective-permute-done | bytes 589856 | tf_op jit(solution)/shard_map/ppermute | solution.py:105
  217.7 4.0 broadcast_multiply_fusion
  228.9 3.8 pad_maximum_fusion.1.down_ref
  235.3 4.8 collective-permute-done.9.one_ref.refs_2_
  241.6 7.1 %pad_maximum_fusion.gateup_ref = bf16[4,2,1024,512]{3,2,1,0:T(8,128)(2,1)} fusion(bf16[4,2,1024,128]{3,2,1,0:T(8,128)(2,1)} %collective-permute-done.4, bf16[4,2,1024,128]{3,2,1,0:T(8,128)(2,1)} %collective-permute-done.3, bf16[4,2,1024,128]{3,2,1,0:T(8,128)(2,1)} %collective-permute-done.2, bf16[4,2,1024,128]{3,2,1,0:T(8,128)(2,1)} %convert_element_type.436), kind=kLoop, calls=%fused_computation | loop fusion | flops 33554432 | bytes 16777216 | tf_op jit(solution)/shard_map/concatenate | solution.py:468
  248.7 2.5 collective-permute-done.16.dy_one_ref.refs_0_
  251.3 4.4 collective-permute-done.13.two_ref.refs_1_
  255.6 6.5 collective-permute-done.10.one_ref.refs_0_
  262.2 19.1 %expert_blocks.5 = (bf16[2,4,512,512]{3,2,1,0:T(8,128)(2,1)}, bf16[4,512,512]{2,1,0:T(8,128)(2,1)}, bf16[256,1024]{1,0:T(8,128)(2,1)S(1)}, bf16[256,1024]{1,0:T(...) custom-call(s32[1]{0:T(128)} %bitcast.32.first_ref, ...), custom_call_target="tpu_custom_call" | custom-call | tf_op jit(solution)/shard_map/expert_blocks/pallas_call | solution.py:244
  284.1 18.8 %expert_blocks.4 = (bf16[2,4,512,512]{3,2,1,0:T(8,128)(2,1)}, bf16[4,512,512]{2,1,0:T(8,128)(2,1)}, bf16[256,1024]{1,0:T(8,128)(2,1)S(1)}, bf16[256,1024]{1,0:T(...) custom-call(s32[1]{0:T(128)} %bitcast.32.first_ref, ...), custom_call_target="tpu_custom_call" | custom-call | tf_op jit(solution)/shard_map/expert_blocks/pallas_call | solution.py:244
  304.5 18.9 %expert_blocks.7 = (bf16[2,4,512,512]{3,2,1,0:T(8,128)(2,1)}, bf16[4,512,512]{2,1,0:T(8,128)(2,1)}, bf16[256,1024]{1,0:T(8,128)(2,1)S(1)}, bf16[256,1024]{1,0:T(...) custom-call(s32[1]{0:T(128)} %bitcast.32.first_ref, ...), custom_call_target="tpu_custom_call" | custom-call | tf_op jit(solution)/shard_map/expert_blocks/pallas_call | solution.py:244
  323.4 19.1 %expert_blocks.6 = (bf16[2,4,512,512]{3,2,1,0:T(8,128)(2,1)}, bf16[4,512,512]{2,1,0:T(8,128)(2,1)}, bf16[256,1024]{1,0:T(8,128)(2,1)S(1)}, bf16[256,1024]{1,0:T(...) custom-call(s32[1]{0:T(128)} %bitcast.32.first_ref, ...), custom_call_target="tpu_custom_call" | custom-call | tf_op jit(solution)/shard_map/expert_blocks/pallas_call | solution.py:244
  342.4 13.6 %down_grad.1 = bf16[4,512,1024]{2,1,0:T(8,128)(2,1)} custom-call(bf16[256,1024]{1,0:T(8,128)(2,1)} %copy-done.17, bf16[256,1024]{1,0:T(8,128)(2,1)} %copy-done.16, bf16[256,1024]{1,0:T(8,128)(2,1)} %collective-permute-done.15.dy_one_ref.refs_2_, bf16[256,1024]{1,0:T(8,128)(2,1)} %copy-done.14, bf16[256,1024]{1,0:T(8,128)(2,1)} %collective-permute-done.14.dy_one_ref.refs_4_, ...), custom_call_target="tpu_custom_call" | custom-call | tf_op jit(solution)/shard_map/down_grad/pallas_call | solution.py:331
  356.1 3.1 fusion.133
  360.2 23.2 %gateup_grad.1 = bf16[4,2,1024,512]{3,2,1,0:T(8,128)(2,1)} custom-call(bf16[256,1152]{1,0:T(8,128)(2,1)} %copy-done.9, bf16[256,1152]{1,0:T(8,128)(2,1)} %copy-done.8, bf16[256,1152]{1,0:T(8,128)(2,1)} %collective-permute-done.9.one_ref.refs_2_, bf16[256,1152]{1,0:T(8,128)(2,1)} %copy-done.7, bf16[256,1152]{1,0:T(8,128)(2,1)} %copy-done.6, ...), custom_call_target="tpu_custom_call" | custom-call | tf_op jit(solution)/shard_map/gateup_grad/pallas_call | solution.py:303
  386.2 4.7 fusion.132
  393.1 7.9 %collective-permute-done.28 = bf16[256,1152]{1,0:T(8,128)(2,1)S(1)} collective-permute-done((bf16[256,1152]{1,0:T(8,128)(2,1)S(1)}, bf16[256,1152]{1,0:T(8,128)(2,1)S(1)}, u32[]{:S(2)}, u32[]{:S(2)}) %collective-permute-start.28) | collective-permute-done | bytes 589856 | tf_op jit(solution)/shard_map/ppermute | solution.py:115
  402.6 8.3 %collective-permute-done.20 = bf16[256,1024]{1,0:T(8,128)(2,1)S(1)} collective-permute-done((bf16[256,1024]{1,0:T(8,128)(2,1)S(1)}, bf16[256,1024]{1,0:T(8,128)(2,1)S(1)}, u32[]{:S(2)}, u32[]{:S(2)}) %collective-permute-start.20) | collective-permute-done | bytes 524320 | tf_op jit(solution)/shard_map/ppermute | solution.py:115
  412.6 5.4 collective-permute-done.32
  419.6 7.6 %collective-permute-done.29 = bf16[256,1152]{1,0:T(8,128)(2,1)S(1)} collective-permute-done((bf16[256,1152]{1,0:T(8,128)(2,1)S(1)}, bf16[256,1152]{1,0:T(8,128)(2,1)S(1)}, u32[]{:S(2)}, u32[]{:S(2)}) %collective-permute-start.29) | collective-permute-done | bytes 589856 | tf_op jit(solution)/shard_map/ppermute | solution.py:115
  430.4 8.0 %collective-permute-done.21 = bf16[256,1024]{1,0:T(8,128)(2,1)S(1)} collective-permute-done((bf16[256,1024]{1,0:T(8,128)(2,1)S(1)}, bf16[256,1024]{1,0:T(8,128)(2,1)S(1)}, u32[]{:S(2)}, u32[]{:S(2)}) %collective-permute-start.21) | collective-permute-done | bytes 524320 | tf_op jit(solution)/shard_map/ppermute | solution.py:115
  440.0 2.9 add_convert_fusion.1
  444.4 4.5 collective-permute-done.30
  452.2 2.2 fusion.123
  461.4 4.1 all-to-all-start.1
  467.5 2.0 add_convert_fusion.9
  470.1 2.0 add_convert_fusion.11
  472.1 2.8 all-to-all-done.1
  477.0 3.9 fusion.9
  487.1 6.5 fusion
  493.6 4.8 fusion.2
  509.1 4.1 add_convert_fusion
  513.2 2.2 convert_element_type.485
  520.6 4.2 all-to-all-start.2
  526.6 2.0 collective-permute-start.54
  530.1 8.1 %multiply_subtract_fusion.1 = (f32[4,128,1024]{2,1,0:T(8,128)}, f32[4,128,1024]{2,1,0:T(8,128)}, f32[4,128,1024]{2,1,0:T(8,128)}) fusion(f32[4,128,1024]{2,1,0:T(8,128)} %param.57, bf16[4,128,1024]{2,1,0:T(8,128)(2,1)} %collective-permute-done.57, bf16[4,128,1024]{2,1,0:T(8,128)(2,1)} %collective-permute-done.55, bf16[4,512,1024]{2,1,0:T(8,128)(2,1)} %down_grad.1, ...), kind=kLoop, calls=%fused_computation.51 | loop fusion | flops 10485760 | bytes 15728640 | tf_op jit(solution)/shard_map/sub | solution.py:70
  538.1 4.2 collective-permute-done.36
  545.2 1.9 fusion.53
  554.3 2.9 add_convert_fusion.7
  562.2 2.1 collective-permute-done.38
  568.0 2.4 collective-permute-done.41
  572.0 32.6 %collective-permute-done.44 = f32[1024,33]{0,1:T(8,128)S(1)} collective-permute-done((f32[1024,33]{0,1:T(8,128)S(1)}, f32[1024,33]{0,1:T(8,128)S(1)}, u32[]{:S(2)}, u32[]{:S(2)}) %collective-permute-start.44) | collective-permute-done | bytes 135200 | tf_op jit(solution)/shard_map/ppermute | solution.py:154
  604.7 2.3 convolution_convert_fusion
  608.8 2.8 collective-permute-done.45
  613.7 2.3 collective-permute-done.46
  617.8 2.7 collective-permute-done.47
  628.8 12.6 %multiply_subtract_fusion = (f32[4,2,1024,128]{3,2,1,0:T(8,128)}, f32[4,2,1024,128]{3,2,1,0:T(8,128)}, f32[4,2,1024,128]{3,2,1,0:T(8,128)}) fusion(f32[4,2,1024,128]{3,2,1,0:T(8,128)} %param.54, bf16[4,2,1024,128]{3,2,1,0:T(8,128)(2,1)} %collective-permute-done.54, bf16[4,2,1024,128]{3,2,1,0:T(8,128)(2,1)} %collective-permute-done.52, ...), kind=kLoop, calls=%fused_computation.27 | loop fusion | flops 20971520 | bytes 31457280 | tf_op jit(solution)/shard_map/sub | solution.py:70
  643.7 3.2 copy.270
  (433 shorter events, 146.0 us)
Async XLA Ops:
  7.2 57.2 %all-gather.7.cloned.1.call-start = ((), (), s32[]{:S(2)}) async-start(), calls=%async_computation.3 | async-start | bytes 1861632 | tf_op jit(solution)/shard_map/all_gather | solution.py:457
  15.5 111.2 %all-gather.15.cloned.1.call-start = ((), (), s32[]{:S(2)}) async-start(), calls=%async_computation.7 | async-start | bytes 7864320 | tf_op jit(solution)/shard_map/all_gather | solution.py:472
  68.4 37.7 %collective-permute-start.1 = (bf16[256,1024]{1,0:T(8,128)(2,1)S(1)}, bf16[256,1024]{1,0:T(8,128)(2,1)S(1)}, u32[]{:S(2)}, u32[]{:S(2)}) collective-permute-start(bf16[256,1024]{1,0:T(8,128)(2,1)S(1)} %constant_dynamic-slice_fusion.dy_two_ref.refs_7_), channel_id=1, source_target_pairs={{0,8},{8,16},{16,24},{24,28},{28,20},{20,12},{12,4},{4,0},{1,9},{9... | collective-permute-start | bytes 1572872 | tf_op jit(solution)/shard_map/ppermute | solution.py:102
  88.7 46.7 %all-to-all-start = ((bf16[4,256,256]{2,1,0:T(8,128)(2,1)}), bf16[4,256,256]{2,1,0:T(8,128)(2,1)S(1)}, u32[]{:S(2)}, u32[]{:S(2)}) async-start(bf16[4,256,256]{2,1,0:T(8,128)(2,1)} %copy.204), calls=%async_computation | async-start | bytes 1048576 | tf_op jit(solution)/shard_map/all_to_all | solution.py:492
  95.1 88.6 %collective-permute-start.5 = (bf16[4,128,1024]{2,1,0:T(8,128)(2,1)}, bf16[4,128,1024]{2,1,0:T(8,128)(2,1)}, u32[]{:S(2)}, u32[]{:S(2)}) collective-permute-start(bf16[4,128,1024]{2,1,0:T(8,128)(2,1)} %convert_element_type.437), channel_id=1, source_target_pairs={{0,2},{1,3},{2,0},{3,1},{4,6},{5,7},{6,4},{7,5},{8,10},{9,11},{10,... | collective-permute-start | bytes 3145736 | tf_op jit(solution)/shard_map/ppermute | solution.py:132
  97.1 88.2 %collective-permute-start.6 = (bf16[4,128,1024]{2,1,0:T(8,128)(2,1)}, bf16[4,128,1024]{2,1,0:T(8,128)(2,1)}, u32[]{:S(2)}, u32[]{:S(2)}) collective-permute-start(bf16[4,128,1024]{2,1,0:T(8,128)(2,1)} %convert_element_type.437), channel_id=1, source_target_pairs={{0,1},{1,0},{2,3},{3,2},{4,5},{5,4},{6,7},{7,6},{8,9},{9,8},{10,11... | collective-permute-start | bytes 3145736 | tf_op jit(solution)/shard_map/ppermute | solution.py:134
  97.1 46.2 %collective-permute-start.17 = (bf16[256,1024]{1,0:T(8,128)(2,1)S(1)}, bf16[256,1024]{1,0:T(8,128)(2,1)S(1)}, u32[]{:S(2)}, u32[]{:S(2)}) collective-permute-start(bf16[256,1024]{1,0:T(8,128)(2,1)S(1)} %constant_dynamic-slice_fusion.dy_two_ref.refs_7_), channel_id=1, source_target_pairs={{0,4},{8,0},{16,8},{24,16},{28,24},{20,28},{12,20},{4,12},{1,5},{9... | collective-permute-start | bytes 1572872 | tf_op jit(solution)/shard_map/ppermute | solution.py:105
  103.1 80.2 %collective-permute-start.2 = (bf16[4,2,1024,128]{3,2,1,0:T(8,128)(2,1)}, bf16[4,2,1024,128]{3,2,1,0:T(8,128)(2,1)}, u32[]{:S(2)}, u32[]{:S(2)}) collective-permute-start(bf16[4,2,1024,128]{3,2,1,0:T(8,128)(2,1)} %convert_element_type.436), channel_id=1, source_target_pairs={{0,2},{1,3},{2,0},{3,1},{4,6},{5,7},{6,4},{7,5},{8,10},{9,11},{10,... | collective-permute-start | bytes 6291464 | tf_op jit(solution)/shard_map/ppermute | solution.py:132
  106.1 79.7 %collective-permute-start.14 = (bf16[256,1024]{1,0:T(8,128)(2,1)S(1)}, bf16[256,1024]{1,0:T(8,128)(2,1)}, u32[]{:S(2)}, u32[]{:S(2)}) collective-permute-start(bf16[256,1024]{1,0:T(8,128)(2,1)S(1)} %collective-permute-done.1.dy_one_ref.refs_6_), channel_id=1, source_target_pairs={{0,8},{8,16},{16,24},{24,28},{28,20},{20,12},{12,4},{4,0},{1,9},{9... | collective-permute-start | bytes 1572872 | tf_op jit(solution)/shard_map/ppermute | solution.py:102
  143.2 90.0 %collective-permute-start.3 = (bf16[4,2,1024,128]{3,2,1,0:T(8,128)(2,1)}, bf16[4,2,1024,128]{3,2,1,0:T(8,128)(2,1)}, u32[]{:S(2)}, u32[]{:S(2)}) collective-permute-start(bf16[4,2,1024,128]{3,2,1,0:T(8,128)(2,1)} %convert_element_type.436), channel_id=1, source_target_pairs={{0,1},{1,0},{2,3},{3,2},{4,5},{5,4},{6,7},{7,6},{8,9},{9,8},{10,11... | collective-permute-start | bytes 6291464 | tf_op jit(solution)/shard_map/ppermute | solution.py:134
  183.3 58.3 %collective-permute-start.4 = (bf16[4,2,1024,128]{3,2,1,0:T(8,128)(2,1)}, bf16[4,2,1024,128]{3,2,1,0:T(8,128)(2,1)}, u32[]{:S(2)}, u32[]{:S(2)}) collective-permute-start(bf16[4,2,1024,128]{3,2,1,0:T(8,128)(2,1)} %collective-permute-done.2), channel_id=1, source_target_pairs={{0,1},{1,0},{2,3},{3,2},{4,5},{5,4},{6,7},{7,6},{8,9},{9,8},{10,11... | collective-permute-start | bytes 6291464 | tf_op jit(solution)/shard_map/ppermute | solution.py:134
  183.7 16.1 %collective-permute-start = (bf16[256,1152]{1,0:T(8,128)(2,1)S(1)}, bf16[256,1152]{1,0:T(8,128)(2,1)S(1)}, u32[]{:S(2)}, u32[]{:S(2)}) collective-permute-start(bf16[256,1152]{1,0:T(8,128)(2,1)S(1)} %concatenate.63.two_ref.refs_7_), channel_id=1, source_target_pairs={{0,8},{8,16},{16,24},{24,28},{28,20},{20,12},{12,4},{4,0},{1,9},{9... | collective-permute-start | bytes 1769480 | tf_op jit(solution)/shard_map/ppermute | solution.py:102
  185.2 14.1 %collective-permute-start.18 = (bf16[256,1024]{1,0:T(8,128)(2,1)S(1)}, bf16[256,1024]{1,0:T(8,128)(2,1)S(1)}, u32[]{:S(2)}, u32[]{:S(2)}) collective-permute-start(bf16[256,1024]{1,0:T(8,128)(2,1)S(1)} %collective-permute-done.17.dy_two_ref.refs_5_), channel_id=1, source_target_pairs={{0,4},{8,0},{16,8},{24,16},{28,24},{20,28},{12,20},{4,12},{1,5},{9... | collective-permute-start | bytes 1572872 | tf_op jit(solution)/shard_map/ppermute | solution.py:105
  185.8 15.6 %collective-permute-start.7 = (bf16[4,128,1024]{2,1,0:T(8,128)(2,1)}, bf16[4,128,1024]{2,1,0:T(8,128)(2,1)S(1)}, u32[]{:S(2)}, u32[]{:S(2)}) collective-permute-start(bf16[4,128,1024]{2,1,0:T(8,128)(2,1)} %collective-permute-done.5), channel_id=1, source_target_pairs={{0,1},{1,0},{2,3},{3,2},{4,5},{5,4},{6,7},{7,6},{8,9},{9,8},{10,11... | collective-permute-start | bytes 3145736 | tf_op jit(solution)/shard_map/ppermute | solution.py:134
  199.3 14.6 %collective-permute-start.11 = (bf16[256,1152]{1,0:T(8,128)(2,1)S(1)}, bf16[256,1152]{1,0:T(8,128)(2,1)S(1)}, u32[]{:S(2)}, u32[]{:S(2)}) collective-permute-start(bf16[256,1152]{1,0:T(8,128)(2,1)S(1)} %concatenate.63.two_ref.refs_7_), channel_id=1, source_target_pairs={{0,4},{8,0},{16,8},{24,16},{28,24},{20,28},{12,20},{4,12},{1,5},{9... | collective-permute-start | bytes 1769480 | tf_op jit(solution)/shard_map/ppermute | solution.py:105
  199.8 16.3 %collective-permute-start.8 = (bf16[256,1152]{1,0:T(8,128)(2,1)S(1)}, bf16[256,1152]{1,0:T(8,128)(2,1)S(1)}, u32[]{:S(2)}, u32[]{:S(2)}) collective-permute-start(bf16[256,1152]{1,0:T(8,128)(2,1)S(1)} %collective-permute-done.one_ref.refs_6_), channel_id=1, source_target_pairs={{0,8},{8,16},{16,24},{24,28},{28,20},{20,12},{12,4},{4,0},{1,9},{9... | collective-permute-start | bytes 1769480 | tf_op jit(solution)/shard_map/ppermute | solution.py:102
  201.4 31.3 %collective-permute-start.15 = (bf16[256,1024]{1,0:T(8,128)(2,1)}, bf16[256,1024]{1,0:T(8,128)(2,1)}, u32[]{:S(2)}, u32[]{:S(2)}) collective-permute-start(bf16[256,1024]{1,0:T(8,128)(2,1)} %collective-permute-done.14.dy_one_ref.refs_4_), channel_id=1, source_target_pairs={{0,8},{8,16},{16,24},{24,28},{28,20},{20,12},{12,4},{4,0},{1,9},{9... | collective-permute-start | bytes 1572872 | tf_op jit(solution)/shard_map/ppermute | solution.py:102
  213.9 20.8 %collective-permute-start.12 = (bf16[256,1152]{1,0:T(8,128)(2,1)S(1)}, bf16[256,1152]{1,0:T(8,128)(2,1)S(1)}, u32[]{:S(2)}, u32[]{:S(2)}) collective-permute-start(bf16[256,1152]{1,0:T(8,128)(2,1)S(1)} %collective-permute-done.11.two_ref.refs_5_), channel_id=1, source_target_pairs={{0,4},{8,0},{16,8},{24,16},{28,24},{20,28},{12,20},{4,12},{1,5},{9... | collective-permute-start | bytes 1769480 | tf_op jit(solution)/shard_map/ppermute | solution.py:105
  216.1 24.0 %collective-permute-start.9 = (bf16[256,1152]{1,0:T(8,128)(2,1)S(1)}, bf16[256,1152]{1,0:T(8,128)(2,1)}, u32[]{:S(2)}, u32[]{:S(2)}) collective-permute-start(bf16[256,1152]{1,0:T(8,128)(2,1)S(1)} %collective-permute-done.8.one_ref.refs_4_), channel_id=1, source_target_pairs={{0,8},{8,16},{16,24},{24,28},{28,20},{20,12},{12,4},{4,0},{1,9},{9... | collective-permute-start | bytes 1769480 | tf_op jit(solution)/shard_map/ppermute | solution.py:102
  232.7 16.0 %collective-permute-start.19 = (bf16[256,1024]{1,0:T(8,128)(2,1)S(1)}, bf16[256,1024]{1,0:T(8,128)(2,1)S(1)}, u32[]{:S(2)}, u32[]{:S(2)}) collective-permute-start(bf16[256,1024]{1,0:T(8,128)(2,1)S(1)} %copy-done.15), channel_id=1, source_target_pairs={{0,4},{8,0},{16,8},{24,16},{28,24},{20,28},{12,20},{4,12},{1,5},{9... | collective-permute-start | bytes 1572872 | tf_op jit(solution)/shard_map/ppermute | solution.py:105
  233.3 18.0 %collective-permute-start.16 = (bf16[256,1024]{1,0:T(8,128)(2,1)}, bf16[256,1024]{1,0:T(8,128)(2,1)S(1)}, u32[]{:S(2)}, u32[]{:S(2)}) collective-permute-start(bf16[256,1024]{1,0:T(8,128)(2,1)} %collective-permute-done.15.dy_one_ref.refs_2_), channel_id=1, source_target_pairs={{0,8},{8,16},{16,24},{24,28},{28,20},{20,12},{12,4},{4,0},{1,9},{9... | collective-permute-start | bytes 1572872 | tf_op jit(solution)/shard_map/ppermute | solution.py:102
  234.8 20.9 %collective-permute-start.13 = (bf16[256,1152]{1,0:T(8,128)(2,1)S(1)}, bf16[256,1152]{1,0:T(8,128)(2,1)S(1)}, u32[]{:S(2)}, u32[]{:S(2)}) collective-permute-start(bf16[256,1152]{1,0:T(8,128)(2,1)S(1)} %collective-permute-done.12.two_ref.refs_3_), channel_id=1, source_target_pairs={{0,4},{8,0},{16,8},{24,16},{28,24},{20,28},{12,20},{4,12},{1,5},{9... | collective-permute-start | bytes 1769480 | tf_op jit(solution)/shard_map/ppermute | solution.py:105
  240.1 22.1 %collective-permute-start.10 = (bf16[256,1152]{1,0:T(8,128)(2,1)}, bf16[256,1152]{1,0:T(8,128)(2,1)S(1)}, u32[]{:S(2)}, u32[]{:S(2)}) collective-permute-start(bf16[256,1152]{1,0:T(8,128)(2,1)} %collective-permute-done.9.one_ref.refs_2_), channel_id=1, source_target_pairs={{0,8},{8,16},{16,24},{24,28},{28,20},{20,12},{12,4},{4,0},{1,9},{9... | collective-permute-start | bytes 1769480 | tf_op jit(solution)/shard_map/ppermute | solution.py:102
  282.2 101.3 %collective-permute-start.27 = (bf16[256,1152]{1,0:T(8,128)(2,1)}, bf16[256,1152]{1,0:T(8,128)(2,1)}, u32[]{:S(2)}, u32[]{:S(2)}) collective-permute-start(bf16[256,1152]{1,0:T(8,128)(2,1)} %get-tuple-element.120), channel_id=1, source_target_pairs={{0,4},{8,0},{16,8},{24,16},{28,24},{20,28},{12,20},{4,12},{1,5},{9... | collective-permute-start | bytes 1769480 | tf_op jit(solution)/shard_map/ppermute | solution.py:115
  359.2 80.3 %collective-permute-start.56 = (bf16[4,128,1024]{2,1,0:T(8,128)(2,1)}, bf16[4,128,1024]{2,1,0:T(8,128)(2,1)}, u32[]{:S(2)}, u32[]{:S(2)}) collective-permute-start(bf16[4,128,1024]{2,1,0:T(8,128)(2,1)} %get-tuple-element.278), channel_id=1, source_target_pairs={{0,1},{1,0},{2,3},{3,2},{4,5},{5,4},{6,7},{7,6},{8,9},{9,8},{10,11... | collective-permute-start | bytes 3145736 | tf_op jit(solution)/shard_map/ppermute | solution.py:142
  359.2 167.4 %collective-permute-start.55 = (bf16[4,128,1024]{2,1,0:T(8,128)(2,1)}, bf16[4,128,1024]{2,1,0:T(8,128)(2,1)}, u32[]{:S(2)}, u32[]{:S(2)}) collective-permute-start(bf16[4,128,1024]{2,1,0:T(8,128)(2,1)} %get-tuple-element.277), channel_id=1, source_target_pairs={{0,1},{1,0},{2,3},{3,2},{4,5},{5,4},{6,7},{7,6},{8,9},{9,8},{10,11... | collective-permute-start | bytes 3145736 | tf_op jit(solution)/shard_map/ppermute | solution.py:142
  359.7 32.7 %collective-permute-start.31 = (bf16[256,1152]{1,0:T(8,128)(2,1)S(1)}, bf16[256,1152]{1,0:T(8,128)(2,1)S(1)}, u32[]{:S(2)}, u32[]{:S(2)}) collective-permute-start(bf16[256,1152]{1,0:T(8,128)(2,1)S(1)} %copy-done.23), channel_id=1, source_target_pairs={{0,8},{8,16},{16,24},{24,28},{28,20},{20,12},{12,4},{4,0},{1,9},{9... | collective-permute-start | bytes 1769480 | tf_op jit(solution)/shard_map/ppermute | solution.py:120
  384.7 16.3 %collective-permute-start.28 = (bf16[256,1152]{1,0:T(8,128)(2,1)S(1)}, bf16[256,1152]{1,0:T(8,128)(2,1)S(1)}, u32[]{:S(2)}, u32[]{:S(2)}) collective-permute-start(bf16[256,1152]{1,0:T(8,128)(2,1)S(1)} %add_convert_fusion.6), channel_id=1, source_target_pairs={{0,4},{8,0},{16,8},{24,16},{28,24},{20,28},{12,20},{4,12},{1,5},{9... | collective-permute-start | bytes 1769480 | tf_op jit(solution)/shard_map/ppermute | solution.py:115
  390.9 20.1 %collective-permute-start.20 = (bf16[256,1024]{1,0:T(8,128)(2,1)S(1)}, bf16[256,1024]{1,0:T(8,128)(2,1)S(1)}, u32[]{:S(2)}, u32[]{:S(2)}) collective-permute-start(bf16[256,1024]{1,0:T(8,128)(2,1)S(1)} %copy-done.27), channel_id=1, source_target_pairs={{0,4},{8,0},{16,8},{24,16},{28,24},{20,28},{12,20},{4,12},{1,5},{9... | collective-permute-start | bytes 1572872 | tf_op jit(solution)/shard_map/ppermute | solution.py:115
  392.4 36.4 %collective-permute-start.24 = (bf16[256,1024]{1,0:T(8,128)(2,1)S(1)}, bf16[256,1024]{1,0:T(8,128)(2,1)S(1)}, u32[]{:S(2)}, u32[]{:S(2)}) collective-permute-start(bf16[256,1024]{1,0:T(8,128)(2,1)S(1)} %copy-done.25), channel_id=1, source_target_pairs={{0,8},{8,16},{16,24},{24,28},{28,20},{20,12},{12,4},{4,0},{1,9},{9... | collective-permute-start | bytes 1572872 | tf_op jit(solution)/shard_map/ppermute | solution.py:120
  401.0 17.0 %collective-permute-start.32 = (bf16[256,1152]{1,0:T(8,128)(2,1)S(1)}, bf16[256,1152]{1,0:T(8,128)(2,1)S(1)}, u32[]{:S(2)}, u32[]{:S(2)}) collective-permute-start(bf16[256,1152]{1,0:T(8,128)(2,1)S(1)} %add_convert_fusion.3), channel_id=1, source_target_pairs={{0,8},{8,16},{16,24},{24,28},{28,20},{20,12},{12,4},{4,0},{1,9},{9... | collective-permute-start | bytes 1769480 | tf_op jit(solution)/shard_map/ppermute | solution.py:120
  410.9 16.3 %collective-permute-start.29 = (bf16[256,1152]{1,0:T(8,128)(2,1)S(1)}, bf16[256,1152]{1,0:T(8,128)(2,1)S(1)}, u32[]{:S(2)}, u32[]{:S(2)}) collective-permute-start(bf16[256,1152]{1,0:T(8,128)(2,1)S(1)} %add_convert_fusion.5), channel_id=1, source_target_pairs={{0,4},{8,0},{16,8},{24,16},{28,24},{20,28},{12,20},{4,12},{1,5},{9... | collective-permute-start | bytes 1769480 | tf_op jit(solution)/shard_map/ppermute | solution.py:115
  418.0 20.4 %collective-permute-start.21 = (bf16[256,1024]{1,0:T(8,128)(2,1)S(1)}, bf16[256,1024]{1,0:T(8,128)(2,1)S(1)}, u32[]{:S(2)}, u32[]{:S(2)}) collective-permute-start(bf16[256,1024]{1,0:T(8,128)(2,1)S(1)} %add_convert_fusion.13), channel_id=1, source_target_pairs={{0,4},{8,0},{16,8},{24,16},{28,24},{20,28},{12,20},{4,12},{1,5},{9... | collective-permute-start | bytes 1572872 | tf_op jit(solution)/shard_map/ppermute | solution.py:115
  427.2 15.7 %collective-permute-start.33 = (bf16[256,1152]{1,0:T(8,128)(2,1)S(1)}, bf16[256,1152]{1,0:T(8,128)(2,1)S(1)}, u32[]{:S(2)}, u32[]{:S(2)}) collective-permute-start(bf16[256,1152]{1,0:T(8,128)(2,1)S(1)} %add_convert_fusion.2), channel_id=1, source_target_pairs={{0,8},{8,16},{16,24},{24,28},{28,20},{20,12},{12,4},{4,0},{1,9},{9... | collective-permute-start | bytes 1769480 | tf_op jit(solution)/shard_map/ppermute | solution.py:120
  428.8 20.0 %collective-permute-start.30 = (bf16[256,1152]{1,0:T(8,128)(2,1)S(1)}, bf16[256,1152]{1,0:T(8,128)(2,1)S(1)}, u32[]{:S(2)}, u32[]{:S(2)}) collective-permute-start(bf16[256,1152]{1,0:T(8,128)(2,1)S(1)} %add_convert_fusion.4), channel_id=1, source_target_pairs={{0,4},{8,0},{16,8},{24,16},{28,24},{20,28},{12,20},{4,12},{1,5},{9... | collective-permute-start | bytes 1769480 | tf_op jit(solution)/shard_map/ppermute | solution.py:115
  438.4 70.5 %collective-permute-start.53 = (bf16[4,2,1024,128]{3,2,1,0:T(8,128)(2,1)}, bf16[4,2,1024,128]{3,2,1,0:T(8,128)(2,1)}, u32[]{:S(2)}, u32[]{:S(2)}) collective-permute-start(bf16[4,2,1024,128]{3,2,1,0:T(8,128)(2,1)} %get-tuple-element.276), channel_id=1, source_target_pairs={{0,1},{1,0},{2,3},{3,2},{4,5},{5,4},{6,7},{7,6},{8,9},{9,8},{10,11... | collective-permute-start | bytes 6291464 | tf_op jit(solution)/shard_map/ppermute | solution.py:142
  439.4 189.4 %collective-permute-start.52 = (bf16[4,2,1024,128]{3,2,1,0:T(8,128)(2,1)}, bf16[4,2,1024,128]{3,2,1,0:T(8,128)(2,1)}, u32[]{:S(2)}, u32[]{:S(2)}) collective-permute-start(bf16[4,2,1024,128]{3,2,1,0:T(8,128)(2,1)} %get-tuple-element.275), channel_id=1, source_target_pairs={{0,1},{1,0},{2,3},{3,2},{4,5},{5,4},{6,7},{7,6},{8,9},{9,8},{10,11... | collective-permute-start | bytes 6291464 | tf_op jit(solution)/shard_map/ppermute | solution.py:142
  442.9 22.7 %collective-permute-start.25 = (bf16[256,1024]{1,0:T(8,128)(2,1)}, bf16[256,1024]{1,0:T(8,128)(2,1)}, u32[]{:S(2)}, u32[]{:S(2)}) collective-permute-start(bf16[256,1024]{1,0:T(8,128)(2,1)} %add_convert_fusion.10), channel_id=1, source_target_pairs={{0,8},{8,16},{16,24},{24,28},{28,20},{20,12},{12,4},{4,0},{1,9},{9... | collective-permute-start | bytes 1572872 | tf_op jit(solution)/shard_map/ppermute | solution.py:120
  448.9 20.6 %collective-permute-start.22 = (bf16[256,1024]{1,0:T(8,128)(2,1)}, bf16[256,1024]{1,0:T(8,128)(2,1)}, u32[]{:S(2)}, u32[]{:S(2)}) collective-permute-start(bf16[256,1024]{1,0:T(8,128)(2,1)} %add_convert_fusion.12), channel_id=1, source_target_pairs={{0,4},{8,0},{16,8},{24,16},{28,24},{20,28},{12,20},{4,12},{1,5},{9... | collective-permute-start | bytes 1572872 | tf_op jit(solution)/shard_map/ppermute | solution.py:115
  461.4 13.5 %all-to-all-start.1 = ((bf16[4,256,256]{2,1,0:T(8,128)(2,1)}), bf16[4,256,256]{2,1,0:T(8,128)(2,1)}, u32[]{:S(2)}, u32[]{:S(2)}) async-start(bf16[4,256,256]{2,1,0:T(8,128)(2,1)} %pad_maximum_fusion.4), calls=%async_computation.1 | async-start | bytes 1048576 | tf_op jit(solution)/shard_map/all_to_all | solution.py:563
  465.5 139.2 %all-gather.13.cloned.1.call-start = ((), (), s32[]{:S(2)}) async-start(), calls=%async_computation.6 | async-start | bytes 2621440 | tf_op jit(solution)/shard_map/all_gather | solution.py:575
  465.6 63.0 %collective-permute-start.57 = (bf16[4,128,1024]{2,1,0:T(8,128)(2,1)}, bf16[4,128,1024]{2,1,0:T(8,128)(2,1)}, u32[]{:S(2)}, u32[]{:S(2)}) collective-permute-start(bf16[4,128,1024]{2,1,0:T(8,128)(2,1)} %add_convert_fusion.1), channel_id=1, source_target_pairs={{0,2},{1,3},{2,0},{3,1},{4,6},{5,7},{6,4},{7,5},{8,10},{9,11},{10,... | collective-permute-start | bytes 3145736 | tf_op jit(solution)/shard_map/ppermute | solution.py:146
  469.5 83.2 %collective-permute-start.26 = (bf16[256,1024]{1,0:T(8,128)(2,1)}, bf16[256,1024]{1,0:T(8,128)(2,1)}, u32[]{:S(2)}, u32[]{:S(2)}) collective-permute-start(bf16[256,1024]{1,0:T(8,128)(2,1)} %add_convert_fusion.9), channel_id=1, source_target_pairs={{0,8},{8,16},{16,24},{24,28},{28,20},{20,12},{12,4},{4,0},{1,9},{9... | collective-permute-start | bytes 1572872 | tf_op jit(solution)/shard_map/ppermute | solution.py:120
  509.0 8.4 %collective-permute-start.34 = (f32[1024,1]{0,1:T(1,128)S(1)}, f32[1024,1]{0,1:T(1,128)S(1)}, u32[]{:S(2)}, u32[]{:S(2)}) collective-permute-start(f32[1024,1]{0,1:T(1,128)S(1)} %bitcast_divide_fusion), channel_id=1, source_target_pairs={{0,1},{1,0},{2,3},{3,2},{4,5},{5,4},{6,7},{7,6},{8,9},{9,8},{10,11... | collective-permute-start | bytes 12296 | tf_op jit(solution)/shard_map/ppermute | solution.py:152
  517.5 7.5 %collective-permute-start.35 = (f32[1024,1]{0,1:T(1,128)S(1)}, f32[1024,1]{0,1:T(1,128)S(1)}, u32[]{:S(2)}, u32[]{:S(2)}) collective-permute-start(f32[1024,1]{0,1:T(1,128)S(1)} %add.554), channel_id=1, source_target_pairs={{0,2},{1,3},{2,0},{3,1},{4,6},{5,7},{6,4},{7,5},{8,10},{9,11},{10,... | collective-permute-start | bytes 12296 | tf_op jit(solution)/shard_map/ppermute | solution.py:154
  520.6 24.5 %all-to-all-start.2 = ((bf16[4,256,512]{1,2,0:T(8,128)(2,1)}), bf16[4,256,512]{1,2,0:T(8,128)(2,1)}, u32[]{:S(2)}, u32[]{:S(2)}) async-start(bf16[4,256,512]{1,2,0:T(8,128)(2,1)} %copy.220), calls=%async_computation.2 | async-start | bytes 2097152 | tf_op jit(solution)/shard_map/all_to_all | solution.py:599
  524.9 118.8 %all-gather.9.cloned.1.call-start = ((), (), s32[]{:S(2)}) async-start(), calls=%async_computation.4 | async-start | bytes 2621440 | tf_op jit(solution)/shard_map/all_gather | solution.py:533
  525.0 29.3 %collective-permute-start.23 = (bf16[256,1024]{1,0:T(8,128)(2,1)}, bf16[256,1024]{1,0:T(8,128)(2,1)}, u32[]{:S(2)}, u32[]{:S(2)}) collective-permute-start(bf16[256,1024]{1,0:T(8,128)(2,1)} %add_convert_fusion.11), channel_id=1, source_target_pairs={{0,4},{8,0},{16,8},{24,16},{28,24},{20,28},{12,20},{4,12},{1,5},{9... | collective-permute-start | bytes 1572872 | tf_op jit(solution)/shard_map/ppermute | solution.py:115
  526.6 102.3 %collective-permute-start.54 = (bf16[4,2,1024,128]{3,2,1,0:T(8,128)(2,1)}, bf16[4,2,1024,128]{3,2,1,0:T(8,128)(2,1)}, u32[]{:S(2)}, u32[]{:S(2)}) collective-permute-start(bf16[4,2,1024,128]{3,2,1,0:T(8,128)(2,1)} %add_convert_fusion), channel_id=1, source_target_pairs={{0,2},{1,3},{2,0},{3,1},{4,6},{5,7},{6,4},{7,5},{8,10},{9,11},{10,... | collective-permute-start | bytes 6291464 | tf_op jit(solution)/shard_map/ppermute | solution.py:146
  528.6 13.7 %collective-permute-start.36 = (bf16[128,513]{0,1:T(8,128)(2,1)S(1)}, bf16[128,513]{0,1:T(8,128)(2,1)S(1)}, u32[]{:S(2)}, u32[]{:S(2)}) collective-permute-start(bf16[128,513]{0,1:T(8,128)(2,1)S(1)} %get-tuple-element.287), channel_id=1, source_target_pairs={{0,4},{8,0},{16,8},{24,16},{28,24},{20,28},{12,20},{4,12},{1,5},{9... | collective-permute-start | bytes 393992 | tf_op jit(solution)/shard_map/ppermute | solution.py:115
  542.3 19.8 %collective-permute-start.40 = (bf16[128,513]{0,1:T(8,128)(2,1)S(1)}, bf16[128,513]{0,1:T(8,128)(2,1)}, u32[]{:S(2)}, u32[]{:S(2)}) collective-permute-start(bf16[128,513]{0,1:T(8,128)(2,1)S(1)} %get-tuple-element.288), channel_id=1, source_target_pairs={{0,8},{8,16},{16,24},{24,28},{28,20},{20,12},{12,4},{4,0},{1,9},{9... | collective-permute-start | bytes 393992 | tf_op jit(solution)/shard_map/ppermute | solution.py:120
  552.7 5.6 collective-permute-start.37
  557.2 86.4 %all-gather.11.cloned.1.call-start = ((), (), s32[]{:S(2)}) async-start(), calls=%async_computation.5 | async-start | bytes 2621440 | tf_op jit(solution)/shard_map/all_gather | solution.py:614
  559.3 5.0 collective-permute-start.38
  562.1 4.8 collective-permute-start.43
  565.4 5.0 collective-permute-start.41
  566.9 37.6 %collective-permute-start.44 = (f32[1024,33]{0,1:T(8,128)S(1)}, f32[1024,33]{0,1:T(8,128)S(1)}, u32[]{:S(2)}, u32[]{:S(2)}) collective-permute-start(f32[1024,33]{0,1:T(8,128)S(1)} %fusion.122), channel_id=1, source_target_pairs={{0,2},{1,3},{2,0},{3,1},{4,6},{5,7},{6,4},{7,5},{8,10},{9,11},{10,... | collective-permute-start | bytes 405512 | tf_op jit(solution)/shard_map/ppermute | solution.py:154
  567.6 37.0 %collective-permute-start.39 = (bf16[128,513]{0,1:T(8,128)(2,1)S(1)}, bf16[128,513]{0,1:T(8,128)(2,1)S(1)}, u32[]{:S(2)}, u32[]{:S(2)}) collective-permute-start(bf16[128,513]{0,1:T(8,128)(2,1)S(1)} %get-tuple-element.285), channel_id=1, source_target_pairs={{0,4},{8,0},{16,8},{24,16},{28,24},{20,28},{12,20},{4,12},{1,5},{9... | collective-permute-start | bytes 393992 | tf_op jit(solution)/shard_map/ppermute | solution.py:115
  570.4 34.2 %collective-permute-start.42 = (bf16[128,513]{0,1:T(8,128)(2,1)S(1)}, bf16[128,513]{0,1:T(8,128)(2,1)S(1)}, u32[]{:S(2)}, u32[]{:S(2)}) collective-permute-start(bf16[128,513]{0,1:T(8,128)(2,1)S(1)} %add_convert_fusion.15), channel_id=1, source_target_pairs={{0,8},{8,16},{16,24},{24,28},{28,20},{20,12},{12,4},{4,0},{1,9},{9... | collective-permute-start | bytes 393992 | tf_op jit(solution)/shard_map/ppermute | solution.py:120
  613.1 4.6 collective-permute-start.49
  616.1 4.4 collective-permute-start.47
  620.5 6.6 %collective-permute-start.50 = (bf16[128,289]{0,1:T(8,128)(2,1)S(1)}, bf16[128,289]{0,1:T(8,128)(2,1)S(1)}, u32[]{:S(2)}, u32[]{:S(2)}) collective-permute-start(bf16[128,289]{0,1:T(8,128)(2,1)S(1)} %get-tuple-element.296), channel_id=1, source_target_pairs={{0,8},{8,16},{16,24},{24,28},{28,20},{20,12},{12,4},{4,0},{1,9},{9... | collective-permute-start | bytes 221960 | tf_op jit(solution)/shard_map/ppermute | solution.py:120
  626.6 14.9 %collective-permute-start.48 = (bf16[128,289]{0,1:T(8,128)(2,1)S(1)}, bf16[128,289]{0,1:T(8,128)(2,1)S(1)}, u32[]{:S(2)}, u32[]{:S(2)}) collective-permute-start(bf16[128,289]{0,1:T(8,128)(2,1)S(1)} %get-tuple-element.295), channel_id=1, source_target_pairs={{0,4},{8,0},{16,8},{24,16},{28,24},{20,28},{12,20},{4,12},{1,5},{9... | collective-permute-start | bytes 221960 | tf_op jit(solution)/shard_map/ppermute | solution.py:115
  627.3 14.2 %collective-permute-start.51 = (bf16[128,289]{0,1:T(8,128)(2,1)S(1)}, bf16[128,289]{0,1:T(8,128)(2,1)S(1)}, u32[]{:S(2)}, u32[]{:S(2)}) collective-permute-start(bf16[128,289]{0,1:T(8,128)(2,1)S(1)} %add_convert_fusion.22), channel_id=1, source_target_pairs={{0,8},{8,16},{16,24},{24,28},{28,20},{20,12},{12,4},{4,0},{1,9},{9... | collective-permute-start | bytes 221960 | tf_op jit(solution)/shard_map/ppermute | solution.py:120
  (98 other events, 2040.8 us)
Sparse Core Ops, SparseCore 0:
  15.6 48.8 all-gather.6
  67.3 59.3 all-gather.14
  513.3 27.4 all-gather.12
  557.3 33.0 all-gather.8
  617.9 21.6 all-gather.10

commit v2 on v1

v2 whole, which is shorter than its diff:
```python
import functools

import jax
import jax.numpy as jnp
from jax import lax
from jax.experimental import pallas as pl
from jax.experimental.pallas import tpu as pltpu
from jax.sharding import PartitionSpec as P

HEADS = 16
KV_HEADS = 8
HD = 64
EXPERTS = 32
STEP = 10
PAD = 128

NORM_EPS = 1e-06
BETA_ONE = 0.9
BETA_TWO = 0.999
ADAM_EPS = 1e-08
MATRIX_RATE = 0.08
GAIN_RATE = 0.6
MATRIX_DECAY = 0.1
NEG_LARGE = -1e30
BF = jnp.bfloat16
F32 = jnp.float32


def dot(left, right, dims):
    return lax.dot_general(left, right, (dims, ((), ())), preferred_element_type=F32)


def normalize(values):
    inverse = lax.rsqrt(jnp.mean(values * values, axis=-1, keepdims=True) + NORM_EPS)
    return (values * inverse, inverse)


def norm_backward(grad_unit, unit, inverse):
    return inverse * (grad_unit - unit * jnp.mean(grad_unit * unit, axis=-1, keepdims=True))


def rope_tables(length, head_size):
    half_size = head_size // 2
    frequency = 10000.0 ** (-(jnp.arange(half_size, dtype=F32) * 2.0) / head_size)
    angles = jnp.arange(length, dtype=F32)[:, None] * frequency[None, :]
    return (jnp.cos(angles), jnp.sin(angles))


def adamw_update(weight, moment, second, gradient, rate, decay):
    moment_new = BETA_ONE * moment + (1.0 - BETA_ONE) * gradient
    second_new = BETA_TWO * second + (1.0 - BETA_TWO) * gradient * gradient
    fix_one = 1.0 - BETA_ONE**STEP
    fix_two = 1.0 - BETA_TWO**STEP
    update = moment_new / fix_one / (jnp.sqrt(second_new / fix_two) + ADAM_EPS)
    return (weight - rate * (update + decay * weight), moment_new, second_new)


def split_pieces(values, count):
    pieces = []
    for _ in range(count):
        high = lax.reduce_precision(values, 8, 7)
        pieces.append(high.astype(BF))
        values = values - high
    return pieces


def ring_order(size):
    return list(range(0, size, 2)) + list(range(1, size, 2))[::-1]


def ring_perm(size, step):
    order = ring_order(size)
    return [(order[i], order[(i + step) % size]) for i in range(size)]


def ring_index(size, offset):
    me = lax.axis_index("expert")
    place = jnp.where(me % 2 == 0, me // 2, size - 1 - me // 2)
    place = (place + offset) % size
    return jnp.where(place < (size + 1) // 2, 2 * place, 2 * (size - 1 - place) + 1)


def ring_gather(block, size):
    blocks = {0: block}
    ahead = behind = block
    for hop in range(1, size // 2 + 1):
        ahead = lax.ppermute(ahead, "expert", ring_perm(size, 1))
        blocks[-hop] = ahead
        if hop <= (size - 1) // 2:
            behind = lax.ppermute(behind, "expert", ring_perm(size, -1))
            blocks[hop] = behind
    return blocks


def ring_reduce(part, size):
    down = up = None
    messages = []
    for hop in range(size // 2, 0, -1):
        mine = part(-hop)
        total = mine if down is None else (down.astype(F32) + mine.astype(F32)).astype(BF)
        messages.append(total)
        down = lax.ppermute(total, "expert", ring_perm(size, -1))
        side = hop - 1
        if side > 0:
            mine = part(side)
            total = mine if up is None else (up.astype(F32) + mine.astype(F32)).astype(BF)
            up = lax.ppermute(total, "expert", ring_perm(size, 1))
    return [part(0), down] + ([] if up is None else [up]), messages


def tensor_perm(size, along, core):
    chips = size // 2
    return [(t, ((t // 2 + along) % chips) * 2 + ((t % 2) ^ core)) for t in range(size)]


def tensor_gather(shard, size):
    own = [shard] + [
        lax.ppermute(shard, "tensor", tensor_perm(size, -step, 0)) for step in range(1, size // 2)
    ]
    other = [lax.ppermute(piece, "tensor", tensor_perm(size, 0, 1)) for piece in own]
    return own + other


def tensor_reduce(parts, size):
    chips = size // 2
    result = []
    for step in reversed(range(chips)):
        came = lax.ppermute(parts[chips + step], "tensor", tensor_perm(size, 0, 1))
        if step == 0:
            result += [parts[0], came]
        else:
            total = (parts[step].astype(F32) + came.astype(F32)).astype(BF)
            result.append(lax.ppermute(total, "tensor", tensor_perm(size, step, 0)))
    return result


def tensor_sum(values, size):
    values = values + lax.ppermute(values, "tensor", tensor_perm(size, 0, 1))
    moved = [
        lax.ppermute(values, "tensor", tensor_perm(size, step, 0)) for step in range(1, size // 2)
    ]
    return sum(moved, values)


def place_kernel(blocks, cuts, *refs):
    index_ref = refs[0]
    outs = refs[len(refs) - len(cuts) :]
    for block in range(blocks):
        source = refs[1 + block]
        size = source.shape[0]
        start = pl.multiple_of(index_ref[block] * size, size)
        for (low, high), out in zip(cuts, outs):
            out[pl.ds(start, size), :] = source[:, low:high]


def place(blocks, index, cuts=None, after=()):
    size, columns = blocks[0].shape
    cuts = cuts or [(0, columns)]
    count = len(blocks)
    vmem = pl.BlockSpec(memory_space=pltpu.VMEM)
    out = pl.pallas_call(
        functools.partial(place_kernel, count, cuts),
        in_specs=[pl.BlockSpec(memory_space=pltpu.SMEM)]
        + [vmem] * count
        + [pl.BlockSpec(memory_space=pl.ANY)] * len(after),
        out_specs=[vmem] * len(cuts),
        out_shape=[
            jax.ShapeDtypeStruct((count * size, high - low), blocks[0].dtype) for low, high in cuts
        ],
        compiler_params=pltpu.CompilerParams(vmem_limit_bytes=32 * 1024 * 1024),
        name="place",
    )(index, *blocks, *after)
    return out if len(cuts) > 1 else out[0]


def tensor_index(size):
    me = lax.axis_index("tensor")
    chips = size // 2
    chip, core = me // 2, me % 2
    own = [((chip + step) % chips) * 2 + core for step in range(chips)]
    other = [((chip + step) % chips) * 2 + (1 - core) for step in range(chips)]
    return jnp.stack(own + other).astype(jnp.int32)


def expert_kernel(count, afters, *refs):
    first_ref = refs[0]
    message_refs = refs[1 : 1 + count]
    cotangent_refs = refs[1 + count : 1 + 2 * count]
    gate_ref, up_ref, down_ref = refs[1 + 2 * count : 4 + 2 * count]
    outs = refs[4 + 2 * count + afters :]
    grads_ref, scaled_ref = outs[:2]
    y_refs = outs[2 : 2 + count]
    back_refs = outs[2 + count : 2 + 2 * count]
    rows_ref, dy_ref, y_acc, back_acc, tail_acc = outs[2 + 2 * count :]
    expert = pl.program_id(0)
    rows, width = cotangent_refs[0].shape

    @pl.when(expert == 0)
    def _():
        for i in range(count):
            rows_ref[i * rows : (i + 1) * rows] = message_refs[i][...]
            dy_ref[i * rows : (i + 1) * rows] = cotangent_refs[i][...]
        y_acc[...] = jnp.zeros_like(y_acc)
        back_acc[...] = jnp.zeros_like(back_acc)
        tail_acc[...] = jnp.zeros_like(tail_acc)

    gate_w = gate_ref[0]
    up_w = up_ref[0]
    down_w = down_ref[0]
    column = first_ref[0] + expert
    for i in range(count):
        part = slice(i * rows, (i + 1) * rows)
        b = rows_ref[part, :width]
        dy = dy_ref[part]
        gate_pre = dot(b, gate_w, ((1,), (0,)))
        up_pre = dot(b, up_w, ((1,), (0,)))
        sig = jax.nn.sigmoid(gate_pre)
        silu = gate_pre * sig
        act = (silu * up_pre).astype(BF).astype(F32)
        grad_act = dot(dy, down_w, ((1,), (1,)))
        grad_gating = jnp.sum(act * grad_act, axis=1, keepdims=True)
        lane = lax.broadcasted_iota(jnp.int32, (rows, PAD), 1)
        chosen = (lane == column) | (lane == column + EXPERTS)
        tail = rows_ref[part, width:].astype(F32)
        gating = jnp.sum(jnp.where(chosen, tail, 0.0), axis=1, keepdims=True)
        tail_acc[part] += jnp.where(chosen, grad_gating, 0.0)
        grad_act = grad_act * gating
        grad_gate = (grad_act * up_pre * (sig * (1.0 + gate_pre * (1.0 - sig)))).astype(BF)
        grad_up = (grad_act * silu).astype(BF)
        scaled = (act * gating).astype(BF)
        grads_ref[0, 0, part] = grad_gate
        grads_ref[1, 0, part] = grad_up
        scaled_ref[0, part] = scaled
        back_acc[part] += dot(grad_gate, gate_w, ((1,), (1,))) + dot(grad_up, up_w, ((1,), (1,)))
        y_acc[part] += dot(scaled, down_w, ((1,), (0,)))

    @pl.when(expert == pl.num_programs(0) - 1)
    def _():
        lane = lax.broadcasted_iota(jnp.int32, (rows, PAD), 1)
        for i in range(count):
            part = slice(i * rows, (i + 1) * rows)
            y_refs[i][...] = y_acc[part].astype(BF)
            total = tail_acc[part]
            high = total.astype(BF).astype(F32)
            back_refs[i][:, :width] = back_acc[part].astype(BF)
            back_refs[i][:, width:] = jnp.where(lane < EXPERTS, high, total - high).astype(BF)


def expert_blocks(first, messages, owners, cotangents, gate, up, down, after):
    experts, width, hidden = gate.shape
    rows, message = messages[0].shape
    count = len(messages)
    block = pl.BlockSpec((rows, message), lambda e, s: (0, 0))
    plain = pl.BlockSpec((rows, width), lambda e, s: (0, 0))
    owned = [pl.BlockSpec((rows, width), lambda e, s, i=i: (s[1 + i], 0)) for i in range(count)]
    shape = jax.ShapeDtypeStruct
    out = pl.pallas_call(
        functools.partial(expert_kernel, count, len(after)),
        grid_spec=pltpu.PrefetchScalarGridSpec(
            num_scalar_prefetch=1,
            grid=(experts,),
            in_specs=[block] * count
            + owned
            + [pl.BlockSpec((1, width, hidden), lambda e, s: (e, 0, 0))] * 2
            + [pl.BlockSpec((1, hidden, width), lambda e, s: (e, 0, 0))]
            + [pl.BlockSpec(memory_space=pl.ANY)] * len(after),
            out_specs=[
                pl.BlockSpec((2, 1, count * rows, hidden), lambda e, s: (0, e, 0, 0)),
                pl.BlockSpec((1, count * rows, hidden), lambda e, s: (e, 0, 0)),
            ]
            + [plain] * count
            + [block] * count,
            scratch_shapes=[
                pltpu.VMEM((count * rows, message), BF),
                pltpu.VMEM((count * rows, width), BF),
                pltpu.VMEM((count * rows, width), F32),
                pltpu.VMEM((count * rows, width), F32),
                pltpu.VMEM((count * rows, PAD), F32),
            ],
        ),
        out_shape=[
            shape((2, experts, count * rows, hidden), BF),
            shape((experts, count * rows, hidden), BF),
        ]
        + [shape((rows, width), BF)] * count
        + [shape((rows, message), BF)] * count,
        compiler_params=pltpu.CompilerParams(vmem_limit_bytes=48 * 1024 * 1024),
        cost_estimate=pl.CostEstimate(
            flops=12 * count * rows * experts * width * hidden,
            bytes_accessed=6 * experts * width * hidden,
            transcendentals=count * rows * experts * hidden,
        ),
        name="expert_blocks",
    )(jnp.stack([first] + owners), *messages, *cotangents, gate, up, down, *after)
    return out[0], out[1], out[2 : 2 + count], out[2 + count :]


def weight_grad_kernel(spots, swap, shards, afters, *refs):
    blocks = len(spots)
    outs = refs[len(refs) - shards :]
    total = None
    for block, (call, part, rows) in enumerate(spots):
        grads_ref = refs[1 + blocks + call]
        lead = (0,) * (len(grads_ref.shape) - 2)
        grads = grads_ref[lead + (slice(part * rows, (part + 1) * rows),)]
        pair = (grads, refs[1 + block][...]) if swap else (refs[1 + block][...], grads)
        term = dot(*pair, ((0,), (0,)))
        total = term if total is None else total + term
    total = total.astype(BF)
    size = total.shape[0 if swap else 1] // shards
    for i, out in enumerate(outs):
        cut = slice(i * size, (i + 1) * size)
        out[0] = total[cut] if swap else total[:, cut]


def weight_grad(inputs, owners, spots, grads, pick, swap, shards, after):
    lead = grads[0].ndim == 4
    experts, _, hidden = grads[0].shape[-3:]
    rows = spots[0][2]
    width = inputs[0].shape[1] - (PAD if lead else 0)
    blocks = len(inputs)
    shape = (hidden // shards, width) if swap else (width, hidden // shards)
    in_specs = [pl.BlockSpec((rows, width), lambda e, s, i=i: (s[i], 0)) for i in range(blocks)]
    for array in grads:
        if lead:
            in_specs.append(pl.BlockSpec((1, 1) + array.shape[2:], lambda e, s: (pick, e, 0, 0)))
        else:
            in_specs.append(pl.BlockSpec((1,) + array.shape[1:], lambda e, s: (e, 0, 0)))
    in_specs += [pl.BlockSpec(memory_space=pl.ANY)] * len(after)
    return pl.pallas_call(
        functools.partial(weight_grad_kernel, spots, swap, shards, len(after)),
        grid_spec=pltpu.PrefetchScalarGridSpec(
            num_scalar_prefetch=1,
            grid=(experts,),
            in_specs=in_specs,
            out_specs=[pl.BlockSpec((1,) + shape, lambda e, s: (e, 0, 0))] * shards,
        ),
        out_shape=[jax.ShapeDtypeStruct((experts,) + shape, BF)] * shards,
        compiler_params=pltpu.CompilerParams(vmem_limit_bytes=56 * 1024 * 1024),
        cost_estimate=pl.CostEstimate(
            flops=2 * blocks * rows * experts * width * hidden,
            bytes_accessed=4 * blocks * rows * width,
            transcendentals=0,
        ),
        name="weight_grad",
    )(owners, *inputs, *grads, *after)


def adamw_kernel(kinds, parts, *refs):
    weight_ref, moment_ref, second_ref = refs[:3]
    outs = refs[len(refs) - 3 :]
    for kind in range(kinds):
        gradient = refs[3 + kind * parts][0].astype(F32)
        for i in range(1, parts):
            gradient += refs[3 + kind * parts + i][0].astype(F32)
        new = adamw_update(
            weight_ref[0, kind],
            moment_ref[0, kind],
            second_ref[0, kind],
            gradient,
            MATRIX_RATE,
            MATRIX_DECAY,
        )
        for out, value in zip(outs, new):
            out[0, kind] = value


def adamw_blocks(weight, moment, second, gradients):
    experts, kinds, high, wide = weight.shape
    parts = len(gradients[0])
    whole = pl.BlockSpec((1, kinds, high, wide), lambda e: (e, 0, 0, 0))
    return pl.pallas_call(
        functools.partial(adamw_kernel, kinds, parts),
        grid=(experts,),
        in_specs=[whole] * 3 + [pl.BlockSpec((1, high, wide), lambda e: (e, 0, 0))] * (kinds * parts),
        out_specs=[whole] * 3,
        out_shape=[jax.ShapeDtypeStruct(weight.shape, F32)] * 3,
        compiler_params=pltpu.CompilerParams(vmem_limit_bytes=48 * 1024 * 1024),
        cost_estimate=pl.CostEstimate(
            flops=20 * weight.size, bytes_accessed=28 * weight.size, transcendentals=weight.size
        ),
        name="adamw",
    )(weight, moment, second, *[part for kind in gradients for part in kind])


def call_whole(kernel, out_shape, operands, name, scalars=None, specs=None, scratch=(), cost=0):
    specs = specs or {}
    scalars = jnp.zeros((1,), jnp.int32) if scalars is None else scalars
    return pl.pallas_call(
        kernel,
        grid_spec=pltpu.PrefetchScalarGridSpec(
            num_scalar_prefetch=1,
            grid=(1,),
            in_specs=[
                specs.get(i, pl.BlockSpec(array.shape, lambda g, s, n=array.ndim: (0,) * n))
                for i, array in enumerate(operands)
            ],
            out_specs=[
                pl.BlockSpec(shape.shape, lambda g, s, n=len(shape.shape): (0,) * n)
                for shape in out_shape
            ],
            scratch_shapes=list(scratch),
        ),
        out_shape=out_shape,
        compiler_params=pltpu.CompilerParams(vmem_limit_bytes=56 * 1024 * 1024),
        cost_estimate=pl.CostEstimate(flops=cost, bytes_accessed=1 << 22, transcendentals=0),
        name=name,
    )(scalars, *operands)


def swap_halves(chunk):
    columns = chunk.shape[1]
    lane = lax.broadcasted_iota(jnp.int32, chunk.shape, 1)
    return jnp.where(
        lane % HD < HD // 2,
        pltpu.roll(chunk, columns - HD // 2, axis=1),
        pltpu.roll(chunk, HD // 2, axis=1),
    )


def turn(chunk, cosine, sine, begin, end):
    if begin >= end:
        return chunk
    turned = chunk * cosine + swap_halves(chunk) * sine
    if begin + chunk.shape[1] <= end:
        return turned
    lane = lax.broadcasted_iota(jnp.int32, chunk.shape, 1)
    return jnp.where(lane + begin < end, turned, chunk)


def soft(query, key, begin):
    scores = dot(query, key, ((1,), (1,))) * HD ** (-0.5)
    row = lax.broadcasted_iota(jnp.int32, scores.shape, 0) + begin
    scores = jnp.where(row >= lax.broadcasted_iota(jnp.int32, scores.shape, 1), scores, NEG_LARGE)
    exponent = jnp.exp(scores - jnp.max(scores, axis=1, keepdims=True))
    return exponent * (1.0 / jnp.sum(exponent, axis=1, keepdims=True))


def front_kernel(q_cols, k_cols, s_ref, x_ref, gains_ref, qkv_ref, cos_ref, sin_ref, a_ref, rot_ref, mix_ref):
    length = x_ref.shape[0]
    step = min(256, length)
    for begin in range(0, length, step):
        part = slice(begin, begin + step)
        x = x_ref[part].astype(F32)
        a = (normalize(x)[0] * gains_ref[0:1]).astype(BF)
        a_ref[part] = a
        pre = dot(a, qkv_ref[...], ((1,), (0,)))
        for low in range(0, pre.shape[1], 128):
            rot_ref[part, low : low + 128] = turn(
                pre[:, low : low + 128], cos_ref[part], sin_ref[part], low, q_cols + k_cols
            ).astype(BF)
    heads = q_cols // HD
    share = q_cols // k_cols
    for head in range(heads):
        at = head * HD
        key_at = q_cols + head // share * HD
        value_at = key_at + k_cols
        for begin in range(0, length, step):
            end = begin + step
            weights = soft(rot_ref[begin:end, at : at + HD], rot_ref[:end, key_at : key_at + HD], begin)
            mix_ref[begin:end, at : at + HD] = dot(
                weights.astype(BF), rot_ref[:end, value_at : value_at + HD], ((1,), (0,))
            ).astype(BF)


def attention_back_kernel(q_cols, k_cols, s_ref, rot_ref, grad_ref, cos_ref, sin_ref, out_ref, acc_ref):
    length = rot_ref.shape[0]
    step = min(256, length)
    acc_ref[...] = jnp.zeros_like(acc_ref)
    heads = q_cols // HD
    share = q_cols // k_cols
    scale = HD ** (-0.5)
    for head in range(heads):
        at = head * HD
        key_at = q_cols + head // share * HD
        value_at = key_at + k_cols
        for begin in range(0, length, step):
            end = begin + step
            query = rot_ref[begin:end, at : at + HD]
            key = rot_ref[:end, key_at : key_at + HD]
            grad = grad_ref[begin:end, at : at + HD]
            weights = soft(query, key, begin)
            grad_weights = dot(grad, rot_ref[:end, value_at : value_at + HD], ((1,), (1,)))
            delta = jnp.sum(weights * grad_weights, axis=1, keepdims=True)
            grad_scores = (weights * (grad_weights - delta)).astype(BF)
            acc_ref[begin:end, at : at + HD] = dot(grad_scores, key, ((1,), (0,))) * scale
            acc_ref[:end, key_at : key_at + HD] += dot(grad_scores, query, ((0,), (0,))) * scale
            acc_ref[:end, value_at : value_at + HD] += dot(weights.astype(BF), grad, ((0,), (0,)))
    for begin in range(0, length, step):
        part = slice(begin, begin + step)
        for low in range(0, out_ref.shape[1], 128):
            out_ref[part, low : low + 128] = turn(
                acc_ref[part, low : low + 128], cos_ref[part], -sin_ref[part], low, q_cols + k_cols
            ).astype(BF)


def middle_kernel(s_ref, mix_ref, out_ref, x_ref, routes_ref, gains_ref, rest_ref, message_ref, mid_ref):
    rows, width = x_ref.shape
    mid = x_ref[...].astype(F32)
    for t in range(mix_ref.shape[0]):
        mid += dot(mix_ref[t], out_ref[t], ((1,), (1,)))
    mid_ref[...] = mid
    b = (normalize(mid)[0] * gains_ref[1:2]).astype(BF)
    message_ref[:, :width] = b
    logits = dot(b, rest_ref[...], ((1,), (0,)))
    lane = lax.broadcasted_iota(jnp.int32, (rows, PAD), 1)
    routed = lane < 0
    for k in range(routes_ref.shape[1]):
        routed |= lane == routes_ref[:, k : k + 1]
    logits = jnp.where(routed, logits, NEG_LARGE)
    exponent = jnp.where(routed, jnp.exp(logits - jnp.max(logits, axis=1, keepdims=True)), 0.0)
    gating = exponent / jnp.sum(exponent, axis=1, keepdims=True)
    high = gating.astype(BF).astype(F32)
    low = pltpu.roll(gating - high, EXPERTS, axis=1)
    message_ref[:, width:] = jnp.where(lane < EXPERTS, high, low).astype(BF)


def join_tail(tail):
    lane = lax.broadcasted_iota(jnp.int32, tail.shape, 1)
    return jnp.where(lane < EXPERTS, tail + pltpu.roll(tail, PAD - EXPERTS, axis=1), 0.0)


def middle_back_kernel(parts, s_ref, *refs):
    sums = refs[:parts]
    mid_ref, message_ref, dy_ref, gains_ref, rest_ref, out_ref = refs[parts : parts + 6]
    grad_mid_ref, attention_ref, mix_ref, tail_ref = refs[parts + 6 :]
    rows, width = mid_ref.shape
    total = sums[0][...].astype(F32)
    for ref in sums[1:]:
        total += ref[...].astype(F32)
    gating = join_tail(message_ref[:, width:].astype(F32))
    grad_gating = join_tail(total[:, width:])
    grad_logits = gating * (grad_gating - jnp.sum(gating * grad_gating, axis=1, keepdims=True))
    grad_logits = grad_logits.astype(BF)
    grad_b = total[:, :width] + dot(grad_logits, rest_ref[...], ((1,), (1,)))
    unit, inverse = normalize(mid_ref[...])
    grad_mid = dy_ref[...].astype(F32) + norm_backward(grad_b * gains_ref[1:2], unit, inverse)
    grad_mid_ref[...] = grad_mid
    attention = grad_mid.astype(BF)
    attention_ref[...] = attention
    for t in range(out_ref.shape[0]):
        mix_ref[t] = dot(attention, out_ref[t], ((1,), (0,))).astype(BF)
    lane = lax.broadcasted_iota(jnp.int32, (rows, PAD), 1)
    ones = jnp.where(lane == EXPERTS, 1.0, 0.0).astype(BF)
    tail_ref[...] = (
        dot(message_ref[:, :width], grad_logits, ((0,), (0,)))
        + dot((grad_b * unit).astype(BF), ones, ((0,), (0,)))
    ).astype(BF)


def pack_kernel(
    s_ref, a_ref, grad_ref, attention_ref, mix_ref, qkv_ref, rest_ref, tail_ref, main_ref, tail_out_ref
):
    late = dot(a_ref[...], grad_ref[...], ((0,), (0,)))
    columns = late.shape[1]
    main_ref[:, :columns] = late.astype(BF)
    main_ref[:, columns:] = dot(attention_ref[...], mix_ref[...], ((0,), (0,))).astype(BF)
    rest = rest_ref[...].astype(F32)
    lane = lax.broadcasted_iota(jnp.int32, rest.shape, 1)
    piece = (lane == EXPERTS) | (lane == EXPERTS + 2) | (lane == EXPERTS + 4)
    gain = jnp.sum(jnp.where(piece, rest, 0.0), axis=1, keepdims=True)
    gain_grad = jnp.sum(late * qkv_ref[...].astype(F32), axis=1, keepdims=True) / gain
    tail = tail_ref[...].astype(F32)
    tail_out_ref[...] = jnp.where(lane == EXPERTS + 1, gain_grad, tail).astype(BF)


def final_kernel(s_ref, rows_ref, qkv_ref, grad_mid_ref, x_ref, gains_ref, out_ref):
    grad_a = dot(rows_ref[0], qkv_ref[0], ((1,), (1,)))
    for t in range(1, rows_ref.shape[0]):
        grad_a += dot(rows_ref[t], qkv_ref[t], ((1,), (1,)))
    unit, inverse = normalize(x_ref[...].astype(F32))
    out_ref[...] = (
        grad_mid_ref[...] + norm_backward(grad_a * gains_ref[0:1], unit, inverse)
    ).astype(BF)


def body(
    ring,
    tensors,
    tokens,
    cotangent,
    routes,
    norm_gains,
    gains_moment,
    gains_second,
    query_weight,
    query_moment,
    query_second,
    keyval_weight,
    keyval_moment,
    keyval_second,
    output_weight,
    output_moment,
    output_second,
    router_weight,
    router_moment,
    router_second,
    gateup_weight,
    gateup_moment,
    gateup_second,
    down_weight,
    down_moment,
    down_second,
):
    length, width = tokens.shape
    rows = length // tensors
    experts = gateup_weight.shape[0]
    shape = jax.ShapeDtypeStruct
    lane_t = lax.axis_index("tensor").astype(jnp.int32).reshape(1)
    own_block = pl.BlockSpec((rows, width), lambda g, s: (s[0], 0))
    chips = tensors // 2

    gate_pieces = tensor_gather(gateup_weight[:, 0].astype(BF), tensors)
    up_pieces = tensor_gather(gateup_weight[:, 1].astype(BF), tensors)
    down_pieces = tensor_gather(down_weight.astype(BF), tensors)
    gate_low = jnp.concatenate(gate_pieces, axis=2)
    up_low = jnp.concatenate(up_pieces, axis=2)
    down_low = jnp.concatenate(down_pieces, axis=1)

    q_cols = query_weight.shape[1]
    k_cols = keyval_weight.shape[2]
    o_cols = output_weight.shape[0]
    heads_cols = q_cols + 2 * k_cols
    packed = jnp.concatenate(
        [
            query_weight.astype(BF),
            keyval_weight[0].astype(BF),
            keyval_weight[1].astype(BF),
            output_weight.T.astype(BF),
            router_weight.astype(BF),
        ]
        + split_pieces(norm_gains.T, 3)
        + [jnp.zeros((query_weight.shape[0], PAD - EXPERTS - 6), BF)],
        axis=1,
    )
    packed_blocks = ring_gather(packed, ring)
    offsets = sorted(packed_blocks)
    qkv_low, out_low, rest = place(
        [packed_blocks[o] for o in offsets],
        jnp.stack([ring_index(ring, o) for o in offsets]).astype(jnp.int32),
        cuts=[
            (0, heads_cols),
            (heads_cols, heads_cols + o_cols),
            (heads_cols + o_cols, heads_cols + o_cols + PAD),
        ],
        after=gate_pieces[1:chips] + up_pieces[1:chips],
    )
    gains_all = (
        rest[:, EXPERTS : EXPERTS + 2].astype(F32)
        + rest[:, EXPERTS + 2 : EXPERTS + 4].astype(F32)
        + rest[:, EXPERTS + 4 : EXPERTS + 6].astype(F32)
    ).T
    one_spot = jnp.zeros((1,), jnp.int32)
    dy_own = lax.dynamic_slice_in_dim(cotangent, lane_t[0] * rows, rows, axis=0)
    dy_all = lax.all_gather(
        place([dy_own], one_spot, after=[qkv_low]), "expert", axis=0, tiled=True
    )

    cosine_table, sine_table = rope_tables(length, HD)
    cosine_table = jnp.concatenate([cosine_table] * 4, axis=1)
    sine_table = jnp.concatenate([-sine_table, sine_table] * 2, axis=1)
    a, rotated, mixture = call_whole(
        functools.partial(front_kernel, q_cols, k_cols),
        [shape((length, width), BF), shape((length, heads_cols), BF), shape((length, q_cols), BF)],
        [tokens, gains_all, qkv_low, cosine_table, sine_table],
        "attention_forward",
        cost=10**10,
    )

    mixture_rows = lax.all_to_all(
        mixture.reshape(tensors, rows, o_cols), "tensor", split_axis=0, concat_axis=0, tiled=True
    )
    owners_t = tensor_index(tensors)
    out_all = place(
        tensor_gather(out_low, tensors), owners_t, after=[mixture_rows] + down_pieces[1:chips]
    ).reshape(tensors, width, o_cols)
    message, x_mid = call_whole(
        middle_kernel,
        [shape((rows, width + PAD), BF), shape((rows, width), F32)],
        [mixture_rows, out_all, tokens, routes, gains_all, rest],
        "middle",
        scalars=lane_t,
        specs={2: own_block, 3: pl.BlockSpec((rows, routes.shape[1]), lambda g, s: (s[0], 0))},
        cost=10**9,
    )
    blocks = ring_gather(message, ring)

    half = ring // 2
    first = (lax.axis_index("expert") * experts).astype(jnp.int32)
    calls = [[0]] + [[-k, k] for k in range(1, half - 1)] + [[-half, half - 1], [1 - half]]
    back = {}
    forth = {}
    grads = []
    scaled = []
    order = []
    spots = []
    after = []
    for number, call in enumerate(calls):
        owners = [ring_index(ring, o).astype(jnp.int32) for o in call]
        result = expert_blocks(
            first,
            [blocks[o] for o in call],
            owners,
            [dy_all] * len(call),
            gate_low,
            up_low,
            down_low,
            after,
        )
        grads.append(result[0])
        scaled.append(result[1])
        after = [result[1]]
        for part, o in enumerate(call):
            forth[o], back[o] = result[2][part], result[3][part]
            order.append(o)
            spots.append((number, part, rows))
    returned, sent = ring_reduce(lambda offset: back[offset], ring)

    still = jnp.zeros((ring,), jnp.int32)
    whose = jnp.stack([ring_index(ring, o) for o in order]).astype(jnp.int32)
    messages = [blocks[o] for o in order]
    hop = lambda number: [sent[min(number, half - 1)]]
    gate_grads = weight_grad(messages, still, spots, grads, 0, False, tensors, hop(1))
    up_grads = weight_grad(messages, still, spots, grads, 1, False, tensors, hop(2))
    down_grads = weight_grad([dy_all] * ring, whose, spots, scaled, 0, True, tensors, hop(3))

    moe_sum = lax.psum_scatter(
        place([forth[o] for o in order], whose, after=[returned[1]]),
        "expert",
        scatter_dimension=0,
        tiled=True,
    )
    block_out = place(tensor_gather((x_mid + moe_sum.astype(F32)).astype(BF), tensors), owners_t)

    grad_mid, grad_attention, grad_mixture, tail = call_whole(
        functools.partial(middle_back_kernel, len(returned)),
        [
            shape((rows, width), F32),
            shape((rows, width), BF),
            shape((tensors, rows, o_cols), BF),
            shape((width, PAD), BF),
        ],
        returned + [x_mid, message, cotangent, gains_all, rest, out_all],
        "middle_backward",
        scalars=lane_t,
        specs={len(returned) + 2: own_block},
        cost=10**9,
    )
    grad_mixture = lax.all_to_all(
        grad_mixture, "tensor", split_axis=0, concat_axis=0, tiled=True
    ).reshape(length, o_cols)
    grad_attention_all = place(tensor_gather(grad_attention, tensors), owners_t)
    (grad_pre,) = call_whole(
        functools.partial(attention_back_kernel, q_cols, k_cols),
        [shape((length, heads_cols), BF)],
        [rotated, grad_mixture, cosine_table, sine_table],
        "attention_backward",
        scratch=[pltpu.VMEM((length, heads_cols), F32)],
        cost=2 * 10**10,
    )
    grad_pre_rows = lax.all_to_all(
        grad_pre.reshape(tensors, rows, heads_cols), "tensor", split_axis=0, concat_axis=0, tiled=True
    )
    main, tail = call_whole(
        pack_kernel,
        [shape((width, heads_cols + o_cols), BF), shape((width, PAD), BF)],
        [a, grad_pre, grad_attention_all, mixture, qkv_low, rest, tail],
        "pack",
        cost=4 * 10**9,
    )
    tail = tensor_sum(tail, tensors)
    piece = width // ring

    def own_piece(offset):
        start = ring_index(ring, offset) * piece
        return jnp.concatenate(
            [lax.dynamic_slice_in_dim(array, start, piece, axis=0) for array in (main, tail)], axis=1
        )

    summed = sum(part.astype(F32) for part in ring_reduce(own_piece, ring)[0])
    qkv_all = lax.all_gather(place([qkv_low], one_spot, after=[scaled[1]]), "tensor")
    (input_grad,) = call_whole(
        final_kernel,
        [shape((rows, width), BF)],
        [grad_pre_rows, qkv_all, grad_mid, tokens, gains_all],
        "input_gradient",
        scalars=lane_t,
        specs={3: own_block},
        cost=2 * 10**9,
    )
    input_grad = place(tensor_gather(input_grad, tensors), owners_t)

    new_gateup = adamw_blocks(
        gateup_weight,
        gateup_moment,
        gateup_second,
        [tensor_reduce(gate_grads, tensors), tensor_reduce(up_grads, tensors)],
    )
    new_down = [
        array[:, 0]
        for array in adamw_blocks(
            down_weight[:, None],
            down_moment[:, None],
            down_second[:, None],
            [tensor_reduce(down_grads, tensors)],
        )
    ]
    query_sum = summed[:, :q_cols]
    keyval_sum = jnp.stack([summed[:, q_cols : q_cols + k_cols], summed[:, q_cols + k_cols : heads_cols]])
    output_sum = summed[:, heads_cols : heads_cols + o_cols].T
    ends = summed[:, heads_cols + o_cols :]
    router_sum = ends[:, :EXPERTS]
    gains_sum = jnp.stack([ends[:, EXPERTS + 1], ends[:, EXPERTS]])
    new_gains = adamw_update(norm_gains, gains_moment, gains_second, gains_sum, GAIN_RATE, 0.0)
    new_query = adamw_update(
        query_weight, query_moment, query_second, query_sum, MATRIX_RATE, MATRIX_DECAY
    )
    new_keyval = adamw_update(
        keyval_weight, keyval_moment, keyval_second, keyval_sum, MATRIX_RATE, MATRIX_DECAY
    )
    new_output = adamw_update(
        output_weight, output_moment, output_second, output_sum, MATRIX_RATE, MATRIX_DECAY
    )
    new_router = adamw_update(
        router_weight, router_moment, router_second, router_sum, MATRIX_RATE, MATRIX_DECAY
    )
    return (
        (block_out, input_grad)
        + tuple(new_gains)
        + tuple(new_query)
        + tuple(new_keyval)
        + tuple(new_output)
        + tuple(new_router)
        + tuple(new_gateup)
        + tuple(new_down)
    )


def solution(mesh):
    rows = P("expert", None)
    gains = P(None, "expert")
    query = P("expert", "tensor")
    keyval = P(None, "expert", "tensor")
    output = P("tensor", "expert")
    gateup = P("expert", None, None, "tensor")
    down = P("expert", "tensor", None)
    weights = tuple(
        spec for spec in (gains, query, keyval, output, rows, gateup, down) for _ in range(3)
    )
    return jax.shard_map(
        functools.partial(body, mesh.shape["expert"], mesh.shape["tensor"]),
        mesh=mesh,
        in_specs=(rows, rows, rows) + weights,
        out_specs=(rows, rows) + weights,
        check_vma=False,
    )
```

time: 666 us -> 593 us (0.89)
  Pallas kernels: 113 us -> 213 us
  waiting for transfers between devices: 250 us -> 174 us
  matrix products: 55.2 us -> 0 us
  other arithmetic: 90 us -> 44.1 us
  local copies, waits for them, and re-layouts: 61.6 us -> 68.7 us
    pallas_call x6 -> x24, Pallas kernels: 113 us -> 213 us  [the longest x5 85.9 us: expert_blocks(): pl.pallas_call(functools.partial(expert_kernel, count, len(after)), grid_...]
    all_gather x5 -> x2, waiting for transfers between devices: 69.5 us -> 0.01 us  [the longest x1 0.01 us: body(): lax.all_gather(place([dy_own], one_spot, after=[qkv_low]), 'expert', axis...]
    dot_general x30 -> x0, matrix products: 55.2 us -> none  [the longest x16 25.8 us: dot(): lax.dot_general(left, right, (dims, ((), ())), preferred_element_type=F32)]
    unnamed x206 -> x182, local copies, waits for them, and re-layouts: 25.4 us -> 57 us
    ppermute x6, waiting for transfers between devices: 29 us -> 0.12 us  [ring_gather(): behind = lax.ppermute(behind, 'expert', ring_perm(size, -1))]
    ppermute x8, waiting for transfers between devices: 15.6 us -> 39.5 us  [ring_gather(): ahead = lax.ppermute(ahead, 'expert', ring_perm(size, 1))]
    convert_element_type x32 -> x15, other arithmetic: 38.7 us -> 16.7 us  [the longest x3 6.32 us: tensor_reduce(): total = (parts[step].astype(F32) + came.astype(F32)).astype(BF)]
    ppermute x2 -> x1, waiting for transfers between devices: 32.6 us -> 12.6 us  [tensor_sum(): lax.ppermute(values, 'tensor', tensor_perm(size, step, 0))]
  transfers between devices with their start and end apart: 66 -> 66, of which waited for: 26 -> 24; matrix products, arithmetic and copies ran while one was open for 28% -> 12% of each run, Pallas kernels for 14% -> 35%
where the time goes in v2:
time: 593 us; the launch traced here: 587 us
  Pallas kernels  213 us (36%)
  waiting for transfers between devices  174 us (29%)
  starting transfers between devices  72.8 us (12%)
  local copies, waits for them, and re-layouts  68.7 us (12%)
  other arithmetic  44.1 us (7%)
  between operations  14.8 us (2%)
    pallas_call x5, Pallas kernels, expert_blocks(): pl.pallas_call(functools.partial(expert_kernel, count, len(after)), grid_...  85.9 us
    ppermute x7, waiting for transfers between devices, tensor_gather(): lax.ppermute(shard, 'tensor', tensor_perm(size, -step, 0))  58.4 us
    unnamed x182, local copies, waits for them, and re-layouts  57 us
    pallas_call x6, Pallas kernels, call_whole(): pl.pallas_call(kernel, grid_spec=pltpu.PrefetchScalarGridSpec(num_scalar_...  53.4 us
    pallas_call x3, Pallas kernels, weight_grad(): pl.pallas_call(functools.partial(weight_grad_kernel, spots, swap, shards,...  44.3 us
    ppermute x8, waiting for transfers between devices, ring_gather(): ahead = lax.ppermute(ahead, 'expert', ring_perm(size, 1))  39.5 us
    ppermute x8, waiting for transfers between devices, ring_reduce(): down = lax.ppermute(total, 'expert', ring_perm(size, -1))  37 us
    pallas_call x2, Pallas kernels, adamw_blocks(): pl.pallas_call(functools.partial(adamw_kernel, kinds, parts), grid=(exper...  18.5 us
  transfers between devices with their start and end apart: 66, of which 24 were waited for; matrix products, arithmetic and copies ran while one was open for 12% of the time, Pallas kernels for 35%

profile of v2, /device:TPU:0, one launch (start us, length us, event | category | flops | bytes accessed | tf_op | source)
XLA Modules:
  0.0 587.3 jit_solution(4752390737078310083)
XLA Ops:
  7.3 4.0 slice_bitcast_fusion
  11.3 2.9 collective-permute-start.7
  18.3 2.1 collective-permute-start
  20.5 5.0 collective-permute-done.refs_4_
  25.5 1.8 collective-permute-start.1
  28.9 2.7 collective-permute-done.1.refs_3_
  34.3 3.7 collective-permute-done.2.refs_2_
  38.0 1.9 collective-permute-start.3
  41.1 3.3 collective-permute-done.3.refs_1_
  45.3 14.9 %collective-permute-done.8.refs_10_ = bf16[4,1024,128]{2,1,0:T(8,128)(2,1)} collective-permute-done((bf16[4,1024,128]{2,1,0:T(8,128)(2,1)}, bf16[4,1024,128]{2,1,0:T(8,128)(2,1)}, u32[]{:S(2)}, u32[]{:S(2)}) %collective-permute-start.8) | collective-permute-done | bytes 1048608 | tf_op jit(solution)/shard_map/ppermute | solution.py:118
  65.2 2.2 place.8
  72.1 2.0 fusion.2
  74.0 1.9 pad_maximum_fusion.3
  76.7 30.1 %collective-permute-done.9.refs_2_ = bf16[1024,256]{1,0:T(8,128)(2,1)} collective-permute-done((bf16[1024,256]{1,0:T(8,128)(2,1)}, bf16[1024,256]{1,0:T(8,128)(2,1)}, u32[]{:S(2)}, u32[]{:S(2)}) %collective-permute-start.9) | collective-permute-done | bytes 524320 | tf_op jit(solution)/shard_map/ppermute | solution.py:118
  106.7 13.5 %attention_forward.1 = (bf16[1024,1024]{1,0:T(8,128)(2,1)}, bf16[1024,512]{1,0:T(8,128)(2,1)}, bf16[1024,256]{1,0:T(8,128)(2,1)}) custom-call(s32[1]{0:T(128)} %constant.396.clone.1.s_ref.refs_0_, bf16[1024,1024]{1,0:T(8,128)(2,1)} %x_ref.5, f32[2,1024]{1,0:T(2,128)} %add_bitcast_fusion.gains_ref.refs_6_, bf16[1024,512]{1,0:T(8,128)(2,1)} %copy-done.5, ...), custom_call_target="tpu_custom_call" | custom-call | flops 10000000000 | bytes 4194304 | tf_op jit(solution)/shard_map/attention_forward/pallas_call | solution.py:389
  120.2 3.5 all-to-all-start
  125.3 7.2 %all-to-all-done.refs_5_.mix_ref = bf16[4,256,256]{2,1,0:T(8,128)(2,1)S(1)} async-done(((bf16[4,256,256]{2,1,0:T(8,128)(2,1)}), bf16[4,256,256]{2,1,0:T(8,128)(2,1)S(1)}, u32[]{:S(2)}, u32[]{:S(2)}) %all-to-all-start) | async-done | bytes 524320 | tf_op jit(solution)/shard_map/all_to_all | solution.py:670
  135.6 4.2 middle.1
  142.6 12.4 %collective-permute-done.19.refs_1_.refs_2_ = bf16[256,1152]{1,0:T(8,128)(2,1)S(1)} collective-permute-done((bf16[256,1152]{1,0:T(8,128)(2,1)}, bf16[256,1152]{1,0:T(8,128)(2,1)S(1)}, u32[]{:S(2)}, u32[]{:S(2)}) %collective-permute-start.19) | collective-permute-done | bytes 589856 | tf_op jit(solution)/shard_map/ppermute | solution.py:87
  156.8 3.8 pad_maximum_fusion.refs_3_.refs_5_
  161.1 8.2 %collective-permute-done.21.refs_1_.refs_4_ = bf16[256,1152]{1,0:T(8,128)(2,1)S(1)} collective-permute-done((bf16[256,1152]{1,0:T(8,128)(2,1)S(1)}, bf16[256,1152]{1,0:T(8,128)(2,1)S(1)}, u32[]{:S(2)}, u32[]{:S(2)}) %collective-permute-start.21) | collective-permute-done | bytes 589856 | tf_op jit(solution)/shard_map/ppermute | solution.py:87
  170.8 3.8 pad_maximum_fusion.1.refs_4_.refs_6_
  174.6 3.5 pad_maximum_fusion.2.refs_5_.refs_7_
  178.5 4.2 collective-permute-done.23.refs_1_.refs_8_
  184.2 11.7 %expert_blocks.5 = (bf16[2,4,256,512]{3,2,1,0:T(8,128)(2,1)S(1)}, bf16[4,256,512]{2,1,0:T(8,128)(2,1)S(1)}, bf16[256,1024]{1,0:T(8,128)(2,1)S(1)}, bf16[256,1152]{1,0:T(8,128)(2,1)S(1)}) custom-call(s32[2]{0:T(128)S(1)} %pad_add_fusion.1.refs_0_, bf16[256,1152]{1,0:T(8,128)(2,1)S(1)} %copy-done.24, ...), custom_call_target="tpu_custom_call" | custom-call | flops 6442450944 | bytes 12582912 | tf_op jit(solution)/shard_map/expert_blocks/pallas_call | solution.py:257
  201.4 20.7 %expert_blocks.6 = (bf16[2,4,512,512]{3,2,1,0:T(8,128)(2,1)}, bf16[4,512,512]{2,1,0:T(8,128)(2,1)}, bf16[256,1024]{1,0:T(8,128)(2,1)S(1)}, bf16[256,1024]{1,0:T(...) custom-call(s32[3]{0:T(128)S(1)} %pad_add_fusion.2.refs_0_, ...), custom_call_target="tpu_custom_call" | custom-call | flops 12884901888 | bytes 12582912 | tf_op jit(solution)/shard_map/expert_blocks/pallas_call | solution.py:257
  226.4 12.4 %reduce-scatter.2.cloned.1.call-start = ((), (), s32[]{:S(2)}) async-start(), calls=%async_computation.5 | async-start | bytes 4718592 | tf_op jit(solution)/shard_map/reduce_scatter | solution.py:727
  239.8 20.7 %expert_blocks.7 = (bf16[2,4,512,512]{3,2,1,0:T(8,128)(2,1)}, bf16[4,512,512]{2,1,0:T(8,128)(2,1)S(1)}, bf16[256,1024]{1,0:T(8,128)(2,1)S(1)}, bf16[256,1024]{1,...) custom-call(s32[3]{0:T(128)S(1)} %pad_add_fusion.3.refs_0_, ...), custom_call_target="tpu_custom_call" | custom-call | flops 12884901888 | bytes 12582912 | tf_op jit(solution)/shard_map/expert_blocks/pallas_call | solution.py:257
  263.5 20.9 %expert_blocks.8 = (bf16[2,4,512,512]{3,2,1,0:T(8,128)(2,1)}, bf16[4,512,512]{2,1,0:T(8,128)(2,1)S(1)}, bf16[256,1024]{1,0:T(8,128)(2,1)S(1)}, bf16[256,1024]{1,...) custom-call(s32[3]{0:T(128)S(1)} %pad_add_fusion.4.refs_0_, ...), custom_call_target="tpu_custom_call" | custom-call | flops 12884901888 | bytes 12582912 | tf_op jit(solution)/shard_map/expert_blocks/pallas_call | solution.py:257
  287.2 11.9 %expert_blocks.9 = (bf16[2,4,256,512]{3,2,1,0:T(8,128)(2,1)S(1)}, bf16[4,256,512]{2,1,0:T(8,128)(2,1)S(1)}, bf16[256,1024]{1,0:T(8,128)(2,1)S(1)}, bf16[256,1152]{1,0:T(8,128)(2,1)S(1)}) custom-call(s32[2]{0:T(128)S(1)} %pad_add_fusion.5.refs_0_, bf16[256,1152]{1,0:T(8,128)(2,1)} %collective-permute-done.23.refs_1_.refs_8_, ...), custom_call_target="tpu_custom_call" | custom-call | flops 6442450944 | bytes 12582912 | tf_op jit(solution)/shard_map/expert_blocks/pallas_call | solution.py:257
  301.3 11.3 %collective-permute-done.27 = bf16[256,1152]{1,0:T(8,128)(2,1)S(1)} collective-permute-done((bf16[256,1152]{1,0:T(8,128)(2,1)S(1)}, bf16[256,1152]{1,0:T(8,128)(2,1)S(1)}, u32[]{:S(2)}, u32[]{:S(2)}) %collective-permute-start.27) | collective-permute-done | bytes 589856 | tf_op jit(solution)/shard_map/ppermute | solution.py:102
  315.8 9.2 %collective-permute-done.28 = bf16[256,1152]{1,0:T(8,128)(2,1)S(1)} collective-permute-done((bf16[256,1152]{1,0:T(8,128)(2,1)S(1)}, bf16[256,1152]{1,0:T(8,128)(2,1)S(1)}, u32[]{:S(2)}, u32[]{:S(2)}) %collective-permute-start.28) | collective-permute-done | bytes 589856 | tf_op jit(solution)/shard_map/ppermute | solution.py:102
  327.6 2.0 add_convert_fusion.3
  330.3 6.3 %collective-permute-done.29.refs_9_.refs_1_ = bf16[256,1152]{1,0:T(8,128)(2,1)S(1)} collective-permute-done((bf16[256,1152]{1,0:T(8,128)(2,1)}, bf16[256,1152]{1,0:T(8,128)(2,1)S(1)}, u32[]{:S(2)}, u32[]{:S(2)}) %collective-permute-start.29) | collective-permute-done | bytes 589856 | tf_op jit(solution)/shard_map/ppermute | solution.py:102
  346.0 2.0 copy-done.1
  348.5 14.5 %weight_grad.3 = (bf16[4,1024,128]{2,1,0:T(8,128)(2,1)}, bf16[4,1024,128]{2,1,0:T(8,128)(2,1)}, bf16[4,1024,128]{2,1,0:T(8,128)(2,1)}, bf16[4,1024,128]{2,1,0:T(8,128)(2,1)}) custom-call(s32[8]{0:T(128)} %broadcast_9_refs_0_.2.refs_0_, bf16[256,1152]{1,0:T(8,128)(2,1)} %get-tuple-element.86.refs_1_.refs_4_, bf16[256,1152]{1,0:T(8,128)(2,1)} %copy-done.50, ...), custom_call_target="tpu_custom_call" | custom-call | flops 8589934592 | bytes 8388608 | tf_op jit(solution)/shard_map/weight_grad/pallas_call | solution.py:330
  364.4 5.5 middle_backward.1
  371.7 4.2 all-to-all-start.1
  375.8 15.2 %weight_grad.4 = (bf16[4,1024,128]{2,1,0:T(8,128)(2,1)}, bf16[4,1024,128]{2,1,0:T(8,128)(2,1)}, bf16[4,1024,128]{2,1,0:T(8,128)(2,1)}, bf16[4,1024,128]{2,1,0:T(8,128)(2,1)}) custom-call(s32[8]{0:T(128)} %broadcast_9_refs_0_.2.refs_0_, bf16[256,1152]{1,0:T(8,128)(2,1)} %get-tuple-element.86.refs_1_.refs_4_, bf16[256,1152]{1,0:T(8,128)(2,1)} %copy-done.50, ...), custom_call_target="tpu_custom_call" | custom-call | flops 8589934592 | bytes 8388608 | tf_op jit(solution)/shard_map/weight_grad/pallas_call | solution.py:330
  392.0 18.7 %attention_backward.1.grad_ref = bf16[1024,512]{1,0:T(8,128)(2,1)} custom-call(s32[1]{0:T(128)} %constant.396.clone.1.s_ref.refs_0_, bf16[1024,512]{1,0:T(8,128)(2,1)} %get-tuple-element.103.rot_ref, bf16[1024,256]{1,0:T(8,128)(2,1)} %bitcast.23.grad_ref, f32[1024,128]{1,0:T(8,128)} %get-tuple-element.253.cos_ref, f32[1024,128]{1,0:T(8,128)} %get-tuple-element.254.sin_ref), custom_call_target="tpu_custom_call" | custom-call | flops 20000000000 | bytes 4194304 | tf_op jit(solution)/shard_map/attention_backward/pallas_call | solution.py:389
  413.5 6.2 %pack.1 = (bf16[1024,768]{1,0:T(8,128)(2,1)}, bf16[1024,128]{1,0:T(8,128)(2,1)}) custom-call(s32[1]{0:T(128)} %constant.396.clone.1.s_ref.refs_0_, bf16[1024,1024]{1,0:T(8,128)(2,1)} %get-tuple-element.110.a_ref, bf16[1024,512]{1,0:T(8,128)(2,1)} %attention_backward.1.grad_ref, bf16[1024,1024]{1,0:T(8,128)(2,1)} %copy-done.15, ...), custom_call_target="tpu_custom_call" | custom-call | flops 4000000000 | bytes 4194304 | tf_op jit(solution)/shard_map/pack/pallas_call | solution.py:389
  420.1 2.5 add_convert_fusion.2
  425.7 14.5 %weight_grad.5 = (bf16[4,128,1024]{2,1,0:T(8,128)(2,1)}, bf16[4,128,1024]{2,1,0:T(8,128)(2,1)}, bf16[4,128,1024]{2,1,0:T(8,128)(2,1)}, bf16[4,128,1024]{2,1,0:T(8,128)(2,1)}) custom-call(s32[8]{0:T(128)} %copy-done.49, bf16[2048,1024]{1,0:T(8,128)(2,1)} %all-gather.4.cloned.1.call-done.refs_2_.refs_3_.refs_4_.refs_1_.refs_5_.refs_6_.refs_7_.refs_8_, ...), custom_call_target="tpu_custom_call" | custom-call | flops 8589934592 | bytes 8388608 | tf_op jit(solution)/shard_map/weight_grad/pallas_call | solution.py:330
  441.1 12.6 %collective-permute-done.43 = bf16[1024,128]{1,0:T(8,128)(2,1)S(1)} collective-permute-done((bf16[1024,128]{1,0:T(8,128)(2,1)S(1)}, bf16[1024,128]{1,0:T(8,128)(2,1)S(1)}, u32[]{:S(2)}, u32[]{:S(2)}) %collective-permute-start.43) | collective-permute-done | bytes 262176 | tf_op jit(solution)/shard_map/ppermute | solution.py:140
  457.2 2.5 add_convert_fusion.1
  459.7 3.9 collective-permute-done.44
  465.3 5.6 collective-permute-done.48
  472.6 4.7 collective-permute-done.45
  482.5 2.7 collective-permute-done.49
  487.1 4.2 all-to-all-start.2
  491.4 1.8 add_convert_fusion.9
  493.2 1.8 add_convert_fusion.11
  504.9 11.8 %adamw.2 = (f32[4,2,1024,128]{3,2,1,0:T(8,128)}, f32[4,2,1024,128]{3,2,1,0:T(8,128)}, f32[4,2,1024,128]{3,2,1,0:T(8,128)}) custom-call(f32[4,2,1024,128]{3,2,1,0:T(8,128)} %refs_0_.1, f32[4,2,1024,128]{3,2,1,0:T(8,128)} %refs_1_.1, f32[4,2,1024,128]{3,2,1,0:T(8,128)} %refs_2_.1, bf16[4,1024,128]{2,1,0:T(8,128)(2,1)} %collective-permute-done.52.refs_3_, ...), custom_call_target="tpu_custom_call" | custom-call | flops 20971520 | bytes 29360128 | tf_op jit(solution)/shard_map/adamw/pallas_call | solution.py:372
  516.7 9.4 %collective-permute-done.58.refs_3_ = bf16[4,128,1024]{2,1,0:T(8,128)(2,1)} collective-permute-done((bf16[4,128,1024]{2,1,0:T(8,128)(2,1)}, bf16[4,128,1024]{2,1,0:T(8,128)(2,1)}, u32[]{:S(2)}, u32[]{:S(2)}) %collective-permute-start.58) | collective-permute-done | bytes 1048608 | tf_op jit(solution)/shard_map/ppermute | solution.py:133
  526.1 6.7 %adamw.3 = (f32[4,1,128,1024]{3,2,1,0:T(8,128)}, f32[4,1,128,1024]{3,2,1,0:T(8,128)}, f32[4,1,128,1024]{3,2,1,0:T(8,128)}) custom-call(f32[4,1,128,1024]{3,2,1,0:T(8,128)S(1)} %bitcast.60, f32[4,1,128,1024]{3,2,1,0:T(8,128)} %bitcast.62, f32[4,1,128,1024]{3,2,1,0:T(8,128)} %bitcast.63, bf16[4,128,1024]{2,1,0:T(8,128)(2,1)} %collective-permute-done.58.refs_3_, ...), custom_call_target="tpu_custom_call" | custom-call | flops 10485760 | bytes 14680064 | tf_op jit(solution)/shard_map/adamw/pallas_call | solution.py:372
  534.7 5.3 input_gradient.1.refs_1_
  540.1 1.8 collective-permute-start.36
  546.2 1.8 multiply_subtract_fusion
  548.0 7.2 %collective-permute-done.36.refs_2_ = bf16[256,1024]{1,0:T(8,128)(2,1)S(1)} collective-permute-done((bf16[256,1024]{1,0:T(8,128)(2,1)}, bf16[256,1024]{1,0:T(8,128)(2,1)S(1)}, u32[]{:S(2)}, u32[]{:S(2)}) %collective-permute-start.36) | collective-permute-done | bytes 524320 | tf_op jit(solution)/shard_map/ppermute | solution.py:118
  555.7 6.3 %collective-permute-done.30.refs_2_ = bf16[256,1024]{1,0:T(8,128)(2,1)S(1)} collective-permute-done((bf16[256,1024]{1,0:T(8,128)(2,1)S(1)}, bf16[256,1024]{1,0:T(8,128)(2,1)S(1)}, u32[]{:S(2)}, u32[]{:S(2)}) %collective-permute-start.30) | collective-permute-done | bytes 524320 | tf_op jit(solution)/shard_map/ppermute | solution.py:118
  572.1 1.8 multiply_subtract_fusion.1
  574.0 1.8 multiply_subtract_fusion.2
  575.8 2.0 place.14
  577.8 2.7 place.12
  (334 shorter events, 121.1 us)
Async XLA Ops:
  7.2 176.9 %all-gather.4.cloned.1.call-start = ((), (), s32[]{:S(2)}) async-start(), calls=%async_computation.4 | async-start | bytes 4718592 | tf_op jit(solution)/shard_map/all_gather | solution.py:655
  11.3 33.0 %collective-permute-start.7 = (bf16[4,1024,128]{2,1,0:T(8,128)(2,1)}, bf16[4,1024,128]{2,1,0:T(8,128)(2,1)S(1)}, u32[]{:S(2)}, u32[]{:S(2)}) collective-permute-start(bf16[4,1024,128]{2,1,0:T(8,128)(2,1)} %get-tuple-element.226), channel_id=1, source_target_pairs={{0,2},{1,3},{2,0},{3,1},{4,6},{5,7},{6,4},{7,5},{8,10},{9,11},{10,... | collective-permute-start | bytes 3145736 | tf_op jit(solution)/shard_map/ppermute | solution.py:118
  14.2 45.9 %collective-permute-start.8 = (bf16[4,1024,128]{2,1,0:T(8,128)(2,1)}, bf16[4,1024,128]{2,1,0:T(8,128)(2,1)}, u32[]{:S(2)}, u32[]{:S(2)}) collective-permute-start(bf16[4,1024,128]{2,1,0:T(8,128)(2,1)} %get-tuple-element.225), channel_id=1, source_target_pairs={{0,2},{1,3},{2,0},{3,1},{4,6},{5,7},{6,4},{7,5},{8,10},{9,11},{10,... | collective-permute-start | bytes 3145736 | tf_op jit(solution)/shard_map/ppermute | solution.py:118
  18.3 7.1 %collective-permute-start = (bf16[128,896]{1,0:T(8,128)(2,1)S(1)}, bf16[128,896]{1,0:T(8,128)(2,1)S(1)}, u32[]{:S(2)}, u32[]{:S(2)}) collective-permute-start(bf16[128,896]{1,0:T(8,128)(2,1)S(1)} %concatenate.42.refs_5_), channel_id=1, source_target_pairs={{0,8},{8,16},{16,24},{24,28},{28,20},{20,12},{12,4},{4,0},{1,9},{9... | collective-permute-start | bytes 688136 | tf_op jit(solution)/shard_map/ppermute | solution.py:87
  20.5 7.5 %collective-permute-start.4 = (bf16[128,896]{1,0:T(8,128)(2,1)S(1)}, bf16[128,896]{1,0:T(8,128)(2,1)S(1)}, u32[]{:S(2)}, u32[]{:S(2)}) collective-permute-start(bf16[128,896]{1,0:T(8,128)(2,1)S(1)} %concatenate.42.refs_5_), channel_id=1, source_target_pairs={{0,4},{8,0},{16,8},{24,16},{28,24},{20,28},{12,20},{4,12},{1,5},{9... | collective-permute-start | bytes 688136 | tf_op jit(solution)/shard_map/ppermute | solution.py:90
  25.5 6.2 %collective-permute-start.1 = (bf16[128,896]{1,0:T(8,128)(2,1)S(1)}, bf16[128,896]{1,0:T(8,128)(2,1)S(1)}, u32[]{:S(2)}, u32[]{:S(2)}) collective-permute-start(bf16[128,896]{1,0:T(8,128)(2,1)S(1)} %collective-permute-done.refs_4_), channel_id=1, source_target_pairs={{0,8},{8,16},{16,24},{24,28},{28,20},{20,12},{12,4},{4,0},{1,9},{9... | collective-permute-start | bytes 688136 | tf_op jit(solution)/shard_map/ppermute | solution.py:87
  27.9 6.1 %collective-permute-start.5 = (bf16[128,896]{1,0:T(8,128)(2,1)S(1)}, bf16[128,896]{1,0:T(8,128)(2,1)}, u32[]{:S(2)}, u32[]{:S(2)}) collective-permute-start(bf16[128,896]{1,0:T(8,128)(2,1)S(1)} %collective-permute-done.4.refs_6_), channel_id=1, source_target_pairs={{0,4},{8,0},{16,8},{24,16},{28,24},{20,28},{12,20},{4,12},{1,5},{9... | collective-permute-start | bytes 688136 | tf_op jit(solution)/shard_map/ppermute | solution.py:90
  31.6 6.4 %collective-permute-start.2 = (bf16[128,896]{1,0:T(8,128)(2,1)S(1)}, bf16[128,896]{1,0:T(8,128)(2,1)}, u32[]{:S(2)}, u32[]{:S(2)}) collective-permute-start(bf16[128,896]{1,0:T(8,128)(2,1)S(1)} %collective-permute-done.1.refs_3_), channel_id=1, source_target_pairs={{0,8},{8,16},{16,24},{24,28},{28,20},{20,12},{12,4},{4,0},{1,9},{9... | collective-permute-start | bytes 688136 | tf_op jit(solution)/shard_map/ppermute | solution.py:87
  34.1 7.0 %collective-permute-start.6 = (bf16[128,896]{1,0:T(8,128)(2,1)}, bf16[128,896]{1,0:T(8,128)(2,1)}, u32[]{:S(2)}, u32[]{:S(2)}) collective-permute-start(bf16[128,896]{1,0:T(8,128)(2,1)} %collective-permute-done.5.refs_7_), channel_id=1, source_target_pairs={{0,4},{8,0},{16,8},{24,16},{28,24},{20,28},{12,20},{4,12},{1,5},{9... | collective-permute-start | bytes 688136 | tf_op jit(solution)/shard_map/ppermute | solution.py:90
  38.0 6.3 %collective-permute-start.3 = (bf16[128,896]{1,0:T(8,128)(2,1)}, bf16[128,896]{1,0:T(8,128)(2,1)}, u32[]{:S(2)}, u32[]{:S(2)}) collective-permute-start(bf16[128,896]{1,0:T(8,128)(2,1)} %collective-permute-done.2.refs_2_), channel_id=1, source_target_pairs={{0,8},{8,16},{16,24},{24,28},{28,20},{20,12},{12,4},{4,0},{1,9},{9... | collective-permute-start | bytes 688136 | tf_op jit(solution)/shard_map/ppermute | solution.py:87
  68.3 73.4 %collective-permute-start.13 = (bf16[4,1024,128]{2,1,0:T(8,128)(2,1)}, bf16[4,1024,128]{2,1,0:T(8,128)(2,1)}, u32[]{:S(2)}, u32[]{:S(2)}) collective-permute-start(bf16[4,1024,128]{2,1,0:T(8,128)(2,1)} %get-tuple-element.226), channel_id=1, source_target_pairs={{0,1},{1,0},{2,3},{3,2},{4,5},{5,4},{6,7},{7,6},{8,9},{9,8},{10,11... | collective-permute-start | bytes 3145736 | tf_op jit(solution)/shard_map/ppermute | solution.py:120
  68.4 73.8 %collective-permute-start.15 = (bf16[4,1024,128]{2,1,0:T(8,128)(2,1)}, bf16[4,1024,128]{2,1,0:T(8,128)(2,1)}, u32[]{:S(2)}, u32[]{:S(2)}) collective-permute-start(bf16[4,1024,128]{2,1,0:T(8,128)(2,1)} %get-tuple-element.225), channel_id=1, source_target_pairs={{0,1},{1,0},{2,3},{3,2},{4,5},{5,4},{6,7},{7,6},{8,9},{9,8},{10,11... | collective-permute-start | bytes 3145736 | tf_op jit(solution)/shard_map/ppermute | solution.py:120
  70.0 53.7 %collective-permute-start.12 = (bf16[4,128,1024]{2,1,0:T(8,128)(2,1)}, bf16[4,128,1024]{2,1,0:T(8,128)(2,1)}, u32[]{:S(2)}, u32[]{:S(2)}) collective-permute-start(bf16[4,128,1024]{2,1,0:T(8,128)(2,1)} %convert_element_type.195), channel_id=1, source_target_pairs={{0,2},{1,3},{2,0},{3,1},{4,6},{5,7},{6,4},{7,5},{8,10},{9,11},{10,... | collective-permute-start | bytes 3145736 | tf_op jit(solution)/shard_map/ppermute | solution.py:118
  71.8 34.9 %collective-permute-start.9 = (bf16[1024,256]{1,0:T(8,128)(2,1)}, bf16[1024,256]{1,0:T(8,128)(2,1)}, u32[]{:S(2)}, u32[]{:S(2)}) collective-permute-start(bf16[1024,256]{1,0:T(8,128)(2,1)} %get-tuple-element.84.refs_1_), channel_id=1, source_target_pairs={{0,2},{1,3},{2,0},{3,1},{4,6},{5,7},{6,4},{7,5},{8,10},{9,11},{10,... | collective-permute-start | bytes 1572872 | tf_op jit(solution)/shard_map/ppermute | solution.py:118
  75.9 56.7 %collective-permute-start.10 = (bf16[1024,256]{1,0:T(8,128)(2,1)}, bf16[1024,256]{1,0:T(8,128)(2,1)}, u32[]{:S(2)}, u32[]{:S(2)}) collective-permute-start(bf16[1024,256]{1,0:T(8,128)(2,1)} %get-tuple-element.84.refs_1_), channel_id=1, source_target_pairs={{0,1},{1,0},{2,3},{3,2},{4,5},{5,4},{6,7},{7,6},{8,9},{9,8},{10,11... | collective-permute-start | bytes 1572872 | tf_op jit(solution)/shard_map/ppermute | solution.py:120
  106.7 25.9 %collective-permute-start.11 = (bf16[1024,256]{1,0:T(8,128)(2,1)}, bf16[1024,256]{1,0:T(8,128)(2,1)S(1)}, u32[]{:S(2)}, u32[]{:S(2)}) collective-permute-start(bf16[1024,256]{1,0:T(8,128)(2,1)} %collective-permute-done.9.refs_2_), channel_id=1, source_target_pairs={{0,1},{1,0},{2,3},{3,2},{4,5},{5,4},{6,7},{7,6},{8,9},{9,8},{10,11... | collective-permute-start | bytes 1572872 | tf_op jit(solution)/shard_map/ppermute | solution.py:120
  120.2 12.4 %all-to-all-start = ((bf16[4,256,256]{2,1,0:T(8,128)(2,1)}), bf16[4,256,256]{2,1,0:T(8,128)(2,1)S(1)}, u32[]{:S(2)}, u32[]{:S(2)}) async-start(bf16[4,256,256]{2,1,0:T(8,128)(2,1)} %bitcast.65), calls=%async_computation | async-start | bytes 1048576 | tf_op jit(solution)/shard_map/all_to_all | solution.py:670
  123.7 411.0 %all-gather.6.cloned.1.call-start = ((), (), s32[]{:S(2)}) async-start(), calls=%async_computation.6 | async-start | bytes 5242880 | tf_op jit(solution)/shard_map/all_gather | solution.py:781
  123.7 18.6 %collective-permute-start.14 = (bf16[4,1024,128]{2,1,0:T(8,128)(2,1)}, bf16[4,1024,128]{2,1,0:T(8,128)(2,1)}, u32[]{:S(2)}, u32[]{:S(2)}) collective-permute-start(bf16[4,1024,128]{2,1,0:T(8,128)(2,1)} %copy-done.8), channel_id=1, source_target_pairs={{0,1},{1,0},{2,3},{3,2},{4,5},{5,4},{6,7},{7,6},{8,9},{9,8},{10,11... | collective-permute-start | bytes 3145736 | tf_op jit(solution)/shard_map/ppermute | solution.py:120
  139.8 15.3 %collective-permute-start.19 = (bf16[256,1152]{1,0:T(8,128)(2,1)}, bf16[256,1152]{1,0:T(8,128)(2,1)S(1)}, u32[]{:S(2)}, u32[]{:S(2)}) collective-permute-start(bf16[256,1152]{1,0:T(8,128)(2,1)} %get-tuple-element.86.refs_1_.refs_4_), channel_id=1, source_target_pairs={{0,8},{8,16},{16,24},{24,28},{28,20},{20,12},{12,4},{4,0},{1,9},{9... | collective-permute-start | bytes 1769480 | tf_op jit(solution)/shard_map/ppermute | solution.py:87
  141.5 29.3 %collective-permute-start.16 = (bf16[4,1024,128]{2,1,0:T(8,128)(2,1)}, bf16[4,1024,128]{2,1,0:T(8,128)(2,1)}, u32[]{:S(2)}, u32[]{:S(2)}) collective-permute-start(bf16[4,1024,128]{2,1,0:T(8,128)(2,1)} %collective-permute-done.8.refs_10_), channel_id=1, source_target_pairs={{0,1},{1,0},{2,3},{3,2},{4,5},{5,4},{6,7},{7,6},{8,9},{9,8},{10,11... | collective-permute-start | bytes 3145736 | tf_op jit(solution)/shard_map/ppermute | solution.py:120
  141.7 32.9 %collective-permute-start.17 = (bf16[4,128,1024]{2,1,0:T(8,128)(2,1)}, bf16[4,128,1024]{2,1,0:T(8,128)(2,1)S(1)}, u32[]{:S(2)}, u32[]{:S(2)}) collective-permute-start(bf16[4,128,1024]{2,1,0:T(8,128)(2,1)} %convert_element_type.195), channel_id=1, source_target_pairs={{0,1},{1,0},{2,3},{3,2},{4,5},{5,4},{6,7},{7,6},{8,9},{9,8},{10,11... | collective-permute-start | bytes 3145736 | tf_op jit(solution)/shard_map/ppermute | solution.py:120
  142.2 32.4 %collective-permute-start.18 = (bf16[4,128,1024]{2,1,0:T(8,128)(2,1)}, bf16[4,128,1024]{2,1,0:T(8,128)(2,1)S(1)}, u32[]{:S(2)}, u32[]{:S(2)}) collective-permute-start(bf16[4,128,1024]{2,1,0:T(8,128)(2,1)} %collective-permute-done.12.refs_6_), channel_id=1, source_target_pairs={{0,1},{1,0},{2,3},{3,2},{4,5},{5,4},{6,7},{7,6},{8,9},{9,8},{10,11... | collective-permute-start | bytes 3145736 | tf_op jit(solution)/shard_map/ppermute | solution.py:120
  142.3 18.3 %collective-permute-start.20 = (bf16[256,1152]{1,0:T(8,128)(2,1)}, bf16[256,1152]{1,0:T(8,128)(2,1)S(1)}, u32[]{:S(2)}, u32[]{:S(2)}) collective-permute-start(bf16[256,1152]{1,0:T(8,128)(2,1)} %get-tuple-element.86.refs_1_.refs_4_), channel_id=1, source_target_pairs={{0,4},{8,0},{16,8},{24,16},{28,24},{20,28},{12,20},{4,12},{1,5},{9... | collective-permute-start | bytes 1769480 | tf_op jit(solution)/shard_map/ppermute | solution.py:90
  155.1 14.2 %collective-permute-start.21 = (bf16[256,1152]{1,0:T(8,128)(2,1)S(1)}, bf16[256,1152]{1,0:T(8,128)(2,1)S(1)}, u32[]{:S(2)}, u32[]{:S(2)}) collective-permute-start(bf16[256,1152]{1,0:T(8,128)(2,1)S(1)} %collective-permute-done.19.refs_1_.refs_2_), channel_id=1, source_target_pairs={{0,8},{8,16},{16,24},{24,28},{28,20},{20,12},{12,4},{4,0},{1,9},{9... | collective-permute-start | bytes 1769480 | tf_op jit(solution)/shard_map/ppermute | solution.py:87
  160.6 17.4 %collective-permute-start.22 = (bf16[256,1152]{1,0:T(8,128)(2,1)S(1)}, bf16[256,1152]{1,0:T(8,128)(2,1)}, u32[]{:S(2)}, u32[]{:S(2)}) collective-permute-start(bf16[256,1152]{1,0:T(8,128)(2,1)S(1)} %collective-permute-done.20.refs_2_.refs_3_), channel_id=1, source_target_pairs={{0,4},{8,0},{16,8},{24,16},{28,24},{20,28},{12,20},{4,12},{1,5},{9... | collective-permute-start | bytes 1769480 | tf_op jit(solution)/shard_map/ppermute | solution.py:90
  169.3 13.5 %collective-permute-start.23 = (bf16[256,1152]{1,0:T(8,128)(2,1)S(1)}, bf16[256,1152]{1,0:T(8,128)(2,1)}, u32[]{:S(2)}, u32[]{:S(2)}) collective-permute-start(bf16[256,1152]{1,0:T(8,128)(2,1)S(1)} %collective-permute-done.21.refs_1_.refs_4_), channel_id=1, source_target_pairs={{0,8},{8,16},{16,24},{24,28},{28,20},{20,12},{12,4},{4,0},{1,9},{9... | collective-permute-start | bytes 1769480 | tf_op jit(solution)/shard_map/ppermute | solution.py:87
  178.0 85.5 %collective-permute-start.25 = (bf16[256,1152]{1,0:T(8,128)(2,1)}, bf16[256,1152]{1,0:T(8,128)(2,1)}, u32[]{:S(2)}, u32[]{:S(2)}) collective-permute-start(bf16[256,1152]{1,0:T(8,128)(2,1)} %collective-permute-done.22.refs_2_.refs_5_), channel_id=1, source_target_pairs={{0,4},{8,0},{16,8},{24,16},{28,24},{20,28},{12,20},{4,12},{1,5},{9... | collective-permute-start | bytes 1769480 | tf_op jit(solution)/shard_map/ppermute | solution.py:90
  182.7 80.7 %collective-permute-start.24 = (bf16[256,1152]{1,0:T(8,128)(2,1)}, bf16[256,1152]{1,0:T(8,128)(2,1)}, u32[]{:S(2)}, u32[]{:S(2)}) collective-permute-start(bf16[256,1152]{1,0:T(8,128)(2,1)} %collective-permute-done.23.refs_1_.refs_8_), channel_id=1, source_target_pairs={{0,8},{8,16},{16,24},{24,28},{28,20},{20,12},{12,4},{4,0},{1,9},{9... | collective-permute-start | bytes 1769480 | tf_op jit(solution)/shard_map/ppermute | solution.py:87
  226.4 315.5 %reduce-scatter.2.cloned.1.call-start = ((), (), s32[]{:S(2)}) async-start(), calls=%async_computation.5 | async-start | bytes 4718592 | tf_op jit(solution)/shard_map/reduce_scatter | solution.py:727
  286.5 12.6 %collective-permute-start.26 = (bf16[256,1152]{1,0:T(8,128)(2,1)S(1)}, bf16[256,1152]{1,0:T(8,128)(2,1)S(1)}, u32[]{:S(2)}, u32[]{:S(2)}) collective-permute-start(bf16[256,1152]{1,0:T(8,128)(2,1)S(1)} %get-tuple-element.99), channel_id=1, source_target_pairs={{0,4},{8,0},{16,8},{24,16},{28,24},{20,28},{12,20},{4,12},{1,5},{9... | collective-permute-start | bytes 1769480 | tf_op jit(solution)/shard_map/ppermute | solution.py:102
  299.3 13.3 %collective-permute-start.27 = (bf16[256,1152]{1,0:T(8,128)(2,1)S(1)}, bf16[256,1152]{1,0:T(8,128)(2,1)S(1)}, u32[]{:S(2)}, u32[]{:S(2)}) collective-permute-start(bf16[256,1152]{1,0:T(8,128)(2,1)S(1)} %add_convert_fusion.7.refs_14_), channel_id=1, source_target_pairs={{0,4},{8,0},{16,8},{24,16},{28,24},{20,28},{12,20},{4,12},{1,5},{9... | collective-permute-start | bytes 1769480 | tf_op jit(solution)/shard_map/ppermute | solution.py:102
  300.7 13.5 %collective-permute-start.33 = (bf16[256,1152]{1,0:T(8,128)(2,1)S(1)}, bf16[256,1152]{1,0:T(8,128)(2,1)S(1)}, u32[]{:S(2)}, u32[]{:S(2)}) collective-permute-start(bf16[256,1152]{1,0:T(8,128)(2,1)S(1)} %get-tuple-element.105), channel_id=1, source_target_pairs={{0,8},{8,16},{16,24},{24,28},{28,20},{20,12},{12,4},{4,0},{1,9},{9... | collective-permute-start | bytes 1769480 | tf_op jit(solution)/shard_map/ppermute | solution.py:107
  312.8 12.3 %collective-permute-start.28 = (bf16[256,1152]{1,0:T(8,128)(2,1)S(1)}, bf16[256,1152]{1,0:T(8,128)(2,1)S(1)}, u32[]{:S(2)}, u32[]{:S(2)}) collective-permute-start(bf16[256,1152]{1,0:T(8,128)(2,1)S(1)} %add_convert_fusion.6.refs_14_), channel_id=1, source_target_pairs={{0,4},{8,0},{16,8},{24,16},{28,24},{20,28},{12,20},{4,12},{1,5},{9... | collective-permute-start | bytes 1769480 | tf_op jit(solution)/shard_map/ppermute | solution.py:102
  315.1 12.4 %collective-permute-start.34 = (bf16[256,1152]{1,0:T(8,128)(2,1)}, bf16[256,1152]{1,0:T(8,128)(2,1)}, u32[]{:S(2)}, u32[]{:S(2)}) collective-permute-start(bf16[256,1152]{1,0:T(8,128)(2,1)} %add_convert_fusion.4), channel_id=1, source_target_pairs={{0,8},{8,16},{16,24},{24,28},{28,20},{20,12},{12,4},{4,0},{1,9},{9... | collective-permute-start | bytes 1769480 | tf_op jit(solution)/shard_map/ppermute | solution.py:107
  326.0 10.5 %collective-permute-start.29 = (bf16[256,1152]{1,0:T(8,128)(2,1)}, bf16[256,1152]{1,0:T(8,128)(2,1)S(1)}, u32[]{:S(2)}, u32[]{:S(2)}) collective-permute-start(bf16[256,1152]{1,0:T(8,128)(2,1)} %add_convert_fusion.5.refs_14_), channel_id=1, source_target_pairs={{0,4},{8,0},{16,8},{24,16},{28,24},{20,28},{12,20},{4,12},{1,5},{9... | collective-permute-start | bytes 1769480 | tf_op jit(solution)/shard_map/ppermute | solution.py:102
  329.6 34.0 %collective-permute-start.35 = (bf16[256,1152]{1,0:T(8,128)(2,1)}, bf16[256,1152]{1,0:T(8,128)(2,1)S(1)}, u32[]{:S(2)}, u32[]{:S(2)}) collective-permute-start(bf16[256,1152]{1,0:T(8,128)(2,1)} %add_convert_fusion.3), channel_id=1, source_target_pairs={{0,8},{8,16},{16,24},{24,28},{28,20},{20,12},{12,4},{4,0},{1,9},{9... | collective-permute-start | bytes 1769480 | tf_op jit(solution)/shard_map/ppermute | solution.py:107
  363.0 57.1 %collective-permute-start.51 = (bf16[4,1024,128]{2,1,0:T(8,128)(2,1)}, bf16[4,1024,128]{2,1,0:T(8,128)(2,1)}, u32[]{:S(2)}, u32[]{:S(2)}) collective-permute-start(bf16[4,1024,128]{2,1,0:T(8,128)(2,1)} %get-tuple-element.121), channel_id=1, source_target_pairs={{0,1},{1,0},{2,3},{3,2},{4,5},{5,4},{6,7},{7,6},{8,9},{9,8},{10,11... | collective-permute-start | bytes 3145736 | tf_op jit(solution)/shard_map/ppermute | solution.py:128
  363.1 115.9 %collective-permute-start.53 = (bf16[4,1024,128]{2,1,0:T(8,128)(2,1)}, bf16[4,1024,128]{2,1,0:T(8,128)(2,1)}, u32[]{:S(2)}, u32[]{:S(2)}) collective-permute-start(bf16[4,1024,128]{2,1,0:T(8,128)(2,1)} %get-tuple-element.123), channel_id=1, source_target_pairs={{0,1},{1,0},{2,3},{3,2},{4,5},{5,4},{6,7},{7,6},{8,9},{9,8},{10,11... | collective-permute-start | bytes 3145736 | tf_op jit(solution)/shard_map/ppermute | solution.py:128
  370.0 21.7 %collective-permute-start.39 = (bf16[256,1024]{1,0:T(8,128)(2,1)}, bf16[256,1024]{1,0:T(8,128)(2,1)S(1)}, u32[]{:S(2)}, u32[]{:S(2)}) collective-permute-start(bf16[256,1024]{1,0:T(8,128)(2,1)} %get-tuple-element.111.refs_1_), channel_id=1, source_target_pairs={{0,2},{1,3},{2,0},{3,1},{4,6},{5,7},{6,4},{7,5},{8,10},{9,11},{10,... | collective-permute-start | bytes 1572872 | tf_op jit(solution)/shard_map/ppermute | solution.py:118
  371.7 20.3 %all-to-all-start.1 = ((bf16[4,256,256]{2,1,0:T(8,128)(2,1)}), bf16[4,256,256]{2,1,0:T(8,128)(2,1)}, u32[]{:S(2)}, u32[]{:S(2)}) async-start(bf16[4,256,256]{2,1,0:T(8,128)(2,1)} %get-tuple-element.108), calls=%async_computation.2 | async-start | bytes 1048576 | tf_op jit(solution)/shard_map/all_to_all | solution.py:749
  391.1 64.5 %collective-permute-start.54 = (bf16[4,1024,128]{2,1,0:T(8,128)(2,1)}, bf16[4,1024,128]{2,1,0:T(8,128)(2,1)}, u32[]{:S(2)}, u32[]{:S(2)}) collective-permute-start(bf16[4,1024,128]{2,1,0:T(8,128)(2,1)} %get-tuple-element.125), channel_id=1, source_target_pairs={{0,1},{1,0},{2,3},{3,2},{4,5},{5,4},{6,7},{7,6},{8,9},{9,8},{10,11... | collective-permute-start | bytes 3145736 | tf_op jit(solution)/shard_map/ppermute | solution.py:128
  391.5 19.2 %collective-permute-start.40 = (bf16[256,1024]{1,0:T(8,128)(2,1)S(1)}, bf16[256,1024]{1,0:T(8,128)(2,1)}, u32[]{:S(2)}, u32[]{:S(2)}) collective-permute-start(bf16[256,1024]{1,0:T(8,128)(2,1)S(1)} %copy-done.42), channel_id=1, source_target_pairs={{0,1},{1,0},{2,3},{3,2},{4,5},{5,4},{6,7},{7,6},{8,9},{9,8},{10,11... | collective-permute-start | bytes 1572872 | tf_op jit(solution)/shard_map/ppermute | solution.py:120
  391.7 19.2 %collective-permute-start.41 = (bf16[256,1024]{1,0:T(8,128)(2,1)S(1)}, bf16[256,1024]{1,0:T(8,128)(2,1)}, u32[]{:S(2)}, u32[]{:S(2)}) collective-permute-start(bf16[256,1024]{1,0:T(8,128)(2,1)S(1)} %collective-permute-done.39.refs_2_), channel_id=1, source_target_pairs={{0,1},{1,0},{2,3},{3,2},{4,5},{5,4},{6,7},{7,6},{8,9},{9,8},{10,11... | collective-permute-start | bytes 1572872 | tf_op jit(solution)/shard_map/ppermute | solution.py:120
  410.7 84.3 %collective-permute-start.56 = (bf16[4,1024,128]{2,1,0:T(8,128)(2,1)}, bf16[4,1024,128]{2,1,0:T(8,128)(2,1)}, u32[]{:S(2)}, u32[]{:S(2)}) collective-permute-start(bf16[4,1024,128]{2,1,0:T(8,128)(2,1)} %get-tuple-element.127), channel_id=1, source_target_pairs={{0,1},{1,0},{2,3},{3,2},{4,5},{5,4},{6,7},{7,6},{8,9},{9,8},{10,11... | collective-permute-start | bytes 3145736 | tf_op jit(solution)/shard_map/ppermute | solution.py:128
  422.6 73.8 %collective-permute-start.52 = (bf16[4,1024,128]{2,1,0:T(8,128)(2,1)}, bf16[4,1024,128]{2,1,0:T(8,128)(2,1)}, u32[]{:S(2)}, u32[]{:S(2)}) collective-permute-start(bf16[4,1024,128]{2,1,0:T(8,128)(2,1)} %add_convert_fusion.2), channel_id=1, source_target_pairs={{0,2},{1,3},{2,0},{3,1},{4,6},{5,7},{6,4},{7,5},{8,10},{9,11},{10,... | collective-permute-start | bytes 3145736 | tf_op jit(solution)/shard_map/ppermute | solution.py:133
  425.3 28.5 %collective-permute-start.43 = (bf16[1024,128]{1,0:T(8,128)(2,1)S(1)}, bf16[1024,128]{1,0:T(8,128)(2,1)S(1)}, u32[]{:S(2)}, u32[]{:S(2)}) collective-permute-start(bf16[1024,128]{1,0:T(8,128)(2,1)S(1)} %add.416), channel_id=1, source_target_pairs={{0,2},{1,3},{2,0},{3,1},{4,6},{5,7},{6,4},{7,5},{8,10},{9,11},{10,... | collective-permute-start | bytes 786440 | tf_op jit(solution)/shard_map/ppermute | solution.py:140
  454.5 26.3 %collective-permute-start.57 = (bf16[4,128,1024]{2,1,0:T(8,128)(2,1)}, bf16[4,128,1024]{2,1,0:T(8,128)(2,1)S(1)}, u32[]{:S(2)}, u32[]{:S(2)}) collective-permute-start(bf16[4,128,1024]{2,1,0:T(8,128)(2,1)} %get-tuple-element.133), channel_id=1, source_target_pairs={{0,1},{1,0},{2,3},{3,2},{4,5},{5,4},{6,7},{7,6},{8,9},{9,8},{10,11... | collective-permute-start | bytes 3145736 | tf_op jit(solution)/shard_map/ppermute | solution.py:128
  455.6 8.1 %collective-permute-start.44 = (bf16[128,896]{1,0:T(8,128)(2,1)S(1)}, bf16[128,896]{1,0:T(8,128)(2,1)S(1)}, u32[]{:S(2)}, u32[]{:S(2)}) collective-permute-start(bf16[128,896]{1,0:T(8,128)(2,1)S(1)} %pad_maximum_fusion.5), channel_id=1, source_target_pairs={{0,4},{8,0},{16,8},{24,16},{28,24},{20,28},{12,20},{4,12},{1,5},{9... | collective-permute-start | bytes 688136 | tf_op jit(solution)/shard_map/ppermute | solution.py:102
  463.7 7.2 %collective-permute-start.48 = (bf16[128,896]{1,0:T(8,128)(2,1)S(1)}, bf16[128,896]{1,0:T(8,128)(2,1)S(1)}, u32[]{:S(2)}, u32[]{:S(2)}) collective-permute-start(bf16[128,896]{1,0:T(8,128)(2,1)S(1)} %pad_maximum_fusion.6), channel_id=1, source_target_pairs={{0,8},{8,16},{16,24},{24,28},{28,20},{20,12},{12,4},{4,0},{1,9},{9... | collective-permute-start | bytes 688136 | tf_op jit(solution)/shard_map/ppermute | solution.py:107
  470.9 6.3 %collective-permute-start.45 = (bf16[128,896]{1,0:T(8,128)(2,1)S(1)}, bf16[128,896]{1,0:T(8,128)(2,1)S(1)}, u32[]{:S(2)}, u32[]{:S(2)}) collective-permute-start(bf16[128,896]{1,0:T(8,128)(2,1)S(1)} %add_convert_fusion.13), channel_id=1, source_target_pairs={{0,4},{8,0},{16,8},{24,16},{28,24},{20,28},{12,20},{4,12},{1,5},{9... | collective-permute-start | bytes 688136 | tf_op jit(solution)/shard_map/ppermute | solution.py:102
  477.2 26.4 %collective-permute-start.55 = (bf16[4,1024,128]{2,1,0:T(8,128)(2,1)}, bf16[4,1024,128]{2,1,0:T(8,128)(2,1)}, u32[]{:S(2)}, u32[]{:S(2)}) collective-permute-start(bf16[4,1024,128]{2,1,0:T(8,128)(2,1)} %add_convert_fusion.1), channel_id=1, source_target_pairs={{0,2},{1,3},{2,0},{3,1},{4,6},{5,7},{6,4},{7,5},{8,10},{9,11},{10,... | collective-permute-start | bytes 3145736 | tf_op jit(solution)/shard_map/ppermute | solution.py:133
  479.1 6.2 %collective-permute-start.49 = (bf16[128,896]{1,0:T(8,128)(2,1)S(1)}, bf16[128,896]{1,0:T(8,128)(2,1)}, u32[]{:S(2)}, u32[]{:S(2)}) collective-permute-start(bf16[128,896]{1,0:T(8,128)(2,1)S(1)} %add_convert_fusion.10), channel_id=1, source_target_pairs={{0,8},{8,16},{16,24},{24,28},{28,20},{20,12},{12,4},{4,0},{1,9},{9... | collective-permute-start | bytes 688136 | tf_op jit(solution)/shard_map/ppermute | solution.py:107
  485.3 31.4 %collective-permute-start.59 = (bf16[4,128,1024]{2,1,0:T(8,128)(2,1)}, bf16[4,128,1024]{2,1,0:T(8,128)(2,1)}, u32[]{:S(2)}, u32[]{:S(2)}) collective-permute-start(bf16[4,128,1024]{2,1,0:T(8,128)(2,1)} %get-tuple-element.135), channel_id=1, source_target_pairs={{0,1},{1,0},{2,3},{3,2},{4,5},{5,4},{6,7},{7,6},{8,9},{9,8},{10,11... | collective-permute-start | bytes 3145736 | tf_op jit(solution)/shard_map/ppermute | solution.py:128
  486.9 39.3 %collective-permute-start.58 = (bf16[4,128,1024]{2,1,0:T(8,128)(2,1)}, bf16[4,128,1024]{2,1,0:T(8,128)(2,1)}, u32[]{:S(2)}, u32[]{:S(2)}) collective-permute-start(bf16[4,128,1024]{2,1,0:T(8,128)(2,1)} %add_convert_fusion), channel_id=1, source_target_pairs={{0,2},{1,3},{2,0},{3,1},{4,6},{5,7},{6,4},{7,5},{8,10},{9,11},{10,... | collective-permute-start | bytes 3145736 | tf_op jit(solution)/shard_map/ppermute | solution.py:133
  487.1 47.5 %all-to-all-start.2 = ((bf16[4,256,512]{2,1,0:T(8,128)(2,1)}), bf16[4,256,512]{2,1,0:T(8,128)(2,1)}, u32[]{:S(2)}, u32[]{:S(2)}) async-start(bf16[4,256,512]{2,1,0:T(8,128)(2,1)} %bitcast.64), calls=%async_computation.3 | async-start | bytes 2097152 | tf_op jit(solution)/shard_map/all_to_all | solution.py:761
  495.0 37.8 %collective-permute-start.50 = (bf16[128,896]{1,0:T(8,128)(2,1)}, bf16[128,896]{1,0:T(8,128)(2,1)}, u32[]{:S(2)}, u32[]{:S(2)}) collective-permute-start(bf16[128,896]{1,0:T(8,128)(2,1)} %add_convert_fusion.9), channel_id=1, source_target_pairs={{0,8},{8,16},{16,24},{24,28},{28,20},{20,12},{12,4},{4,0},{1,9},{9... | collective-permute-start | bytes 688136 | tf_op jit(solution)/shard_map/ppermute | solution.py:107
  496.4 36.4 %collective-permute-start.47 = (bf16[128,896]{1,0:T(8,128)(2,1)}, bf16[128,896]{1,0:T(8,128)(2,1)}, u32[]{:S(2)}, u32[]{:S(2)}) collective-permute-start(bf16[128,896]{1,0:T(8,128)(2,1)} %add_convert_fusion.11), channel_id=1, source_target_pairs={{0,4},{8,0},{16,8},{24,16},{28,24},{20,28},{12,20},{4,12},{1,5},{9... | collective-permute-start | bytes 688136 | tf_op jit(solution)/shard_map/ppermute | solution.py:102
  540.1 15.1 %collective-permute-start.36 = (bf16[256,1024]{1,0:T(8,128)(2,1)}, bf16[256,1024]{1,0:T(8,128)(2,1)S(1)}, u32[]{:S(2)}, u32[]{:S(2)}) collective-permute-start(bf16[256,1024]{1,0:T(8,128)(2,1)} %input_gradient.1.refs_1_), channel_id=1, source_target_pairs={{0,2},{1,3},{2,0},{3,1},{4,6},{5,7},{6,4},{7,5},{8,10},{9,11},{10,... | collective-permute-start | bytes 1572872 | tf_op jit(solution)/shard_map/ppermute | solution.py:118
  543.1 18.9 %collective-permute-start.30 = (bf16[256,1024]{1,0:T(8,128)(2,1)S(1)}, bf16[256,1024]{1,0:T(8,128)(2,1)S(1)}, u32[]{:S(2)}, u32[]{:S(2)}) collective-permute-start(bf16[256,1024]{1,0:T(8,128)(2,1)S(1)} %add_convert_fusion.8.refs_1_), channel_id=1, source_target_pairs={{0,2},{1,3},{2,0},{3,1},{4,6},{5,7},{6,4},{7,5},{8,10},{9,11},{10,... | collective-permute-start | bytes 1572872 | tf_op jit(solution)/shard_map/ppermute | solution.py:118
  548.0 27.8 %collective-permute-start.37 = (bf16[256,1024]{1,0:T(8,128)(2,1)}, bf16[256,1024]{1,0:T(8,128)(2,1)S(1)}, u32[]{:S(2)}, u32[]{:S(2)}) collective-permute-start(bf16[256,1024]{1,0:T(8,128)(2,1)} %input_gradient.1.refs_1_), channel_id=1, source_target_pairs={{0,1},{1,0},{2,3},{3,2},{4,5},{5,4},{6,7},{7,6},{8,9},{9,8},{10,11... | collective-permute-start | bytes 1572872 | tf_op jit(solution)/shard_map/ppermute | solution.py:120
  555.2 20.6 %collective-permute-start.38 = (bf16[256,1024]{1,0:T(8,128)(2,1)S(1)}, bf16[256,1024]{1,0:T(8,128)(2,1)S(1)}, u32[]{:S(2)}, u32[]{:S(2)}) collective-permute-start(bf16[256,1024]{1,0:T(8,128)(2,1)S(1)} %collective-permute-done.36.refs_2_), channel_id=1, source_target_pairs={{0,1},{1,0},{2,3},{3,2},{4,5},{5,4},{6,7},{7,6},{8,9},{9,8},{10,11... | collective-permute-start | bytes 1572872 | tf_op jit(solution)/shard_map/ppermute | solution.py:120
  555.2 22.6 %collective-permute-start.31 = (bf16[256,1024]{1,0:T(8,128)(2,1)S(1)}, bf16[256,1024]{1,0:T(8,128)(2,1)}, u32[]{:S(2)}, u32[]{:S(2)}) collective-permute-start(bf16[256,1024]{1,0:T(8,128)(2,1)S(1)} %add_convert_fusion.8.refs_1_), channel_id=1, source_target_pairs={{0,1},{1,0},{2,3},{3,2},{4,5},{5,4},{6,7},{7,6},{8,9},{9,8},{10,11... | collective-permute-start | bytes 1572872 | tf_op jit(solution)/shard_map/ppermute | solution.py:120
  562.0 15.8 %collective-permute-start.32 = (bf16[256,1024]{1,0:T(8,128)(2,1)S(1)}, bf16[256,1024]{1,0:T(8,128)(2,1)}, u32[]{:S(2)}, u32[]{:S(2)}) collective-permute-start(bf16[256,1024]{1,0:T(8,128)(2,1)S(1)} %collective-permute-done.30.refs_2_), channel_id=1, source_target_pairs={{0,1},{1,0},{2,3},{3,2},{4,5},{5,4},{6,7},{7,6},{8,9},{9,8},{10,11... | collective-permute-start | bytes 1572872 | tf_op jit(solution)/shard_map/ppermute | solution.py:120
  (86 other events, 891.3 us)
Sparse Core Ops, SparseCore 0:
  68.4 74.8 all-gather.3
  226.5 34.4 all-gather.5
  348.1 89.0 reduce-scatter.1

commit v3 on v2

--- a/solution.py
+++ b/solution.py
@@ -92,20 +92,21 @@
     return blocks
 
 
-def ring_reduce(part, size):
+def ring_reduce(part, size, beside=None):
     down = up = None
-    messages = []
+    after = []
     for hop in range(size // 2, 0, -1):
-        mine = part(-hop)
-        total = mine if down is None else (down.astype(F32) + mine.astype(F32)).astype(BF)
-        messages.append(total)
-        down = lax.ppermute(total, "expert", ring_perm(size, -1))
         side = hop - 1
+        if down is None:
+            messages = [part(-hop), part(side)]
+        else:
+            pairs = [(down, part(-hop))] + ([(up, part(side))] if side > 0 else [])
+            messages = add_pairs(pairs, after)
+            after = beside(hop, messages) if beside else []
+        down = lax.ppermute(messages[0], "expert", ring_perm(size, -1))
         if side > 0:
-            mine = part(side)
-            total = mine if up is None else (up.astype(F32) + mine.astype(F32)).astype(BF)
-            up = lax.ppermute(total, "expert", ring_perm(size, 1))
-    return [part(0), down] + ([] if up is None else [up]), messages
+            up = lax.ppermute(messages[1], "expert", ring_perm(size, 1))
+    return [part(0), down, up], after
 
 
 def tensor_perm(size, along, core):
@@ -113,11 +114,12 @@
     return [(t, ((t // 2 + along) % chips) * 2 + ((t % 2) ^ core)) for t in range(size)]
 
 
-def tensor_gather(shard, size):
+def tensor_gather(shard, size, after=()):
     own = [shard] + [
         lax.ppermute(shard, "tensor", tensor_perm(size, -step, 0)) for step in range(1, size // 2)
     ]
-    other = [lax.ppermute(piece, "tensor", tensor_perm(size, 0, 1)) for piece in own]
+    ready = [hold(piece, after) for piece in own] if after else own
+    other = [lax.ppermute(piece, "tensor", tensor_perm(size, 0, 1)) for piece in ready]
     return own + other
 
 
@@ -171,6 +173,53 @@
         name="place",
     )(index, *blocks, *after)
     return out if len(cuts) > 1 else out[0]
+
+
+def hold(array, after):
+    flat = array.reshape(-1, array.shape[-1])
+    return place([flat], jnp.zeros((1,), jnp.int32), after=after).reshape(array.shape)
+
+
+def cut_kernel(blocks, s_ref, main_ref, tail_ref, *refs):
+    outs = refs[len(refs) - blocks :]
+    for i, out in enumerate(outs):
+        size = out.shape[0]
+        part = pl.ds(pl.multiple_of(s_ref[i] * size, size), size)
+        out[:, : main_ref.shape[1]] = main_ref[part, :]
+        out[:, main_ref.shape[1] :] = tail_ref[part, :]
+
+
+def cut(main, tail, index, after):
+    count = index.shape[0]
+    vmem = pl.BlockSpec(memory_space=pltpu.VMEM)
+    block = (main.shape[0] // count, main.shape[1] + tail.shape[1])
+    return pl.pallas_call(
+        functools.partial(cut_kernel, count),
+        in_specs=[pl.BlockSpec(memory_space=pltpu.SMEM), vmem, vmem]
+        + [pl.BlockSpec(memory_space=pl.ANY)] * len(after),
+        out_specs=[vmem] * count,
+        out_shape=[jax.ShapeDtypeStruct(block, main.dtype)] * count,
+        compiler_params=pltpu.CompilerParams(vmem_limit_bytes=32 * 1024 * 1024),
+        name="cut",
+    )(index, main, tail, *after)
+
+
+def add_kernel(count, *refs):
+    outs = refs[len(refs) - count :]
+    for i, out in enumerate(outs):
+        out[...] = (refs[2 * i][...].astype(F32) + refs[2 * i + 1][...].astype(F32)).astype(BF)
+
+
+def add_pairs(pairs, after):
+    vmem = pl.BlockSpec(memory_space=pltpu.VMEM)
+    return pl.pallas_call(
+        functools.partial(add_kernel, len(pairs)),
+        in_specs=[vmem] * (2 * len(pairs)) + [pl.BlockSpec(memory_space=pl.ANY)] * len(after),
+        out_specs=[vmem] * len(pairs),
+        out_shape=[jax.ShapeDtypeStruct(pair[0].shape, BF) for pair in pairs],
+        compiler_params=pltpu.CompilerParams(vmem_limit_bytes=32 * 1024 * 1024),
+        name="add_pairs",
+    )(*[array for pair in pairs for array in pair], *after)
 
 
 def tensor_index(size):
@@ -284,7 +333,7 @@
         ]
         + [shape((rows, width), BF)] * count
         + [shape((rows, message), BF)] * count,
-        compiler_params=pltpu.CompilerParams(vmem_limit_bytes=48 * 1024 * 1024),
+        compiler_params=pltpu.CompilerParams(vmem_limit_bytes=60 * 1024 * 1024),
         cost_estimate=pl.CostEstimate(
             flops=12 * count * rows * experts * width * hidden,
             bytes_accessed=6 * experts * width * hidden,
@@ -336,7 +385,7 @@
             out_specs=[pl.BlockSpec((1,) + shape, lambda e, s: (e, 0, 0))] * shards,
         ),
         out_shape=[jax.ShapeDtypeStruct((experts,) + shape, BF)] * shards,
-        compiler_params=pltpu.CompilerParams(vmem_limit_bytes=56 * 1024 * 1024),
+        compiler_params=pltpu.CompilerParams(vmem_limit_bytes=60 * 1024 * 1024),
         cost_estimate=pl.CostEstimate(
             flops=2 * blocks * rows * experts * width * hidden,
             bytes_accessed=4 * blocks * rows * width,
@@ -375,12 +424,56 @@
         in_specs=[whole] * 3 + [pl.BlockSpec((1, high, wide), lambda e: (e, 0, 0))] * (kinds * parts),
         out_specs=[whole] * 3,
         out_shape=[jax.ShapeDtypeStruct(weight.shape, F32)] * 3,
-        compiler_params=pltpu.CompilerParams(vmem_limit_bytes=48 * 1024 * 1024),
+        compiler_params=pltpu.CompilerParams(vmem_limit_bytes=60 * 1024 * 1024),
         cost_estimate=pl.CostEstimate(
             flops=20 * weight.size, bytes_accessed=28 * weight.size, transcendentals=weight.size
         ),
         name="adamw",
     )(weight, moment, second, *[part for kind in gradients for part in kind])
+
+
+def adamw_rest_kernel(q_cols, k_cols, s_ref, *refs):
+    total = refs[0][...].astype(F32) + refs[1][...].astype(F32) + refs[2][...].astype(F32)
+    arrays, outs = refs[3:18], refs[18:]
+    gains, query, keyval, output, router = (arrays[i : i + 3] for i in range(0, 15, 3))
+    new_gains, new_query, new_keyval, new_output, new_router = (
+        outs[i : i + 3] for i in range(0, 15, 3)
+    )
+
+    def update(refs, outs, where, gradient, rate, decay):
+        new = adamw_update(*[ref[where] for ref in refs], gradient, rate, decay)
+        for out, value in zip(outs, new):
+            out[where] = value
+
+    heads_cols = q_cols + 2 * k_cols
+    o_cols = output[0].shape[0]
+    every = (slice(None), slice(None))
+    update(query, new_query, every, total[:, :q_cols], MATRIX_RATE, MATRIX_DECAY)
+    for kind in range(2):
+        low = q_cols + kind * k_cols
+        update(
+            keyval, new_keyval, (kind,) + every, total[:, low : low + k_cols], MATRIX_RATE, MATRIX_DECAY
+        )
+    turned = total[:, heads_cols : heads_cols + o_cols].T
+    update(output, new_output, every, turned, MATRIX_RATE, MATRIX_DECAY)
+    ends = total[:, heads_cols + o_cols :]
+    update(router, new_router, every, ends[:, :EXPERTS], MATRIX_RATE, MATRIX_DECAY)
+    turned = ends.T
+    for kind in range(2):
+        at = EXPERTS + 1 - kind
+        where = (slice(kind, kind + 1), slice(None))
+        update(gains, new_gains, where, turned[at : at + 1], GAIN_RATE, 0.0)
+
+
+def adamw_rest(q_cols, k_cols, parts, groups):
+    arrays = [array for group in groups for array in group]
+    return call_whole(
+        functools.partial(adamw_rest_kernel, q_cols, k_cols),
+        [jax.ShapeDtypeStruct(array.shape, F32) for array in arrays],
+        parts + arrays,
+        "adamw_rest",
+        cost=10**8,
+    )
 
 
 def call_whole(kernel, out_shape, operands, name, scalars=None, specs=None, scratch=(), cost=0):
@@ -523,7 +616,7 @@
 def middle_back_kernel(parts, s_ref, *refs):
     sums = refs[:parts]
     mid_ref, message_ref, dy_ref, gains_ref, rest_ref, out_ref = refs[parts : parts + 6]
-    grad_mid_ref, attention_ref, mix_ref, tail_ref = refs[parts + 6 :]
+    grad_mid_ref, attention_ref, mix_ref, tail_ref = refs[len(refs) - 4 :]
     rows, width = mid_ref.shape
     total = sums[0][...].astype(F32)
     for ref in sums[1:]:
@@ -612,10 +705,8 @@
 
     gate_pieces = tensor_gather(gateup_weight[:, 0].astype(BF), tensors)
     up_pieces = tensor_gather(gateup_weight[:, 1].astype(BF), tensors)
-    down_pieces = tensor_gather(down_weight.astype(BF), tensors)
     gate_low = jnp.concatenate(gate_pieces, axis=2)
     up_low = jnp.concatenate(up_pieces, axis=2)
-    down_low = jnp.concatenate(down_pieces, axis=1)
 
     q_cols = query_weight.shape[1]
     k_cols = keyval_weight.shape[2]
@@ -635,6 +726,10 @@
     )
     packed_blocks = ring_gather(packed, ring)
     offsets = sorted(packed_blocks)
+    cosine_table, sine_table = rope_tables(length, HD)
+    cosine_table = jnp.concatenate([cosine_table] * 4, axis=1)
+    sine_table = jnp.concatenate([-sine_table, sine_table] * 2, axis=1)
+    down_bf = down_weight.astype(BF)
     qkv_low, out_low, rest = place(
         [packed_blocks[o] for o in offsets],
         jnp.stack([ring_index(ring, o) for o in offsets]).astype(jnp.int32),
@@ -643,22 +738,17 @@
             (heads_cols, heads_cols + o_cols),
             (heads_cols + o_cols, heads_cols + o_cols + PAD),
         ],
-        after=gate_pieces[1:chips] + up_pieces[1:chips],
+        after=gate_pieces[1:chips] + up_pieces[1:chips] + [cosine_table, sine_table, down_bf],
     )
     gains_all = (
         rest[:, EXPERTS : EXPERTS + 2].astype(F32)
         + rest[:, EXPERTS + 2 : EXPERTS + 4].astype(F32)
         + rest[:, EXPERTS + 4 : EXPERTS + 6].astype(F32)
     ).T
-    one_spot = jnp.zeros((1,), jnp.int32)
     dy_own = lax.dynamic_slice_in_dim(cotangent, lane_t[0] * rows, rows, axis=0)
     dy_all = lax.all_gather(
-        place([dy_own], one_spot, after=[qkv_low]), "expert", axis=0, tiled=True
-    )
-
-    cosine_table, sine_table = rope_tables(length, HD)
-    cosine_table = jnp.concatenate([cosine_table] * 4, axis=1)
-    sine_table = jnp.concatenate([-sine_table, sine_table] * 2, axis=1)
+        hold(dy_own, [packed_blocks[-(ring // 4)]]), "expert", axis=0, tiled=True
+    )
     a, rotated, mixture = call_whole(
         functools.partial(front_kernel, q_cols, k_cols),
         [shape((length, width), BF), shape((length, heads_cols), BF), shape((length, q_cols), BF)],
@@ -671,9 +761,10 @@
         mixture.reshape(tensors, rows, o_cols), "tensor", split_axis=0, concat_axis=0, tiled=True
     )
     owners_t = tensor_index(tensors)
-    out_all = place(
-        tensor_gather(out_low, tensors), owners_t, after=[mixture_rows] + down_pieces[1:chips]
-    ).reshape(tensors, width, o_cols)
+    out_pieces = tensor_gather(out_low, tensors, after=[mixture])
+    out_all = place(out_pieces, owners_t, after=[mixture_rows]).reshape(tensors, width, o_cols)
+    down_pieces = tensor_gather(hold(down_bf, out_pieces[1:chips]), tensors)
+    down_low = jnp.concatenate(down_pieces, axis=1)
     message, x_mid = call_whole(
         middle_kernel,
         [shape((rows, width + PAD), BF), shape((rows, width), F32)],
@@ -696,12 +787,12 @@
     spots = []
     after = []
     for number, call in enumerate(calls):
-        owners = [ring_index(ring, o).astype(jnp.int32) for o in call]
+        owners = [ring_index(ring, o).astype(jnp.int32) * min(abs(o), 1) for o in call]
         result = expert_blocks(
             first,
             [blocks[o] for o in call],
             owners,
-            [dy_all] * len(call),
+            [dy_own if o == 0 else dy_all for o in call],
             gate_low,
             up_low,
             down_low,
@@ -714,22 +805,30 @@
             forth[o], back[o] = result[2][part], result[3][part]
             order.append(o)
             spots.append((number, part, rows))
-    returned, sent = ring_reduce(lambda offset: back[offset], ring)
 
     still = jnp.zeros((ring,), jnp.int32)
     whose = jnp.stack([ring_index(ring, o) for o in order]).astype(jnp.int32)
     messages = [blocks[o] for o in order]
-    hop = lambda number: [sent[min(number, half - 1)]]
-    gate_grads = weight_grad(messages, still, spots, grads, 0, False, tensors, hop(1))
-    up_grads = weight_grad(messages, still, spots, grads, 1, False, tensors, hop(2))
-    down_grads = weight_grad([dy_all] * ring, whose, spots, scaled, 0, True, tensors, hop(3))
-
-    moe_sum = lax.psum_scatter(
-        place([forth[o] for o in order], whose, after=[returned[1]]),
-        "expert",
-        scatter_dimension=0,
-        tiled=True,
-    )
+    weights = {}
+
+    def beside(hop, sent):
+        kind = max(hop - 1, 0)
+        if hop > 3 or kind in weights:
+            return []
+        if kind == 0:
+            weights[0] = weight_grad([dy_all] * ring, whose, spots, scaled, 0, True, tensors, sent[:1])
+        else:
+            weights[kind] = weight_grad(
+                messages, still, spots, grads, kind - 1, False, tensors, sent[:1]
+            )
+        if hop == 2:
+            sums = place([forth[o] for o in order], whose, after=sent[:1])
+            weights["sum"] = lax.psum_scatter(sums, "expert", scatter_dimension=0, tiled=True)
+        return [weights[kind][0]]
+
+    returned, after = ring_reduce(lambda offset: back[offset], ring, beside)
+    up_grads, gate_grads, down_grads = weights[2], weights[1], weights[0]
+    moe_sum = weights["sum"]
     block_out = place(tensor_gather((x_mid + moe_sum.astype(F32)).astype(BF), tensors), owners_t)
 
     grad_mid, grad_attention, grad_mixture, tail = call_whole(
@@ -740,10 +839,13 @@
             shape((tensors, rows, o_cols), BF),
             shape((width, PAD), BF),
         ],
-        returned + [x_mid, message, cotangent, gains_all, rest, out_all],
+        returned + [x_mid, message, cotangent, gains_all, rest, out_all] + after,
         "middle_backward",
         scalars=lane_t,
-        specs={len(returned) + 2: own_block},
+        specs={
+            len(returned) + 2: own_block,
+            len(returned) + 6: pl.BlockSpec(memory_space=pl.ANY),
+        },
         cost=10**9,
     )
     grad_mixture = lax.all_to_all(
@@ -769,16 +871,7 @@
         cost=4 * 10**9,
     )
     tail = tensor_sum(tail, tensors)
-    piece = width // ring
-
-    def own_piece(offset):
-        start = ring_index(ring, offset) * piece
-        return jnp.concatenate(
-            [lax.dynamic_slice_in_dim(array, start, piece, axis=0) for array in (main, tail)], axis=1
-        )
-
-    summed = sum(part.astype(F32) for part in ring_reduce(own_piece, ring)[0])
-    qkv_all = lax.all_gather(place([qkv_low], one_spot, after=[scaled[1]]), "tensor")
+    qkv_all = lax.all_gather(hold(qkv_low, [scaled[1]]), "tensor")
     (input_grad,) = call_whole(
         final_kernel,
         [shape((rows, width), BF)],
@@ -788,7 +881,27 @@
         specs={3: own_block},
         cost=2 * 10**9,
     )
+    pieces = cut(
+        main,
+        tail,
+        jnp.stack([ring_index(ring, o) for o in offsets]).astype(jnp.int32),
+        [input_grad],
+    )
+    pieces = dict(zip(offsets, pieces))
+    summed, _ = ring_reduce(lambda offset: pieces[offset], ring)
     input_grad = place(tensor_gather(input_grad, tensors), owners_t)
+    new_rest = adamw_rest(
+        q_cols,
+        k_cols,
+        summed,
+        [
+            [norm_gains, gains_moment, gains_second],
+            [query_weight, query_moment, query_second],
+            [keyval_weight, keyval_moment, keyval_second],
+            [output_weight, output_moment, output_second],
+            [router_weight, router_moment, router_second],
+        ],
+    )
 
     new_gateup = adamw_blocks(
         gateup_weight,
@@ -805,35 +918,7 @@
             [tensor_reduce(down_grads, tensors)],
         )
     ]
-    query_sum = summed[:, :q_cols]
-    keyval_sum = jnp.stack([summed[:, q_cols : q_cols + k_cols], summed[:, q_cols + k_cols : heads_cols]])
-    output_sum = summed[:, heads_cols : heads_cols + o_cols].T
-    ends = summed[:, heads_cols + o_cols :]
-    router_sum = ends[:, :EXPERTS]
-    gains_sum = jnp.stack([ends[:, EXPERTS + 1], ends[:, EXPERTS]])
-    new_gains = adamw_update(norm_gains, gains_moment, gains_second, gains_sum, GAIN_RATE, 0.0)
-    new_query = adamw_update(
-        query_weight, query_moment, query_second, query_sum, MATRIX_RATE, MATRIX_DECAY
-    )
-    new_keyval = adamw_update(
-        keyval_weight, keyval_moment, keyval_second, keyval_sum, MATRIX_RATE, MATRIX_DECAY
-    )
-    new_output = adamw_update(
-        output_weight, output_moment, output_second, output_sum, MATRIX_RATE, MATRIX_DECAY
-    )
-    new_router = adamw_update(
-        router_weight, router_moment, router_second, router_sum, MATRIX_RATE, MATRIX_DECAY
-    )
-    return (
-        (block_out, input_grad)
-        + tuple(new_gains)
-        + tuple(new_query)
-        + tuple(new_keyval)
-        + tuple(new_output)
-        + tuple(new_router)
-        + tuple(new_gateup)
-        + tuple(new_down)
-    )
+    return (block_out, input_grad) + tuple(new_rest) + tuple(new_gateup) + tuple(new_down)
 
 
 def solution(mesh):

time: 593 us -> 574 us (0.968)
  local copies, waits for them, and re-layouts: 68.7 us -> 46.1 us
  Pallas kernels: 213 us -> 227 us
  starting transfers between devices: 72.8 us -> 59.4 us
  waiting for transfers between devices: 174 us -> 184 us
  other arithmetic: 44.1 us -> 35.6 us
    ppermute x6, waiting for transfers between devices: 0.12 us -> 21.4 us  [ring_gather(): behind = lax.ppermute(behind, 'expert', ring_perm(size, -1))]
    unnamed x182 -> x135, local copies, waits for them, and re-layouts: 57 us -> 40 us
    reduce_scatter x1, starting transfers between devices: 12.4 us -> 0.04 us  [beside(): lax.psum_scatter(sums, 'expert', scatter_dimension=0, tiled=True)]
    ppermute x7, waiting for transfers between devices: 58.4 us -> 66.8 us  [tensor_gather(): lax.ppermute(shard, 'tensor', tensor_perm(size, -step, 0))]
    ppermute x1, waiting for transfers between devices: 12.6 us -> 4.36 us  [tensor_sum(): lax.ppermute(values, 'tensor', tensor_perm(size, step, 0))]
    ppermute x8, waiting for transfers between devices: 39.5 us -> 31.6 us  [ring_gather(): ahead = lax.ppermute(ahead, 'expert', ring_perm(size, 1))]
    sub x5 -> x0, other arithmetic: 7.73 us -> none  [adamw_update(): return (weight - rate * (update + decay * weight), moment_new, second_new)]
    convert_element_type x12 -> x1, other arithmetic: 9.17 us -> 1.75 us  [body(): down_bf = down_weight.astype(BF)]
  transfers between devices with their start and end apart: 66 -> 66, of which waited for: 24 -> 25; matrix products, arithmetic and copies ran while one was open for 12% -> 8% of each run, Pallas kernels for 35% -> 35%
where the time goes in v3:
time: 574 us; the launch traced here: 567 us
  Pallas kernels  227 us (40%)
  waiting for transfers between devices  184 us (32%)
  starting transfers between devices  59.4 us (10%)
  local copies, waits for them, and re-layouts  46.1 us (8%)
  other arithmetic  35.6 us (6%)
  between operations  15.2 us (3%)
    pallas_call x5, Pallas kernels, expert_blocks(): pl.pallas_call(functools.partial(expert_kernel, count, len(after)), grid_...  92.7 us
    ppermute x7, waiting for transfers between devices, tensor_gather(): lax.ppermute(shard, 'tensor', tensor_perm(size, -step, 0))  66.8 us
    pallas_call x7, Pallas kernels, call_whole(): pl.pallas_call(kernel, grid_spec=pltpu.PrefetchScalarGridSpec(num_scalar_...  56.3 us
    pallas_call x3, Pallas kernels, weight_grad(): pl.pallas_call(functools.partial(weight_grad_kernel, spots, swap, shards,...  43.7 us
    unnamed x135, local copies, waits for them, and re-layouts  40 us
    ppermute x8, waiting for transfers between devices, ring_gather(): ahead = lax.ppermute(ahead, 'expert', ring_perm(size, 1))  31.6 us
    ppermute x8, waiting for transfers between devices, ring_reduce(): down = lax.ppermute(messages[0], 'expert', ring_perm(size, -1))  25.7 us
    ppermute x6, waiting for transfers between devices, ring_gather(): behind = lax.ppermute(behind, 'expert', ring_perm(size, -1))  21.4 us
  transfers between devices with their start and end apart: 66, of which 25 were waited for; matrix products, arithmetic and copies ran while one was open for 8% of the time, Pallas kernels for 35%

profile of v3, /device:TPU:0, one launch (start us, length us, event | category | flops | bytes accessed | tf_op | source)
XLA Modules:
  0.0 567.5 jit_solution(17249532115575151132)
XLA Ops:
  11.9 3.1 collective-permute-start
  15.0 5.5 collective-permute-done.refs_4_
  20.5 1.8 collective-permute-start.1
  23.4 3.9 collective-permute-done.1.refs_3_.refs_2_
  29.0 3.9 slice_bitcast_fusion
  36.3 6.2 %collective-permute-done.4.refs_6_ = bf16[128,896]{1,0:T(8,128)(2,1)S(1)} collective-permute-done((bf16[128,896]{1,0:T(8,128)(2,1)S(1)}, bf16[128,896]{1,0:T(8,128)(2,1)S(1)}, u32[]{:S(2)}, u32[]{:S(2)}) %collective-permute-start.4) | collective-permute-done | bytes 229408 | tf_op jit(solution)/shard_map/ppermute | solution.py:90
  42.5 2.5 collective-permute-start.5
  45.0 15.2 %collective-permute-done.5.refs_7_ = bf16[128,896]{1,0:T(8,128)(2,1)S(1)} collective-permute-done((bf16[128,896]{1,0:T(8,128)(2,1)S(1)}, bf16[128,896]{1,0:T(8,128)(2,1)S(1)}, u32[]{:S(2)}, u32[]{:S(2)}) %collective-permute-start.5) | collective-permute-done | bytes 229408 | tf_op jit(solution)/shard_map/ppermute | solution.py:90
  60.2 2.0 collective-permute-start.3
  62.3 3.1 fusion.2
  65.5 1.7 convert_element_type.93.refs_13_
  67.4 3.4 pad_maximum_fusion.3
  71.7 7.4 %collective-permute-done.8.refs_10_ = bf16[4,1024,128]{2,1,0:T(8,128)(2,1)} collective-permute-done((bf16[4,1024,128]{2,1,0:T(8,128)(2,1)}, bf16[4,1024,128]{2,1,0:T(8,128)(2,1)}, u32[]{:S(2)}, u32[]{:S(2)}) %collective-permute-start.8) | collective-permute-done | bytes 1048608 | tf_op jit(solution)/shard_map/ppermute | solution.py:119
  86.6 9.2 %collective-permute-done.9.refs_1_.refs_2_ = bf16[1024,256]{1,0:T(8,128)(2,1)S(1)} collective-permute-done((bf16[1024,256]{1,0:T(8,128)(2,1)S(1)}, bf16[1024,256]{1,0:T(8,128)(2,1)S(1)}, u32[]{:S(2)}, u32[]{:S(2)}) %collective-permute-start.9) | collective-permute-done | bytes 524320 | tf_op jit(solution)/shard_map/ppermute | solution.py:119
  97.1 13.4 %attention_forward.1 = (bf16[1024,1024]{1,0:T(8,128)(2,1)}, bf16[1024,512]{1,0:T(8,128)(2,1)}, bf16[1024,256]{1,0:T(8,128)(2,1)}) custom-call(s32[1]{0:T(128)} %constant.336.clone.1.s_ref.refs_0_, bf16[1024,1024]{1,0:T(8,128)(2,1)} %x_ref.5, f32[2,1024]{1,0:T(2,128)} %add_bitcast_fusion.gains_ref.refs_6_, bf16[1024,512]{1,0:T(8,128)(2,1)} %copy-done.16, ...), custom_call_target="tpu_custom_call" | custom-call | flops 10000000000 | bytes 4194304 | tf_op jit(solution)/shard_map/attention_forward/pallas_call | solution.py:482
  113.7 3.5 all-to-all-start
  120.2 5.7 %all-to-all-done.refs_5_.mix_ref = bf16[4,256,256]{2,1,0:T(8,128)(2,1)S(1)} async-done(((bf16[4,256,256]{2,1,0:T(8,128)(2,1)}), bf16[4,256,256]{2,1,0:T(8,128)(2,1)S(1)}, u32[]{:S(2)}, u32[]{:S(2)}) %all-to-all-start) | async-done | bytes 524320 | tf_op jit(solution)/shard_map/all_to_all | solution.py:760
  128.7 4.2 middle.1
  134.5 3.8 pad_maximum_fusion.refs_3_.refs_5_
  138.7 3.8 pad_maximum_fusion.1.refs_4_.refs_6_
  142.5 3.6 pad_maximum_fusion.2.refs_5_.refs_7_
  146.1 13.1 %expert_blocks.5 = (bf16[2,4,256,512]{3,2,1,0:T(8,128)(2,1)}, bf16[4,256,512]{2,1,0:T(8,128)(2,1)}, bf16[256,1024]{1,0:T(8,128)(2,1)}, bf16[256,1152]{1,0:T(8,128)(2,1)}) custom-call(s32[2]{0:T(128)} %pad_add_fusion.1.refs_0_, bf16[256,1152]{1,0:T(8,128)(2,1)} %get-tuple-element.117.refs_1_.refs_4_, bf16[256,1024]{1,0:T(8,128)(2,1)} %copy-done.14, ...), custom_call_target="tpu_custom_call" | custom-call | flops 6442450944 | bytes 12582912 | tf_op jit(solution)/shard_map/expert_blocks/pallas_call | solution.py:306
  159.2 22.2 %expert_blocks.6 = (bf16[2,4,512,512]{3,2,1,0:T(8,128)(2,1)}, bf16[4,512,512]{2,1,0:T(8,128)(2,1)}, bf16[256,1024]{1,0:T(8,128)(2,1)}, bf16[256,1024]{1,0:T(8,12...) custom-call(s32[3]{0:T(128)} %pad_add_fusion.2.refs_0_, ...), custom_call_target="tpu_custom_call" | custom-call | flops 12884901888 | bytes 12582912 | tf_op jit(solution)/shard_map/expert_blocks/pallas_call | solution.py:306
  186.2 12.5 %collective-permute-done.21.refs_1_.refs_4_ = bf16[256,1152]{1,0:T(8,128)(2,1)S(1)} collective-permute-done((bf16[256,1152]{1,0:T(8,128)(2,1)}, bf16[256,1152]{1,0:T(8,128)(2,1)S(1)}, u32[]{:S(2)}, u32[]{:S(2)}) %collective-permute-start.21) | collective-permute-done | bytes 589856 | tf_op jit(solution)/shard_map/ppermute | solution.py:87
  202.6 9.6 %collective-permute-done.23.refs_1_.refs_8_ = bf16[256,1152]{1,0:T(8,128)(2,1)S(1)} collective-permute-done((bf16[256,1152]{1,0:T(8,128)(2,1)S(1)}, bf16[256,1152]{1,0:T(8,128)(2,1)S(1)}, u32[]{:S(2)}, u32[]{:S(2)}) %collective-permute-start.23) | collective-permute-done | bytes 589856 | tf_op jit(solution)/shard_map/ppermute | solution.py:87
  212.2 2.0 collective-permute-start.24
  214.2 22.1 %expert_blocks.7 = (bf16[2,4,512,512]{3,2,1,0:T(8,128)(2,1)}, bf16[4,512,512]{2,1,0:T(8,128)(2,1)}, bf16[256,1024]{1,0:T(8,128)(2,1)}, bf16[256,1024]{1,0:T(8,12...) custom-call(s32[3]{0:T(128)} %pad_add_fusion.3.refs_0_, bf16[256,1152]{1,0:T(8,128)(2,1)} %copy-done.58, ...), custom_call_target="tpu_custom_call" | custom-call | flops 12884901888 | bytes 12582912 | tf_op jit(solution)/shard_map/expert_blocks/pallas_call | solution.py:306
  237.3 22.0 %expert_blocks.8 = (bf16[2,4,512,512]{3,2,1,0:T(8,128)(2,1)}, bf16[4,512,512]{2,1,0:T(8,128)(2,1)}, bf16[256,1024]{1,0:T(8,128)(2,1)}, bf16[256,1024]{1,0:T(8,12...) custom-call(s32[3]{0:T(128)} %pad_add_fusion.4.refs_0_, bf16[256,1152]{1,0:T(8,128)(2,1)} %copy-done.62, ...), custom_call_target="tpu_custom_call" | custom-call | flops 12884901888 | bytes 12582912 | tf_op jit(solution)/shard_map/expert_blocks/pallas_call | solution.py:306
  261.4 13.3 %expert_blocks.9 = (bf16[2,4,256,512]{3,2,1,0:T(8,128)(2,1)}, bf16[4,256,512]{2,1,0:T(8,128)(2,1)}, bf16[256,1024]{1,0:T(8,128)(2,1)}, bf16[256,1152]{1,0:T(8,128)(2,1)}) custom-call(s32[2]{0:T(128)} %pad_add_fusion.5.refs_0_, bf16[256,1152]{1,0:T(8,128)(2,1)} %copy-done.60, ...), custom_call_target="tpu_custom_call" | custom-call | flops 6442450944 | bytes 12582912 | tf_op jit(solution)/shard_map/expert_blocks/pallas_call | solution.py:306
  277.5 1.7 collective-permute-start.29
  279.7 14.7 %weight_grad.3 = (bf16[4,1024,128]{2,1,0:T(8,128)(2,1)}, bf16[4,1024,128]{2,1,0:T(8,128)(2,1)}, bf16[4,1024,128]{2,1,0:T(8,128)(2,1)}, bf16[4,1024,128]{2,1,0:T(8,128)(2,1)}) custom-call(s32[8]{0:T(128)} %broadcast_1_refs_0_.2.refs_0_, bf16[256,1152]{1,0:T(8,128)(2,1)} %get-tuple-element.117.refs_1_.refs_4_, ...), custom_call_target="tpu_custom_call" | custom-call | flops 8589934592 | bytes 8388608 | tf_op jit(solution)/shard_map/weight_grad/pallas_call | solution.py:379
  304.1 2.0 copy-done.1
  308.7 14.6 %weight_grad.4 = (bf16[4,1024,128]{2,1,0:T(8,128)(2,1)}, bf16[4,1024,128]{2,1,0:T(8,128)(2,1)}, bf16[4,1024,128]{2,1,0:T(8,128)(2,1)}, bf16[4,1024,128]{2,1,0:T(8,128)(2,1)}) custom-call(s32[8]{0:T(128)} %broadcast_1_refs_0_.2.refs_0_, bf16[256,1152]{1,0:T(8,128)(2,1)} %get-tuple-element.117.refs_1_.refs_4_, ...), custom_call_target="tpu_custom_call" | custom-call | flops 8589934592 | bytes 8388608 | tf_op jit(solution)/shard_map/weight_grad/pallas_call | solution.py:379
  323.3 4.8 collective-permute-done.33.refs_0_
  330.3 14.4 %weight_grad.5 = (bf16[4,128,1024]{2,1,0:T(8,128)(2,1)}, bf16[4,128,1024]{2,1,0:T(8,128)(2,1)}, bf16[4,128,1024]{2,1,0:T(8,128)(2,1)}, bf16[4,128,1024]{2,1,0:T(8,128)(2,1)}) custom-call(s32[8]{0:T(128)} %copy-done.40, bf16[2048,1024]{1,0:T(8,128)(2,1)} %all-gather.4.cloned.1.call-done.refs_3_.refs_4_.refs_2_.refs_1_.refs_5_.refs_6_.refs_7_.refs_8_, ...), custom_call_target="tpu_custom_call" | custom-call | flops 8589934592 | bytes 8388608 | tf_op jit(solution)/shard_map/weight_grad/pallas_call | solution.py:379
  344.8 14.4 %collective-permute-done.34.refs_1_ = bf16[256,1152]{1,0:T(8,128)(2,1)S(1)} collective-permute-done((bf16[256,1152]{1,0:T(8,128)(2,1)S(1)}, bf16[256,1152]{1,0:T(8,128)(2,1)S(1)}, u32[]{:S(2)}, u32[]{:S(2)}) %collective-permute-start.34) | collective-permute-done | bytes 589856 | tf_op jit(solution)/shard_map/ppermute | solution.py:106
  359.9 5.5 middle_backward.1
  365.5 3.7 all-to-all-start.1
  370.2 7.3 %collective-permute-done.39.refs_2_ = bf16[256,1024]{1,0:T(8,128)(2,1)S(1)} collective-permute-done((bf16[256,1024]{1,0:T(8,128)(2,1)}, bf16[256,1024]{1,0:T(8,128)(2,1)S(1)}, u32[]{:S(2)}, u32[]{:S(2)}) %collective-permute-start.39) | collective-permute-done | bytes 524320 | tf_op jit(solution)/shard_map/ppermute | solution.py:119
  377.5 3.0 all-to-all-done.1
  381.3 18.7 %attention_backward.1.grad_ref = bf16[1024,512]{1,0:T(8,128)(2,1)} custom-call(s32[1]{0:T(128)} %constant.336.clone.1.s_ref.refs_0_, bf16[1024,512]{1,0:T(8,128)(2,1)} %get-tuple-element.145.rot_ref, bf16[1024,256]{1,0:T(8,128)(2,1)} %bitcast.59, f32[1024,128]{1,0:T(8,128)} %copy-done.9, f32[1024,128]{1,0:T(8,128)} %copy-done.10), custom_call_target="tpu_custom_call" | custom-call | flops 20000000000 | bytes 4194304 | tf_op jit(solution)/shard_map/attention_backward/pallas_call | solution.py:482
  400.0 3.5 all-to-all-start.2
  405.6 6.3 %pack.1 = (bf16[1024,768]{1,0:T(8,128)(2,1)}, bf16[1024,128]{1,0:T(8,128)(2,1)}) custom-call(s32[1]{0:T(128)} %constant.336.clone.1.s_ref.refs_0_, bf16[1024,1024]{1,0:T(8,128)(2,1)} %get-tuple-element.154.a_ref, bf16[1024,512]{1,0:T(8,128)(2,1)} %attention_backward.1.grad_ref, bf16[1024,1024]{1,0:T(8,128)(2,1)} %copy-done.13, ...), custom_call_target="tpu_custom_call" | custom-call | flops 4000000000 | bytes 4194304 | tf_op jit(solution)/shard_map/pack/pallas_call | solution.py:482
  415.1 1.7 collective-permute-start.43
  416.8 2.5 add_convert_fusion.1
  419.3 4.4 collective-permute-done.43
  426.4 5.4 input_gradient.1.refs_1_.refs_0_
  432.6 2.5 add_convert_fusion.2
  435.6 3.8 collective-permute-done.44.refs_0_
  439.4 2.6 add_convert_fusion
  442.0 3.4 collective-permute-done.45.refs_2_
  446.3 3.6 collective-permute-start.46
  451.8 2.6 collective-permute-done.46.refs_0_
  456.3 5.1 collective-permute-done.47.refs_2_
  461.7 2.4 collective-permute-start.48
  464.1 8.4 %collective-permute-done.52.refs_3_ = bf16[4,1024,128]{2,1,0:T(8,128)(2,1)} collective-permute-done((bf16[4,1024,128]{2,1,0:T(8,128)(2,1)}, bf16[4,1024,128]{2,1,0:T(8,128)(2,1)}, u32[]{:S(2)}, u32[]{:S(2)}) %collective-permute-start.52) | collective-permute-done | bytes 1048608 | tf_op jit(solution)/shard_map/ppermute | solution.py:135
  472.5 33.6 %collective-permute-done.36.refs_2_ = bf16[256,1024]{1,0:T(8,128)(2,1)S(1)} collective-permute-done((bf16[256,1024]{1,0:T(8,128)(2,1)}, bf16[256,1024]{1,0:T(8,128)(2,1)S(1)}, u32[]{:S(2)}, u32[]{:S(2)}) %collective-permute-start.36) | collective-permute-done | bytes 524320 | tf_op jit(solution)/shard_map/ppermute | solution.py:119
  506.6 9.2 %collective-permute-done.30.refs_2_ = bf16[256,1024]{1,0:T(8,128)(2,1)S(1)} collective-permute-done((bf16[256,1024]{1,0:T(8,128)(2,1)S(1)}, bf16[256,1024]{1,0:T(8,128)(2,1)S(1)}, u32[]{:S(2)}, u32[]{:S(2)}) %collective-permute-start.30) | collective-permute-done | bytes 524320 | tf_op jit(solution)/shard_map/ppermute | solution.py:119
  516.6 7.3 %collective-permute-done.50.refs_2_ = bf16[128,896]{1,0:T(8,128)(2,1)S(1)} collective-permute-done((bf16[128,896]{1,0:T(8,128)(2,1)S(1)}, bf16[128,896]{1,0:T(8,128)(2,1)S(1)}, u32[]{:S(2)}, u32[]{:S(2)}) %collective-permute-start.50) | collective-permute-done | bytes 229408 | tf_op jit(solution)/shard_map/ppermute | solution.py:108
  528.0 12.2 %adamw.2 = (f32[4,2,1024,128]{3,2,1,0:T(8,128)}, f32[4,2,1024,128]{3,2,1,0:T(8,128)}, f32[4,2,1024,128]{3,2,1,0:T(8,128)}) custom-call(f32[4,2,1024,128]{3,2,1,0:T(8,128)} %refs_0_.1, f32[4,2,1024,128]{3,2,1,0:T(8,128)} %refs_1_.1, f32[4,2,1024,128]{3,2,1,0:T(8,128)} %refs_2_.1, bf16[4,1024,128]{2,1,0:T(8,128)(2,1)} %collective-permute-done.52.refs_3_, ...), custom_call_target="tpu_custom_call" | custom-call | flops 20971520 | bytes 29360128 | tf_op jit(solution)/shard_map/adamw/pallas_call | solution.py:421
  540.2 7.3 %adamw.3 = (f32[4,1,128,1024]{3,2,1,0:T(8,128)}, f32[4,1,128,1024]{3,2,1,0:T(8,128)}, f32[4,1,128,1024]{3,2,1,0:T(8,128)}) custom-call(f32[4,1,128,1024]{3,2,1,0:T(8,128)} %bitcast.54, f32[4,1,128,1024]{3,2,1,0:T(8,128)} %bitcast.56, f32[4,1,128,1024]{3,2,1,0:T(8,128)} %bitcast.57, bf16[4,128,1024]{2,1,0:T(8,128)(2,1)} %collective-permute-done.58.refs_3_, ...), custom_call_target="tpu_custom_call" | custom-call | flops 10485760 | bytes 14680064 | tf_op jit(solution)/shard_map/adamw/pallas_call | solution.py:421
  548.2 2.9 adamw_rest.1
  555.6 2.5 place.20
  558.1 2.5 place.18
  (275 shorter events, 88.2 us)
Async XLA Ops:
  7.2 152.0 %all-gather.4.cloned.1.call-start = ((), (), s32[]{:S(2)}) async-start(), calls=%async_computation.4 | async-start | bytes 4718592 | tf_op jit(solution)/shard_map/all_gather | solution.py:749
  11.9 8.6 %collective-permute-start = (bf16[128,896]{1,0:T(8,128)(2,1)S(1)}, bf16[128,896]{1,0:T(8,128)(2,1)S(1)}, u32[]{:S(2)}, u32[]{:S(2)}) collective-permute-start(bf16[128,896]{1,0:T(8,128)(2,1)S(1)} %concatenate.18.refs_5_), channel_id=1, source_target_pairs={{0,8},{8,16},{16,24},{24,28},{28,20},{20,12},{12,4},{4,0},{1,9},{9... | collective-permute-start | bytes 688136 | tf_op jit(solution)/shard_map/ppermute | solution.py:87
  20.5 6.8 %collective-permute-start.1 = (bf16[128,896]{1,0:T(8,128)(2,1)S(1)}, bf16[128,896]{1,0:T(8,128)(2,1)S(1)}, u32[]{:S(2)}, u32[]{:S(2)}) collective-permute-start(bf16[128,896]{1,0:T(8,128)(2,1)S(1)} %collective-permute-done.refs_4_), channel_id=1, source_target_pairs={{0,8},{8,16},{16,24},{24,28},{28,20},{20,12},{12,4},{4,0},{1,9},{9... | collective-permute-start | bytes 688136 | tf_op jit(solution)/shard_map/ppermute | solution.py:87
  32.9 38.8 %collective-permute-start.7 = (bf16[4,1024,128]{2,1,0:T(8,128)(2,1)}, bf16[4,1024,128]{2,1,0:T(8,128)(2,1)}, u32[]{:S(2)}, u32[]{:S(2)}) collective-permute-start(bf16[4,1024,128]{2,1,0:T(8,128)(2,1)} %get-tuple-element.248), channel_id=1, source_target_pairs={{0,2},{1,3},{2,0},{3,1},{4,6},{5,7},{6,4},{7,5},{8,10},{9,11},{10,... | collective-permute-start | bytes 3145736 | tf_op jit(solution)/shard_map/ppermute | solution.py:119
  34.3 44.8 %collective-permute-start.8 = (bf16[4,1024,128]{2,1,0:T(8,128)(2,1)}, bf16[4,1024,128]{2,1,0:T(8,128)(2,1)}, u32[]{:S(2)}, u32[]{:S(2)}) collective-permute-start(bf16[4,1024,128]{2,1,0:T(8,128)(2,1)} %get-tuple-element.247), channel_id=1, source_target_pairs={{0,2},{1,3},{2,0},{3,1},{4,6},{5,7},{6,4},{7,5},{8,10},{9,11},{10,... | collective-permute-start | bytes 3145736 | tf_op jit(solution)/shard_map/ppermute | solution.py:119
  34.9 7.6 %collective-permute-start.4 = (bf16[128,896]{1,0:T(8,128)(2,1)S(1)}, bf16[128,896]{1,0:T(8,128)(2,1)S(1)}, u32[]{:S(2)}, u32[]{:S(2)}) collective-permute-start(bf16[128,896]{1,0:T(8,128)(2,1)S(1)} %concatenate.18.refs_5_), channel_id=1, source_target_pairs={{0,4},{8,0},{16,8},{24,16},{28,24},{20,28},{12,20},{4,12},{1,5},{9... | collective-permute-start | bytes 688136 | tf_op jit(solution)/shard_map/ppermute | solution.py:90
  42.5 17.7 %collective-permute-start.5 = (bf16[128,896]{1,0:T(8,128)(2,1)S(1)}, bf16[128,896]{1,0:T(8,128)(2,1)S(1)}, u32[]{:S(2)}, u32[]{:S(2)}) collective-permute-start(bf16[128,896]{1,0:T(8,128)(2,1)S(1)} %collective-permute-done.4.refs_6_), channel_id=1, source_target_pairs={{0,4},{8,0},{16,8},{24,16},{28,24},{20,28},{12,20},{4,12},{1,5},{9... | collective-permute-start | bytes 688136 | tf_op jit(solution)/shard_map/ppermute | solution.py:90
  45.0 15.2 %collective-permute-start.2 = (bf16[128,896]{1,0:T(8,128)(2,1)S(1)}, bf16[128,896]{1,0:T(8,128)(2,1)S(1)}, u32[]{:S(2)}, u32[]{:S(2)}) collective-permute-start(bf16[128,896]{1,0:T(8,128)(2,1)S(1)} %collective-permute-done.1.refs_3_.refs_2_), channel_id=1, source_target_pairs={{0,8},{8,16},{16,24},{24,28},{28,20},{20,12},{12,4},{4,0},{1,9},{9... | collective-permute-start | bytes 688136 | tf_op jit(solution)/shard_map/ppermute | solution.py:87
  60.2 10.6 %collective-permute-start.6 = (bf16[128,896]{1,0:T(8,128)(2,1)S(1)}, bf16[128,896]{1,0:T(8,128)(2,1)S(1)}, u32[]{:S(2)}, u32[]{:S(2)}) collective-permute-start(bf16[128,896]{1,0:T(8,128)(2,1)S(1)} %collective-permute-done.5.refs_7_), channel_id=1, source_target_pairs={{0,4},{8,0},{16,8},{24,16},{28,24},{20,28},{12,20},{4,12},{1,5},{9... | collective-permute-start | bytes 688136 | tf_op jit(solution)/shard_map/ppermute | solution.py:90
  60.2 11.4 %collective-permute-start.3 = (bf16[128,896]{1,0:T(8,128)(2,1)S(1)}, bf16[128,896]{1,0:T(8,128)(2,1)}, u32[]{:S(2)}, u32[]{:S(2)}) collective-permute-start(bf16[128,896]{1,0:T(8,128)(2,1)S(1)} %collective-permute-done.2.refs_2_), channel_id=1, source_target_pairs={{0,8},{8,16},{16,24},{24,28},{28,20},{20,12},{12,4},{4,0},{1,9},{9... | collective-permute-start | bytes 688136 | tf_op jit(solution)/shard_map/ppermute | solution.py:87
  84.0 11.8 %collective-permute-start.9 = (bf16[1024,256]{1,0:T(8,128)(2,1)S(1)}, bf16[1024,256]{1,0:T(8,128)(2,1)S(1)}, u32[]{:S(2)}, u32[]{:S(2)}) collective-permute-start(bf16[1024,256]{1,0:T(8,128)(2,1)S(1)} %get-tuple-element.115.refs_1_), channel_id=1, source_target_pairs={{0,2},{1,3},{2,0},{3,1},{4,6},{5,7},{6,4},{7,5},{8,10},{9,11},{10,... | collective-permute-start | bytes 1572872 | tf_op jit(solution)/shard_map/ppermute | solution.py:119
  85.9 27.2 %collective-permute-start.12 = (bf16[4,1024,128]{2,1,0:T(8,128)(2,1)}, bf16[4,1024,128]{2,1,0:T(8,128)(2,1)}, u32[]{:S(2)}, u32[]{:S(2)}) collective-permute-start(bf16[4,1024,128]{2,1,0:T(8,128)(2,1)} %get-tuple-element.248), channel_id=1, source_target_pairs={{0,1},{1,0},{2,3},{3,2},{4,5},{5,4},{6,7},{7,6},{8,9},{9,8},{10,11... | collective-permute-start | bytes 3145736 | tf_op jit(solution)/shard_map/ppermute | solution.py:122
  95.9 23.6 %collective-permute-start.16 = (bf16[4,128,1024]{2,1,0:T(8,128)(2,1)S(1)}, bf16[4,128,1024]{2,1,0:T(8,128)(2,1)}, u32[]{:S(2)}, u32[]{:S(2)}) collective-permute-start(bf16[4,128,1024]{2,1,0:T(8,128)(2,1)S(1)} %bitcast.51), channel_id=1, source_target_pairs={{0,2},{1,3},{2,0},{3,1},{4,6},{5,7},{6,4},{7,5},{8,10},{9,11},{10,... | collective-permute-start | bytes 3145736 | tf_op jit(solution)/shard_map/ppermute | solution.py:119
  111.6 21.2 %collective-permute-start.13 = (bf16[4,1024,128]{2,1,0:T(8,128)(2,1)}, bf16[4,1024,128]{2,1,0:T(8,128)(2,1)}, u32[]{:S(2)}, u32[]{:S(2)}) collective-permute-start(bf16[4,1024,128]{2,1,0:T(8,128)(2,1)} %collective-permute-done.7.refs_9_), channel_id=1, source_target_pairs={{0,1},{1,0},{2,3},{3,2},{4,5},{5,4},{6,7},{7,6},{8,9},{9,8},{10,11... | collective-permute-start | bytes 3145736 | tf_op jit(solution)/shard_map/ppermute | solution.py:122
  113.0 6.1 %collective-permute-start.11 = (bf16[1024,256]{1,0:T(8,128)(2,1)}, bf16[1024,256]{1,0:T(8,128)(2,1)}, u32[]{:S(2)}, u32[]{:S(2)}) collective-permute-start(bf16[1024,256]{1,0:T(8,128)(2,1)} %place.13), channel_id=1, source_target_pairs={{0,1},{1,0},{2,3},{3,2},{4,5},{5,4},{6,7},{7,6},{8,9},{9,8},{10,11... | collective-permute-start | bytes 1572872 | tf_op jit(solution)/shard_map/ppermute | solution.py:122
  113.0 25.2 %collective-permute-start.14 = (bf16[4,1024,128]{2,1,0:T(8,128)(2,1)}, bf16[4,1024,128]{2,1,0:T(8,128)(2,1)}, u32[]{:S(2)}, u32[]{:S(2)}) collective-permute-start(bf16[4,1024,128]{2,1,0:T(8,128)(2,1)} %get-tuple-element.247), channel_id=1, source_target_pairs={{0,1},{1,0},{2,3},{3,2},{4,5},{5,4},{6,7},{7,6},{8,9},{9,8},{10,11... | collective-permute-start | bytes 3145736 | tf_op jit(solution)/shard_map/ppermute | solution.py:122
  113.5 25.2 %collective-permute-start.15 = (bf16[4,1024,128]{2,1,0:T(8,128)(2,1)}, bf16[4,1024,128]{2,1,0:T(8,128)(2,1)}, u32[]{:S(2)}, u32[]{:S(2)}) collective-permute-start(bf16[4,1024,128]{2,1,0:T(8,128)(2,1)} %collective-permute-done.8.refs_10_), channel_id=1, source_target_pairs={{0,1},{1,0},{2,3},{3,2},{4,5},{5,4},{6,7},{7,6},{8,9},{9,8},{10,11... | collective-permute-start | bytes 3145736 | tf_op jit(solution)/shard_map/ppermute | solution.py:122
  113.7 12.3 %all-to-all-start = ((bf16[4,256,256]{2,1,0:T(8,128)(2,1)}), bf16[4,256,256]{2,1,0:T(8,128)(2,1)S(1)}, u32[]{:S(2)}, u32[]{:S(2)}) async-start(bf16[4,256,256]{2,1,0:T(8,128)(2,1)} %bitcast.50), calls=%async_computation | async-start | bytes 1048576 | tf_op jit(solution)/shard_map/all_to_all | solution.py:760
  117.1 308.4 %all-gather.6.cloned.1.call-start = ((), (), s32[]{:S(2)}) async-start(), calls=%async_computation.6 | async-start | bytes 5242880 | tf_op jit(solution)/shard_map/all_gather | solution.py:874
  119.1 23.4 %collective-permute-start.17 = (bf16[4,128,1024]{2,1,0:T(8,128)(2,1)S(1)}, bf16[4,128,1024]{2,1,0:T(8,128)(2,1)}, u32[]{:S(2)}, u32[]{:S(2)}) collective-permute-start(bf16[4,128,1024]{2,1,0:T(8,128)(2,1)S(1)} %bitcast.52), channel_id=1, source_target_pairs={{0,1},{1,0},{2,3},{3,2},{4,5},{5,4},{6,7},{7,6},{8,9},{9,8},{10,11... | collective-permute-start | bytes 3145736 | tf_op jit(solution)/shard_map/ppermute | solution.py:122
  119.5 23.0 %collective-permute-start.18 = (bf16[4,128,1024]{2,1,0:T(8,128)(2,1)}, bf16[4,128,1024]{2,1,0:T(8,128)(2,1)}, u32[]{:S(2)}, u32[]{:S(2)}) collective-permute-start(bf16[4,128,1024]{2,1,0:T(8,128)(2,1)} %collective-permute-done.16), channel_id=1, source_target_pairs={{0,1},{1,0},{2,3},{3,2},{4,5},{5,4},{6,7},{7,6},{8,9},{9,8},{10,11... | collective-permute-start | bytes 3145736 | tf_op jit(solution)/shard_map/ppermute | solution.py:122
  132.8 26.4 %collective-permute-start.19 = (bf16[256,1152]{1,0:T(8,128)(2,1)}, bf16[256,1152]{1,0:T(8,128)(2,1)}, u32[]{:S(2)}, u32[]{:S(2)}) collective-permute-start(bf16[256,1152]{1,0:T(8,128)(2,1)} %get-tuple-element.117.refs_1_.refs_4_), channel_id=1, source_target_pairs={{0,8},{8,16},{16,24},{24,28},{28,20},{20,12},{12,4},{4,0},{1,9},{9... | collective-permute-start | bytes 1769480 | tf_op jit(solution)/shard_map/ppermute | solution.py:87
  138.2 21.0 %collective-permute-start.20 = (bf16[256,1152]{1,0:T(8,128)(2,1)S(1)}, bf16[256,1152]{1,0:T(8,128)(2,1)}, u32[]{:S(2)}, u32[]{:S(2)}) collective-permute-start(bf16[256,1152]{1,0:T(8,128)(2,1)S(1)} %copy-done.48), channel_id=1, source_target_pairs={{0,4},{8,0},{16,8},{24,16},{28,24},{20,28},{12,20},{4,12},{1,5},{9... | collective-permute-start | bytes 1769480 | tf_op jit(solution)/shard_map/ppermute | solution.py:90
  184.1 270.7 %reduce-scatter.2.cloned.1.call-start = ((), (), s32[]{:S(2)}) async-start(), calls=%async_computation.5 | async-start | bytes 4718592 | tf_op jit(solution)/shard_map/reduce_scatter | solution.py:826
  184.1 14.6 %collective-permute-start.21 = (bf16[256,1152]{1,0:T(8,128)(2,1)}, bf16[256,1152]{1,0:T(8,128)(2,1)S(1)}, u32[]{:S(2)}, u32[]{:S(2)}) collective-permute-start(bf16[256,1152]{1,0:T(8,128)(2,1)} %collective-permute-done.19.refs_1_.refs_2_), channel_id=1, source_target_pairs={{0,8},{8,16},{16,24},{24,28},{28,20},{20,12},{12,4},{4,0},{1,9},{9... | collective-permute-start | bytes 1769480 | tf_op jit(solution)/shard_map/ppermute | solution.py:87
  185.8 16.4 %collective-permute-start.22 = (bf16[256,1152]{1,0:T(8,128)(2,1)}, bf16[256,1152]{1,0:T(8,128)(2,1)S(1)}, u32[]{:S(2)}, u32[]{:S(2)}) collective-permute-start(bf16[256,1152]{1,0:T(8,128)(2,1)} %collective-permute-done.20.refs_2_.refs_3_), channel_id=1, source_target_pairs={{0,4},{8,0},{16,8},{24,16},{28,24},{20,28},{12,20},{4,12},{1,5},{9... | collective-permute-start | bytes 1769480 | tf_op jit(solution)/shard_map/ppermute | solution.py:90
  198.7 13.5 %collective-permute-start.23 = (bf16[256,1152]{1,0:T(8,128)(2,1)S(1)}, bf16[256,1152]{1,0:T(8,128)(2,1)S(1)}, u32[]{:S(2)}, u32[]{:S(2)}) collective-permute-start(bf16[256,1152]{1,0:T(8,128)(2,1)S(1)} %collective-permute-done.21.refs_1_.refs_4_), channel_id=1, source_target_pairs={{0,8},{8,16},{16,24},{24,28},{28,20},{20,12},{12,4},{4,0},{1,9},{9... | collective-permute-start | bytes 1769480 | tf_op jit(solution)/shard_map/ppermute | solution.py:87
  202.2 34.1 %collective-permute-start.25 = (bf16[256,1152]{1,0:T(8,128)(2,1)S(1)}, bf16[256,1152]{1,0:T(8,128)(2,1)S(1)}, u32[]{:S(2)}, u32[]{:S(2)}) collective-permute-start(bf16[256,1152]{1,0:T(8,128)(2,1)S(1)} %collective-permute-done.22.refs_2_.refs_5_), channel_id=1, source_target_pairs={{0,4},{8,0},{16,8},{24,16},{28,24},{20,28},{12,20},{4,12},{1,5},{9... | collective-permute-start | bytes 1769480 | tf_op jit(solution)/shard_map/ppermute | solution.py:90
  212.2 24.1 %collective-permute-start.24 = (bf16[256,1152]{1,0:T(8,128)(2,1)S(1)}, bf16[256,1152]{1,0:T(8,128)(2,1)S(1)}, u32[]{:S(2)}, u32[]{:S(2)}) collective-permute-start(bf16[256,1152]{1,0:T(8,128)(2,1)S(1)} %collective-permute-done.23.refs_1_.refs_8_), channel_id=1, source_target_pairs={{0,8},{8,16},{16,24},{24,28},{28,20},{20,12},{12,4},{4,0},{1,9},{9... | collective-permute-start | bytes 1769480 | tf_op jit(solution)/shard_map/ppermute | solution.py:87
  259.4 15.4 %collective-permute-start.26 = (bf16[256,1152]{1,0:T(8,128)(2,1)}, bf16[256,1152]{1,0:T(8,128)(2,1)S(1)}, u32[]{:S(2)}, u32[]{:S(2)}) collective-permute-start(bf16[256,1152]{1,0:T(8,128)(2,1)} %get-tuple-element.130), channel_id=1, source_target_pairs={{0,4},{8,0},{16,8},{24,16},{28,24},{20,28},{12,20},{4,12},{1,5},{9... | collective-permute-start | bytes 1769480 | tf_op jit(solution)/shard_map/ppermute | solution.py:106
  259.9 15.0 %collective-permute-start.27 = (bf16[256,1152]{1,0:T(8,128)(2,1)}, bf16[256,1152]{1,0:T(8,128)(2,1)S(1)}, u32[]{:S(2)}, u32[]{:S(2)}) collective-permute-start(bf16[256,1152]{1,0:T(8,128)(2,1)} %get-tuple-element.132), channel_id=1, source_target_pairs={{0,8},{8,16},{16,24},{24,28},{28,20},{20,12},{12,4},{4,0},{1,9},{9... | collective-permute-start | bytes 1769480 | tf_op jit(solution)/shard_map/ppermute | solution.py:108
  277.0 17.4 %collective-permute-start.28 = (bf16[256,1152]{1,0:T(8,128)(2,1)}, bf16[256,1152]{1,0:T(8,128)(2,1)S(1)}, u32[]{:S(2)}, u32[]{:S(2)}) collective-permute-start(bf16[256,1152]{1,0:T(8,128)(2,1)} %get-tuple-element.134.refs_14_), channel_id=1, source_target_pairs={{0,4},{8,0},{16,8},{24,16},{28,24},{20,28},{12,20},{4,12},{1,5},{9... | collective-permute-start | bytes 1769480 | tf_op jit(solution)/shard_map/ppermute | solution.py:106
  277.5 17.0 %collective-permute-start.29 = (bf16[256,1152]{1,0:T(8,128)(2,1)}, bf16[256,1152]{1,0:T(8,128)(2,1)S(1)}, u32[]{:S(2)}, u32[]{:S(2)}) collective-permute-start(bf16[256,1152]{1,0:T(8,128)(2,1)} %get-tuple-element.136), channel_id=1, source_target_pairs={{0,8},{8,16},{16,24},{24,28},{28,20},{20,12},{12,4},{4,0},{1,9},{9... | collective-permute-start | bytes 1769480 | tf_op jit(solution)/shard_map/ppermute | solution.py:108
  306.1 22.0 %collective-permute-start.33 = (bf16[256,1152]{1,0:T(8,128)(2,1)S(1)}, bf16[256,1152]{1,0:T(8,128)(2,1)S(1)}, u32[]{:S(2)}, u32[]{:S(2)}) collective-permute-start(bf16[256,1152]{1,0:T(8,128)(2,1)S(1)} %get-tuple-element.144.refs_9_.refs_14_), channel_id=1, source_target_pairs={{0,4},{8,0},{16,8},{24,16},{28,24},{20,28},{12,20},{4,12},{1,5},{9... | collective-permute-start | bytes 1769480 | tf_op jit(solution)/shard_map/ppermute | solution.py:106
  307.2 37.6 %collective-permute-start.35 = (bf16[256,1152]{1,0:T(8,128)(2,1)S(1)}, bf16[256,1152]{1,0:T(8,128)(2,1)S(1)}, u32[]{:S(2)}, u32[]{:S(2)}) collective-permute-start(bf16[256,1152]{1,0:T(8,128)(2,1)S(1)} %copy-done.42), channel_id=1, source_target_pairs={{0,8},{8,16},{16,24},{24,28},{28,20},{20,12},{12,4},{4,0},{1,9},{9... | collective-permute-start | bytes 1769480 | tf_op jit(solution)/shard_map/ppermute | solution.py:108
  329.5 29.6 %collective-permute-start.34 = (bf16[256,1152]{1,0:T(8,128)(2,1)S(1)}, bf16[256,1152]{1,0:T(8,128)(2,1)S(1)}, u32[]{:S(2)}, u32[]{:S(2)}) collective-permute-start(bf16[256,1152]{1,0:T(8,128)(2,1)S(1)} %add_pairs.8.refs_14_), channel_id=1, source_target_pairs={{0,4},{8,0},{16,8},{24,16},{28,24},{20,28},{12,20},{4,12},{1,5},{9... | collective-permute-start | bytes 1769480 | tf_op jit(solution)/shard_map/ppermute | solution.py:106
  365.5 12.0 %collective-permute-start.39 = (bf16[256,1024]{1,0:T(8,128)(2,1)}, bf16[256,1024]{1,0:T(8,128)(2,1)S(1)}, u32[]{:S(2)}, u32[]{:S(2)}) collective-permute-start(bf16[256,1024]{1,0:T(8,128)(2,1)} %get-tuple-element.155.refs_1_), channel_id=1, source_target_pairs={{0,2},{1,3},{2,0},{3,1},{4,6},{5,7},{6,4},{7,5},{8,10},{9,11},{10,... | collective-permute-start | bytes 1572872 | tf_op jit(solution)/shard_map/ppermute | solution.py:119
  365.5 15.0 %all-to-all-start.1 = ((bf16[4,256,256]{2,1,0:T(8,128)(2,1)}), bf16[4,256,256]{2,1,0:T(8,128)(2,1)S(1)}, u32[]{:S(2)}, u32[]{:S(2)}) async-start(bf16[4,256,256]{2,1,0:T(8,128)(2,1)} %get-tuple-element.152), calls=%async_computation.2 | async-start | bytes 1048576 | tf_op jit(solution)/shard_map/all_to_all | solution.py:851
  369.2 45.9 %collective-permute-start.54 = (bf16[4,1024,128]{2,1,0:T(8,128)(2,1)}, bf16[4,1024,128]{2,1,0:T(8,128)(2,1)}, u32[]{:S(2)}, u32[]{:S(2)}) collective-permute-start(bf16[4,1024,128]{2,1,0:T(8,128)(2,1)} %get-tuple-element.190), channel_id=1, source_target_pairs={{0,1},{1,0},{2,3},{3,2},{4,5},{5,4},{6,7},{7,6},{8,9},{9,8},{10,11... | collective-permute-start | bytes 3145736 | tf_op jit(solution)/shard_map/ppermute | solution.py:130
  369.7 62.9 %collective-permute-start.51 = (bf16[4,1024,128]{2,1,0:T(8,128)(2,1)}, bf16[4,1024,128]{2,1,0:T(8,128)(2,1)}, u32[]{:S(2)}, u32[]{:S(2)}) collective-permute-start(bf16[4,1024,128]{2,1,0:T(8,128)(2,1)} %get-tuple-element.187), channel_id=1, source_target_pairs={{0,1},{1,0},{2,3},{3,2},{4,5},{5,4},{6,7},{7,6},{8,9},{9,8},{10,11... | collective-permute-start | bytes 3145736 | tf_op jit(solution)/shard_map/ppermute | solution.py:130
  369.8 33.8 %collective-permute-start.40 = (bf16[256,1024]{1,0:T(8,128)(2,1)}, bf16[256,1024]{1,0:T(8,128)(2,1)S(1)}, u32[]{:S(2)}, u32[]{:S(2)}) collective-permute-start(bf16[256,1024]{1,0:T(8,128)(2,1)} %get-tuple-element.155.refs_1_), channel_id=1, source_target_pairs={{0,1},{1,0},{2,3},{3,2},{4,5},{5,4},{6,7},{7,6},{8,9},{9,8},{10,11... | collective-permute-start | bytes 1572872 | tf_op jit(solution)/shard_map/ppermute | solution.py:122
  377.5 26.0 %collective-permute-start.41 = (bf16[256,1024]{1,0:T(8,128)(2,1)S(1)}, bf16[256,1024]{1,0:T(8,128)(2,1)S(1)}, u32[]{:S(2)}, u32[]{:S(2)}) collective-permute-start(bf16[256,1024]{1,0:T(8,128)(2,1)S(1)} %collective-permute-done.39.refs_2_), channel_id=1, source_target_pairs={{0,1},{1,0},{2,3},{3,2},{4,5},{5,4},{6,7},{7,6},{8,9},{9,8},{10,11... | collective-permute-start | bytes 1572872 | tf_op jit(solution)/shard_map/ppermute | solution.py:122
  400.0 25.4 %all-to-all-start.2 = ((bf16[4,256,512]{2,1,0:T(8,128)(2,1)}), bf16[4,256,512]{2,1,0:T(8,128)(2,1)S(1)}, u32[]{:S(2)}, u32[]{:S(2)}) async-start(bf16[4,256,512]{2,1,0:T(8,128)(2,1)} %bitcast.58), calls=%async_computation.3 | async-start | bytes 2097152 | tf_op jit(solution)/shard_map/all_to_all | solution.py:863
  412.3 22.8 %collective-permute-start.56 = (bf16[4,1024,128]{2,1,0:T(8,128)(2,1)}, bf16[4,1024,128]{2,1,0:T(8,128)(2,1)S(1)}, u32[]{:S(2)}, u32[]{:S(2)}) collective-permute-start(bf16[4,1024,128]{2,1,0:T(8,128)(2,1)} %get-tuple-element.191), channel_id=1, source_target_pairs={{0,1},{1,0},{2,3},{3,2},{4,5},{5,4},{6,7},{7,6},{8,9},{9,8},{10,11... | collective-permute-start | bytes 3145736 | tf_op jit(solution)/shard_map/ppermute | solution.py:130
  412.4 22.8 %collective-permute-start.57 = (bf16[4,128,1024]{2,1,0:T(8,128)(2,1)}, bf16[4,128,1024]{2,1,0:T(8,128)(2,1)}, u32[]{:S(2)}, u32[]{:S(2)}) collective-permute-start(bf16[4,128,1024]{2,1,0:T(8,128)(2,1)} %get-tuple-element.196), channel_id=1, source_target_pairs={{0,1},{1,0},{2,3},{3,2},{4,5},{5,4},{6,7},{7,6},{8,9},{9,8},{10,11... | collective-permute-start | bytes 3145736 | tf_op jit(solution)/shard_map/ppermute | solution.py:130
  413.7 32.6 %collective-permute-start.53 = (bf16[4,1024,128]{2,1,0:T(8,128)(2,1)}, bf16[4,1024,128]{2,1,0:T(8,128)(2,1)}, u32[]{:S(2)}, u32[]{:S(2)}) collective-permute-start(bf16[4,1024,128]{2,1,0:T(8,128)(2,1)} %get-tuple-element.188), channel_id=1, source_target_pairs={{0,1},{1,0},{2,3},{3,2},{4,5},{5,4},{6,7},{7,6},{8,9},{9,8},{10,11... | collective-permute-start | bytes 3145736 | tf_op jit(solution)/shard_map/ppermute | solution.py:130
  415.1 8.6 %collective-permute-start.43 = (bf16[1024,128]{1,0:T(8,128)(2,1)S(1)}, bf16[1024,128]{1,0:T(8,128)(2,1)S(1)}, u32[]{:S(2)}, u32[]{:S(2)}) collective-permute-start(bf16[1024,128]{1,0:T(8,128)(2,1)S(1)} %add.265), channel_id=1, source_target_pairs={{0,2},{1,3},{2,0},{3,1},{4,6},{5,7},{6,4},{7,5},{8,10},{9,11},{10,... | collective-permute-start | bytes 786440 | tf_op jit(solution)/shard_map/ppermute | solution.py:142
  423.6 26.4 %collective-permute-start.55 = (bf16[4,1024,128]{2,1,0:T(8,128)(2,1)}, bf16[4,1024,128]{2,1,0:T(8,128)(2,1)}, u32[]{:S(2)}, u32[]{:S(2)}) collective-permute-start(bf16[4,1024,128]{2,1,0:T(8,128)(2,1)} %add_convert_fusion.1), channel_id=1, source_target_pairs={{0,2},{1,3},{2,0},{3,1},{4,6},{5,7},{6,4},{7,5},{8,10},{9,11},{10,... | collective-permute-start | bytes 3145736 | tf_op jit(solution)/shard_map/ppermute | solution.py:135
  432.6 6.8 %collective-permute-start.44 = (bf16[128,896]{1,0:T(8,128)(2,1)S(1)}, bf16[128,896]{1,0:T(8,128)(2,1)S(1)}, u32[]{:S(2)}, u32[]{:S(2)}) collective-permute-start(bf16[128,896]{1,0:T(8,128)(2,1)S(1)} %get-tuple-element.160), channel_id=1, source_target_pairs={{0,4},{8,0},{16,8},{24,16},{28,24},{20,28},{12,20},{4,12},{1,5},{9... | collective-permute-start | bytes 688136 | tf_op jit(solution)/shard_map/ppermute | solution.py:106
  435.1 26.6 %collective-permute-start.59 = (bf16[4,128,1024]{2,1,0:T(8,128)(2,1)}, bf16[4,128,1024]{2,1,0:T(8,128)(2,1)}, u32[]{:S(2)}, u32[]{:S(2)}) collective-permute-start(bf16[4,128,1024]{2,1,0:T(8,128)(2,1)} %get-tuple-element.197), channel_id=1, source_target_pairs={{0,1},{1,0},{2,3},{3,2},{4,5},{5,4},{6,7},{7,6},{8,9},{9,8},{10,11... | collective-permute-start | bytes 3145736 | tf_op jit(solution)/shard_map/ppermute | solution.py:130
  435.2 37.3 %collective-permute-start.52 = (bf16[4,1024,128]{2,1,0:T(8,128)(2,1)}, bf16[4,1024,128]{2,1,0:T(8,128)(2,1)}, u32[]{:S(2)}, u32[]{:S(2)}) collective-permute-start(bf16[4,1024,128]{2,1,0:T(8,128)(2,1)} %add_convert_fusion.2), channel_id=1, source_target_pairs={{0,2},{1,3},{2,0},{3,1},{4,6},{5,7},{6,4},{7,5},{8,10},{9,11},{10,... | collective-permute-start | bytes 3145736 | tf_op jit(solution)/shard_map/ppermute | solution.py:135
  439.4 6.0 %collective-permute-start.45 = (bf16[128,896]{1,0:T(8,128)(2,1)S(1)}, bf16[128,896]{1,0:T(8,128)(2,1)S(1)}, u32[]{:S(2)}, u32[]{:S(2)}) collective-permute-start(bf16[128,896]{1,0:T(8,128)(2,1)S(1)} %get-tuple-element.162), channel_id=1, source_target_pairs={{0,8},{8,16},{16,24},{24,28},{28,20},{20,12},{12,4},{4,0},{1,9},{9... | collective-permute-start | bytes 688136 | tf_op jit(solution)/shard_map/ppermute | solution.py:108
  445.4 60.7 %collective-permute-start.58 = (bf16[4,128,1024]{2,1,0:T(8,128)(2,1)}, bf16[4,128,1024]{2,1,0:T(8,128)(2,1)}, u32[]{:S(2)}, u32[]{:S(2)}) collective-permute-start(bf16[4,128,1024]{2,1,0:T(8,128)(2,1)} %add_convert_fusion), channel_id=1, source_target_pairs={{0,2},{1,3},{2,0},{3,1},{4,6},{5,7},{6,4},{7,5},{8,10},{9,11},{10,... | collective-permute-start | bytes 3145736 | tf_op jit(solution)/shard_map/ppermute | solution.py:135
  446.3 8.1 %collective-permute-start.46 = (bf16[128,896]{1,0:T(8,128)(2,1)S(1)}, bf16[128,896]{1,0:T(8,128)(2,1)S(1)}, u32[]{:S(2)}, u32[]{:S(2)}) collective-permute-start(bf16[128,896]{1,0:T(8,128)(2,1)S(1)} %get-tuple-element.164), channel_id=1, source_target_pairs={{0,4},{8,0},{16,8},{24,16},{28,24},{20,28},{12,20},{4,12},{1,5},{9... | collective-permute-start | bytes 688136 | tf_op jit(solution)/shard_map/ppermute | solution.py:106
  450.0 56.1 %collective-permute-start.36 = (bf16[256,1024]{1,0:T(8,128)(2,1)}, bf16[256,1024]{1,0:T(8,128)(2,1)S(1)}, u32[]{:S(2)}, u32[]{:S(2)}) collective-permute-start(bf16[256,1024]{1,0:T(8,128)(2,1)} %input_gradient.1.refs_1_.refs_0_), channel_id=1, source_target_pairs={{0,2},{1,3},{2,0},{3,1},{4,6},{5,7},{6,4},{7,5},{8,10},{9,11},{10,... | collective-permute-start | bytes 1572872 | tf_op jit(solution)/shard_map/ppermute | solution.py:119
  454.4 6.9 %collective-permute-start.47 = (bf16[128,896]{1,0:T(8,128)(2,1)S(1)}, bf16[128,896]{1,0:T(8,128)(2,1)S(1)}, u32[]{:S(2)}, u32[]{:S(2)}) collective-permute-start(bf16[128,896]{1,0:T(8,128)(2,1)S(1)} %get-tuple-element.166), channel_id=1, source_target_pairs={{0,8},{8,16},{16,24},{24,28},{28,20},{20,12},{12,4},{4,0},{1,9},{9... | collective-permute-start | bytes 688136 | tf_op jit(solution)/shard_map/ppermute | solution.py:108
  461.3 54.5 %collective-permute-start.30 = (bf16[256,1024]{1,0:T(8,128)(2,1)S(1)}, bf16[256,1024]{1,0:T(8,128)(2,1)S(1)}, u32[]{:S(2)}, u32[]{:S(2)}) collective-permute-start(bf16[256,1024]{1,0:T(8,128)(2,1)S(1)} %add_convert_fusion.3.refs_1_), channel_id=1, source_target_pairs={{0,2},{1,3},{2,0},{3,1},{4,6},{5,7},{6,4},{7,5},{8,10},{9,11},{10,... | collective-permute-start | bytes 1572872 | tf_op jit(solution)/shard_map/ppermute | solution.py:119
  461.7 54.2 %collective-permute-start.48 = (bf16[128,896]{1,0:T(8,128)(2,1)S(1)}, bf16[128,896]{1,0:T(8,128)(2,1)S(1)}, u32[]{:S(2)}, u32[]{:S(2)}) collective-permute-start(bf16[128,896]{1,0:T(8,128)(2,1)S(1)} %get-tuple-element.168), channel_id=1, source_target_pairs={{0,4},{8,0},{16,8},{24,16},{28,24},{20,28},{12,20},{4,12},{1,5},{9... | collective-permute-start | bytes 688136 | tf_op jit(solution)/shard_map/ppermute | solution.py:106
  472.5 83.1 %collective-permute-start.37 = (bf16[256,1024]{1,0:T(8,128)(2,1)}, bf16[256,1024]{1,0:T(8,128)(2,1)S(1)}, u32[]{:S(2)}, u32[]{:S(2)}) collective-permute-start(bf16[256,1024]{1,0:T(8,128)(2,1)} %input_gradient.1.refs_1_.refs_0_), channel_id=1, source_target_pairs={{0,1},{1,0},{2,3},{3,2},{4,5},{5,4},{6,7},{7,6},{8,9},{9,8},{10,11... | collective-permute-start | bytes 1572872 | tf_op jit(solution)/shard_map/ppermute | solution.py:122
  506.1 49.5 %collective-permute-start.38 = (bf16[256,1024]{1,0:T(8,128)(2,1)S(1)}, bf16[256,1024]{1,0:T(8,128)(2,1)S(1)}, u32[]{:S(2)}, u32[]{:S(2)}) collective-permute-start(bf16[256,1024]{1,0:T(8,128)(2,1)S(1)} %collective-permute-done.36.refs_2_), channel_id=1, source_target_pairs={{0,1},{1,0},{2,3},{3,2},{4,5},{5,4},{6,7},{7,6},{8,9},{9,8},{10,11... | collective-permute-start | bytes 1572872 | tf_op jit(solution)/shard_map/ppermute | solution.py:122
  506.1 52.0 %collective-permute-start.31 = (bf16[256,1024]{1,0:T(8,128)(2,1)S(1)}, bf16[256,1024]{1,0:T(8,128)(2,1)S(1)}, u32[]{:S(2)}, u32[]{:S(2)}) collective-permute-start(bf16[256,1024]{1,0:T(8,128)(2,1)S(1)} %add_convert_fusion.3.refs_1_), channel_id=1, source_target_pairs={{0,1},{1,0},{2,3},{3,2},{4,5},{5,4},{6,7},{7,6},{8,9},{9,8},{10,11... | collective-permute-start | bytes 1572872 | tf_op jit(solution)/shard_map/ppermute | solution.py:122
  515.9 42.3 %collective-permute-start.32 = (bf16[256,1024]{1,0:T(8,128)(2,1)S(1)}, bf16[256,1024]{1,0:T(8,128)(2,1)}, u32[]{:S(2)}, u32[]{:S(2)}) collective-permute-start(bf16[256,1024]{1,0:T(8,128)(2,1)S(1)} %collective-permute-done.30.refs_2_), channel_id=1, source_target_pairs={{0,1},{1,0},{2,3},{3,2},{4,5},{5,4},{6,7},{7,6},{8,9},{9,8},{10,11... | collective-permute-start | bytes 1572872 | tf_op jit(solution)/shard_map/ppermute | solution.py:122
  515.9 8.0 %collective-permute-start.50 = (bf16[128,896]{1,0:T(8,128)(2,1)S(1)}, bf16[128,896]{1,0:T(8,128)(2,1)S(1)}, u32[]{:S(2)}, u32[]{:S(2)}) collective-permute-start(bf16[128,896]{1,0:T(8,128)(2,1)S(1)} %get-tuple-element.170), channel_id=1, source_target_pairs={{0,8},{8,16},{16,24},{24,28},{28,20},{20,12},{12,4},{4,0},{1,9},{9... | collective-permute-start | bytes 688136 | tf_op jit(solution)/shard_map/ppermute | solution.py:108
  524.6 22.9 %collective-permute-start.49 = (bf16[128,896]{1,0:T(8,128)(2,1)}, bf16[128,896]{1,0:T(8,128)(2,1)S(1)}, u32[]{:S(2)}, u32[]{:S(2)}) collective-permute-start(bf16[128,896]{1,0:T(8,128)(2,1)} %add_pairs.11), channel_id=1, source_target_pairs={{0,4},{8,0},{16,8},{24,16},{28,24},{20,28},{12,20},{4,12},{1,5},{9... | collective-permute-start | bytes 688136 | tf_op jit(solution)/shard_map/ppermute | solution.py:106
  (65 other events, 812.0 us)
Sparse Core Ops, SparseCore 0:
  29.1 83.1 all-gather.3
  184.2 34.6 all-gather.5
  306.2 102.0 reduce-scatter.1

commit v4 on v3

--- a/solution.py
+++ b/solution.py
@@ -123,17 +123,20 @@
     return own + other
 
 
-def tensor_reduce(parts, size):
+def core_sums(parts, size):
     chips = size // 2
-    result = []
-    for step in reversed(range(chips)):
-        came = lax.ppermute(parts[chips + step], "tensor", tensor_perm(size, 0, 1))
-        if step == 0:
-            result += [parts[0], came]
-        else:
-            total = (parts[step].astype(F32) + came.astype(F32)).astype(BF)
-            result.append(lax.ppermute(total, "tensor", tensor_perm(size, step, 0)))
-    return result
+    came = [lax.ppermute(part, "tensor", tensor_perm(size, 0, 1)) for part in parts[chips:]]
+    return [parts[0], came[0]] + [
+        (part.astype(F32) + other.astype(F32)).astype(BF)
+        for part, other in zip(parts[1:chips], came[1:])
+    ]
+
+
+def chip_sums(sums, size):
+    return sums[:2] + [
+        lax.ppermute(total, "tensor", tensor_perm(size, step + 1, 0))
+        for step, total in enumerate(sums[2:])
+    ]
 
 
 def tensor_sum(values, size):
@@ -175,6 +178,34 @@
     return out if len(cuts) > 1 else out[0]
 
 
+def place_far_kernel(blocks, *refs):
+    index_ref, out_ref, sems = refs[0], refs[-2], refs[-1]
+    copies = []
+    for block in range(blocks):
+        size = refs[1 + block].shape[0]
+        start = pl.multiple_of(index_ref[block] * size, size)
+        copies.append(
+            pltpu.make_async_copy(refs[1 + block], out_ref.at[pl.ds(start, size)], sems.at[block])
+        )
+        copies[-1].start()
+    for copy in copies:
+        copy.wait()
+
+
+def place_far(blocks, index, after=()):
+    size, columns = blocks[0].shape
+    count = len(blocks)
+    return pl.pallas_call(
+        functools.partial(place_far_kernel, count),
+        in_specs=[pl.BlockSpec(memory_space=pltpu.SMEM)]
+        + [pl.BlockSpec(memory_space=pl.ANY)] * (count + len(after)),
+        out_specs=pl.BlockSpec(memory_space=pl.ANY),
+        out_shape=jax.ShapeDtypeStruct((count * size, columns), blocks[0].dtype),
+        scratch_shapes=[pltpu.SemaphoreType.DMA((count,))],
+        name="place_far",
+    )(index, *blocks, *after)
+
+
 def hold(array, after):
     flat = array.reshape(-1, array.shape[-1])
     return place([flat], jnp.zeros((1,), jnp.int32), after=after).reshape(array.shape)
@@ -257,31 +288,28 @@
     up_w = up_ref[0]
     down_w = down_ref[0]
     column = first_ref[0] + expert
-    for i in range(count):
-        part = slice(i * rows, (i + 1) * rows)
-        b = rows_ref[part, :width]
-        dy = dy_ref[part]
-        gate_pre = dot(b, gate_w, ((1,), (0,)))
-        up_pre = dot(b, up_w, ((1,), (0,)))
-        sig = jax.nn.sigmoid(gate_pre)
-        silu = gate_pre * sig
-        act = (silu * up_pre).astype(BF).astype(F32)
-        grad_act = dot(dy, down_w, ((1,), (1,)))
-        grad_gating = jnp.sum(act * grad_act, axis=1, keepdims=True)
-        lane = lax.broadcasted_iota(jnp.int32, (rows, PAD), 1)
-        chosen = (lane == column) | (lane == column + EXPERTS)
-        tail = rows_ref[part, width:].astype(F32)
-        gating = jnp.sum(jnp.where(chosen, tail, 0.0), axis=1, keepdims=True)
-        tail_acc[part] += jnp.where(chosen, grad_gating, 0.0)
-        grad_act = grad_act * gating
-        grad_gate = (grad_act * up_pre * (sig * (1.0 + gate_pre * (1.0 - sig)))).astype(BF)
-        grad_up = (grad_act * silu).astype(BF)
-        scaled = (act * gating).astype(BF)
-        grads_ref[0, 0, part] = grad_gate
-        grads_ref[1, 0, part] = grad_up
-        scaled_ref[0, part] = scaled
-        back_acc[part] += dot(grad_gate, gate_w, ((1,), (1,))) + dot(grad_up, up_w, ((1,), (1,)))
-        y_acc[part] += dot(scaled, down_w, ((1,), (0,)))
+    b = rows_ref[:, :width]
+    gate_pre = dot(b, gate_w, ((1,), (0,)))
+    up_pre = dot(b, up_w, ((1,), (0,)))
+    grad_act = dot(dy_ref[...], down_w, ((1,), (1,)))
+    sig = 0.5 * jnp.tanh(0.5 * gate_pre) + 0.5
+    silu = gate_pre * sig
+    act = (silu * up_pre).astype(BF).astype(F32)
+    grad_gating = jnp.sum(act * grad_act, axis=1, keepdims=True)
+    lane = lax.broadcasted_iota(jnp.int32, (count * rows, PAD), 1)
+    chosen = (lane == column) | (lane == column + EXPERTS)
+    tail = rows_ref[:, width:].astype(F32)
+    gating = jnp.sum(jnp.where(chosen, tail, 0.0), axis=1, keepdims=True)
+    tail_acc[...] += jnp.where(chosen, grad_gating, 0.0)
+    grad_act = grad_act * gating
+    grad_gate = (grad_act * up_pre * (sig + silu * (1.0 - sig))).astype(BF)
+    grad_up = (grad_act * silu).astype(BF)
+    scaled = (act * gating).astype(BF)
+    grads_ref[0, 0] = grad_gate
+    grads_ref[1, 0] = grad_up
+    scaled_ref[0] = scaled
+    back_acc[...] += dot(grad_gate, gate_w, ((1,), (1,))) + dot(grad_up, up_w, ((1,), (1,)))
+    y_acc[...] += dot(scaled, down_w, ((1,), (0,)))
 
     @pl.when(expert == pl.num_programs(0) - 1)
     def _():
@@ -495,7 +523,7 @@
             scratch_shapes=list(scratch),
         ),
         out_shape=out_shape,
-        compiler_params=pltpu.CompilerParams(vmem_limit_bytes=56 * 1024 * 1024),
+        compiler_params=pltpu.CompilerParams(vmem_limit_bytes=60 * 1024 * 1024),
         cost_estimate=pl.CostEstimate(flops=cost, bytes_accessed=1 << 22, transcendentals=0),
         name=name,
     )(scalars, *operands)
@@ -556,7 +584,9 @@
             ).astype(BF)
 
 
-def attention_back_kernel(q_cols, k_cols, s_ref, rot_ref, grad_ref, cos_ref, sin_ref, out_ref, acc_ref):
+def attention_back_kernel(
+    q_cols, k_cols, s_ref, rot_ref, grad_ref, cos_ref, sin_ref, after_ref, out_ref, acc_ref
+):
     length = rot_ref.shape[0]
     step = min(256, length)
     acc_ref[...] = jnp.zeros_like(acc_ref)
@@ -703,8 +733,10 @@
     own_block = pl.BlockSpec((rows, width), lambda g, s: (s[0], 0))
     chips = tensors // 2
 
-    gate_pieces = tensor_gather(gateup_weight[:, 0].astype(BF), tensors)
-    up_pieces = tensor_gather(gateup_weight[:, 1].astype(BF), tensors)
+    gate_bf = gateup_weight[:, 0].astype(BF)
+    up_bf = gateup_weight[:, 1].astype(BF)
+    gate_pieces = tensor_gather(gate_bf, tensors)
+    up_pieces = tensor_gather(up_bf, tensors)
     gate_low = jnp.concatenate(gate_pieces, axis=2)
     up_low = jnp.concatenate(up_pieces, axis=2)
 
@@ -724,7 +756,7 @@
         + [jnp.zeros((query_weight.shape[0], PAD - EXPERTS - 6), BF)],
         axis=1,
     )
-    packed_blocks = ring_gather(packed, ring)
+    packed_blocks = ring_gather(hold(packed, [gate_bf, up_bf]), ring)
     offsets = sorted(packed_blocks)
     cosine_table, sine_table = rope_tables(length, HD)
     cosine_table = jnp.concatenate([cosine_table] * 4, axis=1)
@@ -747,7 +779,7 @@
     ).T
     dy_own = lax.dynamic_slice_in_dim(cotangent, lane_t[0] * rows, rows, axis=0)
     dy_all = lax.all_gather(
-        hold(dy_own, [packed_blocks[-(ring // 4)]]), "expert", axis=0, tiled=True
+        hold(dy_own, [packed_blocks[1 - ring // 2]]), "expert", axis=0, tiled=True
     )
     a, rotated, mixture = call_whole(
         functools.partial(front_kernel, q_cols, k_cols),
@@ -763,7 +795,7 @@
     owners_t = tensor_index(tensors)
     out_pieces = tensor_gather(out_low, tensors, after=[mixture])
     out_all = place(out_pieces, owners_t, after=[mixture_rows]).reshape(tensors, width, o_cols)
-    down_pieces = tensor_gather(hold(down_bf, out_pieces[1:chips]), tensors)
+    down_pieces = tensor_gather(hold(down_bf, [mixture]), tensors)
     down_low = jnp.concatenate(down_pieces, axis=1)
     message, x_mid = call_whole(
         middle_kernel,
@@ -785,8 +817,10 @@
     scaled = []
     order = []
     spots = []
-    after = []
     for number, call in enumerate(calls):
+        hop = min(number + 1, half)
+        after = [blocks[o] for o in (-hop, hop) if o in blocks and o not in call]
+        after += scaled[-1:]
         owners = [ring_index(ring, o).astype(jnp.int32) * min(abs(o), 1) for o in call]
         result = expert_blocks(
             first,
@@ -800,7 +834,6 @@
         )
         grads.append(result[0])
         scaled.append(result[1])
-        after = [result[1]]
         for part, o in enumerate(call):
             forth[o], back[o] = result[2][part], result[3][part]
             order.append(o)
@@ -810,6 +843,7 @@
     whose = jnp.stack([ring_index(ring, o) for o in order]).astype(jnp.int32)
     messages = [blocks[o] for o in order]
     weights = {}
+    totals = {}
 
     def beside(hop, sent):
         kind = max(hop - 1, 0)
@@ -821,14 +855,13 @@
             weights[kind] = weight_grad(
                 messages, still, spots, grads, kind - 1, False, tensors, sent[:1]
             )
-        if hop == 2:
-            sums = place([forth[o] for o in order], whose, after=sent[:1])
-            weights["sum"] = lax.psum_scatter(sums, "expert", scatter_dimension=0, tiled=True)
-        return [weights[kind][0]]
+        early = [totals[done][-1] for done in totals]
+        totals[kind] = core_sums(weights[kind], tensors)
+        return [weights[kind][0]] + early
 
     returned, after = ring_reduce(lambda offset: back[offset], ring, beside)
-    up_grads, gate_grads, down_grads = weights[2], weights[1], weights[0]
-    moe_sum = weights["sum"]
+    sums = place_far([forth[o] for o in order], whose, after=[returned[1]])
+    moe_sum = lax.psum_scatter(sums, "expert", scatter_dimension=0, tiled=True)
     block_out = place(tensor_gather((x_mid + moe_sum.astype(F32)).astype(BF), tensors), owners_t)
 
     grad_mid, grad_attention, grad_mixture, tail = call_whole(
@@ -844,7 +877,9 @@
         scalars=lane_t,
         specs={
             len(returned) + 2: own_block,
-            len(returned) + 6: pl.BlockSpec(memory_space=pl.ANY),
+            **{
+                len(returned) + 6 + i: pl.BlockSpec(memory_space=pl.ANY) for i in range(len(after))
+            },
         },
         cost=10**9,
     )
@@ -855,8 +890,9 @@
     (grad_pre,) = call_whole(
         functools.partial(attention_back_kernel, q_cols, k_cols),
         [shape((length, heads_cols), BF)],
-        [rotated, grad_mixture, cosine_table, sine_table],
+        [rotated, grad_mixture, cosine_table, sine_table, totals[0][-1]],
         "attention_backward",
+        specs={4: pl.BlockSpec(memory_space=pl.ANY)},
         scratch=[pltpu.VMEM((length, heads_cols), F32)],
         cost=2 * 10**10,
     )
@@ -907,7 +943,7 @@
         gateup_weight,
         gateup_moment,
         gateup_second,
-        [tensor_reduce(gate_grads, tensors), tensor_reduce(up_grads, tensors)],
+        [chip_sums(totals[1], tensors), chip_sums(totals[2], tensors)],
     )
     new_down = [
         array[:, 0]
@@ -915,7 +951,7 @@
             down_weight[:, None],
             down_moment[:, None],
             down_second[:, None],
-            [tensor_reduce(down_grads, tensors)],
+            [chip_sums(totals[0], tensors)],
         )
     ]
     return (block_out, input_grad) + tuple(new_rest) + tuple(new_gateup) + tuple(new_down)

time: 574 us -> 739 us (1.29)
  Pallas kernels: 227 us -> 355 us
  waiting for transfers between devices: 184 us -> 202 us
  starting transfers between devices: 59.4 us -> 76.1 us
    pallas_call x0 -> x1, Pallas kernels: none -> 129 us  [place_far(): pl.pallas_call(functools.partial(place_far_kernel, count), in_specs=[pl.B...]
    ppermute x1, waiting for transfers between devices: 4.36 us -> 26.6 us  [tensor_sum(): lax.ppermute(values, 'tensor', tensor_perm(size, step, 0))]
    ppermute x6, waiting for transfers between devices: 15.8 us -> 31.8 us  [ring_reduce(): up = lax.ppermute(messages[1], 'expert', ring_perm(size, 1))]
    ppermute x8, waiting for transfers between devices: 31.6 us -> 18 us  [ring_gather(): ahead = lax.ppermute(ahead, 'expert', ring_perm(size, 1))]
    ppermute x6, starting transfers between devices: 5.22 us -> 15.1 us  [ring_reduce(): up = lax.ppermute(messages[1], 'expert', ring_perm(size, 1))]
    unnamed x135 -> x149, local copies, waits for them, and re-layouts: 40 us -> 44.2 us
  transfers between devices with their start and end apart: 66 -> 66, of which waited for: 25 -> 22; matrix products, arithmetic and copies ran while one was open for 8% -> 6% of each run, Pallas kernels for 35% -> 48%
where the time goes in v4:
time: 739 us; the launch traced here: 733 us
  Pallas kernels  355 us (48%)
  waiting for transfers between devices  202 us (27%)
  starting transfers between devices  76.1 us (10%)
  local copies, waits for them, and re-layouts  50.1 us (7%)
  other arithmetic  34 us (5%)
  between operations  15.1 us (2%)
    pallas_call x1, Pallas kernels, place_far(): pl.pallas_call(functools.partial(place_far_kernel, count), in_specs=[pl.B...  129 us
    pallas_call x5, Pallas kernels, expert_blocks(): pl.pallas_call(functools.partial(expert_kernel, count, len(after)), grid_...  89.9 us
    ppermute x7, waiting for transfers between devices, tensor_gather(): lax.ppermute(shard, 'tensor', tensor_perm(size, -step, 0))  69.9 us
    pallas_call x7, Pallas kernels, call_whole(): pl.pallas_call(kernel, grid_spec=pltpu.PrefetchScalarGridSpec(num_scalar_...  56.2 us
    unnamed x149, local copies, waits for them, and re-layouts  44.2 us
    pallas_call x3, Pallas kernels, weight_grad(): pl.pallas_call(functools.partial(weight_grad_kernel, spots, swap, shards,...  43.8 us
    ppermute x6, waiting for transfers between devices, ring_reduce(): up = lax.ppermute(messages[1], 'expert', ring_perm(size, 1))  31.8 us
    ppermute x1, waiting for transfers between devices, tensor_sum(): lax.ppermute(values, 'tensor', tensor_perm(size, step, 0))  26.6 us
  transfers between devices with their start and end apart: 66, of which 22 were waited for; matrix products, arithmetic and copies ran while one was open for 6% of the time, Pallas kernels for 48%

profile of v4, /device:TPU:0, one launch (start us, length us, event | category | flops | bytes accessed | tf_op | source)
XLA Modules:
  0.0 732.5 jit_solution(8674902803882472149)
XLA Ops:
  11.8 2.6 slice_bitcast_fusion
  14.5 3.1 collective-permute-start
  17.6 5.5 collective-permute-done.refs_4_
  23.1 1.8 collective-permute-start.1
  25.6 4.3 collective-permute-done.1.refs_3_
  32.5 3.5 collective-permute-done.2.refs_2_
  41.2 6.1 collective-permute-done.4.refs_6_
  47.3 2.1 collective-permute-start.5
  49.4 16.1 %collective-permute-done.5.refs_7_ = bf16[128,896]{1,0:T(8,128)(2,1)} collective-permute-done((bf16[128,896]{1,0:T(8,128)(2,1)S(1)}, bf16[128,896]{1,0:T(8,128)(2,1)}, u32[]{:S(2)}, u32[]{:S(2)}) %collective-permute-start.5) | collective-permute-done | bytes 229408 | tf_op jit(solution)/shard_map/ppermute | solution.py:90
  65.5 2.0 collective-permute-start.3
  67.5 3.1 fusion.2
  72.7 3.2 pad_maximum_fusion.3
  76.0 6.6 collective-permute-done.8.refs_10_
  94.5 13.2 %attention_forward.1 = (bf16[1024,1024]{1,0:T(8,128)(2,1)}, bf16[1024,512]{1,0:T(8,128)(2,1)}, bf16[1024,256]{1,0:T(8,128)(2,1)}) custom-call(s32[1]{0:T(128)} %constant.336.clone.1.refs_0_.s_ref, bf16[1024,1024]{1,0:T(8,128)(2,1)} %x_ref.5, f32[2,1024]{1,0:T(2,128)} %add_bitcast_fusion.gains_ref.refs_6_, bf16[1024,512]{1,0:T(8,128)(2,1)} %copy-done.20, ...), custom_call_target="tpu_custom_call" | custom-call | flops 10000000000 | bytes 4194304 | tf_op jit(solution)/shard_map/attention_forward/pallas_call | solution.py:510
  111.5 1.9 place.14
  114.7 3.5 all-to-all-start
  120.6 13.3 %collective-permute-done.16 = bf16[4,128,1024]{2,1,0:T(8,128)(2,1)} collective-permute-done((bf16[4,128,1024]{2,1,0:T(8,128)(2,1)}, bf16[4,128,1024]{2,1,0:T(8,128)(2,1)}, u32[]{:S(2)}, u32[]{:S(2)}) %collective-permute-start.16) | collective-permute-done | bytes 1048608 | tf_op jit(solution)/shard_map/ppermute | solution.py:119
  134.5 2.0 all-to-all-done.refs_5_.mix_ref
  140.5 4.2 middle.1
  146.7 3.6 pad_maximum_fusion.refs_3_.refs_5_
  150.3 3.6 pad_maximum_fusion.1.refs_4_.refs_6_
  153.9 4.7 collective-permute-done.19.refs_6_.refs_1_.refs_2_
  160.6 3.7 pad_maximum_fusion.2.refs_5_.refs_7_
  164.3 13.1 %expert_blocks.5 = (bf16[2,4,256,512]{3,2,1,0:T(8,128)(2,1)}, bf16[4,256,512]{2,1,0:T(8,128)(2,1)}, bf16[256,1024]{1,0:T(8,128)(2,1)}, bf16[256,1152]{1,0:T(8,128)(2,1)}) custom-call(s32[2]{0:T(128)} %pad_add_fusion.1.refs_0_, bf16[256,1152]{1,0:T(8,128)(2,1)} %get-tuple-element.117.refs_1_.refs_4_, bf16[256,1024]{1,0:T(8,128)(2,1)} %copy-done.18, ...), custom_call_target="tpu_custom_call" | custom-call | flops 6442450944 | bytes 12582912 | tf_op jit(solution)/shard_map/expert_blocks/pallas_call | solution.py:334
  179.5 21.1 %expert_blocks.6 = (bf16[2,4,512,512]{3,2,1,0:T(8,128)(2,1)}, bf16[4,512,512]{2,1,0:T(8,128)(2,1)}, bf16[256,1024]{1,0:T(8,128)(2,1)}, bf16[256,1024]{1,0:T(8,12...) custom-call(s32[3]{0:T(128)} %pad_add_fusion.2.refs_0_, bf16[256,1152]{1,0:T(8,128)(2,1)} %copy-done.67, ...), custom_call_target="tpu_custom_call" | custom-call | flops 12884901888 | bytes 12582912 | tf_op jit(solution)/shard_map/expert_blocks/pallas_call | solution.py:334
  205.1 2.0 collective-permute-start.25
  207.2 21.4 %expert_blocks.7 = (bf16[2,4,512,512]{3,2,1,0:T(8,128)(2,1)}, bf16[4,512,512]{2,1,0:T(8,128)(2,1)}, bf16[256,1024]{1,0:T(8,128)(2,1)}, bf16[256,1024]{1,0:T(8,12...) custom-call(s32[3]{0:T(128)} %pad_add_fusion.3.refs_0_, ...), custom_call_target="tpu_custom_call" | custom-call | flops 12884901888 | bytes 12582912 | tf_op jit(solution)/shard_map/expert_blocks/pallas_call | solution.py:334
  229.4 21.1 %expert_blocks.8 = (bf16[2,4,512,512]{3,2,1,0:T(8,128)(2,1)}, bf16[4,512,512]{2,1,0:T(8,128)(2,1)}, bf16[256,1024]{1,0:T(8,128)(2,1)}, bf16[256,1024]{1,0:T(8,12...) custom-call(s32[3]{0:T(128)} %pad_add_fusion.4.refs_0_, bf16[256,1152]{1,0:T(8,128)(2,1)} %copy-done.69, ...), custom_call_target="tpu_custom_call" | custom-call | flops 12884901888 | bytes 12582912 | tf_op jit(solution)/shard_map/expert_blocks/pallas_call | solution.py:334
  250.6 1.9 collective-permute-start.27
  252.5 13.3 %expert_blocks.9 = (bf16[2,4,256,512]{3,2,1,0:T(8,128)(2,1)}, bf16[4,256,512]{2,1,0:T(8,128)(2,1)}, bf16[256,1024]{1,0:T(8,128)(2,1)}, bf16[256,1152]{1,0:T(8,128)(2,1)}) custom-call(s32[2]{0:T(128)} %pad_add_fusion.5.refs_0_, bf16[256,1152]{1,0:T(8,128)(2,1)} %collective-permute-done.23.refs_8_.refs_1_, ...), custom_call_target="tpu_custom_call" | custom-call | flops 6442450944 | bytes 12582912 | tf_op jit(solution)/shard_map/expert_blocks/pallas_call | solution.py:334
  268.2 1.9 collective-permute-start.29
  270.6 14.6 %weight_grad.3 = (bf16[4,1024,128]{2,1,0:T(8,128)(2,1)}, bf16[4,1024,128]{2,1,0:T(8,128)(2,1)}, bf16[4,1024,128]{2,1,0:T(8,128)(2,1)}, bf16[4,1024,128]{2,1,0:T(8,128)(2,1)}) custom-call(s32[8]{0:T(128)} %broadcast_1_refs_0_.2.refs_0_, bf16[256,1152]{1,0:T(8,128)(2,1)} %get-tuple-element.117.refs_1_.refs_4_, bf16[256,1152]{1,0:T(8,128)(2,1)} %copy-done.67, ...), custom_call_target="tpu_custom_call" | custom-call | flops 8589934592 | bytes 8388608 | tf_op jit(solution)/shard_map/weight_grad/pallas_call | solution.py:407
  288.7 14.7 %weight_grad.4 = (bf16[4,1024,128]{2,1,0:T(8,128)(2,1)}, bf16[4,1024,128]{2,1,0:T(8,128)(2,1)}, bf16[4,1024,128]{2,1,0:T(8,128)(2,1)}, bf16[4,1024,128]{2,1,0:T(8,128)(2,1)}) custom-call(s32[8]{0:T(128)} %broadcast_1_refs_0_.2.refs_0_, bf16[256,1152]{1,0:T(8,128)(2,1)} %get-tuple-element.117.refs_1_.refs_4_, bf16[256,1152]{1,0:T(8,128)(2,1)} %copy-done.67, ...), custom_call_target="tpu_custom_call" | custom-call | flops 8589934592 | bytes 8388608 | tf_op jit(solution)/shard_map/weight_grad/pallas_call | solution.py:407
  308.8 13.6 %collective-permute-done.32.refs_9_.refs_1_ = bf16[256,1152]{1,0:T(8,128)(2,1)S(1)} collective-permute-done((bf16[256,1152]{1,0:T(8,128)(2,1)S(1)}, bf16[256,1152]{1,0:T(8,128)(2,1)S(1)}, u32[]{:S(2)}, u32[]{:S(2)}) %collective-permute-start.32) | collective-permute-done | bytes 589856 | tf_op jit(solution)/shard_map/ppermute | solution.py:106
  323.2 128.9 %place_far.1 = bf16[2048,1024]{1,0:T(8,128)(2,1)} custom-call(s32[8]{0:T(128)} %stack.105.refs_0_, bf16[256,1024]{1,0:T(8,128)(2,1)} %get-tuple-element.118.refs_1_, bf16[256,1024]{1,0:T(8,128)(2,1)} %get-tuple-element.120.refs_2_, bf16[256,1024]{1,0:T(8,128)(2,1)} %get-tuple-element.121.refs_3_, bf16[256,1024]{1,0:T(8,128)(2,1)} %get-tuple-element.123.refs_4_, ...), custom_call_target="tpu_custom_call" | custom-call | tf_op jit(solution)/shard_map/place_far/pallas_call | solution.py:198
  452.3 14.5 %weight_grad.5 = (bf16[4,128,1024]{2,1,0:T(8,128)(2,1)}, bf16[4,128,1024]{2,1,0:T(8,128)(2,1)}, bf16[4,128,1024]{2,1,0:T(8,128)(2,1)}, bf16[4,128,1024]{2,1,0:T(8,128)(2,1)}) custom-call(s32[8]{0:T(128)} %stack.105.refs_0_, bf16[2048,1024]{1,0:T(8,128)(2,1)} %all-gather.4.cloned.1.call-done.refs_3_.refs_4_.refs_2_.refs_1_.refs_5_.refs_6_.refs_7_.refs_8_, ...), custom_call_target="tpu_custom_call" | custom-call | flops 8589934592 | bytes 8388608 | tf_op jit(solution)/shard_map/weight_grad/pallas_call | solution.py:407
  470.2 24.9 %collective-permute-done.36.refs_2_ = bf16[256,1152]{1,0:T(8,128)(2,1)S(1)} collective-permute-done((bf16[256,1152]{1,0:T(8,128)(2,1)S(1)}, bf16[256,1152]{1,0:T(8,128)(2,1)S(1)}, u32[]{:S(2)}, u32[]{:S(2)}) %collective-permute-start.36) | collective-permute-done | bytes 589856 | tf_op jit(solution)/shard_map/ppermute | solution.py:108
  496.0 5.6 middle_backward.1
  501.6 3.5 all-to-all-start.1
  506.1 2.7 add_convert_fusion.after_ref
  508.8 7.9 %collective-permute-done.42.refs_2_ = bf16[256,1024]{1,0:T(8,128)(2,1)S(1)} collective-permute-done((bf16[256,1024]{1,0:T(8,128)(2,1)}, bf16[256,1024]{1,0:T(8,128)(2,1)S(1)}, u32[]{:S(2)}, u32[]{:S(2)}) %collective-permute-start.42) | collective-permute-done | bytes 524320 | tf_op jit(solution)/shard_map/ppermute | solution.py:119
  516.7 4.0 all-to-all-done.1
  521.4 18.7 %attention_backward.1.grad_ref = bf16[1024,512]{1,0:T(8,128)(2,1)} custom-call(s32[1]{0:T(128)} %constant.336.clone.1.refs_0_.s_ref, bf16[1024,512]{1,0:T(8,128)(2,1)} %get-tuple-element.149.rot_ref, bf16[1024,256]{1,0:T(8,128)(2,1)} %bitcast.56, f32[1024,128]{1,0:T(8,128)} %copy-done.12, f32[1024,128]{1,0:T(8,128)} %copy-done.13, ...), custom_call_target="tpu_custom_call" | custom-call | flops 20000000000 | bytes 4194304 | tf_op jit(solution)/shard_map/attention_backward/pallas_call | solution.py:510
  540.1 4.2 all-to-all-start.2
  550.1 6.3 pack.1
  561.2 26.6 %collective-permute-done.46 = bf16[1024,128]{1,0:T(8,128)(2,1)S(1)} collective-permute-done((bf16[1024,128]{1,0:T(8,128)(2,1)S(1)}, bf16[1024,128]{1,0:T(8,128)(2,1)S(1)}, u32[]{:S(2)}, u32[]{:S(2)}) %collective-permute-start.46) | collective-permute-done | bytes 262176 | tf_op jit(solution)/shard_map/ppermute | solution.py:145
  587.9 5.4 input_gradient.1.refs_1_.refs_0_
  595.7 8.1 %collective-permute-start.47 = (bf16[128,896]{1,0:T(8,128)(2,1)S(1)}, bf16[128,896]{1,0:T(8,128)(2,1)S(1)}, u32[]{:S(2)}, u32[]{:S(2)}) collective-permute-start(bf16[128,896]{1,0:T(8,128)(2,1)S(1)} %get-tuple-element.166), channel_id=1, source_target_pairs={{0,4},{8,0},{16,8},{24,16},{28,24},{20,28},{12,20},{4,12},{1,5},{9... | collective-permute-start | bytes 688136 | tf_op jit(solution)/shard_map/ppermute | solution.py:106
  603.8 4.5 collective-permute-done.47.refs_0_
  608.3 1.8 collective-permute-start.55
  610.5 1.8 collective-permute-start.59
  614.8 5.5 collective-permute-done.49.refs_0_
  620.3 3.7 collective-permute-start.50
  625.5 2.0 collective-permute-done.50.refs_2_
  631.3 3.4 collective-permute-done.55.refs_5_
  634.7 33.6 %collective-permute-done.39.refs_2_ = bf16[256,1024]{1,0:T(8,128)(2,1)S(1)} collective-permute-done((bf16[256,1024]{1,0:T(8,128)(2,1)}, bf16[256,1024]{1,0:T(8,128)(2,1)S(1)}, u32[]{:S(2)}, u32[]{:S(2)}) %collective-permute-start.39) | collective-permute-done | bytes 524320 | tf_op jit(solution)/shard_map/ppermute | solution.py:119
  668.8 8.5 %collective-permute-done.33.refs_2_ = bf16[256,1024]{1,0:T(8,128)(2,1)} collective-permute-done((bf16[256,1024]{1,0:T(8,128)(2,1)S(1)}, bf16[256,1024]{1,0:T(8,128)(2,1)}, u32[]{:S(2)}, u32[]{:S(2)}) %collective-permute-start.33) | collective-permute-done | bytes 524320 | tf_op jit(solution)/shard_map/ppermute | solution.py:119
  677.3 5.9 collective-permute-start.53
  684.2 4.5 collective-permute-done.53.refs_2_
  691.0 12.2 %adamw.2 = (f32[4,2,1024,128]{3,2,1,0:T(8,128)}, f32[4,2,1024,128]{3,2,1,0:T(8,128)}, f32[4,2,1024,128]{3,2,1,0:T(8,128)}) custom-call(f32[4,2,1024,128]{3,2,1,0:T(8,128)} %refs_0_.1, f32[4,2,1024,128]{3,2,1,0:T(8,128)} %refs_1_.1, f32[4,2,1024,128]{3,2,1,0:T(8,128)} %refs_2_.1, bf16[4,1024,128]{2,1,0:T(8,128)(2,1)} %get-tuple-element.146.refs_2_.refs_3_, ...), custom_call_target="tpu_custom_call" | custom-call | flops 20971520 | bytes 29360128 | tf_op jit(solution)/shard_map/adamw/pallas_call | solution.py:449
  703.2 7.3 adamw.3
  711.1 2.9 adamw_rest.1
  720.4 2.5 place.20
  722.9 2.8 place.18
  (290 shorter events, 101.1 us)
Async XLA Ops:
  7.2 172.3 %all-gather.4.cloned.1.call-start = ((), (), s32[]{:S(2)}) async-start(), calls=%async_computation.4 | async-start | bytes 4718592 | tf_op jit(solution)/shard_map/all_gather | solution.py:781
  14.5 8.6 %collective-permute-start = (bf16[128,896]{1,0:T(8,128)(2,1)S(1)}, bf16[128,896]{1,0:T(8,128)(2,1)S(1)}, u32[]{:S(2)}, u32[]{:S(2)}) collective-permute-start(bf16[128,896]{1,0:T(8,128)(2,1)S(1)} %place.11.refs_5_), channel_id=1, source_target_pairs={{0,8},{8,16},{16,24},{24,28},{28,20},{20,12},{12,4},{4,0},{1,9},{9... | collective-permute-start | bytes 688136 | tf_op jit(solution)/shard_map/ppermute | solution.py:87
  23.1 6.8 collective-permute-start.1
  29.9 6.0 collective-permute-start.2
  37.7 38.3 %collective-permute-start.7 = (bf16[4,1024,128]{2,1,0:T(8,128)(2,1)S(1)}, bf16[4,1024,128]{2,1,0:T(8,128)(2,1)}, u32[]{:S(2)}, u32[]{:S(2)}) collective-permute-start(bf16[4,1024,128]{2,1,0:T(8,128)(2,1)S(1)} %get-tuple-element.248.refs_2_), channel_id=1, source_target_pairs={{0,2},{1,3},{2,0},{3,1},{4,6},{5,7},{6,4},{7,5},{8,10},{9,11},{10,... | collective-permute-start | bytes 3145736 | tf_op jit(solution)/shard_map/ppermute | solution.py:119
  39.1 43.5 %collective-permute-start.8 = (bf16[4,1024,128]{2,1,0:T(8,128)(2,1)S(1)}, bf16[4,1024,128]{2,1,0:T(8,128)(2,1)}, u32[]{:S(2)}, u32[]{:S(2)}) collective-permute-start(bf16[4,1024,128]{2,1,0:T(8,128)(2,1)S(1)} %get-tuple-element.247.refs_3_), channel_id=1, source_target_pairs={{0,2},{1,3},{2,0},{3,1},{4,6},{5,7},{6,4},{7,5},{8,10},{9,11},{10,... | collective-permute-start | bytes 3145736 | tf_op jit(solution)/shard_map/ppermute | solution.py:119
  39.8 7.5 %collective-permute-start.4 = (bf16[128,896]{1,0:T(8,128)(2,1)S(1)}, bf16[128,896]{1,0:T(8,128)(2,1)S(1)}, u32[]{:S(2)}, u32[]{:S(2)}) collective-permute-start(bf16[128,896]{1,0:T(8,128)(2,1)S(1)} %place.11.refs_5_), channel_id=1, source_target_pairs={{0,4},{8,0},{16,8},{24,16},{28,24},{20,28},{12,20},{4,12},{1,5},{9... | collective-permute-start | bytes 688136 | tf_op jit(solution)/shard_map/ppermute | solution.py:90
  47.3 18.2 %collective-permute-start.5 = (bf16[128,896]{1,0:T(8,128)(2,1)S(1)}, bf16[128,896]{1,0:T(8,128)(2,1)}, u32[]{:S(2)}, u32[]{:S(2)}) collective-permute-start(bf16[128,896]{1,0:T(8,128)(2,1)S(1)} %collective-permute-done.4.refs_6_), channel_id=1, source_target_pairs={{0,4},{8,0},{16,8},{24,16},{28,24},{20,28},{12,20},{4,12},{1,5},{9... | collective-permute-start | bytes 688136 | tf_op jit(solution)/shard_map/ppermute | solution.py:90
  49.4 63.9 %collective-permute-start.12 = (bf16[4,1024,128]{2,1,0:T(8,128)(2,1)S(1)}, bf16[4,1024,128]{2,1,0:T(8,128)(2,1)}, u32[]{:S(2)}, u32[]{:S(2)}) collective-permute-start(bf16[4,1024,128]{2,1,0:T(8,128)(2,1)S(1)} %get-tuple-element.248.refs_2_), channel_id=1, source_target_pairs={{0,1},{1,0},{2,3},{3,2},{4,5},{5,4},{6,7},{7,6},{8,9},{9,8},{10,11... | collective-permute-start | bytes 3145736 | tf_op jit(solution)/shard_map/ppermute | solution.py:122
  65.5 10.4 %collective-permute-start.6 = (bf16[128,896]{1,0:T(8,128)(2,1)}, bf16[128,896]{1,0:T(8,128)(2,1)}, u32[]{:S(2)}, u32[]{:S(2)}) collective-permute-start(bf16[128,896]{1,0:T(8,128)(2,1)} %collective-permute-done.5.refs_7_), channel_id=1, source_target_pairs={{0,4},{8,0},{16,8},{24,16},{28,24},{20,28},{12,20},{4,12},{1,5},{9... | collective-permute-start | bytes 688136 | tf_op jit(solution)/shard_map/ppermute | solution.py:90
  65.5 10.4 %collective-permute-start.3 = (bf16[128,896]{1,0:T(8,128)(2,1)S(1)}, bf16[128,896]{1,0:T(8,128)(2,1)}, u32[]{:S(2)}, u32[]{:S(2)}) collective-permute-start(bf16[128,896]{1,0:T(8,128)(2,1)S(1)} %collective-permute-done.2.refs_2_), channel_id=1, source_target_pairs={{0,8},{8,16},{16,24},{24,28},{28,20},{20,12},{12,4},{4,0},{1,9},{9... | collective-permute-start | bytes 688136 | tf_op jit(solution)/shard_map/ppermute | solution.py:87
  92.0 19.4 %collective-permute-start.9 = (bf16[1024,256]{1,0:T(8,128)(2,1)}, bf16[1024,256]{1,0:T(8,128)(2,1)}, u32[]{:S(2)}, u32[]{:S(2)}) collective-permute-start(bf16[1024,256]{1,0:T(8,128)(2,1)} %copy-done.14), channel_id=1, source_target_pairs={{0,2},{1,3},{2,0},{3,1},{4,6},{5,7},{6,4},{7,5},{8,10},{9,11},{10,... | collective-permute-start | bytes 1572872 | tf_op jit(solution)/shard_map/ppermute | solution.py:119
  109.8 24.0 %collective-permute-start.16 = (bf16[4,128,1024]{2,1,0:T(8,128)(2,1)}, bf16[4,128,1024]{2,1,0:T(8,128)(2,1)}, u32[]{:S(2)}, u32[]{:S(2)}) collective-permute-start(bf16[4,128,1024]{2,1,0:T(8,128)(2,1)} %bitcast.24), channel_id=1, source_target_pairs={{0,2},{1,3},{2,0},{3,1},{4,6},{5,7},{6,4},{7,5},{8,10},{9,11},{10,... | collective-permute-start | bytes 3145736 | tf_op jit(solution)/shard_map/ppermute | solution.py:119
  110.9 33.7 %collective-permute-start.14 = (bf16[4,1024,128]{2,1,0:T(8,128)(2,1)S(1)}, bf16[4,1024,128]{2,1,0:T(8,128)(2,1)}, u32[]{:S(2)}, u32[]{:S(2)}) collective-permute-start(bf16[4,1024,128]{2,1,0:T(8,128)(2,1)S(1)} %get-tuple-element.247.refs_3_), channel_id=1, source_target_pairs={{0,1},{1,0},{2,3},{3,2},{4,5},{5,4},{6,7},{7,6},{8,9},{9,8},{10,11... | collective-permute-start | bytes 3145736 | tf_op jit(solution)/shard_map/ppermute | solution.py:122
  111.4 34.8 %collective-permute-start.13 = (bf16[4,1024,128]{2,1,0:T(8,128)(2,1)}, bf16[4,1024,128]{2,1,0:T(8,128)(2,1)}, u32[]{:S(2)}, u32[]{:S(2)}) collective-permute-start(bf16[4,1024,128]{2,1,0:T(8,128)(2,1)} %collective-permute-done.7.refs_9_), channel_id=1, source_target_pairs={{0,1},{1,0},{2,3},{3,2},{4,5},{5,4},{6,7},{7,6},{8,9},{9,8},{10,11... | collective-permute-start | bytes 3145736 | tf_op jit(solution)/shard_map/ppermute | solution.py:122
  113.4 6.8 collective-permute-start.11
  114.6 35.7 %collective-permute-start.15 = (bf16[4,1024,128]{2,1,0:T(8,128)(2,1)}, bf16[4,1024,128]{2,1,0:T(8,128)(2,1)}, u32[]{:S(2)}, u32[]{:S(2)}) collective-permute-start(bf16[4,1024,128]{2,1,0:T(8,128)(2,1)} %collective-permute-done.8.refs_10_), channel_id=1, source_target_pairs={{0,1},{1,0},{2,3},{3,2},{4,5},{5,4},{6,7},{7,6},{8,9},{9,8},{10,11... | collective-permute-start | bytes 3145736 | tf_op jit(solution)/shard_map/ppermute | solution.py:122
  114.7 21.9 %all-to-all-start = ((bf16[4,256,256]{2,1,0:T(8,128)(2,1)}), bf16[4,256,256]{2,1,0:T(8,128)(2,1)S(1)}, u32[]{:S(2)}, u32[]{:S(2)}) async-start(bf16[4,256,256]{2,1,0:T(8,128)(2,1)} %bitcast.50), calls=%async_computation | async-start | bytes 1048576 | tf_op jit(solution)/shard_map/all_to_all | solution.py:792
  118.2 469.7 %all-gather.6.cloned.1.call-start = ((), (), s32[]{:S(2)}) async-start(), calls=%async_computation.6 | async-start | bytes 5242880 | tf_op jit(solution)/shard_map/all_gather | solution.py:910
  120.1 40.4 %collective-permute-start.17 = (bf16[4,128,1024]{2,1,0:T(8,128)(2,1)}, bf16[4,128,1024]{2,1,0:T(8,128)(2,1)}, u32[]{:S(2)}, u32[]{:S(2)}) collective-permute-start(bf16[4,128,1024]{2,1,0:T(8,128)(2,1)} %bitcast.24), channel_id=1, source_target_pairs={{0,1},{1,0},{2,3},{3,2},{4,5},{5,4},{6,7},{7,6},{8,9},{9,8},{10,11... | collective-permute-start | bytes 3145736 | tf_op jit(solution)/shard_map/ppermute | solution.py:122
  133.9 26.7 %collective-permute-start.18 = (bf16[4,128,1024]{2,1,0:T(8,128)(2,1)}, bf16[4,128,1024]{2,1,0:T(8,128)(2,1)}, u32[]{:S(2)}, u32[]{:S(2)}) collective-permute-start(bf16[4,128,1024]{2,1,0:T(8,128)(2,1)} %collective-permute-done.16), channel_id=1, source_target_pairs={{0,1},{1,0},{2,3},{3,2},{4,5},{5,4},{6,7},{7,6},{8,9},{9,8},{10,11... | collective-permute-start | bytes 3145736 | tf_op jit(solution)/shard_map/ppermute | solution.py:122
  144.6 13.9 %collective-permute-start.19 = (bf16[256,1152]{1,0:T(8,128)(2,1)}, bf16[256,1152]{1,0:T(8,128)(2,1)S(1)}, u32[]{:S(2)}, u32[]{:S(2)}) collective-permute-start(bf16[256,1152]{1,0:T(8,128)(2,1)} %get-tuple-element.117.refs_1_.refs_4_), channel_id=1, source_target_pairs={{0,8},{8,16},{16,24},{24,28},{28,20},{20,12},{12,4},{4,0},{1,9},{9... | collective-permute-start | bytes 1769480 | tf_op jit(solution)/shard_map/ppermute | solution.py:87
  146.2 13.9 %collective-permute-start.20 = (bf16[256,1152]{1,0:T(8,128)(2,1)}, bf16[256,1152]{1,0:T(8,128)(2,1)S(1)}, u32[]{:S(2)}, u32[]{:S(2)}) collective-permute-start(bf16[256,1152]{1,0:T(8,128)(2,1)} %get-tuple-element.117.refs_1_.refs_4_), channel_id=1, source_target_pairs={{0,4},{8,0},{16,8},{24,16},{28,24},{20,28},{12,20},{4,12},{1,5},{9... | collective-permute-start | bytes 1769480 | tf_op jit(solution)/shard_map/ppermute | solution.py:90
  158.5 18.9 %collective-permute-start.21 = (bf16[256,1152]{1,0:T(8,128)(2,1)S(1)}, bf16[256,1152]{1,0:T(8,128)(2,1)}, u32[]{:S(2)}, u32[]{:S(2)}) collective-permute-start(bf16[256,1152]{1,0:T(8,128)(2,1)S(1)} %collective-permute-done.19.refs_6_.refs_1_.refs_2_), channel_id=1, source_target_pairs={{0,8},{8,16},{16,24},{24,28},{28,20},{20,12},{12,4},{4,0},{1,9},{9... | collective-permute-start | bytes 1769480 | tf_op jit(solution)/shard_map/ppermute | solution.py:87
  160.1 18.9 %collective-permute-start.22 = (bf16[256,1152]{1,0:T(8,128)(2,1)S(1)}, bf16[256,1152]{1,0:T(8,128)(2,1)}, u32[]{:S(2)}, u32[]{:S(2)}) collective-permute-start(bf16[256,1152]{1,0:T(8,128)(2,1)S(1)} %collective-permute-done.20.refs_7_.refs_2_.refs_3_), channel_id=1, source_target_pairs={{0,4},{8,0},{16,8},{24,16},{28,24},{20,28},{12,20},{4,12},{1,5},{9... | collective-permute-start | bytes 1769480 | tf_op jit(solution)/shard_map/ppermute | solution.py:90
  177.4 27.7 %collective-permute-start.23 = (bf16[256,1152]{1,0:T(8,128)(2,1)}, bf16[256,1152]{1,0:T(8,128)(2,1)}, u32[]{:S(2)}, u32[]{:S(2)}) collective-permute-start(bf16[256,1152]{1,0:T(8,128)(2,1)} %collective-permute-done.21.refs_8_.refs_1_.refs_4_), channel_id=1, source_target_pairs={{0,8},{8,16},{16,24},{24,28},{28,20},{20,12},{12,4},{4,0},{1,9},{9... | collective-permute-start | bytes 1769480 | tf_op jit(solution)/shard_map/ppermute | solution.py:87
  179.1 28.1 %collective-permute-start.24 = (bf16[256,1152]{1,0:T(8,128)(2,1)}, bf16[256,1152]{1,0:T(8,128)(2,1)}, u32[]{:S(2)}, u32[]{:S(2)}) collective-permute-start(bf16[256,1152]{1,0:T(8,128)(2,1)} %collective-permute-done.22.refs_9_.refs_2_.refs_5_), channel_id=1, source_target_pairs={{0,4},{8,0},{16,8},{24,16},{28,24},{20,28},{12,20},{4,12},{1,5},{9... | collective-permute-start | bytes 1769480 | tf_op jit(solution)/shard_map/ppermute | solution.py:90
  203.3 420.7 %reduce-scatter.2.cloned.1.call-start = ((), (), s32[]{:S(2)}) async-start(), calls=%async_computation.5 | async-start | bytes 4718592 | tf_op jit(solution)/shard_map/reduce_scatter | solution.py:864
  205.1 23.4 %collective-permute-start.25 = (bf16[256,1152]{1,0:T(8,128)(2,1)}, bf16[256,1152]{1,0:T(8,128)(2,1)S(1)}, u32[]{:S(2)}, u32[]{:S(2)}) collective-permute-start(bf16[256,1152]{1,0:T(8,128)(2,1)} %collective-permute-done.23.refs_8_.refs_1_), channel_id=1, source_target_pairs={{0,8},{8,16},{16,24},{24,28},{28,20},{20,12},{12,4},{4,0},{1,9},{9... | collective-permute-start | bytes 1769480 | tf_op jit(solution)/shard_map/ppermute | solution.py:87
  250.5 15.3 %collective-permute-start.26 = (bf16[256,1152]{1,0:T(8,128)(2,1)}, bf16[256,1152]{1,0:T(8,128)(2,1)S(1)}, u32[]{:S(2)}, u32[]{:S(2)}) collective-permute-start(bf16[256,1152]{1,0:T(8,128)(2,1)} %get-tuple-element.130), channel_id=1, source_target_pairs={{0,4},{8,0},{16,8},{24,16},{28,24},{20,28},{12,20},{4,12},{1,5},{9... | collective-permute-start | bytes 1769480 | tf_op jit(solution)/shard_map/ppermute | solution.py:106
  250.6 15.2 %collective-permute-start.27 = (bf16[256,1152]{1,0:T(8,128)(2,1)}, bf16[256,1152]{1,0:T(8,128)(2,1)S(1)}, u32[]{:S(2)}, u32[]{:S(2)}) collective-permute-start(bf16[256,1152]{1,0:T(8,128)(2,1)} %get-tuple-element.132), channel_id=1, source_target_pairs={{0,8},{8,16},{16,24},{24,28},{28,20},{20,12},{12,4},{4,0},{1,9},{9... | collective-permute-start | bytes 1769480 | tf_op jit(solution)/shard_map/ppermute | solution.py:108
  268.1 17.3 %collective-permute-start.28 = (bf16[256,1152]{1,0:T(8,128)(2,1)}, bf16[256,1152]{1,0:T(8,128)(2,1)S(1)}, u32[]{:S(2)}, u32[]{:S(2)}) collective-permute-start(bf16[256,1152]{1,0:T(8,128)(2,1)} %get-tuple-element.134.refs_14_), channel_id=1, source_target_pairs={{0,4},{8,0},{16,8},{24,16},{28,24},{20,28},{12,20},{4,12},{1,5},{9... | collective-permute-start | bytes 1769480 | tf_op jit(solution)/shard_map/ppermute | solution.py:106
  268.2 17.2 %collective-permute-start.29 = (bf16[256,1152]{1,0:T(8,128)(2,1)}, bf16[256,1152]{1,0:T(8,128)(2,1)S(1)}, u32[]{:S(2)}, u32[]{:S(2)}) collective-permute-start(bf16[256,1152]{1,0:T(8,128)(2,1)} %get-tuple-element.136), channel_id=1, source_target_pairs={{0,8},{8,16},{16,24},{24,28},{28,20},{20,12},{12,4},{4,0},{1,9},{9... | collective-permute-start | bytes 1769480 | tf_op jit(solution)/shard_map/ppermute | solution.py:108
  285.3 18.2 %collective-permute-start.31 = (bf16[4,1024,128]{2,1,0:T(8,128)(2,1)}, bf16[4,1024,128]{2,1,0:T(8,128)(2,1)}, u32[]{:S(2)}, u32[]{:S(2)}) collective-permute-start(bf16[4,1024,128]{2,1,0:T(8,128)(2,1)} %get-tuple-element.148), channel_id=1, source_target_pairs={{0,1},{1,0},{2,3},{3,2},{4,5},{5,4},{6,7},{7,6},{8,9},{9,8},{10,11... | collective-permute-start | bytes 3145736 | tf_op jit(solution)/shard_map/ppermute | solution.py:128
  288.5 16.5 %collective-permute-start.30 = (bf16[256,1152]{1,0:T(8,128)(2,1)}, bf16[256,1152]{1,0:T(8,128)(2,1)S(1)}, u32[]{:S(2)}, u32[]{:S(2)}) collective-permute-start(bf16[256,1152]{1,0:T(8,128)(2,1)} %get-tuple-element.144.refs_14_), channel_id=1, source_target_pairs={{0,4},{8,0},{16,8},{24,16},{28,24},{20,28},{12,20},{4,12},{1,5},{9... | collective-permute-start | bytes 1769480 | tf_op jit(solution)/shard_map/ppermute | solution.py:106
  306.7 15.7 %collective-permute-start.32 = (bf16[256,1152]{1,0:T(8,128)(2,1)S(1)}, bf16[256,1152]{1,0:T(8,128)(2,1)S(1)}, u32[]{:S(2)}, u32[]{:S(2)}) collective-permute-start(bf16[256,1152]{1,0:T(8,128)(2,1)S(1)} %add_pairs.8.refs_14_), channel_id=1, source_target_pairs={{0,4},{8,0},{16,8},{24,16},{28,24},{20,28},{12,20},{4,12},{1,5},{9... | collective-permute-start | bytes 1769480 | tf_op jit(solution)/shard_map/ppermute | solution.py:106
  452.2 16.8 %collective-permute-start.37 = (bf16[4,1024,128]{2,1,0:T(8,128)(2,1)}, bf16[4,1024,128]{2,1,0:T(8,128)(2,1)S(1)}, u32[]{:S(2)}, u32[]{:S(2)}) collective-permute-start(bf16[4,1024,128]{2,1,0:T(8,128)(2,1)} %get-tuple-element.155), channel_id=1, source_target_pairs={{0,1},{1,0},{2,3},{3,2},{4,5},{5,4},{6,7},{7,6},{8,9},{9,8},{10,11... | collective-permute-start | bytes 3145736 | tf_op jit(solution)/shard_map/ppermute | solution.py:128
  466.8 39.3 %collective-permute-start.38 = (bf16[4,128,1024]{2,1,0:T(8,128)(2,1)}, bf16[4,128,1024]{2,1,0:T(8,128)(2,1)}, u32[]{:S(2)}, u32[]{:S(2)}) collective-permute-start(bf16[4,128,1024]{2,1,0:T(8,128)(2,1)} %get-tuple-element.158), channel_id=1, source_target_pairs={{0,1},{1,0},{2,3},{3,2},{4,5},{5,4},{6,7},{7,6},{8,9},{9,8},{10,11... | collective-permute-start | bytes 3145736 | tf_op jit(solution)/shard_map/ppermute | solution.py:128
  467.3 27.8 %collective-permute-start.36 = (bf16[256,1152]{1,0:T(8,128)(2,1)S(1)}, bf16[256,1152]{1,0:T(8,128)(2,1)S(1)}, u32[]{:S(2)}, u32[]{:S(2)}) collective-permute-start(bf16[256,1152]{1,0:T(8,128)(2,1)S(1)} %copy-done.54), channel_id=1, source_target_pairs={{0,8},{8,16},{16,24},{24,28},{28,20},{20,12},{12,4},{4,0},{1,9},{9... | collective-permute-start | bytes 1769480 | tf_op jit(solution)/shard_map/ppermute | solution.py:108
  501.6 15.1 %collective-permute-start.42 = (bf16[256,1024]{1,0:T(8,128)(2,1)}, bf16[256,1024]{1,0:T(8,128)(2,1)S(1)}, u32[]{:S(2)}, u32[]{:S(2)}) collective-permute-start(bf16[256,1024]{1,0:T(8,128)(2,1)} %get-tuple-element.161.refs_1_), channel_id=1, source_target_pairs={{0,2},{1,3},{2,0},{3,1},{4,6},{5,7},{6,4},{7,5},{8,10},{9,11},{10,... | collective-permute-start | bytes 1572872 | tf_op jit(solution)/shard_map/ppermute | solution.py:119
  501.6 19.0 %all-to-all-start.1 = ((bf16[4,256,256]{2,1,0:T(8,128)(2,1)}), bf16[4,256,256]{2,1,0:T(8,128)(2,1)S(1)}, u32[]{:S(2)}, u32[]{:S(2)}) async-start(bf16[4,256,256]{2,1,0:T(8,128)(2,1)} %get-tuple-element.156), calls=%async_computation.2 | async-start | bytes 1048576 | tf_op jit(solution)/shard_map/all_to_all | solution.py:886
  505.1 98.7 %collective-permute-start.56 = (bf16[4,1024,128]{2,1,0:T(8,128)(2,1)}, bf16[4,1024,128]{2,1,0:T(8,128)(2,1)}, u32[]{:S(2)}, u32[]{:S(2)}) collective-permute-start(bf16[4,1024,128]{2,1,0:T(8,128)(2,1)} %get-tuple-element.193), channel_id=1, source_target_pairs={{0,1},{1,0},{2,3},{3,2},{4,5},{5,4},{6,7},{7,6},{8,9},{9,8},{10,11... | collective-permute-start | bytes 3145736 | tf_op jit(solution)/shard_map/ppermute | solution.py:128
  505.6 106.9 %collective-permute-start.54 = (bf16[4,1024,128]{2,1,0:T(8,128)(2,1)}, bf16[4,1024,128]{2,1,0:T(8,128)(2,1)}, u32[]{:S(2)}, u32[]{:S(2)}) collective-permute-start(bf16[4,1024,128]{2,1,0:T(8,128)(2,1)} %get-tuple-element.192), channel_id=1, source_target_pairs={{0,1},{1,0},{2,3},{3,2},{4,5},{5,4},{6,7},{7,6},{8,9},{9,8},{10,11... | collective-permute-start | bytes 3145736 | tf_op jit(solution)/shard_map/ppermute | solution.py:128
  505.7 38.7 %collective-permute-start.43 = (bf16[256,1024]{1,0:T(8,128)(2,1)}, bf16[256,1024]{1,0:T(8,128)(2,1)S(1)}, u32[]{:S(2)}, u32[]{:S(2)}) collective-permute-start(bf16[256,1024]{1,0:T(8,128)(2,1)} %get-tuple-element.161.refs_1_), channel_id=1, source_target_pairs={{0,1},{1,0},{2,3},{3,2},{4,5},{5,4},{6,7},{7,6},{8,9},{9,8},{10,11... | collective-permute-start | bytes 1572872 | tf_op jit(solution)/shard_map/ppermute | solution.py:122
  516.6 28.5 %collective-permute-start.44 = (bf16[256,1024]{1,0:T(8,128)(2,1)S(1)}, bf16[256,1024]{1,0:T(8,128)(2,1)S(1)}, u32[]{:S(2)}, u32[]{:S(2)}) collective-permute-start(bf16[256,1024]{1,0:T(8,128)(2,1)S(1)} %collective-permute-done.42.refs_2_), channel_id=1, source_target_pairs={{0,1},{1,0},{2,3},{3,2},{4,5},{5,4},{6,7},{7,6},{8,9},{9,8},{10,11... | collective-permute-start | bytes 1572872 | tf_op jit(solution)/shard_map/ppermute | solution.py:122
  540.1 47.7 %all-to-all-start.2 = ((bf16[4,256,512]{2,1,0:T(8,128)(2,1)}), bf16[4,256,512]{2,1,0:T(8,128)(2,1)}, u32[]{:S(2)}, u32[]{:S(2)}) async-start(bf16[4,256,512]{2,1,0:T(8,128)(2,1)} %bitcast.55), calls=%async_computation.3 | async-start | bytes 2097152 | tf_op jit(solution)/shard_map/all_to_all | solution.py:899
  556.8 56.2 %collective-permute-start.57 = (bf16[4,1024,128]{2,1,0:T(8,128)(2,1)S(1)}, bf16[4,1024,128]{2,1,0:T(8,128)(2,1)}, u32[]{:S(2)}, u32[]{:S(2)}) collective-permute-start(bf16[4,1024,128]{2,1,0:T(8,128)(2,1)S(1)} %copy-done.2), channel_id=1, source_target_pairs={{0,2},{1,3},{2,0},{3,1},{4,6},{5,7},{6,4},{7,5},{8,10},{9,11},{10,... | collective-permute-start | bytes 3145736 | tf_op jit(solution)/shard_map/ppermute | solution.py:137
  559.5 28.3 %collective-permute-start.46 = (bf16[1024,128]{1,0:T(8,128)(2,1)S(1)}, bf16[1024,128]{1,0:T(8,128)(2,1)S(1)}, u32[]{:S(2)}, u32[]{:S(2)}) collective-permute-start(bf16[1024,128]{1,0:T(8,128)(2,1)S(1)} %add.268), channel_id=1, source_target_pairs={{0,2},{1,3},{2,0},{3,1},{4,6},{5,7},{6,4},{7,5},{8,10},{9,11},{10,... | collective-permute-start | bytes 786440 | tf_op jit(solution)/shard_map/ppermute | solution.py:145
  595.7 12.6 %collective-permute-start.47 = (bf16[128,896]{1,0:T(8,128)(2,1)S(1)}, bf16[128,896]{1,0:T(8,128)(2,1)S(1)}, u32[]{:S(2)}, u32[]{:S(2)}) collective-permute-start(bf16[128,896]{1,0:T(8,128)(2,1)S(1)} %get-tuple-element.166), channel_id=1, source_target_pairs={{0,4},{8,0},{16,8},{24,16},{28,24},{20,28},{12,20},{4,12},{1,5},{9... | collective-permute-start | bytes 688136 | tf_op jit(solution)/shard_map/ppermute | solution.py:106
  603.8 6.7 collective-permute-start.48
  603.8 27.4 %collective-permute-start.58 = (bf16[4,128,1024]{2,1,0:T(8,128)(2,1)}, bf16[4,128,1024]{2,1,0:T(8,128)(2,1)}, u32[]{:S(2)}, u32[]{:S(2)}) collective-permute-start(bf16[4,128,1024]{2,1,0:T(8,128)(2,1)} %get-tuple-element.197), channel_id=1, source_target_pairs={{0,1},{1,0},{2,3},{3,2},{4,5},{5,4},{6,7},{7,6},{8,9},{9,8},{10,11... | collective-permute-start | bytes 3145736 | tf_op jit(solution)/shard_map/ppermute | solution.py:128
  608.3 26.4 %collective-permute-start.55 = (bf16[4,1024,128]{2,1,0:T(8,128)(2,1)}, bf16[4,1024,128]{2,1,0:T(8,128)(2,1)}, u32[]{:S(2)}, u32[]{:S(2)}) collective-permute-start(bf16[4,1024,128]{2,1,0:T(8,128)(2,1)} %add_convert_fusion.1.refs_11_), channel_id=1, source_target_pairs={{0,2},{1,3},{2,0},{3,1},{4,6},{5,7},{6,4},{7,5},{8,10},{9,11},{10,... | collective-permute-start | bytes 3145736 | tf_op jit(solution)/shard_map/ppermute | solution.py:137
  610.5 57.8 %collective-permute-start.59 = (bf16[4,128,1024]{2,1,0:T(8,128)(2,1)}, bf16[4,128,1024]{2,1,0:T(8,128)(2,1)}, u32[]{:S(2)}, u32[]{:S(2)}) collective-permute-start(bf16[4,128,1024]{2,1,0:T(8,128)(2,1)} %add_convert_fusion.after_ref), channel_id=1, source_target_pairs={{0,2},{1,3},{2,0},{3,1},{4,6},{5,7},{6,4},{7,5},{8,10},{9,11},{10,... | collective-permute-start | bytes 3145736 | tf_op jit(solution)/shard_map/ppermute | solution.py:137
  612.4 7.9 %collective-permute-start.49 = (bf16[128,896]{1,0:T(8,128)(2,1)S(1)}, bf16[128,896]{1,0:T(8,128)(2,1)S(1)}, u32[]{:S(2)}, u32[]{:S(2)}) collective-permute-start(bf16[128,896]{1,0:T(8,128)(2,1)S(1)} %get-tuple-element.170), channel_id=1, source_target_pairs={{0,4},{8,0},{16,8},{24,16},{28,24},{20,28},{12,20},{4,12},{1,5},{9... | collective-permute-start | bytes 688136 | tf_op jit(solution)/shard_map/ppermute | solution.py:106
  613.0 55.3 %collective-permute-start.39 = (bf16[256,1024]{1,0:T(8,128)(2,1)}, bf16[256,1024]{1,0:T(8,128)(2,1)S(1)}, u32[]{:S(2)}, u32[]{:S(2)}) collective-permute-start(bf16[256,1024]{1,0:T(8,128)(2,1)} %input_gradient.1.refs_1_.refs_0_), channel_id=1, source_target_pairs={{0,2},{1,3},{2,0},{3,1},{4,6},{5,7},{6,4},{7,5},{8,10},{9,11},{10,... | collective-permute-start | bytes 1572872 | tf_op jit(solution)/shard_map/ppermute | solution.py:119
  620.3 7.2 collective-permute-start.50
  627.5 49.8 %collective-permute-start.33 = (bf16[256,1024]{1,0:T(8,128)(2,1)S(1)}, bf16[256,1024]{1,0:T(8,128)(2,1)}, u32[]{:S(2)}, u32[]{:S(2)}) collective-permute-start(bf16[256,1024]{1,0:T(8,128)(2,1)S(1)} %add_convert_fusion.3.refs_1_), channel_id=1, source_target_pairs={{0,2},{1,3},{2,0},{3,1},{4,6},{5,7},{6,4},{7,5},{8,10},{9,11},{10,... | collective-permute-start | bytes 1572872 | tf_op jit(solution)/shard_map/ppermute | solution.py:119
  631.2 46.1 %collective-permute-start.51 = (bf16[128,896]{1,0:T(8,128)(2,1)S(1)}, bf16[128,896]{1,0:T(8,128)(2,1)S(1)}, u32[]{:S(2)}, u32[]{:S(2)}) collective-permute-start(bf16[128,896]{1,0:T(8,128)(2,1)S(1)} %get-tuple-element.174), channel_id=1, source_target_pairs={{0,4},{8,0},{16,8},{24,16},{28,24},{20,28},{12,20},{4,12},{1,5},{9... | collective-permute-start | bytes 688136 | tf_op jit(solution)/shard_map/ppermute | solution.py:106
  634.7 83.8 %collective-permute-start.40 = (bf16[256,1024]{1,0:T(8,128)(2,1)S(1)}, bf16[256,1024]{1,0:T(8,128)(2,1)S(1)}, u32[]{:S(2)}, u32[]{:S(2)}) collective-permute-start(bf16[256,1024]{1,0:T(8,128)(2,1)S(1)} %copy-done.7), channel_id=1, source_target_pairs={{0,1},{1,0},{2,3},{3,2},{4,5},{5,4},{6,7},{7,6},{8,9},{9,8},{10,11... | collective-permute-start | bytes 1572872 | tf_op jit(solution)/shard_map/ppermute | solution.py:122
  668.3 51.0 %collective-permute-start.41 = (bf16[256,1024]{1,0:T(8,128)(2,1)S(1)}, bf16[256,1024]{1,0:T(8,128)(2,1)}, u32[]{:S(2)}, u32[]{:S(2)}) collective-permute-start(bf16[256,1024]{1,0:T(8,128)(2,1)S(1)} %collective-permute-done.39.refs_2_), channel_id=1, source_target_pairs={{0,1},{1,0},{2,3},{3,2},{4,5},{5,4},{6,7},{7,6},{8,9},{9,8},{10,11... | collective-permute-start | bytes 1572872 | tf_op jit(solution)/shard_map/ppermute | solution.py:122
  668.3 54.6 %collective-permute-start.34 = (bf16[256,1024]{1,0:T(8,128)(2,1)S(1)}, bf16[256,1024]{1,0:T(8,128)(2,1)}, u32[]{:S(2)}, u32[]{:S(2)}) collective-permute-start(bf16[256,1024]{1,0:T(8,128)(2,1)S(1)} %add_convert_fusion.3.refs_1_), channel_id=1, source_target_pairs={{0,1},{1,0},{2,3},{3,2},{4,5},{5,4},{6,7},{7,6},{8,9},{9,8},{10,11... | collective-permute-start | bytes 1572872 | tf_op jit(solution)/shard_map/ppermute | solution.py:122
  677.3 45.6 %collective-permute-start.35 = (bf16[256,1024]{1,0:T(8,128)(2,1)}, bf16[256,1024]{1,0:T(8,128)(2,1)}, u32[]{:S(2)}, u32[]{:S(2)}) collective-permute-start(bf16[256,1024]{1,0:T(8,128)(2,1)} %collective-permute-done.33.refs_2_), channel_id=1, source_target_pairs={{0,1},{1,0},{2,3},{3,2},{4,5},{5,4},{6,7},{7,6},{8,9},{9,8},{10,11... | collective-permute-start | bytes 1572872 | tf_op jit(solution)/shard_map/ppermute | solution.py:122
  677.3 11.4 %collective-permute-start.53 = (bf16[128,896]{1,0:T(8,128)(2,1)S(1)}, bf16[128,896]{1,0:T(8,128)(2,1)S(1)}, u32[]{:S(2)}, u32[]{:S(2)}) collective-permute-start(bf16[128,896]{1,0:T(8,128)(2,1)S(1)} %get-tuple-element.176), channel_id=1, source_target_pairs={{0,8},{8,16},{16,24},{24,28},{28,20},{20,12},{12,4},{4,0},{1,9},{9... | collective-permute-start | bytes 688136 | tf_op jit(solution)/shard_map/ppermute | solution.py:108
  688.8 21.7 %collective-permute-start.52 = (bf16[128,896]{1,0:T(8,128)(2,1)S(1)}, bf16[128,896]{1,0:T(8,128)(2,1)S(1)}, u32[]{:S(2)}, u32[]{:S(2)}) collective-permute-start(bf16[128,896]{1,0:T(8,128)(2,1)S(1)} %add_pairs.11), channel_id=1, source_target_pairs={{0,4},{8,0},{16,8},{24,16},{28,24},{20,28},{12,20},{4,12},{1,5},{9... | collective-permute-start | bytes 688136 | tf_op jit(solution)/shard_map/ppermute | solution.py:106
  (72 other events, 1177.1 us)
Sparse Core Ops, SparseCore 0:
  37.8 81.0 all-gather.3
  203.5 34.7 all-gather.5
  452.3 100.6 reduce-scatter.1

commit v5 on v4

--- a/solution.py
+++ b/solution.py
@@ -95,18 +95,20 @@
 def ring_reduce(part, size, beside=None):
     down = up = None
     after = []
+    move = lambda arrays, step: [lax.ppermute(x, "expert", ring_perm(size, step)) for x in arrays]
     for hop in range(size // 2, 0, -1):
         side = hop - 1
-        if down is None:
-            messages = [part(-hop), part(side)]
-        else:
-            pairs = [(down, part(-hop))] + ([(up, part(side))] if side > 0 else [])
+        lower = part(-hop)
+        upper = part(side) if side > 0 else []
+        if down is not None:
+            pairs = list(zip(down, lower)) + (list(zip(up, upper)) if side > 0 else [])
             messages = add_pairs(pairs, after)
+            lower, upper = messages[: len(lower)], messages[len(lower) :]
             after = beside(hop, messages) if beside else []
-        down = lax.ppermute(messages[0], "expert", ring_perm(size, -1))
+        down = move(lower, -1)
         if side > 0:
-            up = lax.ppermute(messages[1], "expert", ring_perm(size, 1))
-    return [part(0), down, up], after
+            up = move(upper, 1)
+    return [list(terms) for terms in zip(part(0), down, up)], after
 
 
 def tensor_perm(size, along, core):
@@ -178,34 +180,6 @@
     return out if len(cuts) > 1 else out[0]
 
 
-def place_far_kernel(blocks, *refs):
-    index_ref, out_ref, sems = refs[0], refs[-2], refs[-1]
-    copies = []
-    for block in range(blocks):
-        size = refs[1 + block].shape[0]
-        start = pl.multiple_of(index_ref[block] * size, size)
-        copies.append(
-            pltpu.make_async_copy(refs[1 + block], out_ref.at[pl.ds(start, size)], sems.at[block])
-        )
-        copies[-1].start()
-    for copy in copies:
-        copy.wait()
-
-
-def place_far(blocks, index, after=()):
-    size, columns = blocks[0].shape
-    count = len(blocks)
-    return pl.pallas_call(
-        functools.partial(place_far_kernel, count),
-        in_specs=[pl.BlockSpec(memory_space=pltpu.SMEM)]
-        + [pl.BlockSpec(memory_space=pl.ANY)] * (count + len(after)),
-        out_specs=pl.BlockSpec(memory_space=pl.ANY),
-        out_shape=jax.ShapeDtypeStruct((count * size, columns), blocks[0].dtype),
-        scratch_shapes=[pltpu.SemaphoreType.DMA((count,))],
-        name="place_far",
-    )(index, *blocks, *after)
-
-
 def hold(array, after):
     flat = array.reshape(-1, array.shape[-1])
     return place([flat], jnp.zeros((1,), jnp.int32), after=after).reshape(array.shape)
@@ -242,13 +216,16 @@
 
 
 def add_pairs(pairs, after):
-    vmem = pl.BlockSpec(memory_space=pltpu.VMEM)
+    steps = 4 if pairs[0][0].shape[0] >= 256 else 1
+    spec = lambda array: pl.BlockSpec((array.shape[0] // steps, array.shape[1]), lambda i: (i, 0))
     return pl.pallas_call(
         functools.partial(add_kernel, len(pairs)),
-        in_specs=[vmem] * (2 * len(pairs)) + [pl.BlockSpec(memory_space=pl.ANY)] * len(after),
-        out_specs=[vmem] * len(pairs),
+        grid=(steps,),
+        in_specs=[spec(array) for pair in pairs for array in pair]
+        + [pl.BlockSpec(memory_space=pl.ANY)] * len(after),
+        out_specs=[spec(pair[0]) for pair in pairs],
         out_shape=[jax.ShapeDtypeStruct(pair[0].shape, BF) for pair in pairs],
-        compiler_params=pltpu.CompilerParams(vmem_limit_bytes=32 * 1024 * 1024),
+        compiler_params=pltpu.CompilerParams(vmem_limit_bytes=60 * 1024 * 1024),
         name="add_pairs",
     )(*[array for pair in pairs for array in pair], *after)
 
@@ -266,8 +243,8 @@
     first_ref = refs[0]
     message_refs = refs[1 : 1 + count]
     cotangent_refs = refs[1 + count : 1 + 2 * count]
-    gate_ref, up_ref, down_ref = refs[1 + 2 * count : 4 + 2 * count]
-    outs = refs[4 + 2 * count + afters :]
+    weights_ref = refs[1 + 2 * count]
+    outs = refs[2 + 2 * count + afters :]
     grads_ref, scaled_ref = outs[:2]
     y_refs = outs[2 : 2 + count]
     back_refs = outs[2 + count : 2 + 2 * count]
@@ -284,14 +261,14 @@
         back_acc[...] = jnp.zeros_like(back_acc)
         tail_acc[...] = jnp.zeros_like(tail_acc)
 
-    gate_w = gate_ref[0]
-    up_w = up_ref[0]
-    down_w = down_ref[0]
+    gate_w = weights_ref[0, 0]
+    up_w = weights_ref[1, 0]
+    down_w = weights_ref[2, 0]
     column = first_ref[0] + expert
     b = rows_ref[:, :width]
     gate_pre = dot(b, gate_w, ((1,), (0,)))
     up_pre = dot(b, up_w, ((1,), (0,)))
-    grad_act = dot(dy_ref[...], down_w, ((1,), (1,)))
+    grad_act = dot(dy_ref[...], down_w, ((1,), (0,)))
     sig = 0.5 * jnp.tanh(0.5 * gate_pre) + 0.5
     silu = gate_pre * sig
     act = (silu * up_pre).astype(BF).astype(F32)
@@ -309,7 +286,7 @@
     grads_ref[1, 0] = grad_up
     scaled_ref[0] = scaled
     back_acc[...] += dot(grad_gate, gate_w, ((1,), (1,))) + dot(grad_up, up_w, ((1,), (1,)))
-    y_acc[...] += dot(scaled, down_w, ((1,), (0,)))
+    y_acc[...] += dot(scaled, down_w, ((1,), (1,)))
 
     @pl.when(expert == pl.num_programs(0) - 1)
     def _():
@@ -323,8 +300,8 @@
             back_refs[i][:, width:] = jnp.where(lane < EXPERTS, high, total - high).astype(BF)
 
 
-def expert_blocks(first, messages, owners, cotangents, gate, up, down, after):
-    experts, width, hidden = gate.shape
+def expert_blocks(first, messages, owners, cotangents, weights, after):
+    _, experts, width, hidden = weights.shape
     rows, message = messages[0].shape
     count = len(messages)
     block = pl.BlockSpec((rows, message), lambda e, s: (0, 0))
@@ -338,8 +315,7 @@
             grid=(experts,),
             in_specs=[block] * count
             + owned
-            + [pl.BlockSpec((1, width, hidden), lambda e, s: (e, 0, 0))] * 2
-            + [pl.BlockSpec((1, hidden, width), lambda e, s: (e, 0, 0))]
+            + [pl.BlockSpec((3, 1, width, hidden), lambda e, s: (0, e, 0, 0))]
             + [pl.BlockSpec(memory_space=pl.ANY)] * len(after),
             out_specs=[
                 pl.BlockSpec((2, 1, count * rows, hidden), lambda e, s: (0, e, 0, 0)),
@@ -368,7 +344,7 @@
             transcendentals=count * rows * experts * hidden,
         ),
         name="expert_blocks",
-    )(jnp.stack([first] + owners), *messages, *cotangents, gate, up, down, *after)
+    )(jnp.stack([first] + owners), *messages, *cotangents, weights, *after)
     return out[0], out[1], out[2 : 2 + count], out[2 + count :]
 
 
@@ -585,7 +561,7 @@
 
 
 def attention_back_kernel(
-    q_cols, k_cols, s_ref, rot_ref, grad_ref, cos_ref, sin_ref, after_ref, out_ref, acc_ref
+    q_cols, k_cols, s_ref, rot_ref, grad_ref, cos_ref, sin_ref, after_ref, last_ref, out_ref, acc_ref
 ):
     length = rot_ref.shape[0]
     step = min(256, length)
@@ -617,7 +593,8 @@
             ).astype(BF)
 
 
-def middle_kernel(s_ref, mix_ref, out_ref, x_ref, routes_ref, gains_ref, rest_ref, message_ref, mid_ref):
+def middle_kernel(s_ref, mix_ref, out_ref, x_ref, routes_ref, gains_ref, rest_ref, *more):
+    message_ref, mid_ref = more[-2:]
     rows, width = x_ref.shape
     mid = x_ref[...].astype(F32)
     for t in range(mix_ref.shape[0]):
@@ -672,8 +649,9 @@
 
 
 def pack_kernel(
-    s_ref, a_ref, grad_ref, attention_ref, mix_ref, qkv_ref, rest_ref, tail_ref, main_ref, tail_out_ref
+    s_ref, a_ref, grad_ref, attention_ref, mix_ref, qkv_ref, rest_ref, tail_ref, *more
 ):
+    main_ref, tail_out_ref = more[1:]
     late = dot(a_ref[...], grad_ref[...], ((0,), (0,)))
     columns = late.shape[1]
     main_ref[:, :columns] = late.astype(BF)
@@ -733,12 +711,12 @@
     own_block = pl.BlockSpec((rows, width), lambda g, s: (s[0], 0))
     chips = tensors // 2
 
-    gate_bf = gateup_weight[:, 0].astype(BF)
-    up_bf = gateup_weight[:, 1].astype(BF)
-    gate_pieces = tensor_gather(gate_bf, tensors)
-    up_pieces = tensor_gather(up_bf, tensors)
-    gate_low = jnp.concatenate(gate_pieces, axis=2)
-    up_low = jnp.concatenate(up_pieces, axis=2)
+    shard = jnp.stack(
+        [gateup_weight[:, 0], gateup_weight[:, 1], jnp.swapaxes(down_weight, 1, 2)]
+    ).astype(BF)
+    weight_pieces = [shard] + [
+        lax.ppermute(shard, "tensor", tensor_perm(tensors, -step, 0)) for step in range(1, chips)
+    ]
 
     q_cols = query_weight.shape[1]
     k_cols = keyval_weight.shape[2]
@@ -756,12 +734,11 @@
         + [jnp.zeros((query_weight.shape[0], PAD - EXPERTS - 6), BF)],
         axis=1,
     )
-    packed_blocks = ring_gather(hold(packed, [gate_bf, up_bf]), ring)
+    packed_blocks = ring_gather(packed, ring)
     offsets = sorted(packed_blocks)
     cosine_table, sine_table = rope_tables(length, HD)
     cosine_table = jnp.concatenate([cosine_table] * 4, axis=1)
     sine_table = jnp.concatenate([-sine_table, sine_table] * 2, axis=1)
-    down_bf = down_weight.astype(BF)
     qkv_low, out_low, rest = place(
         [packed_blocks[o] for o in offsets],
         jnp.stack([ring_index(ring, o) for o in offsets]).astype(jnp.int32),
@@ -770,7 +747,7 @@
             (heads_cols, heads_cols + o_cols),
             (heads_cols + o_cols, heads_cols + o_cols + PAD),
         ],
-        after=gate_pieces[1:chips] + up_pieces[1:chips] + [cosine_table, sine_table, down_bf],
+        after=[cosine_table, sine_table],
     )
     gains_all = (
         rest[:, EXPERTS : EXPERTS + 2].astype(F32)
@@ -778,9 +755,7 @@
         + rest[:, EXPERTS + 4 : EXPERTS + 6].astype(F32)
     ).T
     dy_own = lax.dynamic_slice_in_dim(cotangent, lane_t[0] * rows, rows, axis=0)
-    dy_all = lax.all_gather(
-        hold(dy_own, [packed_blocks[1 - ring // 2]]), "expert", axis=0, tiled=True
-    )
+    dy_all = lax.all_gather(dy_own, "expert", axis=0, tiled=True)
     a, rotated, mixture = call_whole(
         functools.partial(front_kernel, q_cols, k_cols),
         [shape((length, width), BF), shape((length, heads_cols), BF), shape((length, q_cols), BF)],
@@ -793,20 +768,37 @@
         mixture.reshape(tensors, rows, o_cols), "tensor", split_axis=0, concat_axis=0, tiled=True
     )
     owners_t = tensor_index(tensors)
-    out_pieces = tensor_gather(out_low, tensors, after=[mixture])
+    weight_pieces += [
+        lax.ppermute(piece, "tensor", tensor_perm(tensors, 0, 1))
+        for piece in [shard] + [hold(piece, [mixture_rows]) for piece in weight_pieces[1:]]
+    ]
+    expert_low = jnp.concatenate(weight_pieces, axis=3)
+    out_pieces = tensor_gather(out_low, tensors, after=[mixture_rows])
     out_all = place(out_pieces, owners_t, after=[mixture_rows]).reshape(tensors, width, o_cols)
-    down_pieces = tensor_gather(hold(down_bf, [mixture]), tensors)
-    down_low = jnp.concatenate(down_pieces, axis=1)
     message, x_mid = call_whole(
         middle_kernel,
         [shape((rows, width + PAD), BF), shape((rows, width), F32)],
-        [mixture_rows, out_all, tokens, routes, gains_all, rest],
+        [mixture_rows, out_all, tokens, routes, gains_all, rest] + weight_pieces[1:chips],
         "middle",
         scalars=lane_t,
-        specs={2: own_block, 3: pl.BlockSpec((rows, routes.shape[1]), lambda g, s: (s[0], 0))},
+        specs={
+            2: own_block,
+            3: pl.BlockSpec((rows, routes.shape[1]), lambda g, s: (s[0], 0)),
+            **{5 + i: pl.BlockSpec(memory_space=pl.ANY) for i in range(1, chips)},
+        },
         cost=10**9,
     )
-    blocks = ring_gather(message, ring)
+    blocks = {0: message}
+
+    def next_hop(hop, after):
+        for sign, last in ((-1, ring // 2), (1, (ring - 1) // 2)):
+            if hop <= last:
+                block = blocks[sign * (hop - 1)]
+                block = hold(block, after) if after else block
+                blocks[sign * hop] = lax.ppermute(block, "expert", ring_perm(ring, -sign))
+
+    next_hop(1, [])
+    next_hop(2, [])
 
     half = ring // 2
     first = (lax.axis_index("expert") * experts).astype(jnp.int32)
@@ -827,13 +819,12 @@
             [blocks[o] for o in call],
             owners,
             [dy_own if o == 0 else dy_all for o in call],
-            gate_low,
-            up_low,
-            down_low,
+            expert_low,
             after,
         )
         grads.append(result[0])
         scaled.append(result[1])
+        next_hop(number + 3, [result[1]])
         for part, o in enumerate(call):
             forth[o], back[o] = result[2][part], result[3][part]
             order.append(o)
@@ -859,10 +850,11 @@
         totals[kind] = core_sums(weights[kind], tensors)
         return [weights[kind][0]] + early
 
-    returned, after = ring_reduce(lambda offset: back[offset], ring, beside)
-    sums = place_far([forth[o] for o in order], whose, after=[returned[1]])
-    moe_sum = lax.psum_scatter(sums, "expert", scatter_dimension=0, tiled=True)
-    block_out = place(tensor_gather((x_mid + moe_sum.astype(F32)).astype(BF), tensors), owners_t)
+    (returned, forward), after = ring_reduce(lambda offset: [back[offset], forth[offset]], ring, beside)
+    moe_sum = sum(term.astype(F32) for term in forward)
+    sums = {kind: chip_sums(total, tensors) for kind, total in totals.items()}
+    after = after + [sums[2][-1]]
+    block_out = place(tensor_gather((x_mid + moe_sum).astype(BF), tensors), owners_t)
 
     grad_mid, grad_attention, grad_mixture, tail = call_whole(
         functools.partial(middle_back_kernel, len(returned)),
@@ -890,9 +882,9 @@
     (grad_pre,) = call_whole(
         functools.partial(attention_back_kernel, q_cols, k_cols),
         [shape((length, heads_cols), BF)],
-        [rotated, grad_mixture, cosine_table, sine_table, totals[0][-1]],
+        [rotated, grad_mixture, cosine_table, sine_table, sums[1][-1], totals[0][-1]],
         "attention_backward",
-        specs={4: pl.BlockSpec(memory_space=pl.ANY)},
+        specs={i: pl.BlockSpec(memory_space=pl.ANY) for i in (4, 5)},
         scratch=[pltpu.VMEM((length, heads_cols), F32)],
         cost=2 * 10**10,
     )
@@ -902,8 +894,9 @@
     main, tail = call_whole(
         pack_kernel,
         [shape((width, heads_cols + o_cols), BF), shape((width, PAD), BF)],
-        [a, grad_pre, grad_attention_all, mixture, qkv_low, rest, tail],
+        [a, grad_pre, grad_attention_all, mixture, qkv_low, rest, tail, sums[0][-1]],
         "pack",
+        specs={7: pl.BlockSpec(memory_space=pl.ANY)},
         cost=4 * 10**9,
     )
     tail = tensor_sum(tail, tensors)
@@ -924,7 +917,25 @@
         [input_grad],
     )
     pieces = dict(zip(offsets, pieces))
-    summed, _ = ring_reduce(lambda offset: pieces[offset], ring)
+    new_gateup = adamw_blocks(
+        gateup_weight,
+        gateup_moment,
+        gateup_second,
+        [sums[1], sums[2]],
+    )
+    new_down = [
+        array[:, 0]
+        for array in adamw_blocks(
+            down_weight[:, None],
+            down_moment[:, None],
+            down_second[:, None],
+            [sums[0]],
+        )
+    ]
+    fill = {half - 1: [new_gateup[0]], half - 2: [new_down[0]]}
+    (summed,), _ = ring_reduce(
+        lambda offset: [pieces[offset]], ring, lambda hop, sent: fill.get(hop, [])
+    )
     input_grad = place(tensor_gather(input_grad, tensors), owners_t)
     new_rest = adamw_rest(
         q_cols,
@@ -939,21 +950,6 @@
         ],
     )
 
-    new_gateup = adamw_blocks(
-        gateup_weight,
-        gateup_moment,
-        gateup_second,
-        [chip_sums(totals[1], tensors), chip_sums(totals[2], tensors)],
-    )
-    new_down = [
-        array[:, 0]
-        for array in adamw_blocks(
-            down_weight[:, None],
-            down_moment[:, None],
-            down_second[:, None],
-            [chip_sums(totals[0], tensors)],
-        )
-    ]
     return (block_out, input_grad) + tuple(new_rest) + tuple(new_gateup) + tuple(new_down)
 
 

time: 739 us -> 517 us (0.70)
  Pallas kernels: 355 us -> 241 us
  waiting for transfers between devices: 202 us -> 120 us
  local copies, waits for them, and re-layouts: 50.1 us -> 36.6 us
  starting transfers between devices: 76.1 us -> 68.7 us
    pallas_call x7 -> x6, Pallas kernels: 132 us -> 18.4 us  [add_pairs(): pl.pallas_call(functools.partial(add_kernel, len(pairs)), grid=(steps,),...]
    ppermute x7 -> x4, waiting for transfers between devices: 69.9 us -> 20.1 us  [tensor_gather(): lax.ppermute(shard, 'tensor', tensor_perm(size, -step, 0))]
    ppermute x6 -> x3, waiting for transfers between devices: 22.2 us -> 0.01 us  [ring_gather(): behind = lax.ppermute(behind, 'expert', ring_perm(size, -1))]
    ppermute x1, waiting for transfers between devices: 26.6 us -> 6.12 us  [tensor_sum(): lax.ppermute(values, 'tensor', tensor_perm(size, step, 0))]
    unnamed x149 -> x132, local copies, waits for them, and re-layouts: 44.2 us -> 27.4 us
    all_to_all x1, waiting for transfers between devices: 2.04 us -> 16.9 us  [body(): lax.all_to_all(mixture.reshape(tensors, rows, o_cols), 'tensor', split_ax...]
    ppermute x8 -> x4, starting transfers between devices: 15.1 us -> 6.51 us  [ring_gather(): ahead = lax.ppermute(ahead, 'expert', ring_perm(size, 1))]
    ppermute x14 -> x31, starting transfers between devices: 25.8 us -> 34.1 us  [the longest x21 22.4 us: ring_reduce(): lax.ppermute(x, 'expert', ring_perm(size, step))]
  transfers between devices with their start and end apart: 66 -> 66, of which waited for: 22 -> 22; matrix products, arithmetic and copies ran while one was open for 6% -> 8% of each run, Pallas kernels for 48% -> 47%
where the time goes in v5:
time: 517 us; the launch traced here: 513 us
  Pallas kernels  241 us (47%)
  waiting for transfers between devices  120 us (23%)
  starting transfers between devices  68.7 us (13%)
  local copies, waits for them, and re-layouts  36.6 us (7%)
  other arithmetic  31.1 us (6%)
  between operations  15.2 us (3%)
    pallas_call x5, Pallas kernels, expert_blocks(): pl.pallas_call(functools.partial(expert_kernel, count, len(after)), grid_...  87.6 us
    pallas_call x7, Pallas kernels, call_whole(): pl.pallas_call(kernel, grid_spec=pltpu.PrefetchScalarGridSpec(num_scalar_...  56.1 us
    ppermute x21, waiting for transfers between devices, ring_reduce(): lax.ppermute(x, 'expert', ring_perm(size, step))  47.6 us
    pallas_call x3, Pallas kernels, weight_grad(): pl.pallas_call(functools.partial(weight_grad_kernel, spots, swap, shards,...  43.5 us
    unnamed x132, local copies, waits for them, and re-layouts  27.4 us
    ppermute x21, starting transfers between devices, ring_reduce(): lax.ppermute(x, 'expert', ring_perm(size, step))  22.4 us
    ppermute x4, waiting for transfers between devices, tensor_gather(): lax.ppermute(shard, 'tensor', tensor_perm(size, -step, 0))  20.1 us
    pallas_call x2, Pallas kernels, adamw_blocks(): pl.pallas_call(functools.partial(adamw_kernel, kinds, parts), grid=(exper...  19.2 us
  transfers between devices with their start and end apart: 66, of which 22 were waited for; matrix products, arithmetic and copies ran while one was open for 8% of the time, Pallas kernels for 47%

profile of v5, /device:TPU:0, one launch (start us, length us, event | category | flops | bytes accessed | tf_op | source)
XLA Modules:
  0.0 513.0 jit_solution(18285585899522617878)
XLA Ops:
  7.2 1.8 copy.69
  9.1 2.9 slice_bitcast_fusion.1
  12.1 2.0 pad_maximum_fusion.1
  14.1 2.9 collective-permute-start.10
  22.5 5.1 %collective-permute-done.refs_4_ = bf16[128,896]{1,0:T(8,128)(2,1)} collective-permute-done((bf16[128,896]{1,0:T(8,128)(2,1)S(1)}, bf16[128,896]{1,0:T(8,128)(2,1)}, u32[]{:S(2)}, u32[]{:S(2)}) %collective-permute-start) | collective-permute-done | bytes 229408 | tf_op jit(solution)/shard_map/ppermute | solution.py:87
  29.6 4.4 collective-permute-done.1.refs_3_
  35.7 1.9 constant_dynamic-slice_fusion.refs_2_
  38.1 2.4 collective-permute-done.2.refs_2_
  42.3 2.9 fusion.2
  45.3 3.8 pad_maximum_fusion.2
  56.1 13.2 %attention_forward.1 = (bf16[1024,1024]{1,0:T(8,128)(2,1)}, bf16[1024,512]{1,0:T(8,128)(2,1)}, bf16[1024,256]{1,0:T(8,128)(2,1)}) custom-call(s32[1]{0:T(128)} %constant.336.clone.1.s_ref.refs_0_, bf16[1024,1024]{1,0:T(8,128)(2,1)} %x_ref.5, f32[2,1024]{1,0:T(2,128)} %add_bitcast_fusion.gains_ref.refs_6_, bf16[1024,512]{1,0:T(8,128)(2,1)} %copy-done.14, ...), custom_call_target="tpu_custom_call" | custom-call | flops 10000000000 | bytes 4194304 | tf_op jit(solution)/shard_map/attention_forward/pallas_call | solution.py:486
  69.3 4.2 all-to-all-start
  74.2 16.9 %all-to-all-done.refs_2_.refs_5_.mix_ref = bf16[4,256,256]{2,1,0:T(8,128)(2,1)} async-done(((bf16[4,256,256]{2,1,0:T(8,128)(2,1)}), bf16[4,256,256]{2,1,0:T(8,128)(2,1)}, u32[]{:S(2)}, u32[]{:S(2)}) %all-to-all-start) | async-done | bytes 524320 | tf_op jit(solution)/shard_map/all_to_all | solution.py:767
  91.1 1.9 place.16
  93.8 1.8 collective-permute-start.7
  95.9 12.3 %collective-permute-done.7.refs_1_.refs_2_ = bf16[1024,256]{1,0:T(8,128)(2,1)S(1)} collective-permute-done((bf16[1024,256]{1,0:T(8,128)(2,1)S(1)}, bf16[1024,256]{1,0:T(8,128)(2,1)S(1)}, u32[]{:S(2)}, u32[]{:S(2)}) %collective-permute-start.7) | collective-permute-done | bytes 524320 | tf_op jit(solution)/shard_map/ppermute | solution.py:121
  112.2 4.3 middle.1
  116.5 1.8 collective-permute-start.13
  121.5 10.7 %collective-permute-done.13.refs_4_.refs_1_.refs_2_ = bf16[256,1152]{1,0:T(8,128)(2,1)} collective-permute-done((bf16[256,1152]{1,0:T(8,128)(2,1)}, bf16[256,1152]{1,0:T(8,128)(2,1)}, u32[]{:S(2)}, u32[]{:S(2)}) %collective-permute-start.13) | collective-permute-done | bytes 589856 | tf_op jit(solution)/shard_map/ppermute | solution.py:798
  132.2 1.8 collective-permute-start.15
  134.3 9.4 %pad_maximum_fusion.refs_3_.refs_5_ = bf16[3,4,1024,512]{3,2,1,0:T(8,128)(2,1)} fusion(bf16[3,4,1024,128]{3,2,1,0:T(8,128)(2,1)} %collective-permute-done.12, bf16[3,4,1024,128]{3,2,1,0:T(8,128)(2,1)} %collective-permute-done.11, bf16[3,4,1024,128]{3,2,1,0:T(8,128)(2,1)S(1)} %copy-done.1, bf16[1,4,1024,128]{3,2,1,0:T(8,128)(2,1)} %bitcast.56, ...), kind=kLoop, calls=%fused_computation | loop fusion | flops 75497472 | bytes 25165824 | tf_op jit(solution)/shard_map/concatenate | solution.py:775
  143.7 12.8 %expert_blocks.5 = (bf16[2,4,256,512]{3,2,1,0:T(8,128)(2,1)}, bf16[4,256,512]{2,1,0:T(8,128)(2,1)}, bf16[256,1024]{1,0:T(8,128)(2,1)}, bf16[256,1152]{1,0:T(8,128)(2,1)}) custom-call(s32[2]{0:T(128)} %pad_add_fusion.1.refs_0_, bf16[256,1152]{1,0:T(8,128)(2,1)} %get-tuple-element.123.refs_1_.refs_4_, bf16[256,1024]{1,0:T(8,128)(2,1)} %constant_dynamic-slice_fusion.refs_2_, ...), custom_call_target="tpu_custom_call" | custom-call | flops 6442450944 | bytes 12582912 | tf_op jit(solution)/shard_map/expert_blocks/pallas_call | solution.py:311
  157.7 1.9 place.17
  159.7 1.8 collective-permute-start.16
  161.5 1.9 place.19
  163.6 20.8 %expert_blocks.6 = (bf16[2,4,512,512]{3,2,1,0:T(8,128)(2,1)}, bf16[4,512,512]{2,1,0:T(8,128)(2,1)}, bf16[256,1024]{1,0:T(8,128)(2,1)}, bf16[256,1024]{1,0:T(8,12...) custom-call(s32[3]{0:T(128)} %pad_add_fusion.3.refs_0_, ...), custom_call_target="tpu_custom_call" | custom-call | flops 12884901888 | bytes 12582912 | tf_op jit(solution)/shard_map/expert_blocks/pallas_call | solution.py:311
  189.1 2.1 collective-permute-start.18
  191.2 20.6 %expert_blocks.7 = (bf16[2,4,512,512]{3,2,1,0:T(8,128)(2,1)}, bf16[4,512,512]{2,1,0:T(8,128)(2,1)}, bf16[256,1024]{1,0:T(8,128)(2,1)}, bf16[256,1024]{1,0:T(8,12...) custom-call(s32[3]{0:T(128)} %pad_add_fusion.4.refs_0_, ...), custom_call_target="tpu_custom_call" | custom-call | flops 12884901888 | bytes 12582912 | tf_op jit(solution)/shard_map/expert_blocks/pallas_call | solution.py:311
  212.7 20.6 %expert_blocks.8 = (bf16[2,4,512,512]{3,2,1,0:T(8,128)(2,1)}, bf16[4,512,512]{2,1,0:T(8,128)(2,1)}, bf16[256,1024]{1,0:T(8,128)(2,1)}, bf16[256,1024]{1,0:T(8,12...) custom-call(s32[3]{0:T(128)} %pad_add_fusion.2.refs_0_, bf16[256,1152]{1,0:T(8,128)(2,1)} %copy-done.60, ...), custom_call_target="tpu_custom_call" | custom-call | flops 12884901888 | bytes 12582912 | tf_op jit(solution)/shard_map/expert_blocks/pallas_call | solution.py:311
  237.4 12.8 %expert_blocks.9 = (bf16[2,4,256,512]{3,2,1,0:T(8,128)(2,1)}, bf16[4,256,512]{2,1,0:T(8,128)(2,1)}, bf16[256,1024]{1,0:T(8,128)(2,1)}, bf16[256,1152]{1,0:T(8,128)(2,1)}) custom-call(s32[2]{0:T(128)} %pad_add_fusion.5.refs_0_, bf16[256,1152]{1,0:T(8,128)(2,1)} %collective-permute-done.16.refs_1_.refs_6_.refs_8_, ...), custom_call_target="tpu_custom_call" | custom-call | flops 6442450944 | bytes 12582912 | tf_op jit(solution)/shard_map/expert_blocks/pallas_call | solution.py:311
  250.2 7.8 %collective-permute-done.21.refs_2_ = bf16[256,1024]{1,0:T(8,128)(2,1)S(1)} collective-permute-done((bf16[256,1024]{1,0:T(8,128)(2,1)}, bf16[256,1024]{1,0:T(8,128)(2,1)S(1)}, u32[]{:S(2)}, u32[]{:S(2)}) %collective-permute-start.21) | collective-permute-done | bytes 524320 | tf_op jit(solution)/shard_map/ppermute | solution.py:98
  260.5 4.4 add_pairs.6
  269.7 14.6 %weight_grad.3 = (bf16[4,1024,128]{2,1,0:T(8,128)(2,1)}, bf16[4,1024,128]{2,1,0:T(8,128)(2,1)}, bf16[4,1024,128]{2,1,0:T(8,128)(2,1)}, bf16[4,1024,128]{2,1,0:T(8,128)(2,1)}) custom-call(s32[8]{0:T(128)} %broadcast_1_refs_0_.2.refs_0_, bf16[256,1152]{1,0:T(8,128)(2,1)} %get-tuple-element.123.refs_1_.refs_4_, ...), custom_call_target="tpu_custom_call" | custom-call | flops 8589934592 | bytes 8388608 | tf_op jit(solution)/shard_map/weight_grad/pallas_call | solution.py:383
  284.9 3.2 collective-permute-done.25.refs_2_
  288.1 2.7 collective-permute-done.27.refs_6_
  291.8 4.3 add_pairs.7
  298.5 14.6 %weight_grad.4 = (bf16[4,1024,128]{2,1,0:T(8,128)(2,1)}, bf16[4,1024,128]{2,1,0:T(8,128)(2,1)}, bf16[4,1024,128]{2,1,0:T(8,128)(2,1)}, bf16[4,1024,128]{2,1,0:T(8,128)(2,1)}) custom-call(s32[8]{0:T(128)} %broadcast_1_refs_0_.2.refs_0_, bf16[256,1152]{1,0:T(8,128)(2,1)} %get-tuple-element.123.refs_1_.refs_4_, ...), custom_call_target="tpu_custom_call" | custom-call | flops 8589934592 | bytes 8388608 | tf_op jit(solution)/shard_map/weight_grad/pallas_call | solution.py:383
  315.1 2.7 collective-permute-done.29.refs_2_
  318.6 3.7 add_pairs.8
  322.3 14.3 %weight_grad.5 = (bf16[4,128,1024]{2,1,0:T(8,128)(2,1)}, bf16[4,128,1024]{2,1,0:T(8,128)(2,1)}, bf16[4,128,1024]{2,1,0:T(8,128)(2,1)}, bf16[4,128,1024]{2,1,0:T(8,128)(2,1)}) custom-call(s32[8]{0:T(128)} %stack.121.refs_0_, bf16[2048,1024]{1,0:T(8,128)(2,1)} %all-gather.4.cloned.1.call-done.refs_3_.refs_4_.refs_2_.refs_1_.refs_5_.refs_6_.refs_7_.refs_8_, ...), custom_call_target="tpu_custom_call" | custom-call | flops 8589934592 | bytes 8388608 | tf_op jit(solution)/shard_map/weight_grad/pallas_call | solution.py:383
  338.7 1.8 add_convert_fusion.1.refs_11_
  342.0 10.6 %collective-permute-done.37.refs_2_ = bf16[256,1152]{1,0:T(8,128)(2,1)S(1)} collective-permute-done((bf16[256,1152]{1,0:T(8,128)(2,1)}, bf16[256,1152]{1,0:T(8,128)(2,1)S(1)}, u32[]{:S(2)}, u32[]{:S(2)}) %collective-permute-start.37) | collective-permute-done | bytes 589856 | tf_op jit(solution)/shard_map/ppermute | solution.py:98
  354.4 5.5 %middle_backward.1 = (f32[256,1024]{1,0:T(8,128)}, bf16[256,1024]{1,0:T(8,128)(2,1)}, bf16[4,256,256]{2,1,0:T(8,128)(2,1)}, bf16[1024,128]{1,0:T(8,128)(2,1)}) custom-call(s32[1]{0:T(128)} %bitcast.4.s_ref, bf16[256,1152]{1,0:T(8,128)(2,1)} %get-tuple-element.161.refs_0_, bf16[256,1152]{1,0:T(8,128)(2,1)} %copy-done.39, bf16[256,1152]{1,0:T(8,128)(2,1)} %copy-done.38, ...), custom_call_target="tpu_custom_call" | custom-call | flops 1000000000 | bytes 4194304 | tf_op jit(solution)/shard_map/middle_backward/pallas_call | solution.py:486
  361.3 3.7 all-to-all-start.1
  365.5 2.9 add_convert_fusion.last_ref
  370.1 7.8 %collective-permute-done.45.refs_2_ = bf16[256,1024]{1,0:T(8,128)(2,1)S(1)} collective-permute-done((bf16[256,1024]{1,0:T(8,128)(2,1)}, bf16[256,1024]{1,0:T(8,128)(2,1)S(1)}, u32[]{:S(2)}, u32[]{:S(2)}) %collective-permute-start.45) | collective-permute-done | bytes 524320 | tf_op jit(solution)/shard_map/ppermute | solution.py:121
  377.9 5.6 %all-to-all-done.1 = bf16[4,256,256]{2,1,0:T(8,128)(2,1)S(1)} async-done(((bf16[4,256,256]{2,1,0:T(8,128)(2,1)}), bf16[4,256,256]{2,1,0:T(8,128)(2,1)S(1)}, u32[]{:S(2)}, u32[]{:S(2)}) %all-to-all-start.1) | async-done | bytes 524320 | tf_op jit(solution)/shard_map/all_to_all | solution.py:878
  384.3 18.7 %attention_backward.1.grad_ref = bf16[1024,512]{1,0:T(8,128)(2,1)} custom-call(s32[1]{0:T(128)} %constant.336.clone.1.s_ref.refs_0_, bf16[1024,512]{1,0:T(8,128)(2,1)} %get-tuple-element.160.rot_ref, bf16[1024,256]{1,0:T(8,128)(2,1)} %bitcast.65, f32[1024,128]{1,0:T(8,128)} %copy-done.11, f32[1024,128]{1,0:T(8,128)} %copy-done.12, ...), custom_call_target="tpu_custom_call" | custom-call | flops 20000000000 | bytes 4194304 | tf_op jit(solution)/shard_map/attention_backward/pallas_call | solution.py:486
  403.0 3.5 all-to-all-start.2
  408.6 6.1 %pack.1 = (bf16[1024,768]{1,0:T(8,128)(2,1)}, bf16[1024,128]{1,0:T(8,128)(2,1)}) custom-call(s32[1]{0:T(128)} %constant.336.clone.1.s_ref.refs_0_, bf16[1024,1024]{1,0:T(8,128)(2,1)} %get-tuple-element.172.a_ref, bf16[1024,512]{1,0:T(8,128)(2,1)} %attention_backward.1.grad_ref, bf16[1024,1024]{1,0:T(8,128)(2,1)} %copy-done.10, ...), custom_call_target="tpu_custom_call" | custom-call | flops 4000000000 | bytes 4194304 | tf_op jit(solution)/shard_map/pack/pallas_call | solution.py:486
  420.5 6.1 %collective-permute-done.50 = bf16[1024,128]{1,0:T(8,128)(2,1)S(1)} collective-permute-done((bf16[1024,128]{1,0:T(8,128)(2,1)S(1)}, bf16[1024,128]{1,0:T(8,128)(2,1)S(1)}, u32[]{:S(2)}, u32[]{:S(2)}) %collective-permute-start.50) | collective-permute-done | bytes 262176 | tf_op jit(solution)/shard_map/ppermute | solution.py:147
  427.7 5.4 %input_gradient.1.refs_1_.refs_0_ = bf16[256,1024]{1,0:T(8,128)(2,1)} custom-call(s32[1]{0:T(128)} %bitcast.4.s_ref, bf16[4,256,512]{2,1,0:T(8,128)(2,1)} %copy-done.32, bf16[4,1024,512]{2,1,0:T(8,128)(2,1)} %bitcast.58, f32[256,1024]{1,0:T(8,128)} %get-tuple-element.171.grad_mid_ref, bf16[1024,1024]{1,0:T(8,128)(2,1)} %x_ref.5, ...), custom_call_target="tpu_custom_call" | custom-call | flops 2000000000 | bytes 4194304 | tf_op jit(solution)/shard_map/input_gradient/pallas_call | solution.py:486
  438.5 3.4 collective-permute-done.51.refs_0_
  442.4 6.8 %collective-permute-done.52.refs_2_ = bf16[128,896]{1,0:T(8,128)(2,1)S(1)} collective-permute-done((bf16[128,896]{1,0:T(8,128)(2,1)S(1)}, bf16[128,896]{1,0:T(8,128)(2,1)S(1)}, u32[]{:S(2)}, u32[]{:S(2)}) %collective-permute-start.52) | collective-permute-done | bytes 229408 | tf_op jit(solution)/shard_map/ppermute | solution.py:98
  450.6 2.1 add_pairs.9
  454.8 4.2 collective-permute-done.53.refs_0_
  459.0 3.4 collective-permute-done.54.refs_2_
  462.9 12.0 %adamw.2 = (f32[4,2,1024,128]{3,2,1,0:T(8,128)}, f32[4,2,1024,128]{3,2,1,0:T(8,128)}, f32[4,2,1024,128]{3,2,1,0:T(8,128)}) custom-call(f32[4,2,1024,128]{3,2,1,0:T(8,128)} %refs_0_.1, f32[4,2,1024,128]{3,2,1,0:T(8,128)} %refs_1_.1, f32[4,2,1024,128]{3,2,1,0:T(8,128)} %refs_2_.1, bf16[4,1024,128]{2,1,0:T(8,128)(2,1)} %get-tuple-element.155.refs_4_.refs_3_, ...), custom_call_target="tpu_custom_call" | custom-call | flops 20971520 | bytes 29360128 | tf_op jit(solution)/shard_map/adamw/pallas_call | solution.py:425
  474.9 2.1 add_pairs.10
  478.6 7.3 %adamw.3 = (f32[4,1,128,1024]{3,2,1,0:T(8,128)}, f32[4,1,128,1024]{3,2,1,0:T(8,128)}, f32[4,1,128,1024]{3,2,1,0:T(8,128)}) custom-call(f32[4,1,128,1024]{3,2,1,0:T(8,128)} %bitcast.57, f32[4,1,128,1024]{3,2,1,0:T(8,128)} %bitcast.61, f32[4,1,128,1024]{3,2,1,0:T(8,128)} %bitcast.62, bf16[4,128,1024]{2,1,0:T(8,128)(2,1)} %get-tuple-element.165.refs_9_.refs_3_, ...), custom_call_target="tpu_custom_call" | custom-call | flops 10485760 | bytes 14680064 | tf_op jit(solution)/shard_map/adamw/pallas_call | solution.py:425
  486.5 1.8 add_pairs.11
  492.1 2.5 place.20
  496.0 2.9 adamw_rest.1
  503.4 2.5 place.22
  (270 shorter events, 92.9 us)
Async XLA Ops:
  7.2 156.4 %all-gather.4.cloned.1.call-start = ((), (), s32[]{:S(2)}) async-start(), calls=%async_computation.3 | async-start | bytes 4718592 | tf_op jit(solution)/shard_map/all_gather | solution.py:758
  14.1 77.0 %collective-permute-start.10 = (bf16[3,4,1024,128]{3,2,1,0:T(8,128)(2,1)}, bf16[3,4,1024,128]{3,2,1,0:T(8,128)(2,1)S(1)}, u32[]{:S(2)}, u32[]{:S(2)}) collective-permute-start(bf16[3,4,1024,128]{3,2,1,0:T(8,128)(2,1)} %pad_maximum_fusion.1), channel_id=1, source_target_pairs={{0,2},{1,3},{2,0},{3,1},{4,6},{5,7},{6,4},{7,5},{8,10},{9,11},{10,... | collective-permute-start | bytes 9437192 | tf_op jit(solution)/shard_map/ppermute | solution.py:718
  20.4 7.2 %collective-permute-start = (bf16[128,896]{1,0:T(8,128)(2,1)S(1)}, bf16[128,896]{1,0:T(8,128)(2,1)}, u32[]{:S(2)}, u32[]{:S(2)}) collective-permute-start(bf16[128,896]{1,0:T(8,128)(2,1)S(1)} %concatenate.12.refs_5_), channel_id=1, source_target_pairs={{0,8},{8,16},{16,24},{24,28},{28,20},{20,12},{12,4},{4,0},{1,9},{9... | collective-permute-start | bytes 688136 | tf_op jit(solution)/shard_map/ppermute | solution.py:87
  22.0 7.2 %collective-permute-start.4 = (bf16[128,896]{1,0:T(8,128)(2,1)S(1)}, bf16[128,896]{1,0:T(8,128)(2,1)}, u32[]{:S(2)}, u32[]{:S(2)}) collective-permute-start(bf16[128,896]{1,0:T(8,128)(2,1)S(1)} %concatenate.12.refs_5_), channel_id=1, source_target_pairs={{0,4},{8,0},{16,8},{24,16},{28,24},{20,28},{12,20},{4,12},{1,5},{9... | collective-permute-start | bytes 688136 | tf_op jit(solution)/shard_map/ppermute | solution.py:90
  27.6 6.5 %collective-permute-start.1 = (bf16[128,896]{1,0:T(8,128)(2,1)}, bf16[128,896]{1,0:T(8,128)(2,1)}, u32[]{:S(2)}, u32[]{:S(2)}) collective-permute-start(bf16[128,896]{1,0:T(8,128)(2,1)} %collective-permute-done.refs_4_), channel_id=1, source_target_pairs={{0,8},{8,16},{16,24},{24,28},{28,20},{20,12},{12,4},{4,0},{1,9},{9... | collective-permute-start | bytes 688136 | tf_op jit(solution)/shard_map/ppermute | solution.py:87
  29.2 8.4 %collective-permute-start.5 = (bf16[128,896]{1,0:T(8,128)(2,1)}, bf16[128,896]{1,0:T(8,128)(2,1)}, u32[]{:S(2)}, u32[]{:S(2)}) collective-permute-start(bf16[128,896]{1,0:T(8,128)(2,1)} %collective-permute-done.4.refs_6_), channel_id=1, source_target_pairs={{0,4},{8,0},{16,8},{24,16},{28,24},{20,28},{12,20},{4,12},{1,5},{9... | collective-permute-start | bytes 688136 | tf_op jit(solution)/shard_map/ppermute | solution.py:90
  34.1 6.4 %collective-permute-start.2 = (bf16[128,896]{1,0:T(8,128)(2,1)}, bf16[128,896]{1,0:T(8,128)(2,1)}, u32[]{:S(2)}, u32[]{:S(2)}) collective-permute-start(bf16[128,896]{1,0:T(8,128)(2,1)} %collective-permute-done.1.refs_3_), channel_id=1, source_target_pairs={{0,8},{8,16},{16,24},{24,28},{28,20},{20,12},{12,4},{4,0},{1,9},{9... | collective-permute-start | bytes 688136 | tf_op jit(solution)/shard_map/ppermute | solution.py:87
  37.6 11.5 %collective-permute-start.6 = (bf16[128,896]{1,0:T(8,128)(2,1)}, bf16[128,896]{1,0:T(8,128)(2,1)}, u32[]{:S(2)}, u32[]{:S(2)}) collective-permute-start(bf16[128,896]{1,0:T(8,128)(2,1)} %collective-permute-done.5.refs_7_), channel_id=1, source_target_pairs={{0,4},{8,0},{16,8},{24,16},{28,24},{20,28},{12,20},{4,12},{1,5},{9... | collective-permute-start | bytes 688136 | tf_op jit(solution)/shard_map/ppermute | solution.py:90
  40.5 8.6 %collective-permute-start.3 = (bf16[128,896]{1,0:T(8,128)(2,1)}, bf16[128,896]{1,0:T(8,128)(2,1)}, u32[]{:S(2)}, u32[]{:S(2)}) collective-permute-start(bf16[128,896]{1,0:T(8,128)(2,1)} %collective-permute-done.2.refs_2_), channel_id=1, source_target_pairs={{0,8},{8,16},{16,24},{24,28},{28,20},{20,12},{12,4},{4,0},{1,9},{9... | collective-permute-start | bytes 688136 | tf_op jit(solution)/shard_map/ppermute | solution.py:87
  69.3 21.8 %all-to-all-start = ((bf16[4,256,256]{2,1,0:T(8,128)(2,1)}), bf16[4,256,256]{2,1,0:T(8,128)(2,1)}, u32[]{:S(2)}, u32[]{:S(2)}) async-start(bf16[4,256,256]{2,1,0:T(8,128)(2,1)} %bitcast.64), calls=%async_computation | async-start | bytes 1048576 | tf_op jit(solution)/shard_map/all_to_all | solution.py:767
  73.5 353.3 %all-gather.6.cloned.1.call-start = ((), (), s32[]{:S(2)}) async-start(), calls=%async_computation.4 | async-start | bytes 5242880 | tf_op jit(solution)/shard_map/all_gather | solution.py:903
  73.7 60.6 %collective-permute-start.11 = (bf16[3,4,1024,128]{3,2,1,0:T(8,128)(2,1)}, bf16[3,4,1024,128]{3,2,1,0:T(8,128)(2,1)}, u32[]{:S(2)}, u32[]{:S(2)}) collective-permute-start(bf16[3,4,1024,128]{3,2,1,0:T(8,128)(2,1)} %pad_maximum_fusion.1), channel_id=1, source_target_pairs={{0,1},{1,0},{2,3},{3,2},{4,5},{5,4},{6,7},{7,6},{8,9},{9,8},{10,11... | collective-permute-start | bytes 9437192 | tf_op jit(solution)/shard_map/ppermute | solution.py:772
  93.8 40.5 %collective-permute-start.12 = (bf16[3,4,1024,128]{3,2,1,0:T(8,128)(2,1)}, bf16[3,4,1024,128]{3,2,1,0:T(8,128)(2,1)}, u32[]{:S(2)}, u32[]{:S(2)}) collective-permute-start(bf16[3,4,1024,128]{3,2,1,0:T(8,128)(2,1)} %bitcast.26), channel_id=1, source_target_pairs={{0,1},{1,0},{2,3},{3,2},{4,5},{5,4},{6,7},{7,6},{8,9},{9,8},{10,11... | collective-permute-start | bytes 9437192 | tf_op jit(solution)/shard_map/ppermute | solution.py:772
  93.8 14.3 %collective-permute-start.7 = (bf16[1024,256]{1,0:T(8,128)(2,1)S(1)}, bf16[1024,256]{1,0:T(8,128)(2,1)S(1)}, u32[]{:S(2)}, u32[]{:S(2)}) collective-permute-start(bf16[1024,256]{1,0:T(8,128)(2,1)S(1)} %copy-done.8), channel_id=1, source_target_pairs={{0,2},{1,3},{2,0},{3,1},{4,6},{5,7},{6,4},{7,5},{8,10},{9,11},{10,... | collective-permute-start | bytes 1572872 | tf_op jit(solution)/shard_map/ppermute | solution.py:121
  95.7 13.8 %collective-permute-start.8 = (bf16[1024,256]{1,0:T(8,128)(2,1)S(1)}, bf16[1024,256]{1,0:T(8,128)(2,1)S(1)}, u32[]{:S(2)}, u32[]{:S(2)}) collective-permute-start(bf16[1024,256]{1,0:T(8,128)(2,1)S(1)} %place.13), channel_id=1, source_target_pairs={{0,1},{1,0},{2,3},{3,2},{4,5},{5,4},{6,7},{7,6},{8,9},{9,8},{10,11... | collective-permute-start | bytes 1572872 | tf_op jit(solution)/shard_map/ppermute | solution.py:124
  116.5 15.7 %collective-permute-start.13 = (bf16[256,1152]{1,0:T(8,128)(2,1)}, bf16[256,1152]{1,0:T(8,128)(2,1)}, u32[]{:S(2)}, u32[]{:S(2)}) collective-permute-start(bf16[256,1152]{1,0:T(8,128)(2,1)} %get-tuple-element.123.refs_1_.refs_4_), channel_id=1, source_target_pairs={{0,8},{8,16},{16,24},{24,28},{28,20},{20,12},{12,4},{4,0},{1,9},{9... | collective-permute-start | bytes 1769480 | tf_op jit(solution)/shard_map/ppermute | solution.py:798
  118.4 15.7 %collective-permute-start.14 = (bf16[256,1152]{1,0:T(8,128)(2,1)}, bf16[256,1152]{1,0:T(8,128)(2,1)}, u32[]{:S(2)}, u32[]{:S(2)}) collective-permute-start(bf16[256,1152]{1,0:T(8,128)(2,1)} %get-tuple-element.123.refs_1_.refs_4_), channel_id=1, source_target_pairs={{0,4},{8,0},{16,8},{24,16},{28,24},{20,28},{12,20},{4,12},{1,5},{9... | collective-permute-start | bytes 1769480 | tf_op jit(solution)/shard_map/ppermute | solution.py:798
  132.2 24.3 %collective-permute-start.15 = (bf16[256,1152]{1,0:T(8,128)(2,1)}, bf16[256,1152]{1,0:T(8,128)(2,1)}, u32[]{:S(2)}, u32[]{:S(2)}) collective-permute-start(bf16[256,1152]{1,0:T(8,128)(2,1)} %collective-permute-done.13.refs_4_.refs_1_.refs_2_), channel_id=1, source_target_pairs={{0,8},{8,16},{16,24},{24,28},{28,20},{20,12},{12,4},{4,0},{1,9},{9... | collective-permute-start | bytes 1769480 | tf_op jit(solution)/shard_map/ppermute | solution.py:798
  134.0 27.4 %collective-permute-start.17 = (bf16[256,1152]{1,0:T(8,128)(2,1)}, bf16[256,1152]{1,0:T(8,128)(2,1)}, u32[]{:S(2)}, u32[]{:S(2)}) collective-permute-start(bf16[256,1152]{1,0:T(8,128)(2,1)} %collective-permute-done.14.refs_5_.refs_2_.refs_3_), channel_id=1, source_target_pairs={{0,4},{8,0},{16,8},{24,16},{28,24},{20,28},{12,20},{4,12},{1,5},{9... | collective-permute-start | bytes 1769480 | tf_op jit(solution)/shard_map/ppermute | solution.py:798
  159.7 27.4 %collective-permute-start.16 = (bf16[256,1152]{1,0:T(8,128)(2,1)}, bf16[256,1152]{1,0:T(8,128)(2,1)}, u32[]{:S(2)}, u32[]{:S(2)}) collective-permute-start(bf16[256,1152]{1,0:T(8,128)(2,1)} %place.17), channel_id=1, source_target_pairs={{0,8},{8,16},{16,24},{24,28},{28,20},{20,12},{12,4},{4,0},{1,9},{9... | collective-permute-start | bytes 1769480 | tf_op jit(solution)/shard_map/ppermute | solution.py:798
  163.4 27.9 %collective-permute-start.19 = (bf16[256,1152]{1,0:T(8,128)(2,1)}, bf16[256,1152]{1,0:T(8,128)(2,1)}, u32[]{:S(2)}, u32[]{:S(2)}) collective-permute-start(bf16[256,1152]{1,0:T(8,128)(2,1)} %place.19), channel_id=1, source_target_pairs={{0,4},{8,0},{16,8},{24,16},{28,24},{20,28},{12,20},{4,12},{1,5},{9... | collective-permute-start | bytes 1769480 | tf_op jit(solution)/shard_map/ppermute | solution.py:798
  189.1 22.8 %collective-permute-start.18 = (bf16[256,1152]{1,0:T(8,128)(2,1)S(1)}, bf16[256,1152]{1,0:T(8,128)(2,1)S(1)}, u32[]{:S(2)}, u32[]{:S(2)}) collective-permute-start(bf16[256,1152]{1,0:T(8,128)(2,1)S(1)} %place.18), channel_id=1, source_target_pairs={{0,8},{8,16},{16,24},{24,28},{28,20},{20,12},{12,4},{4,0},{1,9},{9... | collective-permute-start | bytes 1769480 | tf_op jit(solution)/shard_map/ppermute | solution.py:798
  233.3 26.0 %collective-permute-start.20 = (bf16[256,1152]{1,0:T(8,128)(2,1)}, bf16[256,1152]{1,0:T(8,128)(2,1)S(1)}, u32[]{:S(2)}, u32[]{:S(2)}) collective-permute-start(bf16[256,1152]{1,0:T(8,128)(2,1)} %get-tuple-element.128), channel_id=1, source_target_pairs={{0,4},{8,0},{16,8},{24,16},{28,24},{20,28},{12,20},{4,12},{1,5},{9... | collective-permute-start | bytes 1769480 | tf_op jit(solution)/shard_map/ppermute | solution.py:98
  233.7 24.4 %collective-permute-start.21 = (bf16[256,1024]{1,0:T(8,128)(2,1)}, bf16[256,1024]{1,0:T(8,128)(2,1)S(1)}, u32[]{:S(2)}, u32[]{:S(2)}) collective-permute-start(bf16[256,1024]{1,0:T(8,128)(2,1)} %get-tuple-element.131), channel_id=1, source_target_pairs={{0,4},{8,0},{16,8},{24,16},{28,24},{20,28},{12,20},{4,12},{1,5},{9... | collective-permute-start | bytes 1572872 | tf_op jit(solution)/shard_map/ppermute | solution.py:98
  235.3 24.1 %collective-permute-start.22 = (bf16[256,1152]{1,0:T(8,128)(2,1)}, bf16[256,1152]{1,0:T(8,128)(2,1)S(1)}, u32[]{:S(2)}, u32[]{:S(2)}) collective-permute-start(bf16[256,1152]{1,0:T(8,128)(2,1)} %get-tuple-element.133), channel_id=1, source_target_pairs={{0,8},{8,16},{16,24},{24,28},{28,20},{20,12},{12,4},{4,0},{1,9},{9... | collective-permute-start | bytes 1769480 | tf_op jit(solution)/shard_map/ppermute | solution.py:98
  235.7 23.7 %collective-permute-start.23 = (bf16[256,1024]{1,0:T(8,128)(2,1)}, bf16[256,1024]{1,0:T(8,128)(2,1)S(1)}, u32[]{:S(2)}, u32[]{:S(2)}) collective-permute-start(bf16[256,1024]{1,0:T(8,128)(2,1)} %get-tuple-element.135), channel_id=1, source_target_pairs={{0,8},{8,16},{16,24},{24,28},{28,20},{20,12},{12,4},{4,0},{1,9},{9... | collective-permute-start | bytes 1572872 | tf_op jit(solution)/shard_map/ppermute | solution.py:98
  264.9 25.8 %collective-permute-start.24 = (bf16[256,1152]{1,0:T(8,128)(2,1)}, bf16[256,1152]{1,0:T(8,128)(2,1)S(1)}, u32[]{:S(2)}, u32[]{:S(2)}) collective-permute-start(bf16[256,1152]{1,0:T(8,128)(2,1)} %get-tuple-element.137.refs_14_), channel_id=1, source_target_pairs={{0,4},{8,0},{16,8},{24,16},{28,24},{20,28},{12,20},{4,12},{1,5},{9... | collective-permute-start | bytes 1769480 | tf_op jit(solution)/shard_map/ppermute | solution.py:98
  266.5 21.6 %collective-permute-start.25 = (bf16[256,1024]{1,0:T(8,128)(2,1)}, bf16[256,1024]{1,0:T(8,128)(2,1)S(1)}, u32[]{:S(2)}, u32[]{:S(2)}) collective-permute-start(bf16[256,1024]{1,0:T(8,128)(2,1)} %get-tuple-element.139), channel_id=1, source_target_pairs={{0,4},{8,0},{16,8},{24,16},{28,24},{20,28},{12,20},{4,12},{1,5},{9... | collective-permute-start | bytes 1572872 | tf_op jit(solution)/shard_map/ppermute | solution.py:98
  268.1 22.7 %collective-permute-start.26 = (bf16[256,1152]{1,0:T(8,128)(2,1)}, bf16[256,1152]{1,0:T(8,128)(2,1)S(1)}, u32[]{:S(2)}, u32[]{:S(2)}) collective-permute-start(bf16[256,1152]{1,0:T(8,128)(2,1)} %get-tuple-element.141), channel_id=1, source_target_pairs={{0,8},{8,16},{16,24},{24,28},{28,20},{20,12},{12,4},{4,0},{1,9},{9... | collective-permute-start | bytes 1769480 | tf_op jit(solution)/shard_map/ppermute | solution.py:98
  268.5 22.2 %collective-permute-start.27 = (bf16[256,1024]{1,0:T(8,128)(2,1)}, bf16[256,1024]{1,0:T(8,128)(2,1)}, u32[]{:S(2)}, u32[]{:S(2)}) collective-permute-start(bf16[256,1024]{1,0:T(8,128)(2,1)} %get-tuple-element.143), channel_id=1, source_target_pairs={{0,8},{8,16},{16,24},{24,28},{28,20},{20,12},{12,4},{4,0},{1,9},{9... | collective-permute-start | bytes 1572872 | tf_op jit(solution)/shard_map/ppermute | solution.py:98
  284.2 28.9 %collective-permute-start.30 = (bf16[4,1024,128]{2,1,0:T(8,128)(2,1)}, bf16[4,1024,128]{2,1,0:T(8,128)(2,1)S(1)}, u32[]{:S(2)}, u32[]{:S(2)}) collective-permute-start(bf16[4,1024,128]{2,1,0:T(8,128)(2,1)} %get-tuple-element.157), channel_id=1, source_target_pairs={{0,1},{1,0},{2,3},{3,2},{4,5},{5,4},{6,7},{7,6},{8,9},{9,8},{10,11... | collective-permute-start | bytes 3145736 | tf_op jit(solution)/shard_map/ppermute | solution.py:130
  296.1 21.7 %collective-permute-start.28 = (bf16[256,1152]{1,0:T(8,128)(2,1)}, bf16[256,1152]{1,0:T(8,128)(2,1)}, u32[]{:S(2)}, u32[]{:S(2)}) collective-permute-start(bf16[256,1152]{1,0:T(8,128)(2,1)} %get-tuple-element.151.refs_14_), channel_id=1, source_target_pairs={{0,4},{8,0},{16,8},{24,16},{28,24},{20,28},{12,20},{4,12},{1,5},{9... | collective-permute-start | bytes 1769480 | tf_op jit(solution)/shard_map/ppermute | solution.py:98
  297.7 20.1 %collective-permute-start.29 = (bf16[256,1024]{1,0:T(8,128)(2,1)}, bf16[256,1024]{1,0:T(8,128)(2,1)S(1)}, u32[]{:S(2)}, u32[]{:S(2)}) collective-permute-start(bf16[256,1024]{1,0:T(8,128)(2,1)} %get-tuple-element.153), channel_id=1, source_target_pairs={{0,4},{8,0},{16,8},{24,16},{28,24},{20,28},{12,20},{4,12},{1,5},{9... | collective-permute-start | bytes 1572872 | tf_op jit(solution)/shard_map/ppermute | solution.py:98
  313.1 25.7 %collective-permute-start.38 = (bf16[4,1024,128]{2,1,0:T(8,128)(2,1)}, bf16[4,1024,128]{2,1,0:T(8,128)(2,1)}, u32[]{:S(2)}, u32[]{:S(2)}) collective-permute-start(bf16[4,1024,128]{2,1,0:T(8,128)(2,1)} %get-tuple-element.167), channel_id=1, source_target_pairs={{0,1},{1,0},{2,3},{3,2},{4,5},{5,4},{6,7},{7,6},{8,9},{9,8},{10,11... | collective-permute-start | bytes 3145736 | tf_op jit(solution)/shard_map/ppermute | solution.py:130
  313.5 39.3 %collective-permute-start.39 = (bf16[4,1024,128]{2,1,0:T(8,128)(2,1)S(1)}, bf16[4,1024,128]{2,1,0:T(8,128)(2,1)S(1)}, u32[]{:S(2)}, u32[]{:S(2)}) collective-permute-start(bf16[4,1024,128]{2,1,0:T(8,128)(2,1)S(1)} %add_convert_fusion.2.refs_5_.refs_10_), channel_id=1, source_target_pairs={{0,2},{1,3},{2,0},{3,1},{4,6},{5,7},{6,4},{7,5},{8,10},{9,11},{10,... | collective-permute-start | bytes 3145736 | tf_op jit(solution)/shard_map/ppermute | solution.py:139
  336.6 28.9 %collective-permute-start.41 = (bf16[4,128,1024]{2,1,0:T(8,128)(2,1)}, bf16[4,128,1024]{2,1,0:T(8,128)(2,1)}, u32[]{:S(2)}, u32[]{:S(2)}) collective-permute-start(bf16[4,128,1024]{2,1,0:T(8,128)(2,1)} %get-tuple-element.170), channel_id=1, source_target_pairs={{0,1},{1,0},{2,3},{3,2},{4,5},{5,4},{6,7},{7,6},{8,9},{9,8},{10,11... | collective-permute-start | bytes 3145736 | tf_op jit(solution)/shard_map/ppermute | solution.py:130
  336.7 15.9 %collective-permute-start.37 = (bf16[256,1152]{1,0:T(8,128)(2,1)}, bf16[256,1152]{1,0:T(8,128)(2,1)S(1)}, u32[]{:S(2)}, u32[]{:S(2)}) collective-permute-start(bf16[256,1152]{1,0:T(8,128)(2,1)} %get-tuple-element.163), channel_id=1, source_target_pairs={{0,8},{8,16},{16,24},{24,28},{28,20},{20,12},{12,4},{4,0},{1,9},{9... | collective-permute-start | bytes 1769480 | tf_op jit(solution)/shard_map/ppermute | solution.py:98
  337.2 15.6 %collective-permute-start.36 = (bf16[256,1152]{1,0:T(8,128)(2,1)}, bf16[256,1152]{1,0:T(8,128)(2,1)S(1)}, u32[]{:S(2)}, u32[]{:S(2)}) collective-permute-start(bf16[256,1152]{1,0:T(8,128)(2,1)} %get-tuple-element.162.refs_14_), channel_id=1, source_target_pairs={{0,4},{8,0},{16,8},{24,16},{28,24},{20,28},{12,20},{4,12},{1,5},{9... | collective-permute-start | bytes 1769480 | tf_op jit(solution)/shard_map/ppermute | solution.py:98
  340.6 43.0 %collective-permute-start.40 = (bf16[4,1024,128]{2,1,0:T(8,128)(2,1)S(1)}, bf16[4,1024,128]{2,1,0:T(8,128)(2,1)}, u32[]{:S(2)}, u32[]{:S(2)}) collective-permute-start(bf16[4,1024,128]{2,1,0:T(8,128)(2,1)S(1)} %add_convert_fusion.1.refs_11_), channel_id=1, source_target_pairs={{0,2},{1,3},{2,0},{3,1},{4,6},{5,7},{6,4},{7,5},{8,10},{9,11},{10,... | collective-permute-start | bytes 3145736 | tf_op jit(solution)/shard_map/ppermute | solution.py:139
  359.8 18.1 %collective-permute-start.45 = (bf16[256,1024]{1,0:T(8,128)(2,1)}, bf16[256,1024]{1,0:T(8,128)(2,1)S(1)}, u32[]{:S(2)}, u32[]{:S(2)}) collective-permute-start(bf16[256,1024]{1,0:T(8,128)(2,1)} %get-tuple-element.173.refs_1_), channel_id=1, source_target_pairs={{0,2},{1,3},{2,0},{3,1},{4,6},{5,7},{6,4},{7,5},{8,10},{9,11},{10,... | collective-permute-start | bytes 1572872 | tf_op jit(solution)/shard_map/ppermute | solution.py:121
  361.3 22.3 %all-to-all-start.1 = ((bf16[4,256,256]{2,1,0:T(8,128)(2,1)}), bf16[4,256,256]{2,1,0:T(8,128)(2,1)S(1)}, u32[]{:S(2)}, u32[]{:S(2)}) async-start(bf16[4,256,256]{2,1,0:T(8,128)(2,1)} %get-tuple-element.168), calls=%async_computation.1 | async-start | bytes 1048576 | tf_op jit(solution)/shard_map/all_to_all | solution.py:878
  364.9 41.6 %collective-permute-start.46 = (bf16[256,1024]{1,0:T(8,128)(2,1)}, bf16[256,1024]{1,0:T(8,128)(2,1)S(1)}, u32[]{:S(2)}, u32[]{:S(2)}) collective-permute-start(bf16[256,1024]{1,0:T(8,128)(2,1)} %get-tuple-element.173.refs_1_), channel_id=1, source_target_pairs={{0,1},{1,0},{2,3},{3,2},{4,5},{5,4},{6,7},{7,6},{8,9},{9,8},{10,11... | collective-permute-start | bytes 1572872 | tf_op jit(solution)/shard_map/ppermute | solution.py:124
  368.4 40.2 %collective-permute-start.48 = (bf16[4,128,1024]{2,1,0:T(8,128)(2,1)}, bf16[4,128,1024]{2,1,0:T(8,128)(2,1)}, u32[]{:S(2)}, u32[]{:S(2)}) collective-permute-start(bf16[4,128,1024]{2,1,0:T(8,128)(2,1)} %add_convert_fusion.last_ref), channel_id=1, source_target_pairs={{0,2},{1,3},{2,0},{3,1},{4,6},{5,7},{6,4},{7,5},{8,10},{9,11},{10,... | collective-permute-start | bytes 3145736 | tf_op jit(solution)/shard_map/ppermute | solution.py:139
  377.9 28.7 %collective-permute-start.47 = (bf16[256,1024]{1,0:T(8,128)(2,1)S(1)}, bf16[256,1024]{1,0:T(8,128)(2,1)S(1)}, u32[]{:S(2)}, u32[]{:S(2)}) collective-permute-start(bf16[256,1024]{1,0:T(8,128)(2,1)S(1)} %collective-permute-done.45.refs_2_), channel_id=1, source_target_pairs={{0,1},{1,0},{2,3},{3,2},{4,5},{5,4},{6,7},{7,6},{8,9},{9,8},{10,11... | collective-permute-start | bytes 1572872 | tf_op jit(solution)/shard_map/ppermute | solution.py:124
  403.0 23.7 %all-to-all-start.2 = ((bf16[4,256,512]{2,1,0:T(8,128)(2,1)}), bf16[4,256,512]{2,1,0:T(8,128)(2,1)S(1)}, u32[]{:S(2)}, u32[]{:S(2)}) async-start(bf16[4,256,512]{2,1,0:T(8,128)(2,1)} %bitcast.63), calls=%async_computation.2 | async-start | bytes 2097152 | tf_op jit(solution)/shard_map/all_to_all | solution.py:891
  415.2 18.7 %collective-permute-start.32 = (bf16[256,1024]{1,0:T(8,128)(2,1)}, bf16[256,1024]{1,0:T(8,128)(2,1)}, u32[]{:S(2)}, u32[]{:S(2)}) collective-permute-start(bf16[256,1024]{1,0:T(8,128)(2,1)} %get-tuple-element.159), channel_id=1, source_target_pairs={{0,8},{8,16},{16,24},{24,28},{28,20},{20,12},{12,4},{4,0},{1,9},{9... | collective-permute-start | bytes 1572872 | tf_op jit(solution)/shard_map/ppermute | solution.py:98
  415.6 19.8 %collective-permute-start.31 = (bf16[256,1024]{1,0:T(8,128)(2,1)}, bf16[256,1024]{1,0:T(8,128)(2,1)}, u32[]{:S(2)}, u32[]{:S(2)}) collective-permute-start(bf16[256,1024]{1,0:T(8,128)(2,1)} %get-tuple-element.158), channel_id=1, source_target_pairs={{0,4},{8,0},{16,8},{24,16},{28,24},{20,28},{12,20},{4,12},{1,5},{9... | collective-permute-start | bytes 1572872 | tf_op jit(solution)/shard_map/ppermute | solution.py:98
  418.2 8.4 %collective-permute-start.50 = (bf16[1024,128]{1,0:T(8,128)(2,1)S(1)}, bf16[1024,128]{1,0:T(8,128)(2,1)S(1)}, u32[]{:S(2)}, u32[]{:S(2)}) collective-permute-start(bf16[1024,128]{1,0:T(8,128)(2,1)S(1)} %add.274), channel_id=1, source_target_pairs={{0,2},{1,3},{2,0},{3,1},{4,6},{5,7},{6,4},{7,5},{8,10},{9,11},{10,... | collective-permute-start | bytes 786440 | tf_op jit(solution)/shard_map/ppermute | solution.py:147
  420.0 32.7 %collective-permute-start.56 = (bf16[4,1024,128]{2,1,0:T(8,128)(2,1)}, bf16[4,1024,128]{2,1,0:T(8,128)(2,1)}, u32[]{:S(2)}, u32[]{:S(2)}) collective-permute-start(bf16[4,1024,128]{2,1,0:T(8,128)(2,1)} %get-tuple-element.187), channel_id=1, source_target_pairs={{0,1},{1,0},{2,3},{3,2},{4,5},{5,4},{6,7},{7,6},{8,9},{9,8},{10,11... | collective-permute-start | bytes 3145736 | tf_op jit(solution)/shard_map/ppermute | solution.py:130
  420.0 34.2 %collective-permute-start.55 = (bf16[4,1024,128]{2,1,0:T(8,128)(2,1)}, bf16[4,1024,128]{2,1,0:T(8,128)(2,1)}, u32[]{:S(2)}, u32[]{:S(2)}) collective-permute-start(bf16[4,1024,128]{2,1,0:T(8,128)(2,1)} %get-tuple-element.186), channel_id=1, source_target_pairs={{0,1},{1,0},{2,3},{3,2},{4,5},{5,4},{6,7},{7,6},{8,9},{9,8},{10,11... | collective-permute-start | bytes 3145736 | tf_op jit(solution)/shard_map/ppermute | solution.py:130
  426.6 50.4 %collective-permute-start.58 = (bf16[4,128,1024]{2,1,0:T(8,128)(2,1)}, bf16[4,128,1024]{2,1,0:T(8,128)(2,1)}, u32[]{:S(2)}, u32[]{:S(2)}) collective-permute-start(bf16[4,128,1024]{2,1,0:T(8,128)(2,1)} %get-tuple-element.191), channel_id=1, source_target_pairs={{0,1},{1,0},{2,3},{3,2},{4,5},{5,4},{6,7},{7,6},{8,9},{9,8},{10,11... | collective-permute-start | bytes 3145736 | tf_op jit(solution)/shard_map/ppermute | solution.py:130
  433.9 8.1 %collective-permute-start.51 = (bf16[128,896]{1,0:T(8,128)(2,1)S(1)}, bf16[128,896]{1,0:T(8,128)(2,1)S(1)}, u32[]{:S(2)}, u32[]{:S(2)}) collective-permute-start(bf16[128,896]{1,0:T(8,128)(2,1)S(1)} %get-tuple-element.178), channel_id=1, source_target_pairs={{0,4},{8,0},{16,8},{24,16},{28,24},{20,28},{12,20},{4,12},{1,5},{9... | collective-permute-start | bytes 688136 | tf_op jit(solution)/shard_map/ppermute | solution.py:98
  437.1 17.1 %collective-permute-start.33 = (bf16[256,1024]{1,0:T(8,128)(2,1)S(1)}, bf16[256,1024]{1,0:T(8,128)(2,1)S(1)}, u32[]{:S(2)}, u32[]{:S(2)}) collective-permute-start(bf16[256,1024]{1,0:T(8,128)(2,1)S(1)} %add_convert_fusion.3.refs_1_), channel_id=1, source_target_pairs={{0,2},{1,3},{2,0},{3,1},{4,6},{5,7},{6,4},{7,5},{8,10},{9,11},{10,... | collective-permute-start | bytes 1572872 | tf_op jit(solution)/shard_map/ppermute | solution.py:121
  441.9 7.2 %collective-permute-start.52 = (bf16[128,896]{1,0:T(8,128)(2,1)S(1)}, bf16[128,896]{1,0:T(8,128)(2,1)S(1)}, u32[]{:S(2)}, u32[]{:S(2)}) collective-permute-start(bf16[128,896]{1,0:T(8,128)(2,1)S(1)} %get-tuple-element.180), channel_id=1, source_target_pairs={{0,8},{8,16},{16,24},{24,28},{28,20},{20,12},{12,4},{4,0},{1,9},{9... | collective-permute-start | bytes 688136 | tf_op jit(solution)/shard_map/ppermute | solution.py:98
  449.2 13.2 %collective-permute-start.42 = (bf16[256,1024]{1,0:T(8,128)(2,1)}, bf16[256,1024]{1,0:T(8,128)(2,1)S(1)}, u32[]{:S(2)}, u32[]{:S(2)}) collective-permute-start(bf16[256,1024]{1,0:T(8,128)(2,1)} %input_gradient.1.refs_1_.refs_0_), channel_id=1, source_target_pairs={{0,2},{1,3},{2,0},{3,1},{4,6},{5,7},{6,4},{7,5},{8,10},{9,11},{10,... | collective-permute-start | bytes 1572872 | tf_op jit(solution)/shard_map/ppermute | solution.py:121
  452.7 6.3 %collective-permute-start.53 = (bf16[128,896]{1,0:T(8,128)(2,1)}, bf16[128,896]{1,0:T(8,128)(2,1)S(1)}, u32[]{:S(2)}, u32[]{:S(2)}) collective-permute-start(bf16[128,896]{1,0:T(8,128)(2,1)} %get-tuple-element.182), channel_id=1, source_target_pairs={{0,4},{8,0},{16,8},{24,16},{28,24},{20,28},{12,20},{4,12},{1,5},{9... | collective-permute-start | bytes 688136 | tf_op jit(solution)/shard_map/ppermute | solution.py:98
  454.2 34.2 %collective-permute-start.34 = (bf16[256,1024]{1,0:T(8,128)(2,1)S(1)}, bf16[256,1024]{1,0:T(8,128)(2,1)S(1)}, u32[]{:S(2)}, u32[]{:S(2)}) collective-permute-start(bf16[256,1024]{1,0:T(8,128)(2,1)S(1)} %add_convert_fusion.3.refs_1_), channel_id=1, source_target_pairs={{0,1},{1,0},{2,3},{3,2},{4,5},{5,4},{6,7},{7,6},{8,9},{9,8},{10,11... | collective-permute-start | bytes 1572872 | tf_op jit(solution)/shard_map/ppermute | solution.py:124
  454.2 8.2 %collective-permute-start.54 = (bf16[128,896]{1,0:T(8,128)(2,1)}, bf16[128,896]{1,0:T(8,128)(2,1)S(1)}, u32[]{:S(2)}, u32[]{:S(2)}) collective-permute-start(bf16[128,896]{1,0:T(8,128)(2,1)} %get-tuple-element.184), channel_id=1, source_target_pairs={{0,8},{8,16},{16,24},{24,28},{28,20},{20,12},{12,4},{4,0},{1,9},{9... | collective-permute-start | bytes 688136 | tf_op jit(solution)/shard_map/ppermute | solution.py:98
  459.0 33.1 %collective-permute-start.35 = (bf16[256,1024]{1,0:T(8,128)(2,1)S(1)}, bf16[256,1024]{1,0:T(8,128)(2,1)}, u32[]{:S(2)}, u32[]{:S(2)}) collective-permute-start(bf16[256,1024]{1,0:T(8,128)(2,1)S(1)} %collective-permute-done.33.refs_2_), channel_id=1, source_target_pairs={{0,1},{1,0},{2,3},{3,2},{4,5},{5,4},{6,7},{7,6},{8,9},{9,8},{10,11... | collective-permute-start | bytes 1572872 | tf_op jit(solution)/shard_map/ppermute | solution.py:124
  462.4 41.0 %collective-permute-start.43 = (bf16[256,1024]{1,0:T(8,128)(2,1)}, bf16[256,1024]{1,0:T(8,128)(2,1)S(1)}, u32[]{:S(2)}, u32[]{:S(2)}) collective-permute-start(bf16[256,1024]{1,0:T(8,128)(2,1)} %input_gradient.1.refs_1_.refs_0_), channel_id=1, source_target_pairs={{0,1},{1,0},{2,3},{3,2},{4,5},{5,4},{6,7},{7,6},{8,9},{9,8},{10,11... | collective-permute-start | bytes 1572872 | tf_op jit(solution)/shard_map/ppermute | solution.py:124
  462.4 41.0 %collective-permute-start.44 = (bf16[256,1024]{1,0:T(8,128)(2,1)S(1)}, bf16[256,1024]{1,0:T(8,128)(2,1)S(1)}, u32[]{:S(2)}, u32[]{:S(2)}) collective-permute-start(bf16[256,1024]{1,0:T(8,128)(2,1)S(1)} %collective-permute-done.42.refs_2_), channel_id=1, source_target_pairs={{0,1},{1,0},{2,3},{3,2},{4,5},{5,4},{6,7},{7,6},{8,9},{9,8},{10,11... | collective-permute-start | bytes 1572872 | tf_op jit(solution)/shard_map/ppermute | solution.py:124
  477.0 8.8 %collective-permute-start.57 = (bf16[128,896]{1,0:T(8,128)(2,1)}, bf16[128,896]{1,0:T(8,128)(2,1)S(1)}, u32[]{:S(2)}, u32[]{:S(2)}) collective-permute-start(bf16[128,896]{1,0:T(8,128)(2,1)} %get-tuple-element.189), channel_id=1, source_target_pairs={{0,4},{8,0},{16,8},{24,16},{28,24},{20,28},{12,20},{4,12},{1,5},{9... | collective-permute-start | bytes 688136 | tf_op jit(solution)/shard_map/ppermute | solution.py:98
  485.9 8.7 %collective-permute-start.60 = (bf16[128,896]{1,0:T(8,128)(2,1)}, bf16[128,896]{1,0:T(8,128)(2,1)S(1)}, u32[]{:S(2)}, u32[]{:S(2)}) collective-permute-start(bf16[128,896]{1,0:T(8,128)(2,1)} %get-tuple-element.193), channel_id=1, source_target_pairs={{0,8},{8,16},{16,24},{24,28},{28,20},{20,12},{12,4},{4,0},{1,9},{9... | collective-permute-start | bytes 688136 | tf_op jit(solution)/shard_map/ppermute | solution.py:98
  488.4 7.6 %collective-permute-start.59 = (bf16[128,896]{1,0:T(8,128)(2,1)}, bf16[128,896]{1,0:T(8,128)(2,1)}, u32[]{:S(2)}, u32[]{:S(2)}) collective-permute-start(bf16[128,896]{1,0:T(8,128)(2,1)} %add_pairs.11), channel_id=1, source_target_pairs={{0,4},{8,0},{16,8},{24,16},{28,24},{20,28},{12,20},{4,12},{1,5},{9... | collective-permute-start | bytes 688136 | tf_op jit(solution)/shard_map/ppermute | solution.py:98
  (63 other events, 430.7 us)
Sparse Core Ops, SparseCore 0:
  37.7 72.7 all-gather.3
  191.4 34.6 all-gather.5
